TPU v7x, 32 devices: a whole 2x2x4 slice. The times are simulated.
32 devices in a mesh: view: 8 (over z, y), tok: 4 (over x, core).
Axes of the slice: x: 2, y: 2, z: 4, core: 2. Of those that a mesh axis runs over, the one named last changes fastest.
Arguments:
- queries: bfloat16 [8, 2, 512, 1024], P('view', None, 'tok'), may hold values from -6 to 6
- keys: bfloat16 [8, 2, 512, 1024], P('view', None, 'tok'), may hold values from -6 to 6
- values: bfloat16 [8, 2, 512, 1024], P('view', None, 'tok'), may hold values from -6 to 6
- tile_mask: int32 [8, 2, 4, 4], P('view'), may hold values from 0 to 1, as said below
- offsets: int32 [8, 2], P('view'), may hold values from -2 to 2, as said below
- branch_slots: int32 [8, 2], replicated, may hold values from 0 to 1, each once within a row
Outputs:
- attended: bfloat16 [8, 2, 512, 1024], P('view', None, 'tok')
Inputs may be any that keep to these rules, and one draw needn't show every extreme that they name: Each row tile_mask[v, j, t, :] holds 1 to 4 ones at consecutive tiles modulo 4; for every v and j some row holds exactly 4. `offsets`: each row holds two different values of -2, -1, 1, 2. `branch_slots`: each row is 0, 1 or 1, 0.
All inputs are finite; a program needn't handle non-finite values.
Results may differ from a plain program's by a relative error of at most 0.0049.
Values may be sent and summed in bfloat16 or wider, within the bound.
No kernel may reach another device: no remote copies, remote signals or barrier semaphores. Data moves between devices by JAX's collectives and lax.ppermute only.
A program may use at most 128 MiB of HBM per device.

v0:
```python
import math

import jax
import jax.numpy as jnp
from jax import lax
from jax.sharding import PartitionSpec as P

HD = 64
TILE = 128
BAND = 6
NB = 2


NEG_SCORE = -1e30


def from_behind(shard, axis, by):
    size = lax.axis_size(axis)
    return lax.ppermute(shard, axis, [(i, (i + by) % size) for i in range(size)])


def fetch_views(stacked):
    nearby = {}
    for distance in (1, -1, 2, -2):
        nearby[distance] = from_behind(stacked, "view", -distance)
    return nearby


def pick_neighbour(nearby, offsets, branch_slots, member):
    offset_value = offsets[0, member]
    picked = nearby[1]
    for distance in (-1, 2, -2):
        picked = jnp.where(offset_value == distance, nearby[distance], picked)
    view_count = branch_slots.shape[0]
    view_index = lax.axis_index("view")
    other_view = (view_index + offset_value) % view_count
    rows = jnp.arange(view_count, dtype=jnp.int32)
    other_slot = jnp.sum(jnp.where(rows == other_view, branch_slots[:, 0], 0))
    own_slot = jnp.sum(jnp.where(rows == view_index, branch_slots[:, 0], 0))
    return jnp.where(other_slot != own_slot, picked[:, ::-1], picked)


def local(queries, keys, values, tile_mask, offsets, branch_slots):
    stacked = jnp.concatenate([keys, values], axis=0)
    heads_q, heads_kv = (
        lax.all_to_all(queries, "tok", split_axis=3, concat_axis=2, tiled=True),
        lax.all_to_all(stacked, "tok", split_axis=3, concat_axis=2, tiled=True),
    )
    nearby = fetch_views(heads_kv)
    first_nb = pick_neighbour(nearby, offsets, branch_slots, 0)
    second_nb = pick_neighbour(nearby, offsets, branch_slots, 1)
    tile_len = TILE
    view_len = heads_q.shape[2]
    heads_width = heads_q.shape[3]
    heads_here = heads_width // HD
    key_tiles = view_len // tile_len
    tile_most = min(BAND, key_tiles)
    group_len = math.gcd(key_tiles, max(1, 512 // tile_len))
    group_count = key_tiles // group_len
    masks = tile_mask[0]
    tile_count = jnp.sum(masks, axis=-1)
    chosen = jnp.argsort(1 - masks, axis=-1, stable=True)[..., :tile_most]
    valid = jnp.arange(tile_most, dtype=jnp.int32)[None, None, :] < tile_count[..., None]
    query_all = heads_q[0].reshape(2, key_tiles, tile_len, heads_here, HD)
    own_kv = heads_kv.reshape(2, 2, key_tiles, tile_len, heads_here, HD)
    neighbours = jnp.stack([first_nb, second_nb]).reshape(
        NB, 2, 2, key_tiles, tile_len, heads_here, HD
    )

    def block_attend(group_index):
        start = group_index * group_len
        query_block = lax.dynamic_slice_in_dim(query_all, start, group_len, 1)
        own_block = lax.dynamic_slice_in_dim(own_kv, start, group_len, 2)
        picked_tiles = lax.dynamic_slice_in_dim(chosen, start, group_len, 1)
        picked_valid = lax.dynamic_slice_in_dim(valid, start, group_len, 1)
        gathered = jnp.stack(
            [neighbours[member][:, :, picked_tiles[member]] for member in range(NB)], axis=3
        )
        gathered = gathered.reshape(2, 2, group_len, NB * tile_most * tile_len, heads_here, HD)
        key_block = jnp.concatenate([own_block, gathered], axis=3)
        keep_far = jnp.repeat(picked_valid, tile_len, axis=-1)
        keep_far = jnp.transpose(keep_far, (1, 0, 2)).reshape(group_len, NB * tile_most * tile_len)
        keep_mask = jnp.concatenate([jnp.ones((group_len, tile_len), bool), keep_far], axis=1)
        scores = jnp.einsum(
            "bgqhd,bgkhd->bghqk", query_block, key_block[0], preferred_element_type=jnp.float32
        ) * HD ** (-0.5)
        scores = jnp.where(keep_mask[None, :, None, None, :], scores, NEG_SCORE)
        row_max = jnp.max(scores, axis=-1, keepdims=True)
        expo = jnp.exp(scores - row_max)
        row_total = jnp.sum(expo, axis=-1, keepdims=True)
        weights = (expo / row_total).astype(jnp.bfloat16)
        result = jnp.einsum(
            "bghqk,bgkhd->bgqhd", weights, key_block[1], preferred_element_type=jnp.float32
        )
        return result.astype(jnp.bfloat16)

    blocks = lax.map(block_attend, jnp.arange(group_count, dtype=jnp.int32))
    attended_heads = jnp.moveaxis(blocks, 0, 1).reshape(1, 2, view_len, heads_width)
    return lax.all_to_all(attended_heads, "tok", split_axis=2, concat_axis=3, tiled=True)


def solution(mesh):
    in_specs = (
        P("view", None, "tok", None),
        P("view", None, "tok", None),
        P("view", None, "tok", None),
        P("view", None, None, None),
        P("view", None),
        P(),
    )
    out_specs = P("view", None, "tok", None)
    return jax.shard_map(local, mesh=mesh, in_specs=in_specs, out_specs=out_specs, check_vma=False)
```

profile of v0, /device:TPU:0, one launch (start us, length us, event | category | flops | bytes accessed | tf_op | source)
XLA Modules:
  0.0 208.8 jit_solution(10811268173891379103)
XLA Ops:
  0.0 1.3 copy.40
  1.3 1.3 copy.41
  2.6 2.5 %pad_maximum_fusion.2 = bf16[2,2,128,1024]{2,1,0,3:T(2,128)(2,1)} fusion(bf16[1,2,128,1024]{2,1,0,3:T(2,128)(2,1)S(1)} %copy.41, bf16[1,2,128,1024]{2,1,0,3:T(2,128)(2,1)S(1)} %copy.40), kind=kLoop, calls=%fused_computation.26 | loop fusion | flops 524288 | bytes 2097152 | tf_op jit(solution)/shard_map/concatenate | solution.py:44
  5.1 4.2 %all-to-all-start = ((bf16[2,2,128,1024]{2,1,0,3:T(2,128)(2,1)}), bf16[2,2,128,1024]{2,1,0,3:T(2,128)(2,1)S(1)}, u32[]{:S(2)}, u32[]{:S(2)}) async-start(bf16[2,2,128,1024]{2,1,0,3:T(2,128)(2,1)} %pad_maximum_fusion.2), calls=%async_computation | async-start | bytes 2097152 | tf_op jit(solution)/shard_map/all_to_all | solution.py:47
  9.3 1.4 fusion.31
  16.1 1.4 fusion.22
  20.0 2.0 copy.52
  22.0 0.8 fusion.29
  22.8 1.0 all-to-all-done
  23.8 3.5 %all-to-all-start.1 = ((bf16[1,2,128,1024]{2,1,0,3:T(2,128)(2,1)}), bf16[1,2,128,1024]{2,1,0,3:T(2,128)(2,1)S(1)}, u32[]{:S(2)}, u32[]{:S(2)}) async-start(bf16[1,2,128,1024]{2,1,0,3:T(2,128)(2,1)} %copy.52), calls=%async_computation.1 | async-start | bytes 1048576 | tf_op jit(solution)/shard_map/all_to_all | solution.py:46
  27.3 0.1 copy.42
  27.4 1.3 copy.43
  28.7 5.3 %collective-permute-start.3 = (bf16[2,2,512,256]{3,2,1,0:T(8,128)(2,1)}, bf16[2,2,512,256]{3,2,1,0:T(8,128)(2,1)S(1)}, u32[]{:S(2)}, u32[]{:S(2)}) collective-permute-start(bf16[2,2,512,256]{3,2,1,0:T(8,128)(2,1)} %bitcast.84), channel_id=1, source_target_pairs={{0,28},{4,0},{8,4},{12,8},{16,12},{20,16},{24,20},{28,24},{1,29},{... | collective-permute-start | bytes 3145736 | tf_op jit(solution)/shard_map/ppermute | solution.py:19
  34.0 1.1 collective-permute-start.1
  35.1 1.0 collective-permute-start
  36.1 0.1 iota_compare_fusion
  36.1 0.1 broadcast_in_dim.44
  36.2 0.1 copy.45
  36.3 0.7 sort.17
  37.0 0.1 copy.46
  37.1 0.1 reshape.93
  37.2 0.1 copy.49
  37.3 0.1 reshape.101
  37.4 0.9 copy.53
  38.3 39.1 %collective-permute-done.3 = bf16[2,2,512,256]{3,2,1,0:T(8,128)(2,1)S(1)} collective-permute-done((bf16[2,2,512,256]{3,2,1,0:T(8,128)(2,1)}, bf16[2,2,512,256]{3,2,1,0:T(8,128)(2,1)S(1)}, u32[]{:S(2)}, u32[]{:S(2)}) %collective-permute-start.3) | collective-permute-done | bytes 1048608 | tf_op jit(solution)/shard_map/ppermute | solution.py:19
  77.5 0.3 collective-permute-done.2
  77.7 2.6 %collective-permute-done.1 = bf16[2,2,512,256]{3,2,1,0:T(8,128)(2,1)} collective-permute-done((bf16[2,2,512,256]{3,2,1,0:T(8,128)(2,1)}, bf16[2,2,512,256]{3,2,1,0:T(8,128)(2,1)}, u32[]{:S(2)}, u32[]{:S(2)}) %collective-permute-start.1) | collective-permute-done | bytes 1048608 | tf_op jit(solution)/shard_map/ppermute | solution.py:19
  80.3 22.9 %collective-permute-done = bf16[2,2,512,256]{3,2,1,0:T(8,128)(2,1)} collective-permute-done((bf16[2,2,512,256]{3,2,1,0:T(8,128)(2,1)}, bf16[2,2,512,256]{3,2,1,0:T(8,128)(2,1)}, u32[]{:S(2)}, u32[]{:S(2)}) %collective-permute-start) | collective-permute-done | bytes 1048608 | tf_op jit(solution)/shard_map/ppermute | solution.py:19
  103.3 2.1 select_select_fusion.1
  105.4 0.4 reverse_select_fusion
  105.8 1.9 reshape.110
  107.7 2.8 %copy.50 = bf16[2,2,4,128,4,64]{3,5,4,2,1,0:T(8,128)(2,1)S(1)} copy(bf16[2,2,4,128,4,64]{5,4,3,2,1,0:T(4,128)(2,1)} %reshape.110) | data formatting | bytes 2097152 | tf_op jit(solution)/shard_map/while/body/eval_jaxpr/squeeze | solution.py:77
  110.5 1.9 reshape.109
  112.4 2.8 %copy.47 = bf16[2,2,4,128,4,64]{3,5,4,2,1,0:T(8,128)(2,1)S(1)} copy(bf16[2,2,4,128,4,64]{5,4,3,2,1,0:T(4,128)(2,1)} %reshape.109) | data formatting | bytes 2097152 | tf_op jit(solution)/shard_map/while/body/eval_jaxpr/squeeze | solution.py:77
  115.2 3.0 %gather_fusion = bf16[16,2,2,128,4,64]{3,5,4,2,1,0:T(8,128)(2,1)} fusion(bf16[2,2,4,128,4,64]{3,5,4,2,1,0:T(8,128)(2,1)S(1)} %copy.47, s32[1024]{0:T(1024)S(1)} %pad_clamp_fusion.1), kind=kCustom, calls=%fused_computation | custom fusion | bytes 8388672 | tf_op jit(solution)/shard_map/while/body/eval_jaxpr/gather | solution.py:77
  118.3 3.1 %gather_fusion.1 = bf16[16,2,2,128,4,64]{3,5,4,2,1,0:T(8,128)(2,1)} fusion(bf16[2,2,4,128,4,64]{3,5,4,2,1,0:T(8,128)(2,1)S(1)} %copy.50, s32[1024]{0:T(1024)S(1)} %pad_clamp_fusion), kind=kCustom, calls=%fused_computation.1 | custom fusion | bytes 8388672 | tf_op jit(solution)/shard_map/while/body/eval_jaxpr/gather | solution.py:77
  121.3 7.5 %pad_maximum_fusion = bf16[2,2,4,2,4,128,4,64]{5,7,6,1,0,4,2,3:T(8,128)(2,1)} fusion(bf16[2,2,4,1,4,128,4,64]{5,7,6,1,0,4,2,3:T(8,128)(2,1)} %bitcast.76, bf16[2,2,4,1,4,128,4,64]{5,7,6,1,0,4,2,3:T(8,128)(2,1)} %bitcast.75), kind=kLoop, calls=%fused_computation.15 | loop fusion | flops 4194304 | bytes 16777216 | tf_op jit(solution)/shard_map/while/body/eval_jaxpr/stack | solution.py:76
  128.8 11.1 %copy.51 = bf16[2,2,4,2,4,128,4,64]{5,4,3,7,6,2,1,0:T(4,128)(2,1)} copy(bf16[2,2,4,2,4,128,4,64]{5,7,6,1,0,4,2,3:T(8,128)(2,1)} %pad_maximum_fusion) | data formatting | bytes 16777216 | tf_op jit(solution)/shard_map/while/body/eval_jaxpr/stack | solution.py:76
  139.9 14.3 %reshape.88 = bf16[2,2,4,1024,4,64]{3,5,4,2,1,0:T(8,128)(2,1)} reshape(bf16[2,2,4,2,4,128,4,64]{5,4,3,7,6,2,1,0:T(4,128)(2,1)} %copy.51) | data formatting | bytes 16777216 | tf_op jit(solution)/shard_map/while/body/eval_jaxpr/reshape | solution.py:79
  154.2 9.5 %fusion.13 = f32[2,4,4,1152,128]{4,3,2,1,0:T(8,128)} fusion(bf16[2,4,128,4,64]{2,4,3,1,0:T(8,128)(2,1)S(1)} %bitcast.80, bf16[2,2,4,1024,4,64]{3,5,4,2,1,0:T(8,128)(2,1)} %reshape.88, bf16[2,2,4,128,4,64]{3,5,4,2,1,0:T(8,128)(2,1)S(1)} %bitcast.78), kind=kOutput, calls=%fused_computation.20 | convolution fusion | flops 613416960 | bytes 28835840 | tf_op jit(solution)/shard_map/while/body/eval_jaxpr/bgqhd,bgkhd->bghqk/dot_general | solution.py:84
  163.8 21.5 %fusion.32 = (f32[2,4,4,128]{3,2,1,0:T(4,128)S(1)}, f32[2,4,4,128,1152]{3,4,2,1,0:T(8,128)}) fusion(f32[2,4,4,1152,128]{4,3,2,1,0:T(8,128)} %fusion.13, pred[4,1152]{1,0:T(4,128)(4,1)S(1)} %concatenate.13), kind=kOutput, calls=%fused_computation.48 | output fusion | flops 28312704 | bytes 37769728 | tf_op jit(solution)/shard_map/while/body/eval_jaxpr/sub | solution.py:89
  185.3 9.2 %fusion.19 = bf16[2,4,128,4,64]{2,4,3,1,0:T(8,128)(2,1)S(1)} fusion(f32[2,4,4,128,1152]{3,4,2,1,0:T(8,128)} %get-tuple-element.40, f32[2,4,4,128]{3,2,1,0:T(4,128)S(1)} %get-tuple-element.39, bf16[2,2,4,128,4,64]{3,5,4,2,1,0:T(8,128)(2,1)S(1)} %bitcast.79, bf16[2,2,4,1024,4,64]{3,5,4,2,1,0:T(8,128)(2,1)} %reshape.88), kind=kOutput, calls=%fused_computation.25 | convolution fusion | flops 623116288 | bytes 28852224 | tf_op jit(solution)/shard_map/while/body/eval_jaxpr/bghqk,bgkhd->bgqhd/dot_general | solution.py:92
  194.5 0.7 copy.65
  195.2 0.6 reshape.111
  195.9 11.6 %all_to_all.51 = bf16[1,2,512,256]{3,1,0,2:T(2,128)(2,1)S(1)} all-to-all(bf16[1,2,512,256]{3,1,0,2:T(2,128)(2,1)S(1)} %reshape.111), channel_id=1, replica_groups=mesh['view'=8,'tok'=4] {'tok'}, dimensions={2} | all-to-all | bytes 1048576 | tf_op jit(solution)/shard_map/all_to_all | solution.py:99
  207.4 0.1 copy.57
  207.5 0.3 copy.58
  207.8 1.0 copy.59
  (12 shorter events, 0.1 us)
Async XLA Ops:
  5.1 18.7 %all-to-all-start = ((bf16[2,2,128,1024]{2,1,0,3:T(2,128)(2,1)}), bf16[2,2,128,1024]{2,1,0,3:T(2,128)(2,1)S(1)}, u32[]{:S(2)}, u32[]{:S(2)}) async-start(bf16[2,2,128,1024]{2,1,0,3:T(2,128)(2,1)} %pad_maximum_fusion.2), calls=%async_computation | async-start | bytes 2097152 | tf_op jit(solution)/shard_map/all_to_all | solution.py:47
  23.8 13.7 %all-to-all-start.1 = ((bf16[1,2,128,1024]{2,1,0,3:T(2,128)(2,1)}), bf16[1,2,128,1024]{2,1,0,3:T(2,128)(2,1)S(1)}, u32[]{:S(2)}, u32[]{:S(2)}) async-start(bf16[1,2,128,1024]{2,1,0,3:T(2,128)(2,1)} %copy.52), calls=%async_computation.1 | async-start | bytes 1048576 | tf_op jit(solution)/shard_map/all_to_all | solution.py:46
  28.7 48.7 %collective-permute-start.3 = (bf16[2,2,512,256]{3,2,1,0:T(8,128)(2,1)}, bf16[2,2,512,256]{3,2,1,0:T(8,128)(2,1)S(1)}, u32[]{:S(2)}, u32[]{:S(2)}) collective-permute-start(bf16[2,2,512,256]{3,2,1,0:T(8,128)(2,1)} %bitcast.84), channel_id=1, source_target_pairs={{0,28},{4,0},{8,4},{12,8},{16,12},{20,16},{24,20},{28,24},{1,29},{... | collective-permute-start | bytes 3145736 | tf_op jit(solution)/shard_map/ppermute | solution.py:19
  34.0 43.7 %collective-permute-start.2 = (bf16[2,2,512,256]{3,2,1,0:T(8,128)(2,1)}, bf16[2,2,512,256]{3,2,1,0:T(8,128)(2,1)}, u32[]{:S(2)}, u32[]{:S(2)}) collective-permute-start(bf16[2,2,512,256]{3,2,1,0:T(8,128)(2,1)} %bitcast.85), channel_id=1, source_target_pairs={{0,4},{4,8},{8,12},{12,16},{16,20},{20,24},{24,28},{28,0},{1,5},{5... | collective-permute-start | bytes 3145736 | tf_op jit(solution)/shard_map/ppermute | solution.py:19
  34.0 46.3 %collective-permute-start.1 = (bf16[2,2,512,256]{3,2,1,0:T(8,128)(2,1)}, bf16[2,2,512,256]{3,2,1,0:T(8,128)(2,1)}, u32[]{:S(2)}, u32[]{:S(2)}) collective-permute-start(bf16[2,2,512,256]{3,2,1,0:T(8,128)(2,1)} %bitcast.86), channel_id=1, source_target_pairs={{0,24},{4,28},{8,0},{12,4},{16,8},{20,12},{24,16},{28,20},{1,25},{... | collective-permute-start | bytes 3145736 | tf_op jit(solution)/shard_map/ppermute | solution.py:19
  35.1 68.2 %collective-permute-start = (bf16[2,2,512,256]{3,2,1,0:T(8,128)(2,1)}, bf16[2,2,512,256]{3,2,1,0:T(8,128)(2,1)}, u32[]{:S(2)}, u32[]{:S(2)}) collective-permute-start(bf16[2,2,512,256]{3,2,1,0:T(8,128)(2,1)} %bitcast.87), channel_id=1, source_target_pairs={{0,8},{4,12},{8,16},{12,20},{16,24},{20,28},{24,0},{28,4},{1,9},{5... | collective-permute-start | bytes 3145736 | tf_op jit(solution)/shard_map/ppermute | solution.py:19
  139.9 14.3 %copy-start = (bf16[1,2,128,4,256]{2,4,3,1,0:T(8,128)(2,1)S(1)}, bf16[1,2,128,4,256]{2,4,3,1,0:T(8,128)(2,1)}, u32[]{:S(2)}) copy-start(bf16[1,2,128,4,256]{2,4,3,1,0:T(8,128)(2,1)} %copy.53) | copy-start | bytes 1572868
where the time goes:
time: 211 us; the launch traced here: 209 us
  waiting for transfers between devices  66 us (31%)
  local copies, waits for them, and re-layouts  52.5 us (25%)
  other arithmetic  37 us (18%)
  matrix products  18.8 us (9%)
  starting transfers between devices  15 us (7%)
  blocking collectives  11.6 us (5%)
  between operations  7.99 us (4%)
    ppermute x4, waiting for transfers between devices, from_behind(): lax.ppermute(shard, axis, [(i, (i + by) % size) for i in range(size)])  65 us
    sub x1, other arithmetic, block_attend(): expo = jnp.exp(scores - row_max)  21.5 us
    reshape x1, local copies, waits for them, and re-layouts, block_attend(): gathered.reshape(2, 2, group_len, NB * tile_most * tile_len, heads_here, HD)  14.3 us
    all_to_all x1, blocking collectives, local(): lax.all_to_all(attended_heads, 'tok', split_axis=2, concat_axis=3, tiled=...  11.6 us
    another operation x1, local copies, waits for them, and re-layouts, block_attend(): jnp.stack([neighbours[member][:, :, picked_tiles[member]] for member in r...  11.1 us
    dot_general x1, matrix products, block_attend(): jnp.einsum('bgqhd,bgkhd->bghqk', query_block, key_block[0], preferred_ele...  9.55 us
    squeeze x4, local copies, waits for them, and re-layouts, block_attend(): neighbours[member][:, :, picked_tiles[member]]  9.38 us
    dot_general x1, matrix products, block_attend(): jnp.einsum('bghqk,bgkhd->bgqhd', weights, key_block[1], preferred_element...  9.23 us
  transfers between devices with their start and end apart: 6, of which 5 were waited for; matrix products, arithmetic and copies ran while one was open for 4% of the time, Pallas kernels for 0%

commit v1 on v0

v1 whole, which is shorter than its diff:
```python
import functools
import math

import jax
import jax.numpy as jnp
from jax import lax
from jax.experimental import pallas as pl
from jax.experimental.pallas import tpu as pltpu
from jax.sharding import Mesh, PartitionSpec as P

HD = 64
TILE = 128
NB = 2
REACH = 2
MARK_FLOPS = (4 * 10 ** 9, 10 ** 10)
GROUP = ("sub", "tok")

NEG_SCORE = -1e30

SMEM = pl.BlockSpec(memory_space=pltpu.SMEM)
VMEM = pl.BlockSpec(memory_space=pltpu.VMEM)
ANY = pl.BlockSpec(memory_space=pl.ANY)


def after(x, *others):
    return lax.optimization_barrier((x, others))[0]


def from_plane(x, by):
    size = lax.axis_size("plane")
    return lax.ppermute(x, "plane", [((i + by) % size, i) for i in range(size)])


def exchange(x):
    return lax.all_to_all(x, GROUP, split_axis=0, concat_axis=0, tiled=True)


class Move:
    def __init__(self, array, branch, piece, planes=0, row=0, rows=TILE, pitch=TILE, to=0):
        self.array, self.branch, self.piece, self.planes = array, branch, piece, planes
        self.row, self.rows, self.pitch, self.to = row, rows, pitch, to


def slot_of(plan, slots_ref, planes, branch):
    views = slots_ref.shape[1]
    view = (lax.axis_index("plane") + planes) * plan.sub + lax.axis_index("sub") + views
    return slots_ref[branch, lax.rem(view, views)]


def pack_kernel(plan, moves, staged, slots_ref, mark_ref, *refs):
    if staged:
        *ins, out, sem, stage, stage_sem = refs
    else:
        *ins, out, sem = refs
    ways, tiles, _, _, share = out.shape
    sources = []
    for i, move in enumerate(moves):
        slot = slot_of(plan, slots_ref, move.planes, move.branch)
        for m in range(tiles):
            rows = pl.ds(m * move.pitch + move.row, move.rows)
            source = ins[move.array].at[0, slot, rows]
            if staged:
                there = stage.at[i, m, pl.ds(0, move.rows)]
                copy = pltpu.make_async_copy(source, there, stage_sem.at[i, m])
                copy.start()
                sources.append((move, m, there, copy))
            else:
                sources.append((move, m, source, None))
    for move, m, source, copy in sources:
        if copy is not None:
            copy.wait()
        for w in range(ways):
            to, lanes = pl.ds(move.to, move.rows), pl.ds(w * share, share)
            if plan.whole_lanes:
                pltpu.make_async_copy(
                    source.at[:, lanes], out.at[w, m, move.piece, to], sem
                ).start()
            else:
                out[w, m, move.piece, to] = source[:, lanes]
    if plan.whole_lanes:
        pltpu.make_async_copy(out, out, sem).wait()


def last_kernel(plan, slots_ref, x0, x1, out, sem):
    ways, tiles, _, _, share = x0.shape
    for b, x in enumerate((x0, x1)):
        slot = slot_of(plan, slots_ref, 0, b)
        for m in range(tiles):
            for w in range(ways):
                rows, lanes = pl.ds(m * TILE, TILE), pl.ds(w * share, share)
                if plan.whole_lanes:
                    pltpu.make_async_copy(x.at[w, m, 0], out.at[0, slot, rows, lanes], sem).start()
                else:
                    out[0, slot, rows, lanes] = x[w, m, 0]
    if plan.whole_lanes:
        pltpu.make_async_copy(out, out, sem).wait()


class Plan:
    def __init__(self, sub, kt, hops, share):
        self.sub, self.kt, self.hops, self.share = sub, kt, hops, share
        self.planes = 2 * hops + 1
        self.heads = share // HD
        self.rows = self.heads * TILE
        self.cols = (1 + NB * kt) * TILE
        self.pairs = sub * kt * self.rows * self.cols
        self.whole_lanes = share % 128 == 0


def fact(plan, facts, g, i):
    own_ref, other_ref = facts
    if plan.sub == 1:
        return own_ref[i]
    return jnp.where(lax.axis_index("sub") == g, own_ref[i], other_ref[i])


def start_far(plan, facts, copies_of):
    for g in range(plan.sub):
        for j in range(NB):
            at = fact(plan, facts, g, NB * plan.kt * plan.kt + j) + (plan.hops * plan.sub + g)
            tiles_at = lax.rem(at, plan.sub) * plan.kt
            for d in range(plan.planes):
                @pl.when(lax.div(at, plan.sub) == d)
                def _():
                    for copy in copies_of(g, j, d, tiles_at):
                        copy.start()


def mark_kernel(*refs):
    refs[-1][...] = jnp.zeros_like(refs[-1])


def head_of_lane(plan):
    return lax.broadcasted_iota(jnp.int32, (TILE, plan.share), 1) // HD


def split_heads(plan, q):
    if plan.heads == 1:
        return q
    block = head_of_lane(plan)
    return jnp.concatenate([jnp.where(block == h, q, 0) for h in range(plan.heads)], axis=0)


def scores_of(q, k):
    return lax.dot_general(q, k, (((1,), (1,)), ((), ())), preferred_element_type=jnp.float32)


def numerators(plan, facts, g, t, own, far):
    factor = HD ** -0.5 * math.log2(math.e)
    parts = [own]
    for j in range(NB):
        for k in range(plan.kt):
            keep = fact(plan, facts, g, (j * plan.kt + t) * plan.kt + k) == 1
            bias = jnp.where(keep, 0.0, NEG_SCORE)
            parts.append(far[j][:, k * TILE:(k + 1) * TILE] + bias)
    top = functools.reduce(jnp.maximum, parts)
    top = jnp.max(top, axis=1, keepdims=True)
    return [jnp.exp2((part - top) * factor).astype(jnp.bfloat16) for part in parts]


def weigh(p, v):
    v = jnp.concatenate([v, jnp.ones_like(v)], axis=1)
    return jnp.dot(p, v, preferred_element_type=jnp.float32)


def finish(plan, total):
    result = total[:TILE]
    block = head_of_lane(plan)
    both = jnp.concatenate([block, block], axis=1)
    for h in range(1, plan.heads):
        result = jnp.where(both == h, total[h * TILE:(h + 1) * TILE], result)
    return (result[:, :plan.share] / result[:, plan.share:]).astype(jnp.bfloat16)


def far_rows(plan, buffer, g, j):
    return buffer[g, j].reshape(plan.kt * TILE, plan.share)


def attend_kernel(plan, branch, weighs, n_early, n_late, own, other, *refs):
    scores = n_early > 0
    h = plan.hops
    facts = (own, other)
    given, refs = refs[0], refs[1:]
    planes, late = refs[:n_early], refs[n_early:n_early + n_late]
    out, result, k_far, v_far, far_sem, out_sem = refs[-6:]
    mixed = given
    half = TILE // 2
    mine, low, high = pl.ds(branch * half, half), pl.ds(0, half), pl.ds(half, half)

    def values_at(d, tiles):
        return late[d].at[tiles, 0] if late else planes[d].at[tiles, 1]

    def far_copies(g, j, d, tiles_at):
        tiles = pl.ds(tiles_at, plan.kt)
        found = []
        if scores:
            found.append((mixed.at[tiles, 2 + d, mine], k_far.at[g, j, :, low]))
            found.append((planes[d].at[tiles, 0, mine], k_far.at[g, j, :, high]))
        if weighs:
            found.append((values_at(d, tiles), v_far.at[g, j]))
        return [
            pltpu.make_async_copy(src, to, far_sem.at[i, g, j]) for i, (src, to) in enumerate(found)
        ]

    start_far(plan, facts, far_copies)
    count = math.gcd(plan.kt, 4)
    rows, wide = plan.rows, plan.kt * TILE

    def some_tiles(g, t0):
        tiles = [(g * plan.kt + t0 + i, t0 + i) for i in range(count)]
        if scores:
            q = [split_heads(plan, mixed[at, branch]) for at, _ in tiles]
            k_own = [
                jnp.concatenate([mixed[at, 2 + h, mine], planes[h][at, 0, mine]], axis=0)
                for at, _ in tiles
            ]
            own_scores = [scores_of(a, b) for a, b in zip(q, k_own)]
            q = jnp.concatenate(q, axis=0)
            far = [scores_of(q, far_rows(plan, k_far, g, j)) for j in range(NB)]
            expo = [
                numerators(
                    plan, facts, g, t, own_scores[i],
                    [far[j][i * rows:(i + 1) * rows] for j in range(NB)],
                )
                for i, (_, t) in enumerate(tiles)
            ]
            if not weighs:
                for (at, _), parts in zip(tiles, expo):
                    for i, part in enumerate(parts):
                        out[at, :, i * TILE:(i + 1) * TILE] = part
                return
            expo_own = [parts[0] for parts in expo]
            expo_far = [
                jnp.concatenate([
                    jnp.concatenate(parts[1 + j * plan.kt:1 + (j + 1) * plan.kt], axis=1)
                    for parts in expo
                ], axis=0)
                for j in range(NB)
            ]
        else:
            expo_own = [given[at, :, :TILE] for at, _ in tiles]
            expo_far = [
                jnp.concatenate([
                    given[at, :, TILE + j * wide:TILE + (j + 1) * wide] for at, _ in tiles
                ], axis=0)
                for j in range(NB)
            ]
        total = sum(weigh(expo_far[j], far_rows(plan, v_far, g, j)) for j in range(NB))
        for i, (at, _) in enumerate(tiles):
            v_own = late[h][at, 0] if late else planes[h][at, 1]
            mine_too = total[i * rows:(i + 1) * rows] + weigh(expo_own[i], v_own)
            result[at, 0] = finish(plan, mine_too)

    def one_view(g, carry):
        for j in range(NB):
            for copy in far_copies(g, j, plan.hops, 0):
                copy.wait()
        if count == plan.kt:
            some_tiles(g, 0)
        else:
            def some(i, c):
                some_tiles(g, i * count)
                return c
            lax.fori_loop(0, plan.kt // count, some, 0)
        if weighs:
            tiles = pl.ds(g * plan.kt, plan.kt)
            pltpu.make_async_copy(result.at[tiles], out.at[tiles], out_sem).start()
        return carry

    lax.fori_loop(0, plan.sub, one_view, 0)
    if weighs:
        pltpu.make_async_copy(result, out, out_sem).wait()


def call(kernel, name, out_shape, in_specs, out_specs, scratch, args, flops=0, exps=0, moved=0,
         mib=8):
    return pl.pallas_call(
        kernel,
        out_shape=out_shape,
        in_specs=in_specs,
        out_specs=out_specs,
        scratch_shapes=scratch,
        compiler_params=pltpu.CompilerParams(vmem_limit_bytes=mib * 2 ** 20),
        cost_estimate=pl.CostEstimate(flops=flops, bytes_accessed=moved, transcendentals=exps),
        name=name,
    )(*args)


def local(queries, keys, values, tile_mask, offsets, branch_slots):
    sub, toks = lax.axis_size("sub"), lax.axis_size("tok")
    ways = sub * toks
    dtype = queries.dtype
    _, _, tokens, width = queries.shape
    tiles, share = tokens // TILE, width // ways
    kt = toks * tiles
    hops = -(-REACH // sub)
    plan = Plan(sub, kt, hops, share)
    shifts = [d for d in range(-hops, hops + 1) if d]
    order = range(-hops, hops + 1)
    half = TILE // 2
    size = queries.size * 2

    slots = branch_slots.T
    own = jnp.concatenate([tile_mask.reshape(-1), offsets.reshape(-1)])
    other = own
    if sub == 2:
        other = lax.ppermute(own, "sub", [(0, 1), (1, 0)])
    facts = (own, other)

    place = ANY if plan.whole_lanes else VMEM
    sem = pltpu.SemaphoreType.DMA(())

    def pack(name, arrays, moves, pieces, staged=False, mark=None):
        staged = staged and plan.whole_lanes
        scratch = [sem]
        if staged:
            scratch.append(pltpu.VMEM((len(moves), tiles, TILE, width), dtype))
            scratch.append(pltpu.SemaphoreType.DMA((len(moves), tiles)))
        return call(
            functools.partial(pack_kernel, plan, moves, staged), name,
            jax.ShapeDtypeStruct((ways, tiles, pieces, TILE, share), dtype),
            [SMEM, ANY] + [ANY if staged else VMEM] * len(arrays), place, scratch,
            (slots, slots if mark is None else mark, *arrays), moved=pieces * size,
            mib=62 if staged else 16,
        )

    def spread(x):
        return exchange(x).reshape(ways * tiles, x.shape[2], TILE, share)

    def around(x, chain=False):
        found, last = {0: x}, ()
        for d in shifts:
            found[d] = from_plane(after(x, last), d)
            last = found[d] if chain else ()
        return found

    def mark(arrays, flops):
        return call(
            mark_kernel, "mark", jax.ShapeDtypeStruct((8, 128), jnp.float32),
            [ANY] * len(arrays), VMEM, [], arrays, flops=flops,
        )

    raw = keys.reshape(1, 2, tiles, TILE, width)[:, :, :, :half].reshape(1, 2, tiles * half, width)
    raw = around(raw, chain=True)
    packed = pack(
        "first", [keys, values],
        [Move(0, b, 0, row=half, rows=half, to=b * half) for b in range(2)]
        + [Move(1, b, 1 + b) for b in range(2)], 3, staged=True,
    )
    early = spread(packed)
    arrived = mark([raw[d] for d in shifts], MARK_FLOPS[0])
    early, arrived, facts = lax.optimization_barrier((early, arrived, facts))

    planes = around(early[:, :2])
    brought = mark([planes[d] for d in shifts], MARK_FLOPS[1])
    last_values, brought = lax.optimization_barrier((early[:, 2:], brought))
    late = around(last_values)
    moves = [Move(0, 0, 0), Move(0, 1, 1)]
    for d in order:
        for b in range(2):
            moves.append(Move(
                1 + d + hops, b, 2 + d + hops, planes=d, rows=half, pitch=half, to=b * half
            ))
    packed = pack(
        "second", [queries, *[raw[d] for d in order]], moves, 2 + plan.planes, mark=arrived
    )
    mixed = spread(packed)
    planes[0] = early
    planes = [planes[d] for d in order]
    late = [late[d] for d in order]

    result = (ways * tiles, 1, TILE, share)

    def attend(name, branch, given, planes, late, weighs, out_shape):
        far = pltpu.VMEM((sub, NB, kt, TILE, share), dtype)
        ins = [given] + planes + late
        parts = (1 if planes else 0) + (1 if weighs else 0)
        return call(
            functools.partial(attend_kernel, plan, branch, weighs, len(planes), len(late)), name,
            jax.ShapeDtypeStruct(out_shape, dtype),
            [SMEM] * 2 + [VMEM] * len(ins) + [ANY], ANY if weighs else VMEM,
            [pltpu.VMEM(result, dtype), far, far, pltpu.SemaphoreType.DMA((3, sub, NB)), sem],
            (*facts, *ins, brought), flops=plan.pairs * HD * 2 * parts,
            exps=plan.pairs if planes else 0, moved=2 * size, mib=24,
        )

    def back(x):
        return exchange(x.reshape(ways, tiles, 1, TILE, share))

    x0 = back(attend("attend", 0, mixed, planes, [], True, result))
    expo = attend(
        "scores", 1, mixed, planes, [], False, (sub * kt, plan.rows, plan.cols)
    )
    x1 = back(attend("weigh", 1, expo, [], late, True, result))
    return call(
        functools.partial(last_kernel, plan), "last",
        jax.ShapeDtypeStruct(queries.shape, dtype), [SMEM, place, place], place, [sem],
        (slots, x0, x1), moved=2 * size,
    )


def solution(mesh):
    views, toks = mesh.shape["view"], mesh.shape["tok"]

    def run(queries, keys, values, tile_mask, offsets, branch_slots):
        heads = queries.shape[-1] // HD
        sub = 2 if views % 2 == 0 and heads % (2 * toks) == 0 else 1
        fine = Mesh(mesh.devices.reshape(views // sub, sub, toks), ("plane", "sub", "tok"))
        view = ("plane", "sub")
        shard = P(view, None, "tok", None)
        in_specs = (shard, shard, shard, P(view, None, None, None), P(view, None), P())
        return jax.shard_map(
            local, mesh=fine, in_specs=in_specs, out_specs=shard, check_vma=False
        )(queries, keys, values, tile_mask, offsets, branch_slots)

    return run
```

time: 211 us -> 84.5 us (0.40)
  local copies, waits for them, and re-layouts: 52.5 us -> 1.82 us
  waiting for transfers between devices: 66 us -> 23.6 us
  other arithmetic: 37 us -> 0.08 us
  Pallas kernels: 0 us -> 21.2 us
  matrix products: 18.8 us -> 0 us
  starting transfers between devices: 15 us -> 26.2 us
  between operations: 7.99 us -> 0.11 us
    ppermute x4 -> x7, waiting for transfers between devices: 65 us -> 20.6 us  [the longest x6 20.3 us: from_plane(): return lax.ppermute(x, 'plane', [((i + by) % size, i) for i in range(size)])]
    sub x1 -> x0, other arithmetic: 21.5 us -> none  [block_attend(): expo = jnp.exp(scores - row_max)]
    pallas_call x0 -> x8, Pallas kernels: none -> 21.2 us  [call(): pl.pallas_call(kernel, out_shape=out_shape, in_specs=in_specs, out_specs=...]
    dot_general x2 -> x0, matrix products: 18.8 us -> none  [the longest x1 9.55 us: block_attend(): jnp.einsum('bgqhd,bgkhd->bghqk', query_block, key_block[0], preferred_ele...]
    reshape x2, local copies, waits for them, and re-layouts: 14.3 us -> 1.05 us  [the longest x1 0.97 us: local(): keys.reshape(1, 2, tiles, TILE, width)[:, :, :, :half]]
    another operation x3 -> x0, local copies, waits for them, and re-layouts: 12.5 us -> none  [the longest x1 11.1 us: block_attend(): jnp.stack([neighbours[member][:, :, picked_tiles[member]] for member in r...]
    squeeze x4 -> x0, local copies, waits for them, and re-layouts: 9.38 us -> none  [block_attend(): neighbours[member][:, :, picked_tiles[member]]]
    another operation x1 -> x0, other arithmetic: 7.45 us -> none  [block_attend(): jnp.stack([neighbours[member][:, :, picked_tiles[member]] for member in r...]
  transfers between devices with their start and end apart: 6 -> 10, of which waited for: 5 -> 6; matrix products, arithmetic and copies ran while one was open for 4% -> 0% of each run, Pallas kernels for 0% -> 24%
where the time goes in v1:
time: 84.5 us; the launch traced here: 83.9 us
  starting transfers between devices  26.2 us (31%)
  waiting for transfers between devices  23.6 us (28%)
  Pallas kernels  21.2 us (25%)
  blocking collectives  10.9 us (13%)
  local copies, waits for them, and re-layouts  1.82 us (2%)
    pallas_call x8, Pallas kernels, call(): pl.pallas_call(kernel, out_shape=out_shape, in_specs=in_specs, out_specs=...  21.2 us
    ppermute x6, waiting for transfers between devices, from_plane(): return lax.ppermute(x, 'plane', [((i + by) % size, i) for i in range(size)])  20.3 us
    ppermute x6, starting transfers between devices, from_plane(): return lax.ppermute(x, 'plane', [((i + by) % size, i) for i in range(size)])  12.5 us
    all_to_all x3, starting transfers between devices, exchange(): return lax.all_to_all(x, GROUP, split_axis=0, concat_axis=0, tiled=True)  12.1 us
    all_to_all x1, blocking collectives, exchange(): return lax.all_to_all(x, GROUP, split_axis=0, concat_axis=0, tiled=True)  10.9 us
    all_to_all x3, waiting for transfers between devices, exchange(): return lax.all_to_all(x, GROUP, split_axis=0, concat_axis=0, tiled=True)  2.99 us
  transfers between devices with their start and end apart: 10, of which 6 were waited for; matrix products, arithmetic and copies ran while one was open for 0% of the time, Pallas kernels for 24%

profile of v1, /device:TPU:0, one launch (start us, length us, event | category | flops | bytes accessed | tf_op | source)
XLA Modules:
  0.0 83.9 jit_solution(15092925376376792930)
XLA Ops:
  0.0 1.0 %slice_bitcast_fusion.refs_2_ = bf16[1,2,64,1024]{3,2,1,0:T(8,128)(2,1)S(1)} fusion(bf16[1,2,1,128,1024]{4,3,1,2,0:T(8,128)(2,1)} %bitcast.21), kind=kLoop, calls=%fused_computation | loop fusion | bytes 524288 | tf_op jit(solution)/shard_map/reshape | solution.py:343
  1.0 3.1 %collective-permute-start = (bf16[1,2,64,1024]{3,2,1,0:T(8,128)(2,1)S(1)}, bf16[1,2,64,1024]{3,2,1,0:T(8,128)(2,1)S(1)}, u32[]{:S(2)}, u32[]{:S(2)}) collective-permute-start(bf16[1,2,64,1024]{3,2,1,0:T(8,128)(2,1)S(1)} %slice_bitcast_fusion.refs_2_), channel_id=1, source_target_pairs={{24,0},{0,8},{8,16},{16,24},{25,1},{1,9},{9,17},{17,25},{26,2},{2,... | collective-permute-start | bytes 786440 | tf_op jit(solution)/shard_map/ppermute | solution.py:31
  4.0 0.0 copy-start.3
  4.0 0.0 copy-start.4
  4.1 2.8 %first.1 = bf16[8,1,3,128,128]{4,3,2,1,0:T(8,128)(2,1)} custom-call(s32[2,8]{1,0:T(2,128)} %bitcast.17, s32[2,8]{1,0:T(2,128)} %bitcast.18, bf16[1,2,128,1024]{3,2,1,0:T(8,128)(2,1)} %refs_0_.2, bf16[1,2,128,1024]{3,2,1,0:T(8,128)(2,1)} %refs_1_.1), custom_call_target="tpu_custom_call" | custom-call | bytes 1572864 | tf_op jit(solution)/shard_map/first/pallas_call | solution.py:277
  6.8 3.7 %all-to-all-start = ((bf16[8,1,3,128,128]{4,3,2,1,0:T(8,128)(2,1)}), bf16[8,1,3,128,128]{4,3,2,1,0:T(8,128)(2,1)S(1)}, u32[]{:S(2)}, u32[]{:S(2)}) async-start(bf16[8,1,3,128,128]{4,3,2,1,0:T(8,128)(2,1)} %first.1), calls=%async_computation | async-start | bytes 1572864 | tf_op jit(solution)/shard_map/all_to_all | solution.py:35
  10.6 1.8 %collective-permute-done.refs_0_.refs_1_ = bf16[1,2,64,1024]{3,2,1,0:T(8,128)(2,1)S(1)} collective-permute-done((bf16[1,2,64,1024]{3,2,1,0:T(8,128)(2,1)S(1)}, bf16[1,2,64,1024]{3,2,1,0:T(8,128)(2,1)S(1)}, u32[]{:S(2)}, u32[]{:S(2)}) %collective-permute-start) | collective-permute-done | bytes 262176 | tf_op jit(solution)/shard_map/ppermute | solution.py:31
  12.4 1.7 %collective-permute-start.1 = (bf16[1,2,64,1024]{3,2,1,0:T(8,128)(2,1)S(1)}, bf16[1,2,64,1024]{3,2,1,0:T(8,128)(2,1)S(1)}, u32[]{:S(2)}, u32[]{:S(2)}) collective-permute-start(bf16[1,2,64,1024]{3,2,1,0:T(8,128)(2,1)S(1)} %slice_bitcast_fusion.refs_2_), channel_id=1, source_target_pairs={{8,0},{16,8},{24,16},{0,24},{9,1},{17,9},{25,17},{1,25},{10,2},{18... | collective-permute-start | bytes 786440 | tf_op jit(solution)/shard_map/ppermute | solution.py:31
  14.1 0.0 copy-done.3
  14.1 0.1 reshape.27
  14.2 0.0 copy-done.4
  14.2 0.1 pad_add_fusion.own
  14.3 0.0 copy-start.2
  14.3 1.5 %collective-permute-start.2 = (s32[34]{0:T(128)S(1)}, s32[34]{0:T(128)S(1)}, u32[]{:S(2)}, u32[]{:S(2)}) collective-permute-start(s32[34]{0:T(128)S(1)} %pad_add_fusion.own), channel_id=1, source_target_pairs={{0,4},{4,0},{1,5},{5,1},{2,6},{6,2},{3,7},{7,3},{8,12},{12,8},{9,1... | collective-permute-start | bytes 416 | tf_op jit(solution)/shard_map/ppermute | solution.py:307
  15.8 4.1 %collective-permute-done.1.refs_1_.refs_3_ = bf16[1,2,64,1024]{3,2,1,0:T(8,128)(2,1)S(1)} collective-permute-done((bf16[1,2,64,1024]{3,2,1,0:T(8,128)(2,1)S(1)}, bf16[1,2,64,1024]{3,2,1,0:T(8,128)(2,1)S(1)}, u32[]{:S(2)}, u32[]{:S(2)}) %collective-permute-start.1) | collective-permute-done | bytes 262176 | tf_op jit(solution)/shard_map/ppermute | solution.py:31
  19.9 0.0 copy-start
  19.9 0.3 collective-permute-done.2.other
  20.2 3.0 %all-to-all-done = bf16[8,1,3,128,128]{4,3,2,1,0:T(8,128)(2,1)S(1)} async-done(((bf16[8,1,3,128,128]{4,3,2,1,0:T(8,128)(2,1)}), bf16[8,1,3,128,128]{4,3,2,1,0:T(8,128)(2,1)S(1)}, u32[]{:S(2)}, u32[]{:S(2)}) %all-to-all-start) | async-done | bytes 786464 | tf_op jit(solution)/shard_map/all_to_all | solution.py:35
  23.2 1.6 %collective-permute-start.3 = (bf16[8,2,128,128]{3,2,1,0:T(8,128)(2,1)S(1)}, bf16[8,2,128,128]{3,2,1,0:T(8,128)(2,1)S(1)}, u32[]{:S(2)}, u32[]{:S(2)}) collective-permute-start(bf16[8,2,128,128]{3,2,1,0:T(8,128)(2,1)S(1)} %slice.10), channel_id=1, source_target_pairs={{24,0},{0,8},{8,16},{16,24},{25,1},{1,9},{9,17},{17,25},{26,2},{2,... | collective-permute-start | bytes 1572872 | tf_op jit(solution)/shard_map/ppermute | solution.py:31
  24.8 2.2 %collective-permute-start.4 = (bf16[8,2,128,128]{3,2,1,0:T(8,128)(2,1)S(1)}, bf16[8,2,128,128]{3,2,1,0:T(8,128)(2,1)}, u32[]{:S(2)}, u32[]{:S(2)}) collective-permute-start(bf16[8,2,128,128]{3,2,1,0:T(8,128)(2,1)S(1)} %slice.10), channel_id=1, source_target_pairs={{8,0},{16,8},{24,16},{0,24},{9,1},{17,9},{25,17},{1,25},{10,2},{18... | collective-permute-start | bytes 1572872 | tf_op jit(solution)/shard_map/ppermute | solution.py:31
  27.1 0.0 copy-done.2
  27.1 0.0 copy-done
  27.1 1.7 %second.1 = bf16[8,1,5,128,128]{4,3,2,1,0:T(8,128)(2,1)} custom-call(s32[2,8]{1,0:T(2,128)S(1)} %bitcast.19, f32[8,128]{1,0:T(8,128)S(1)} %mark.2.mark_ref, bf16[1,2,128,1024]{3,2,1,0:T(8,128)(2,1)S(1)} %copy-done, bf16[1,2,64,1024]{3,2,1,0:T(8,128)(2,1)S(1)} %collective-permute-done.refs_0_.refs_1_, bf16[1,2,64,1024]{3,2,1,0:T(8,128)(2,1)S(1)} %slice_bitcast_fusion.refs_2_, ...), custom_call_target="tpu_custom_call" | custom-call | bytes 2621440 | tf_op jit(solution)/shard_map/second/pallas_call | solution.py:277
  28.7 3.6 %all-to-all-start.1 = ((bf16[8,1,5,128,128]{4,3,2,1,0:T(8,128)(2,1)}), bf16[8,1,5,128,128]{4,3,2,1,0:T(8,128)(2,1)S(1)}, u32[]{:S(2)}, u32[]{:S(2)}) async-start(bf16[8,1,5,128,128]{4,3,2,1,0:T(8,128)(2,1)} %second.1), calls=%async_computation.1 | async-start | bytes 2621440 | tf_op jit(solution)/shard_map/all_to_all | solution.py:35
  32.4 7.6 %collective-permute-done.3.refs_0_.refs_1_ = bf16[8,2,128,128]{3,2,1,0:T(8,128)(2,1)S(1)} collective-permute-done((bf16[8,2,128,128]{3,2,1,0:T(8,128)(2,1)S(1)}, bf16[8,2,128,128]{3,2,1,0:T(8,128)(2,1)S(1)}, u32[]{:S(2)}, u32[]{:S(2)}) %collective-permute-start.3) | collective-permute-done | bytes 524320 | tf_op jit(solution)/shard_map/ppermute | solution.py:31
  39.9 6.8 %collective-permute-done.4.refs_1_.refs_3_ = bf16[8,2,128,128]{3,2,1,0:T(8,128)(2,1)} collective-permute-done((bf16[8,2,128,128]{3,2,1,0:T(8,128)(2,1)S(1)}, bf16[8,2,128,128]{3,2,1,0:T(8,128)(2,1)}, u32[]{:S(2)}, u32[]{:S(2)}) %collective-permute-start.4) | collective-permute-done | bytes 524320 | tf_op jit(solution)/shard_map/ppermute | solution.py:31
  46.8 1.1 %collective-permute-start.5 = (bf16[8,1,128,128]{3,2,1,0:T(8,128)(2,1)S(1)}, bf16[8,1,128,128]{3,2,1,0:T(8,128)(2,1)S(1)}, u32[]{:S(2)}, u32[]{:S(2)}) collective-permute-start(bf16[8,1,128,128]{3,2,1,0:T(8,128)(2,1)S(1)} %slice.11.refs_2_), channel_id=1, source_target_pairs={{24,0},{0,8},{8,16},{16,24},{25,1},{1,9},{9,17},{17,25},{26,2},{2,... | collective-permute-start | bytes 786440 | tf_op jit(solution)/shard_map/ppermute | solution.py:31
  47.8 2.8 %collective-permute-start.6 = (bf16[8,1,128,128]{3,2,1,0:T(8,128)(2,1)S(1)}, bf16[8,1,128,128]{3,2,1,0:T(8,128)(2,1)}, u32[]{:S(2)}, u32[]{:S(2)}) collective-permute-start(bf16[8,1,128,128]{3,2,1,0:T(8,128)(2,1)S(1)} %slice.11.refs_2_), channel_id=1, source_target_pairs={{8,0},{16,8},{24,16},{0,24},{9,1},{17,9},{25,17},{1,25},{10,2},{18... | collective-permute-start | bytes 786440 | tf_op jit(solution)/shard_map/ppermute | solution.py:31
  50.6 0.0 all-to-all-done.1
  50.6 7.2 %attend.1 = bf16[8,1,128,128]{3,2,1,0:T(8,128)(2,1)S(1)} custom-call(s32[34]{0:T(128)S(1)} %pad_add_fusion.own, s32[34]{0:T(128)S(1)} %collective-permute-done.2.other, bf16[8,5,128,128]{3,2,1,0:T(8,128)(2,1)S(1)} %bitcast.13, bf16[8,2,128,128]{3,2,1,0:T(8,128)(2,1)S(1)} %collective-permute-done.3.refs_0_.refs_1_, bf16[8,3,128,128]{3,2,1,0:T(8,128)(2,1)S(1)} %bitcast.11, ...), custom_call_target="tpu_custom_call" | custom-call | flops 603979776 | bytes 1048576 | tf_op jit(solution)/shard_map/attend/pallas_call | solution.py:277
  57.8 0.0 copy-start.1
  57.9 0.7 copy-done.1
  58.5 4.8 %all-to-all-start.2 = ((bf16[8,1,1,128,128]{4,3,2,1,0:T(8,128)(2,1)}), bf16[8,1,1,128,128]{4,3,2,1,0:T(8,128)(2,1)S(1)}, u32[]{:S(2)}, u32[]{:S(2)}) async-start(bf16[8,1,1,128,128]{4,3,2,1,0:T(8,128)(2,1)} %bitcast.16), calls=%async_computation.2 | async-start | bytes 524288 | tf_op jit(solution)/shard_map/all_to_all | solution.py:35
  63.4 4.3 %scores.1.refs_0_ = bf16[8,256,1152]{2,1,0:T(8,128)(2,1)S(1)} custom-call(s32[34]{0:T(128)S(1)} %pad_add_fusion.own, s32[34]{0:T(128)S(1)} %collective-permute-done.2.other, bf16[8,5,128,128]{3,2,1,0:T(8,128)(2,1)S(1)} %bitcast.14, bf16[8,2,128,128]{3,2,1,0:T(8,128)(2,1)S(1)} %collective-permute-done.3.refs_0_.refs_1_, ...), custom_call_target="tpu_custom_call" | custom-call | flops 301989888 | bytes 1048576 | tf_op jit(solution)/shard_map/scores/pallas_call | solution.py:277
  67.7 0.0 collective-permute-done.5.refs_1_
  67.7 0.0 collective-permute-done.6.refs_3_
  67.7 3.9 %weigh.1 = bf16[8,1,128,128]{3,2,1,0:T(8,128)(2,1)S(1)} custom-call(s32[34]{0:T(128)S(1)} %pad_add_fusion.own, s32[34]{0:T(128)S(1)} %collective-permute-done.2.other, bf16[8,256,1152]{2,1,0:T(8,128)(2,1)S(1)} %scores.1.refs_0_, bf16[8,1,128,128]{3,2,1,0:T(8,128)(2,1)S(1)} %collective-permute-done.5.refs_1_, bf16[8,1,128,128]{3,2,1,0:T(8,128)(2,1)S(1)} %slice.11.refs_2_, ...), custom_call_target="tpu_custom_call" | custom-call | flops 301989888 | bytes 1048576 | tf_op jit(solution)/shard_map/weigh/pallas_call | solution.py:277
  71.6 0.0 all-to-all-done.2.x0
  71.6 10.9 %all_to_all.20.x1 = bf16[8,1,1,128,128]{4,3,2,1,0:T(8,128)(2,1)S(1)} all-to-all(bf16[8,1,1,128,128]{4,3,2,1,0:T(8,128)(2,1)S(1)} %bitcast.15), channel_id=1, replica_groups=mesh['plane'=4,'sub'=2,'tok'=4] {'sub','tok'}, dimensions={0} | all-to-all | bytes 524288 | tf_op jit(solution)/shard_map/all_to_all | solution.py:35
  82.5 1.3 %last.1 = bf16[1,2,128,1024]{3,2,1,0:T(8,128)(2,1)} custom-call(s32[2,8]{1,0:T(2,128)S(1)} %bitcast.20, bf16[8,1,1,128,128]{4,3,2,1,0:T(8,128)(2,1)S(1)} %all-to-all-done.2.x0, bf16[8,1,1,128,128]{4,3,2,1,0:T(8,128)(2,1)S(1)} %all_to_all.20.x1), custom_call_target="tpu_custom_call" | custom-call | bytes 1048576 | tf_op jit(solution)/shard_map/last/pallas_call | solution.py:277
  (4 shorter events, 0.1 us)
Async XLA Ops:
  1.0 11.4 %collective-permute-start = (bf16[1,2,64,1024]{3,2,1,0:T(8,128)(2,1)S(1)}, bf16[1,2,64,1024]{3,2,1,0:T(8,128)(2,1)S(1)}, u32[]{:S(2)}, u32[]{:S(2)}) collective-permute-start(bf16[1,2,64,1024]{3,2,1,0:T(8,128)(2,1)S(1)} %slice_bitcast_fusion.refs_2_), channel_id=1, source_target_pairs={{24,0},{0,8},{8,16},{16,24},{25,1},{1,9},{9,17},{17,25},{26,2},{2,... | collective-permute-start | bytes 786440 | tf_op jit(solution)/shard_map/ppermute | solution.py:31
  4.0 10.1 %copy-start.3 = (s32[1,2,4,4]{3,2,1,0:T(4,128)S(1)}, s32[1,2,4,4]{3,2,1,0:T(4,128)}, u32[]{:S(2)}) copy-start(s32[1,2,4,4]{3,2,1,0:T(4,128)} %param.9) | copy-start | bytes 388
  4.0 10.2 %copy-start.4 = (s32[1,2]{1,0:T(1,128)S(1)}, s32[1,2]{1,0:T(1,128)}, u32[]{:S(2)}) copy-start(s32[1,2]{1,0:T(1,128)} %param.10) | copy-start | bytes 28
  6.8 16.3 %all-to-all-start = ((bf16[8,1,3,128,128]{4,3,2,1,0:T(8,128)(2,1)}), bf16[8,1,3,128,128]{4,3,2,1,0:T(8,128)(2,1)S(1)}, u32[]{:S(2)}, u32[]{:S(2)}) async-start(bf16[8,1,3,128,128]{4,3,2,1,0:T(8,128)(2,1)} %first.1), calls=%async_computation | async-start | bytes 1572864 | tf_op jit(solution)/shard_map/all_to_all | solution.py:35
  12.4 7.5 %collective-permute-start.1 = (bf16[1,2,64,1024]{3,2,1,0:T(8,128)(2,1)S(1)}, bf16[1,2,64,1024]{3,2,1,0:T(8,128)(2,1)S(1)}, u32[]{:S(2)}, u32[]{:S(2)}) collective-permute-start(bf16[1,2,64,1024]{3,2,1,0:T(8,128)(2,1)S(1)} %slice_bitcast_fusion.refs_2_), channel_id=1, source_target_pairs={{8,0},{16,8},{24,16},{0,24},{9,1},{17,9},{25,17},{1,25},{10,2},{18... | collective-permute-start | bytes 786440 | tf_op jit(solution)/shard_map/ppermute | solution.py:31
  14.3 12.8 %copy-start.2 = (s32[8,2]{0,1:T(2,128)S(1)}, s32[8,2]{0,1:T(2,128)}, u32[]{:S(2)}) copy-start(s32[8,2]{0,1:T(2,128)} %param.11) | copy-start | bytes 196
  14.3 5.9 %collective-permute-start.2 = (s32[34]{0:T(128)S(1)}, s32[34]{0:T(128)S(1)}, u32[]{:S(2)}, u32[]{:S(2)}) collective-permute-start(s32[34]{0:T(128)S(1)} %pad_add_fusion.own), channel_id=1, source_target_pairs={{0,4},{4,0},{1,5},{5,1},{2,6},{6,2},{3,7},{7,3},{8,12},{12,8},{9,1... | collective-permute-start | bytes 416 | tf_op jit(solution)/shard_map/ppermute | solution.py:307
  19.9 7.2 %copy-start = (bf16[1,2,128,1024]{3,2,1,0:T(8,128)(2,1)S(1)}, bf16[1,2,128,1024]{3,2,1,0:T(8,128)(2,1)}, u32[]{:S(2)}) copy-start(bf16[1,2,128,1024]{3,2,1,0:T(8,128)(2,1)} %refs_0_.3) | copy-start | bytes 1572868
  23.2 16.7 %collective-permute-start.3 = (bf16[8,2,128,128]{3,2,1,0:T(8,128)(2,1)S(1)}, bf16[8,2,128,128]{3,2,1,0:T(8,128)(2,1)S(1)}, u32[]{:S(2)}, u32[]{:S(2)}) collective-permute-start(bf16[8,2,128,128]{3,2,1,0:T(8,128)(2,1)S(1)} %slice.10), channel_id=1, source_target_pairs={{24,0},{0,8},{8,16},{16,24},{25,1},{1,9},{9,17},{17,25},{26,2},{2,... | collective-permute-start | bytes 1572872 | tf_op jit(solution)/shard_map/ppermute | solution.py:31
  24.8 21.9 %collective-permute-start.4 = (bf16[8,2,128,128]{3,2,1,0:T(8,128)(2,1)S(1)}, bf16[8,2,128,128]{3,2,1,0:T(8,128)(2,1)}, u32[]{:S(2)}, u32[]{:S(2)}) collective-permute-start(bf16[8,2,128,128]{3,2,1,0:T(8,128)(2,1)S(1)} %slice.10), channel_id=1, source_target_pairs={{8,0},{16,8},{24,16},{0,24},{9,1},{17,9},{25,17},{1,25},{10,2},{18... | collective-permute-start | bytes 1572872 | tf_op jit(solution)/shard_map/ppermute | solution.py:31
  28.7 21.8 %all-to-all-start.1 = ((bf16[8,1,5,128,128]{4,3,2,1,0:T(8,128)(2,1)}), bf16[8,1,5,128,128]{4,3,2,1,0:T(8,128)(2,1)S(1)}, u32[]{:S(2)}, u32[]{:S(2)}) async-start(bf16[8,1,5,128,128]{4,3,2,1,0:T(8,128)(2,1)} %second.1), calls=%async_computation.1 | async-start | bytes 2621440 | tf_op jit(solution)/shard_map/all_to_all | solution.py:35
  46.8 20.9 %collective-permute-start.5 = (bf16[8,1,128,128]{3,2,1,0:T(8,128)(2,1)S(1)}, bf16[8,1,128,128]{3,2,1,0:T(8,128)(2,1)S(1)}, u32[]{:S(2)}, u32[]{:S(2)}) collective-permute-start(bf16[8,1,128,128]{3,2,1,0:T(8,128)(2,1)S(1)} %slice.11.refs_2_), channel_id=1, source_target_pairs={{24,0},{0,8},{8,16},{16,24},{25,1},{1,9},{9,17},{17,25},{26,2},{2,... | collective-permute-start | bytes 786440 | tf_op jit(solution)/shard_map/ppermute | solution.py:31
  47.8 19.8 %collective-permute-start.6 = (bf16[8,1,128,128]{3,2,1,0:T(8,128)(2,1)S(1)}, bf16[8,1,128,128]{3,2,1,0:T(8,128)(2,1)}, u32[]{:S(2)}, u32[]{:S(2)}) collective-permute-start(bf16[8,1,128,128]{3,2,1,0:T(8,128)(2,1)S(1)} %slice.11.refs_2_), channel_id=1, source_target_pairs={{8,0},{16,8},{24,16},{0,24},{9,1},{17,9},{25,17},{1,25},{10,2},{18... | collective-permute-start | bytes 786440 | tf_op jit(solution)/shard_map/ppermute | solution.py:31
  57.8 0.7 copy-start.1
  58.5 13.0 %all-to-all-start.2 = ((bf16[8,1,1,128,128]{4,3,2,1,0:T(8,128)(2,1)}), bf16[8,1,1,128,128]{4,3,2,1,0:T(8,128)(2,1)S(1)}, u32[]{:S(2)}, u32[]{:S(2)}) async-start(bf16[8,1,1,128,128]{4,3,2,1,0:T(8,128)(2,1)} %bitcast.16), calls=%async_computation.2 | async-start | bytes 524288 | tf_op jit(solution)/shard_map/all_to_all | solution.py:35

commit v2 on v1

v2 whole, which is shorter than its diff:
```python
import functools
import math

import jax
import jax.numpy as jnp
from jax import lax
from jax.experimental import pallas as pl
from jax.experimental.pallas import tpu as pltpu
from jax.sharding import Mesh, PartitionSpec as P

HD = 64
TILE = 128
NB = 2
REACH = 2
GROUP = ("sub", "tok")
MARK_FLOPS = 4 * 10 ** 9
EXPO_MOST = 16 * 2 ** 20

NEG_SCORE = -1e30

SMEM = pl.BlockSpec(memory_space=pltpu.SMEM)
VMEM = pl.BlockSpec(memory_space=pltpu.VMEM)
ANY = pl.BlockSpec(memory_space=pl.ANY)


def from_plane(x, by):
    size = lax.axis_size("plane")
    return lax.ppermute(x, "plane", [((i + by) % size, i) for i in range(size)])


def exchange(x):
    return lax.all_to_all(x, GROUP, split_axis=0, concat_axis=0, tiled=True)


def pack_kernel(whole_lanes, staged, moves, mark_ref, *refs):
    if staged:
        *ins, out, sem, stage, stage_sem = refs
    else:
        *ins, out, sem = refs
    ways, tiles, _, _, share = out.shape
    sources = []
    for i, (array, slot) in enumerate(moves):
        for m in range(tiles):
            source = ins[array].at[0, slot, pl.ds(m * TILE, TILE)]
            copy = None
            if staged:
                there = stage.at[i, m]
                copy = pltpu.make_async_copy(source, there, stage_sem.at[i, m])
                copy.start()
                source = there
            sources.append((i, m, source, copy))
    for i, m, source, copy in sources:
        if copy is not None:
            copy.wait()
        for w in range(ways):
            lanes = pl.ds(w * share, share)
            if whole_lanes:
                pltpu.make_async_copy(source.at[:, lanes], out.at[w, m, i], sem).start()
            else:
                out[w, m, i] = source[:, lanes]
    if whole_lanes:
        pltpu.make_async_copy(out, out, sem).wait()


def last_kernel(whole_lanes, x, out, sem):
    ways, tiles, slots, _, share = x.shape
    for s in range(slots):
        for m in range(tiles):
            for w in range(ways):
                rows, lanes = pl.ds(m * TILE, TILE), pl.ds(w * share, share)
                if whole_lanes:
                    pltpu.make_async_copy(x.at[w, m, s], out.at[0, s, rows, lanes], sem).start()
                else:
                    out[0, s, rows, lanes] = x[w, m, s]
    if whole_lanes:
        pltpu.make_async_copy(out, out, sem).wait()


def mark_kernel(*refs):
    refs[-1][...] = jnp.zeros_like(refs[-1])


class Plan:
    def __init__(self, sub, kt, hops, share):
        self.sub, self.kt, self.hops, self.share = sub, kt, hops, share
        self.planes = 2 * hops + 1
        self.heads = share // HD
        self.rows = self.heads * TILE
        self.cols = (1 + NB * kt) * TILE
        self.pairs = 2 * sub * kt * self.rows * self.cols
        self.whole_lanes = share % 128 == 0


def fact(plan, facts, g, i):
    own_ref, other_ref, _ = facts
    if plan.sub == 1:
        return own_ref[i]
    return jnp.where(lax.axis_index("sub") == g, own_ref[i], other_ref[i])


def start_far(plan, facts, copies_of):
    slots_ref = facts[2]
    views = slots_ref.shape[1]
    for g in range(plan.sub):
        view = lax.axis_index("plane") * plan.sub + g
        for j in range(NB):
            step = fact(plan, facts, g, NB * plan.kt * plan.kt + j)
            other = lax.rem(view + step + views, views)
            swap = jnp.where(slots_ref[0, other] == slots_ref[0, view], 0, 1)
            at = step + (plan.hops * plan.sub + g)
            tiles_at = lax.rem(at, plan.sub) * plan.kt
            for d in range(plan.planes):
                @pl.when(lax.div(at, plan.sub) == d)
                def _():
                    for copy in copies_of(g, j, d, tiles_at, swap):
                        copy.start()


def head_of_lane(plan):
    return lax.broadcasted_iota(jnp.int32, (TILE, plan.share), 1) // HD


def split_heads(plan, q):
    if plan.heads == 1:
        return q
    block = head_of_lane(plan)
    return jnp.concatenate([jnp.where(block == h, q, 0) for h in range(plan.heads)], axis=0)


def scores_of(q, k):
    return lax.dot_general(q, k, (((1,), (1,)), ((), ())), preferred_element_type=jnp.float32)


def numerators(plan, facts, g, t, own, far):
    factor = HD ** -0.5 * math.log2(math.e)
    parts = [own]
    for j in range(NB):
        for k in range(plan.kt):
            keep = fact(plan, facts, g, (j * plan.kt + t) * plan.kt + k) == 1
            bias = jnp.where(keep, 0.0, NEG_SCORE)
            parts.append(far[j][:, k * TILE:(k + 1) * TILE] + bias)
    top = functools.reduce(jnp.maximum, parts)
    top = jnp.max(top, axis=1, keepdims=True)
    return [jnp.exp2((part - top) * factor).astype(jnp.bfloat16) for part in parts]


def with_ones(v):
    return jnp.concatenate([v, jnp.ones_like(v)], axis=1)


def weigh(p, v):
    return jnp.dot(p, v, preferred_element_type=jnp.float32)


def finish(plan, total):
    result = total[:TILE]
    block = head_of_lane(plan)
    both = jnp.concatenate([block, block], axis=1)
    for h in range(1, plan.heads):
        result = jnp.where(both == h, total[h * TILE:(h + 1) * TILE], result)
    return (result[:, :plan.share] / result[:, plan.share:]).astype(jnp.bfloat16)


def attend_kernel(plan, scores, weighs, own, other, slots, *refs):
    n, h = plan.planes, plan.hops
    facts = (own, other, slots)
    refs = list(refs)
    if scores:
        q, ks = refs[0], refs[1:1 + n]
        refs = refs[1 + n:]
    if weighs:
        v0s, v1 = refs[:n], refs[n]
        refs = refs[1 + n:]
    if not scores:
        expo_ref = refs[0]
    out, result, k_far, v_far, far_sem, out_sem = refs[-6:]

    def far_copies(g, j, d, tiles_at, swap):
        tiles = pl.ds(tiles_at, plan.kt)
        found = []
        for s in range(2):
            here = swap if s == 0 else 1 - swap
            if scores:
                found.append((ks[d].at[tiles, s], k_far.at[g, j, here], 0, here))
            if weighs:
                src = v0s[d].at[tiles, 0] if s == 0 else v1.at[tiles, d]
                found.append((src, v_far.at[g, j, here], 1, here))
        return [
            pltpu.make_async_copy(src, to, far_sem.at[i, g, j, here]) for src, to, i, here in found
        ]

    start_far(plan, facts, far_copies)
    count = math.gcd(plan.kt, 4)
    wide = plan.kt * TILE

    def one_tile(s, g, t, k, v):
        at = g * plan.kt + t
        if scores:
            expo = split_heads(plan, q[at, s])
            expo = numerators(
                plan, facts, g, t, scores_of(expo, ks[h][at, s]),
                [scores_of(expo, k[j]) for j in range(NB)],
            )
            if not weighs:
                for i, part in enumerate(expo):
                    out[s, at, :, i * TILE:(i + 1) * TILE] = part
                return
            expo_own = expo[0]
            expo_far = [
                jnp.concatenate(expo[1 + j * plan.kt:1 + (j + 1) * plan.kt], axis=1)
                for j in range(NB)
            ]
        else:
            expo_own = expo_ref[s, at, :, :TILE]
            expo_far = [
                expo_ref[s, at, :, TILE + j * wide:TILE + (j + 1) * wide] for j in range(NB)
            ]
        total = weigh(expo_own, with_ones(jnp.where(s == 0, v0s[h][at, 0], v1[at, h])))
        for j in range(NB):
            total += weigh(expo_far[j], v[j])
        result[at, s] = finish(plan, total)

    def some_tiles(s, g, t0):
        def rows(buffer, j):
            return buffer[g, j, s].reshape(wide, plan.share)

        k = [rows(k_far, j) for j in range(NB)] if scores else None
        v = [with_ones(rows(v_far, j)) for j in range(NB)] if weighs else None
        for i in range(count):
            one_tile(s, g, t0 + i, k, v)

    def one_view(i, carry):
        s, g = lax.div(i, plan.sub), lax.rem(i, plan.sub)
        for j in range(NB):
            kinds = ([(0, k_far)] if scores else []) + ([(1, v_far)] if weighs else [])
            for kind, buffer in kinds:
                there = buffer.at[g, j, s]
                pltpu.make_async_copy(there, there, far_sem.at[kind, g, j, s]).wait()
        if count == plan.kt:
            some_tiles(s, g, 0)
        else:
            def some(t, c):
                some_tiles(s, g, t * count)
                return c
            lax.fori_loop(0, plan.kt // count, some, 0)
        if weighs:
            tiles = pl.ds(g * plan.kt, plan.kt)
            pltpu.make_async_copy(result.at[tiles, s], out.at[tiles, s], out_sem).start()
        return carry

    lax.fori_loop(0, 2 * plan.sub, one_view, 0)
    if weighs:
        pltpu.make_async_copy(result, out, out_sem).wait()


def call(kernel, name, out_shape, in_specs, out_specs, scratch, args, flops=0, exps=0, moved=0,
         mib=8):
    return pl.pallas_call(
        kernel,
        out_shape=out_shape,
        in_specs=in_specs,
        out_specs=out_specs,
        scratch_shapes=scratch,
        compiler_params=pltpu.CompilerParams(vmem_limit_bytes=mib * 2 ** 20),
        cost_estimate=pl.CostEstimate(flops=flops, bytes_accessed=moved, transcendentals=exps),
        name=name,
    )(*args)


def local(queries, keys, values, tile_mask, offsets, branch_slots):
    sub, toks = lax.axis_size("sub"), lax.axis_size("tok")
    ways = sub * toks
    dtype = queries.dtype
    _, _, tokens, width = queries.shape
    tiles, share = tokens // TILE, width // ways
    kt = toks * tiles
    hops = -(-REACH // sub)
    plan = Plan(sub, kt, hops, share)
    order = list(range(-hops, hops + 1))
    shifts = [d for d in order if d]
    size = queries.size * 2

    slots = branch_slots.T
    own = jnp.concatenate([tile_mask.reshape(-1), offsets.reshape(-1)])
    other = own
    if sub == 2:
        other = lax.ppermute(own, "sub", [(0, 1), (1, 0)])
    facts = (own, other, slots)

    place = ANY if plan.whole_lanes else VMEM
    sem = pltpu.SemaphoreType.DMA(())

    def pack(name, arrays, moves, mark, staged=False):
        staged = staged and plan.whole_lanes
        scratch = [sem]
        if staged:
            scratch.append(pltpu.VMEM((len(moves), tiles, TILE, width), dtype))
            scratch.append(pltpu.SemaphoreType.DMA((len(moves), tiles)))
        return call(
            functools.partial(pack_kernel, plan.whole_lanes, staged, moves), name,
            jax.ShapeDtypeStruct((ways, tiles, len(moves), TILE, share), dtype),
            [ANY] + [ANY if staged else VMEM] * len(arrays), place, scratch, (mark, *arrays),
            moved=len(moves) * size, mib=62 if staged else 16,
        )

    def spread(x):
        return exchange(x).reshape(ways * tiles, x.shape[2], TILE, share)

    def around(x, chain=False):
        found, last = {0: x}, ()
        for d in shifts:
            found[d] = from_plane(lax.optimization_barrier((x, last))[0], d)
            last = found[d] if chain else ()
        return [found[d] for d in order]

    raw = around(values[:, 1:], chain=True)
    keys = spread(pack("first", [keys], [(0, 0), (0, 1)], slots, staged=True))
    keys, raw = lax.optimization_barrier((keys, raw))

    planes = around(keys)
    arrived = call(
        mark_kernel, "mark", jax.ShapeDtypeStruct((8, 128), jnp.float32),
        [ANY] * plan.planes, VMEM, [], planes, flops=MARK_FLOPS,
    )
    mixed = spread(pack("second", [queries, values], [(0, 0), (0, 1), (1, 0)], keys))

    packed = pack("third", raw, [(i, 0) for i in range(plan.planes)], slots)
    packed, mixed = lax.optimization_barrier((packed, mixed))
    late = spread(packed)
    v_planes = around(mixed[:, 2:])

    result = (ways * tiles, 2, TILE, share)
    far = pltpu.VMEM((sub, NB, 2, kt, TILE, share), dtype)

    def attend(name, scores, weighs, ins, out_shape, rest=()):
        return call(
            functools.partial(attend_kernel, plan, scores, weighs), name,
            jax.ShapeDtypeStruct(out_shape, dtype),
            [SMEM] * 3 + [VMEM] * len(ins) + [ANY] * len(rest), ANY if weighs else VMEM,
            [pltpu.VMEM(result, dtype), far, far, pltpu.SemaphoreType.DMA((2, sub, NB, 2)), sem],
            (*facts, *ins, *rest), exps=plan.pairs if weighs else 0, moved=size, mib=28,
        )

    ins_k, ins_v = [mixed, *planes], [*v_planes, late]
    if plan.pairs * 2 <= EXPO_MOST:
        shape = (2, sub * kt, plan.rows, plan.cols)
        expo = attend("scores", True, False, ins_k, shape, rest=(arrived,))
        x = attend("weigh", False, True, [*ins_v, expo], result)
    else:
        x = attend("attend", True, True, [*ins_k, *ins_v], result, rest=(arrived,))
    x = exchange(x.reshape(ways, tiles, 2, TILE, share))
    return call(
        functools.partial(last_kernel, plan.whole_lanes), "last",
        jax.ShapeDtypeStruct(queries.shape, dtype), [place], place, [sem], (x,), moved=2 * size,
    )


def solution(mesh):
    views, toks = mesh.shape["view"], mesh.shape["tok"]

    def run(queries, keys, values, tile_mask, offsets, branch_slots):
        heads = queries.shape[-1] // HD
        sub = 2 if views % 2 == 0 and heads % (2 * toks) == 0 else 1
        fine = Mesh(mesh.devices.reshape(views // sub, sub, toks), ("plane", "sub", "tok"))
        view = ("plane", "sub")
        shard = P(view, None, "tok", None)
        in_specs = (shard, shard, shard, P(view, None, None, None), P(view, None), P())
        return jax.shard_map(
            local, mesh=fine, in_specs=in_specs, out_specs=shard, check_vma=False
        )(queries, keys, values, tile_mask, offsets, branch_slots)

    return run
```

time: 84.5 us -> 92.2 us (1.091)
  local copies, waits for them, and re-layouts: 1.82 us -> 14.5 us
  Pallas kernels: 21.2 us -> 16.5 us
  blocking collectives: 10.9 us -> 14.1 us
  waiting for transfers between devices: 23.6 us -> 20.9 us
    unnamed x10 -> x24, local copies, waits for them, and re-layouts: 0.71 us -> 13.4 us
    ppermute x6, waiting for transfers between devices: 20.3 us -> 8.67 us  [from_plane(): return lax.ppermute(x, 'plane', [((i + by) % size, i) for i in range(size)])]
    all_to_all x3, waiting for transfers between devices: 2.99 us -> 12.2 us  [exchange(): return lax.all_to_all(x, GROUP, split_axis=0, concat_axis=0, tiled=True)]
    pallas_call x8 -> x7, Pallas kernels: 21.2 us -> 16.5 us  [call(): pl.pallas_call(kernel, out_shape=out_shape, in_specs=in_specs, out_specs=...]
    all_to_all x1, blocking collectives: 10.9 us -> 14.1 us  [exchange(): return lax.all_to_all(x, GROUP, split_axis=0, concat_axis=0, tiled=True)]
    all_to_all x3, starting transfers between devices: 12.1 us -> 10.8 us  [exchange(): return lax.all_to_all(x, GROUP, split_axis=0, concat_axis=0, tiled=True)]
    reshape x1 -> x0, local copies, waits for them, and re-layouts: 0.97 us -> none  [local(): keys.reshape(1, 2, tiles, TILE, width)[:, :, :, :half]]
    slice x2, local copies, waits for them, and re-layouts: 0.05 us -> 1.01 us  [the longest x1 0.99 us: local(): raw = around(values[:, 1:], chain=True)]
  transfers between devices with their start and end apart: 10 -> 10, of which waited for: 6 -> 5; matrix products, arithmetic and copies ran while one was open for 0% -> 0% of each run, Pallas kernels for 24% -> 10%
where the time goes in v2:
time: 92.2 us; the launch traced here: 91.6 us
  starting transfers between devices  25.4 us (28%)
  waiting for transfers between devices  20.9 us (23%)
  Pallas kernels  16.5 us (18%)
  local copies, waits for them, and re-layouts  14.5 us (16%)
  blocking collectives  14.1 us (15%)
    pallas_call x7, Pallas kernels, call(): pl.pallas_call(kernel, out_shape=out_shape, in_specs=in_specs, out_specs=...  16.5 us
    all_to_all x1, blocking collectives, exchange(): return lax.all_to_all(x, GROUP, split_axis=0, concat_axis=0, tiled=True)  14.1 us
    unnamed x24, local copies, waits for them, and re-layouts  13.4 us
    ppermute x6, starting transfers between devices, from_plane(): return lax.ppermute(x, 'plane', [((i + by) % size, i) for i in range(size)])  12.6 us
    all_to_all x3, waiting for transfers between devices, exchange(): return lax.all_to_all(x, GROUP, split_axis=0, concat_axis=0, tiled=True)  12.2 us
    all_to_all x3, starting transfers between devices, exchange(): return lax.all_to_all(x, GROUP, split_axis=0, concat_axis=0, tiled=True)  10.8 us
    ppermute x6, waiting for transfers between devices, from_plane(): return lax.ppermute(x, 'plane', [((i + by) % size, i) for i in range(size)])  8.67 us
    ppermute x1, starting transfers between devices, local(): other = lax.ppermute(own, 'sub', [(0, 1), (1, 0)])  1.94 us
  transfers between devices with their start and end apart: 10, of which 5 were waited for; matrix products, arithmetic and copies ran while one was open for 0% of the time, Pallas kernels for 10%

profile of v2, /device:TPU:0, one launch (start us, length us, event | category | flops | bytes accessed | tf_op | source)
XLA Modules:
  0.0 91.6 jit_solution(11981211435955821377)
XLA Ops:
  0.0 0.0 copy-start.10
  0.0 0.0 copy-start.11
  0.0 1.0 %slice.6.refs_1_ = bf16[1,1,128,1024]{3,2,1,0:T(8,128)(2,1)S(1)} slice(bf16[1,2,128,1024]{3,2,1,0:T(8,128)(2,1)} %refs_1_.1), slice={[0:1], [1:2], [0:128], [0:1024]} | slice | bytes 524288 | tf_op jit(solution)/shard_map/slice | solution.py:316
  1.0 3.1 %collective-permute-start.1 = (bf16[1,1,128,1024]{3,2,1,0:T(8,128)(2,1)S(1)}, bf16[1,1,128,1024]{3,2,1,0:T(8,128)(2,1)S(1)}, u32[]{:S(2)}, u32[]{:S(2)}) collective-permute-start(bf16[1,1,128,1024]{3,2,1,0:T(8,128)(2,1)S(1)} %slice.6.refs_1_), channel_id=1, source_target_pairs={{24,0},{0,8},{8,16},{16,24},{25,1},{1,9},{9,17},{17,25},{26,2},{2,... | collective-permute-start | bytes 786440 | tf_op jit(solution)/shard_map/ppermute | solution.py:28
  4.1 1.7 %first.1 = bf16[8,1,2,128,128]{4,3,2,1,0:T(8,128)(2,1)} custom-call(s32[2,8]{1,0:T(2,128)} %bitcast.15, bf16[1,2,128,1024]{3,2,1,0:T(8,128)(2,1)} %refs_0_.2), custom_call_target="tpu_custom_call" | custom-call | bytes 1048576 | tf_op jit(solution)/shard_map/first/pallas_call | solution.py:258
  5.8 3.7 %all-to-all-start = ((bf16[8,1,2,128,128]{4,3,2,1,0:T(8,128)(2,1)}), bf16[8,1,2,128,128]{4,3,2,1,0:T(8,128)(2,1)S(1)}, u32[]{:S(2)}, u32[]{:S(2)}) async-start(bf16[8,1,2,128,128]{4,3,2,1,0:T(8,128)(2,1)} %first.1), calls=%async_computation | async-start | bytes 1048576 | tf_op jit(solution)/shard_map/all_to_all | solution.py:32
  9.6 2.8 %collective-permute-done.1.refs_0_ = bf16[1,1,128,1024]{3,2,1,0:T(8,128)(2,1)S(1)} collective-permute-done((bf16[1,1,128,1024]{3,2,1,0:T(8,128)(2,1)S(1)}, bf16[1,1,128,1024]{3,2,1,0:T(8,128)(2,1)S(1)}, u32[]{:S(2)}, u32[]{:S(2)}) %collective-permute-start.1) | collective-permute-done | bytes 262176 | tf_op jit(solution)/shard_map/ppermute | solution.py:28
  12.4 1.7 %collective-permute-start.2 = (bf16[1,1,128,1024]{3,2,1,0:T(8,128)(2,1)S(1)}, bf16[1,1,128,1024]{3,2,1,0:T(8,128)(2,1)S(1)}, u32[]{:S(2)}, u32[]{:S(2)}) collective-permute-start(bf16[1,1,128,1024]{3,2,1,0:T(8,128)(2,1)S(1)} %slice.6.refs_1_), channel_id=1, source_target_pairs={{8,0},{16,8},{24,16},{0,24},{9,1},{17,9},{25,17},{1,25},{10,2},{18... | collective-permute-start | bytes 786440 | tf_op jit(solution)/shard_map/ppermute | solution.py:28
  14.2 5.2 %all-to-all-done = bf16[8,1,2,128,128]{4,3,2,1,0:T(8,128)(2,1)S(1)} async-done(((bf16[8,1,2,128,128]{4,3,2,1,0:T(8,128)(2,1)}), bf16[8,1,2,128,128]{4,3,2,1,0:T(8,128)(2,1)S(1)}, u32[]{:S(2)}, u32[]{:S(2)}) %all-to-all-start) | async-done | bytes 524320 | tf_op jit(solution)/shard_map/all_to_all | solution.py:32
  19.3 0.6 collective-permute-done.2.refs_2_
  19.9 0.0 copy-start.2
  19.9 1.0 %copy-done.2 = bf16[1,2,128,1024]{3,2,1,0:T(8,128)(2,1)S(1)} copy-done((bf16[1,2,128,1024]{3,2,1,0:T(8,128)(2,1)S(1)}, bf16[1,2,128,1024]{3,2,1,0:T(8,128)(2,1)}, u32[]{:S(2)}) %copy-start.2) | copy-done | bytes 524312
  20.9 0.0 copy-start.3
  20.9 1.0 %copy-done.3 = bf16[1,2,128,1024]{3,2,1,0:T(8,128)(2,1)S(1)} copy-done((bf16[1,2,128,1024]{3,2,1,0:T(8,128)(2,1)S(1)}, bf16[1,2,128,1024]{3,2,1,0:T(8,128)(2,1)}, u32[]{:S(2)}) %copy-start.3) | copy-done | bytes 524312
  22.0 0.9 %second.1 = bf16[8,1,3,128,128]{4,3,2,1,0:T(8,128)(2,1)} custom-call(bf16[8,2,128,128]{3,2,1,0:T(8,128)(2,1)S(1)} %bitcast.6, bf16[1,2,128,1024]{3,2,1,0:T(8,128)(2,1)S(1)} %copy-done.3, bf16[1,2,128,1024]{3,2,1,0:T(8,128)(2,1)S(1)} %copy-done.2), custom_call_target="tpu_custom_call" | custom-call | bytes 1572864 | tf_op jit(solution)/shard_map/second/pallas_call | solution.py:258
  22.9 0.0 copy-start.9
  23.0 3.6 %all-to-all-start.1 = ((bf16[8,1,3,128,128]{4,3,2,1,0:T(8,128)(2,1)}), bf16[8,1,3,128,128]{4,3,2,1,0:T(8,128)(2,1)S(1)}, u32[]{:S(2)}, u32[]{:S(2)}) async-start(bf16[8,1,3,128,128]{4,3,2,1,0:T(8,128)(2,1)} %second.1), calls=%async_computation.1 | async-start | bytes 1572864 | tf_op jit(solution)/shard_map/all_to_all | solution.py:32
  26.5 1.0 %collective-permute-start.5 = (bf16[8,2,128,128]{3,2,1,0:T(8,128)(2,1)S(1)}, bf16[8,2,128,128]{3,2,1,0:T(8,128)(2,1)S(1)}, u32[]{:S(2)}, u32[]{:S(2)}) collective-permute-start(bf16[8,2,128,128]{3,2,1,0:T(8,128)(2,1)S(1)} %bitcast.7), channel_id=1, source_target_pairs={{24,0},{0,8},{8,16},{16,24},{25,1},{1,9},{9,17},{17,25},{26,2},{2,... | collective-permute-start | bytes 1572872 | tf_op jit(solution)/shard_map/ppermute | solution.py:28
  27.6 2.8 %collective-permute-start.6 = (bf16[8,2,128,128]{3,2,1,0:T(8,128)(2,1)S(1)}, bf16[8,2,128,128]{3,2,1,0:T(8,128)(2,1)S(1)}, u32[]{:S(2)}, u32[]{:S(2)}) collective-permute-start(bf16[8,2,128,128]{3,2,1,0:T(8,128)(2,1)S(1)} %bitcast.8), channel_id=1, source_target_pairs={{8,0},{16,8},{24,16},{0,24},{9,1},{17,9},{25,17},{1,25},{10,2},{18... | collective-permute-start | bytes 1572872 | tf_op jit(solution)/shard_map/ppermute | solution.py:28
  30.4 0.7 copy-done.8
  31.1 0.9 third.1
  32.0 7.1 %all-to-all-done.1 = bf16[8,1,3,128,128]{4,3,2,1,0:T(8,128)(2,1)S(1)} async-done(((bf16[8,1,3,128,128]{4,3,2,1,0:T(8,128)(2,1)}), bf16[8,1,3,128,128]{4,3,2,1,0:T(8,128)(2,1)S(1)}, u32[]{:S(2)}, u32[]{:S(2)}) %all-to-all-start.1) | async-done | bytes 786464 | tf_op jit(solution)/shard_map/all_to_all | solution.py:32
  39.1 3.5 %all-to-all-start.2 = ((bf16[8,1,3,128,128]{4,3,2,1,0:T(8,128)(2,1)}), bf16[8,1,3,128,128]{4,3,2,1,0:T(8,128)(2,1)S(1)}, u32[]{:S(2)}, u32[]{:S(2)}) async-start(bf16[8,1,3,128,128]{4,3,2,1,0:T(8,128)(2,1)} %third.1), calls=%async_computation.2 | async-start | bytes 1572864 | tf_op jit(solution)/shard_map/all_to_all | solution.py:32
  42.6 0.0 copy-done.10
  42.6 0.1 reshape.18
  42.7 0.0 copy-done.11
  42.7 0.1 pad_add_fusion.own
  42.8 1.9 %collective-permute-start = (s32[34]{0:T(128)S(1)}, s32[34]{0:T(128)S(1)}, u32[]{:S(2)}, u32[]{:S(2)}) collective-permute-start(s32[34]{0:T(128)S(1)} %pad_add_fusion.own), channel_id=1, source_target_pairs={{0,4},{4,0},{1,5},{5,1},{2,6},{6,2},{3,7},{7,3},{8,12},{12,8},{9,1... | collective-permute-start | bytes 416 | tf_op jit(solution)/shard_map/ppermute | solution.py:287
  44.7 1.0 %collective-permute-start.3 = (bf16[8,1,128,128]{3,2,1,0:T(8,128)(2,1)S(1)}, bf16[8,1,128,128]{3,2,1,0:T(8,128)(2,1)S(1)}, u32[]{:S(2)}, u32[]{:S(2)}) collective-permute-start(bf16[8,1,128,128]{3,2,1,0:T(8,128)(2,1)S(1)} %slice.7.refs_1_), channel_id=1, source_target_pairs={{24,0},{0,8},{8,16},{16,24},{25,1},{1,9},{9,17},{17,25},{26,2},{2,... | collective-permute-start | bytes 786440 | tf_op jit(solution)/shard_map/ppermute | solution.py:28
  45.8 2.8 %collective-permute-start.4 = (bf16[8,1,128,128]{3,2,1,0:T(8,128)(2,1)S(1)}, bf16[8,1,128,128]{3,2,1,0:T(8,128)(2,1)S(1)}, u32[]{:S(2)}, u32[]{:S(2)}) collective-permute-start(bf16[8,1,128,128]{3,2,1,0:T(8,128)(2,1)S(1)} %slice.7.refs_1_), channel_id=1, source_target_pairs={{8,0},{16,8},{24,16},{0,24},{9,1},{17,9},{25,17},{1,25},{10,2},{18... | collective-permute-start | bytes 786440 | tf_op jit(solution)/shard_map/ppermute | solution.py:28
  48.6 0.0 collective-permute-done.5.refs_0_.refs_1_
  48.6 5.2 %collective-permute-done.6.refs_2_.refs_3_ = bf16[8,2,128,128]{3,2,1,0:T(8,128)(2,1)S(1)} collective-permute-done((bf16[8,2,128,128]{3,2,1,0:T(8,128)(2,1)S(1)}, bf16[8,2,128,128]{3,2,1,0:T(8,128)(2,1)S(1)}, u32[]{:S(2)}, u32[]{:S(2)}) %collective-permute-start.6) | collective-permute-done | bytes 524320 | tf_op jit(solution)/shard_map/ppermute | solution.py:28
  53.9 0.0 collective-permute-done.other
  53.9 0.0 copy-done.9
  53.9 6.8 %scores.1.refs_4_ = bf16[2,8,256,1152]{3,2,1,0:T(8,128)(2,1)S(1)} custom-call(s32[34]{0:T(128)S(1)} %pad_add_fusion.own, s32[34]{0:T(128)S(1)} %collective-permute-done.other, s32[2,8]{1,0:T(2,128)S(1)} %bitcast.17, bf16[8,3,128,128]{3,2,1,0:T(8,128)(2,1)S(1)} %bitcast.12, bf16[8,2,128,128]{3,2,1,0:T(8,128)(2,1)S(1)} %collective-permute-done.5.refs_0_.refs_1_, ...), custom_call_target="tpu_custom_call" | custom-call | bytes 524288 | tf_op jit(solution)/shard_map/scores/pallas_call | solution.py:258
  60.7 0.0 copy-start
  60.7 3.7 %copy-done = bf16[2,8,256,1152]{3,2,1,0:T(8,128)(2,1)} copy-done((bf16[2,8,256,1152]{3,2,1,0:T(8,128)(2,1)}, bf16[2,8,256,1152]{3,2,1,0:T(8,128)(2,1)S(1)}, u32[]{:S(2)}) %copy-start) | copy-done | bytes 9437208
  64.4 0.0 collective-permute-done.3.refs_0_
  64.4 0.7 copy-done.4
  65.1 0.0 collective-permute-done.4.refs_2_
  65.1 0.7 copy-done.6
  65.8 0.0 all-to-all-done.2
  65.8 3.7 %copy-done.1 = bf16[2,8,256,1152]{3,2,1,0:T(8,128)(2,1)S(1)} copy-done((bf16[2,8,256,1152]{3,2,1,0:T(8,128)(2,1)S(1)}, bf16[2,8,256,1152]{3,2,1,0:T(8,128)(2,1)}, u32[]{:S(2)}) %copy-start.1) | copy-done | bytes 9437208
  69.5 0.9 %copy-done.5 = bf16[8,1,128,128]{3,2,1,0:T(8,128)(2,1)S(1)} copy-done((bf16[8,1,128,128]{3,2,1,0:T(8,128)(2,1)S(1)}, bf16[8,1,128,128]{3,2,1,0:T(8,128)(2,1)}, u32[]{:S(2)}) %copy-start.5) | copy-done | bytes 262168
  70.5 0.9 %copy-done.7 = bf16[8,1,128,128]{3,2,1,0:T(8,128)(2,1)S(1)} copy-done((bf16[8,1,128,128]{3,2,1,0:T(8,128)(2,1)S(1)}, bf16[8,1,128,128]{3,2,1,0:T(8,128)(2,1)}, u32[]{:S(2)}) %copy-start.7) | copy-done | bytes 262168
  71.4 5.3 %weigh.1 = bf16[8,2,128,128]{3,2,1,0:T(8,128)(2,1)S(1)} custom-call(s32[34]{0:T(128)S(1)} %pad_add_fusion.own, s32[34]{0:T(128)S(1)} %collective-permute-done.other, s32[2,8]{1,0:T(2,128)S(1)} %bitcast.18, bf16[8,1,128,128]{3,2,1,0:T(8,128)(2,1)S(1)} %copy-done.5, bf16[8,1,128,128]{3,2,1,0:T(8,128)(2,1)S(1)} %slice.7.refs_1_, ...), custom_call_target="tpu_custom_call" | custom-call | bytes 524288 | tf_op jit(solution)/shard_map/weigh/pallas_call | solution.py:258
  76.7 14.1 %all_to_all.20.x = bf16[8,1,2,128,128]{4,3,2,1,0:T(8,128)(2,1)S(1)} all-to-all(bf16[8,1,2,128,128]{4,3,2,1,0:T(8,128)(2,1)S(1)} %bitcast.14), channel_id=1, replica_groups=mesh['plane'=4,'sub'=2,'tok'=4] {'sub','tok'}, dimensions={0} | all-to-all | bytes 1048576 | tf_op jit(solution)/shard_map/all_to_all | solution.py:32
  90.8 0.8 last.1
  (8 shorter events, 0.0 us)
Async XLA Ops:
  0.0 42.6 %copy-start.10 = (s32[1,2,4,4]{3,2,1,0:T(4,128)S(1)}, s32[1,2,4,4]{3,2,1,0:T(4,128)}, u32[]{:S(2)}) copy-start(s32[1,2,4,4]{3,2,1,0:T(4,128)} %param.9) | copy-start | bytes 388
  0.0 42.7 %copy-start.11 = (s32[1,2]{1,0:T(1,128)S(1)}, s32[1,2]{1,0:T(1,128)}, u32[]{:S(2)}) copy-start(s32[1,2]{1,0:T(1,128)} %param.10) | copy-start | bytes 28
  1.0 11.4 %collective-permute-start.1 = (bf16[1,1,128,1024]{3,2,1,0:T(8,128)(2,1)S(1)}, bf16[1,1,128,1024]{3,2,1,0:T(8,128)(2,1)S(1)}, u32[]{:S(2)}, u32[]{:S(2)}) collective-permute-start(bf16[1,1,128,1024]{3,2,1,0:T(8,128)(2,1)S(1)} %slice.6.refs_1_), channel_id=1, source_target_pairs={{24,0},{0,8},{8,16},{16,24},{25,1},{1,9},{9,17},{17,25},{26,2},{2,... | collective-permute-start | bytes 786440 | tf_op jit(solution)/shard_map/ppermute | solution.py:28
  5.8 13.5 %all-to-all-start = ((bf16[8,1,2,128,128]{4,3,2,1,0:T(8,128)(2,1)}), bf16[8,1,2,128,128]{4,3,2,1,0:T(8,128)(2,1)S(1)}, u32[]{:S(2)}, u32[]{:S(2)}) async-start(bf16[8,1,2,128,128]{4,3,2,1,0:T(8,128)(2,1)} %first.1), calls=%async_computation | async-start | bytes 1048576 | tf_op jit(solution)/shard_map/all_to_all | solution.py:32
  12.4 7.5 %collective-permute-start.2 = (bf16[1,1,128,1024]{3,2,1,0:T(8,128)(2,1)S(1)}, bf16[1,1,128,1024]{3,2,1,0:T(8,128)(2,1)S(1)}, u32[]{:S(2)}, u32[]{:S(2)}) collective-permute-start(bf16[1,1,128,1024]{3,2,1,0:T(8,128)(2,1)S(1)} %slice.6.refs_1_), channel_id=1, source_target_pairs={{8,0},{16,8},{24,16},{0,24},{9,1},{17,9},{25,17},{1,25},{10,2},{18... | collective-permute-start | bytes 786440 | tf_op jit(solution)/shard_map/ppermute | solution.py:28
  19.9 1.0 %copy-start.2 = (bf16[1,2,128,1024]{3,2,1,0:T(8,128)(2,1)S(1)}, bf16[1,2,128,1024]{3,2,1,0:T(8,128)(2,1)}, u32[]{:S(2)}) copy-start(bf16[1,2,128,1024]{3,2,1,0:T(8,128)(2,1)} %refs_1_.1) | copy-start | bytes 1572868
  20.9 1.0 %copy-start.3 = (bf16[1,2,128,1024]{3,2,1,0:T(8,128)(2,1)S(1)}, bf16[1,2,128,1024]{3,2,1,0:T(8,128)(2,1)}, u32[]{:S(2)}) copy-start(bf16[1,2,128,1024]{3,2,1,0:T(8,128)(2,1)} %refs_0_.3) | copy-start | bytes 1572868
  22.9 30.9 %copy-start.9 = (s32[8,2]{0,1:T(2,128)S(1)}, s32[8,2]{0,1:T(2,128)}, u32[]{:S(2)}) copy-start(s32[8,2]{0,1:T(2,128)} %param.11) | copy-start | bytes 196
  23.0 16.1 %all-to-all-start.1 = ((bf16[8,1,3,128,128]{4,3,2,1,0:T(8,128)(2,1)}), bf16[8,1,3,128,128]{4,3,2,1,0:T(8,128)(2,1)S(1)}, u32[]{:S(2)}, u32[]{:S(2)}) async-start(bf16[8,1,3,128,128]{4,3,2,1,0:T(8,128)(2,1)} %second.1), calls=%async_computation.1 | async-start | bytes 1572864 | tf_op jit(solution)/shard_map/all_to_all | solution.py:32
  26.5 22.1 %collective-permute-start.5 = (bf16[8,2,128,128]{3,2,1,0:T(8,128)(2,1)S(1)}, bf16[8,2,128,128]{3,2,1,0:T(8,128)(2,1)S(1)}, u32[]{:S(2)}, u32[]{:S(2)}) collective-permute-start(bf16[8,2,128,128]{3,2,1,0:T(8,128)(2,1)S(1)} %bitcast.7), channel_id=1, source_target_pairs={{24,0},{0,8},{8,16},{16,24},{25,1},{1,9},{9,17},{17,25},{26,2},{2,... | collective-permute-start | bytes 1572872 | tf_op jit(solution)/shard_map/ppermute | solution.py:28
  27.6 26.3 %collective-permute-start.6 = (bf16[8,2,128,128]{3,2,1,0:T(8,128)(2,1)S(1)}, bf16[8,2,128,128]{3,2,1,0:T(8,128)(2,1)S(1)}, u32[]{:S(2)}, u32[]{:S(2)}) collective-permute-start(bf16[8,2,128,128]{3,2,1,0:T(8,128)(2,1)S(1)} %bitcast.8), channel_id=1, source_target_pairs={{8,0},{16,8},{24,16},{0,24},{9,1},{17,9},{25,17},{1,25},{10,2},{18... | collective-permute-start | bytes 1572872 | tf_op jit(solution)/shard_map/ppermute | solution.py:28
  30.4 0.7 copy-start.8
  39.1 26.8 %all-to-all-start.2 = ((bf16[8,1,3,128,128]{4,3,2,1,0:T(8,128)(2,1)}), bf16[8,1,3,128,128]{4,3,2,1,0:T(8,128)(2,1)S(1)}, u32[]{:S(2)}, u32[]{:S(2)}) async-start(bf16[8,1,3,128,128]{4,3,2,1,0:T(8,128)(2,1)} %third.1), calls=%async_computation.2 | async-start | bytes 1572864 | tf_op jit(solution)/shard_map/all_to_all | solution.py:32
  42.8 11.1 %collective-permute-start = (s32[34]{0:T(128)S(1)}, s32[34]{0:T(128)S(1)}, u32[]{:S(2)}, u32[]{:S(2)}) collective-permute-start(s32[34]{0:T(128)S(1)} %pad_add_fusion.own), channel_id=1, source_target_pairs={{0,4},{4,0},{1,5},{5,1},{2,6},{6,2},{3,7},{7,3},{8,12},{12,8},{9,1... | collective-permute-start | bytes 416 | tf_op jit(solution)/shard_map/ppermute | solution.py:287
  44.7 19.7 %collective-permute-start.3 = (bf16[8,1,128,128]{3,2,1,0:T(8,128)(2,1)S(1)}, bf16[8,1,128,128]{3,2,1,0:T(8,128)(2,1)S(1)}, u32[]{:S(2)}, u32[]{:S(2)}) collective-permute-start(bf16[8,1,128,128]{3,2,1,0:T(8,128)(2,1)S(1)} %slice.7.refs_1_), channel_id=1, source_target_pairs={{24,0},{0,8},{8,16},{16,24},{25,1},{1,9},{9,17},{17,25},{26,2},{2,... | collective-permute-start | bytes 786440 | tf_op jit(solution)/shard_map/ppermute | solution.py:28
  45.8 19.3 %collective-permute-start.4 = (bf16[8,1,128,128]{3,2,1,0:T(8,128)(2,1)S(1)}, bf16[8,1,128,128]{3,2,1,0:T(8,128)(2,1)S(1)}, u32[]{:S(2)}, u32[]{:S(2)}) collective-permute-start(bf16[8,1,128,128]{3,2,1,0:T(8,128)(2,1)S(1)} %slice.7.refs_1_), channel_id=1, source_target_pairs={{8,0},{16,8},{24,16},{0,24},{9,1},{17,9},{25,17},{1,25},{10,2},{18... | collective-permute-start | bytes 786440 | tf_op jit(solution)/shard_map/ppermute | solution.py:28
  60.7 3.7 %copy-start = (bf16[2,8,256,1152]{3,2,1,0:T(8,128)(2,1)}, bf16[2,8,256,1152]{3,2,1,0:T(8,128)(2,1)S(1)}, u32[]{:S(2)}) copy-start(bf16[2,8,256,1152]{3,2,1,0:T(8,128)(2,1)S(1)} %scores.1.refs_4_) | copy-start | bytes 28311556
  64.4 0.7 copy-start.4
  65.1 0.7 copy-start.6
  65.8 3.7 %copy-start.1 = (bf16[2,8,256,1152]{3,2,1,0:T(8,128)(2,1)S(1)}, bf16[2,8,256,1152]{3,2,1,0:T(8,128)(2,1)}, u32[]{:S(2)}) copy-start(bf16[2,8,256,1152]{3,2,1,0:T(8,128)(2,1)} %copy-done) | copy-start | bytes 28311556
  69.5 0.9 %copy-start.5 = (bf16[8,1,128,128]{3,2,1,0:T(8,128)(2,1)S(1)}, bf16[8,1,128,128]{3,2,1,0:T(8,128)(2,1)}, u32[]{:S(2)}) copy-start(bf16[8,1,128,128]{3,2,1,0:T(8,128)(2,1)} %copy-done.4) | copy-start | bytes 786436
  70.5 0.9 %copy-start.7 = (bf16[8,1,128,128]{3,2,1,0:T(8,128)(2,1)S(1)}, bf16[8,1,128,128]{3,2,1,0:T(8,128)(2,1)}, u32[]{:S(2)}) copy-start(bf16[8,1,128,128]{3,2,1,0:T(8,128)(2,1)} %copy-done.6) | copy-start | bytes 786436

commit v3 on v1

--- a/solution.py
+++ b/solution.py
@@ -81,17 +81,16 @@
         pltpu.make_async_copy(out, out, sem).wait()
 
 
-def last_kernel(plan, slots_ref, x0, x1, out, sem):
-    ways, tiles, _, _, share = x0.shape
-    for b, x in enumerate((x0, x1)):
-        slot = slot_of(plan, slots_ref, 0, b)
+def last_kernel(plan, x, out, sem):
+    ways, tiles, slots, _, share = x.shape
+    for s in range(slots):
         for m in range(tiles):
             for w in range(ways):
                 rows, lanes = pl.ds(m * TILE, TILE), pl.ds(w * share, share)
                 if plan.whole_lanes:
-                    pltpu.make_async_copy(x.at[w, m, 0], out.at[0, slot, rows, lanes], sem).start()
+                    pltpu.make_async_copy(x.at[w, m, s], out.at[0, s, rows, lanes], sem).start()
                 else:
-                    out[0, slot, rows, lanes] = x[w, m, 0]
+                    out[0, s, rows, lanes] = x[w, m, s]
     if plan.whole_lanes:
         pltpu.make_async_copy(out, out, sem).wait()
 
@@ -158,8 +157,11 @@
     return [jnp.exp2((part - top) * factor).astype(jnp.bfloat16) for part in parts]
 
 
+def with_ones(v):
+    return jnp.concatenate([v, jnp.ones_like(v)], axis=1)
+
+
 def weigh(p, v):
-    v = jnp.concatenate([v, jnp.ones_like(v)], axis=1)
     return jnp.dot(p, v, preferred_element_type=jnp.float32)
 
 
@@ -176,85 +178,16 @@
     return buffer[g, j].reshape(plan.kt * TILE, plan.share)
 
 
-def attend_kernel(plan, branch, weighs, n_early, n_late, own, other, *refs):
-    scores = n_early > 0
-    h = plan.hops
-    facts = (own, other)
-    given, refs = refs[0], refs[1:]
-    planes, late = refs[:n_early], refs[n_early:n_early + n_late]
-    out, result, k_far, v_far, far_sem, out_sem = refs[-6:]
-    mixed = given
-    half = TILE // 2
-    mine, low, high = pl.ds(branch * half, half), pl.ds(0, half), pl.ds(half, half)
-
-    def values_at(d, tiles):
-        return late[d].at[tiles, 0] if late else planes[d].at[tiles, 1]
-
-    def far_copies(g, j, d, tiles_at):
-        tiles = pl.ds(tiles_at, plan.kt)
-        found = []
-        if scores:
-            found.append((mixed.at[tiles, 2 + d, mine], k_far.at[g, j, :, low]))
-            found.append((planes[d].at[tiles, 0, mine], k_far.at[g, j, :, high]))
-        if weighs:
-            found.append((values_at(d, tiles), v_far.at[g, j]))
-        return [
-            pltpu.make_async_copy(src, to, far_sem.at[i, g, j]) for i, (src, to) in enumerate(found)
-        ]
-
-    start_far(plan, facts, far_copies)
+def each_view(plan, wait, one_tile, prepare):
     count = math.gcd(plan.kt, 4)
-    rows, wide = plan.rows, plan.kt * TILE
 
     def some_tiles(g, t0):
-        tiles = [(g * plan.kt + t0 + i, t0 + i) for i in range(count)]
-        if scores:
-            q = [split_heads(plan, mixed[at, branch]) for at, _ in tiles]
-            k_own = [
-                jnp.concatenate([mixed[at, 2 + h, mine], planes[h][at, 0, mine]], axis=0)
-                for at, _ in tiles
-            ]
-            own_scores = [scores_of(a, b) for a, b in zip(q, k_own)]
-            q = jnp.concatenate(q, axis=0)
-            far = [scores_of(q, far_rows(plan, k_far, g, j)) for j in range(NB)]
-            expo = [
-                numerators(
-                    plan, facts, g, t, own_scores[i],
-                    [far[j][i * rows:(i + 1) * rows] for j in range(NB)],
-                )
-                for i, (_, t) in enumerate(tiles)
-            ]
-            if not weighs:
-                for (at, _), parts in zip(tiles, expo):
-                    for i, part in enumerate(parts):
-                        out[at, :, i * TILE:(i + 1) * TILE] = part
-                return
-            expo_own = [parts[0] for parts in expo]
-            expo_far = [
-                jnp.concatenate([
-                    jnp.concatenate(parts[1 + j * plan.kt:1 + (j + 1) * plan.kt], axis=1)
-                    for parts in expo
-                ], axis=0)
-                for j in range(NB)
-            ]
-        else:
-            expo_own = [given[at, :, :TILE] for at, _ in tiles]
-            expo_far = [
-                jnp.concatenate([
-                    given[at, :, TILE + j * wide:TILE + (j + 1) * wide] for at, _ in tiles
-                ], axis=0)
-                for j in range(NB)
-            ]
-        total = sum(weigh(expo_far[j], far_rows(plan, v_far, g, j)) for j in range(NB))
-        for i, (at, _) in enumerate(tiles):
-            v_own = late[h][at, 0] if late else planes[h][at, 1]
-            mine_too = total[i * rows:(i + 1) * rows] + weigh(expo_own[i], v_own)
-            result[at, 0] = finish(plan, mine_too)
+        ready = prepare(g)
+        for i in range(count):
+            one_tile(g, t0 + i, ready)
 
     def one_view(g, carry):
-        for j in range(NB):
-            for copy in far_copies(g, j, plan.hops, 0):
-                copy.wait()
+        wait(g)
         if count == plan.kt:
             some_tiles(g, 0)
         else:
@@ -262,14 +195,107 @@
                 some_tiles(g, i * count)
                 return c
             lax.fori_loop(0, plan.kt // count, some, 0)
-        if weighs:
-            tiles = pl.ds(g * plan.kt, plan.kt)
-            pltpu.make_async_copy(result.at[tiles], out.at[tiles], out_sem).start()
         return carry
 
     lax.fori_loop(0, plan.sub, one_view, 0)
-    if weighs:
-        pltpu.make_async_copy(result, out, out_sem).wait()
+
+
+def core_kernel(plan, own, other, mixed, *refs):
+    n, h = plan.planes, plan.hops
+    planes = refs[:n]
+    out, expo_ref, k_far, v_far, k_sem, v_sem = refs[-6:]
+    facts = (own, other)
+    half = TILE // 2
+    low, high = pl.ds(0, half), pl.ds(half, half)
+    mine = [pl.ds(b * half, half) for b in range(2)]
+
+    def far_copies(g, j, d, tiles_at):
+        tiles = pl.ds(tiles_at, plan.kt)
+        found = []
+        for b in range(2):
+            found.append((mixed.at[tiles, 2 + d, mine[b]], k_far.at[b, g, j, :, low], k_sem.at[0, b, g, j]))
+            found.append((planes[d].at[tiles, 0, mine[b]], k_far.at[b, g, j, :, high], k_sem.at[1, b, g, j]))
+            if b == 0:
+                found.append((planes[d].at[tiles, 1], v_far.at[g, j], v_sem.at[g, j]))
+        return [pltpu.make_async_copy(*copy) for copy in found]
+
+    start_far(plan, facts, far_copies)
+
+    def wait(b, g):
+        for j in range(NB):
+            for part, rows in enumerate((low, high)):
+                there = k_far.at[b, g, j, :, rows]
+                pltpu.make_async_copy(there, there, k_sem.at[part, b, g, j]).wait()
+            if b == 0:
+                there = v_far.at[g, j]
+                pltpu.make_async_copy(there, there, v_sem.at[g, j]).wait()
+
+    def expo_of(b, g, t, k):
+        at = g * plan.kt + t
+        q = split_heads(plan, mixed[at, b])
+        k_own = jnp.concatenate([mixed[at, 2 + h, mine[b]], planes[h][at, 0, mine[b]]], axis=0)
+        return numerators(
+            plan, facts, g, t, scores_of(q, k_own), [scores_of(q, k[j]) for j in range(NB)]
+        )
+
+    def keys(b, g):
+        return [far_rows(plan, k_far.at[b], g, j) for j in range(NB)]
+
+    def attended(g, t, ready):
+        k, v = ready
+        at = g * plan.kt + t
+        expo = expo_of(0, g, t, k)
+        total = weigh(expo[0], with_ones(planes[h][at, 1]))
+        for j in range(NB):
+            p = jnp.concatenate(expo[1 + j * plan.kt:1 + (j + 1) * plan.kt], axis=1)
+            total += weigh(p, v[j])
+        out[at, 0] = finish(plan, total)
+
+    def scored(g, t, k):
+        for i, part in enumerate(expo_of(1, g, t, k)):
+            expo_ref[g * plan.kt + t, :, i * TILE:(i + 1) * TILE] = part
+
+    each_view(
+        plan, functools.partial(wait, 0), attended,
+        lambda g: (keys(0, g), [with_ones(far_rows(plan, v_far, g, j)) for j in range(NB)]),
+    )
+    each_view(plan, functools.partial(wait, 1), scored, functools.partial(keys, 1))
+
+
+def weigh_kernel(plan, own, other, slots, expo, done, *refs):
+    n, h = plan.planes, plan.hops
+    late = refs[:n]
+    out, v_far, far_sem = refs[-3:]
+
+    def stored(g, b):
+        return slots[b, lax.axis_index("plane") * plan.sub + g]
+
+    def far_copies(g, j, d, tiles_at):
+        src = late[d].at[pl.ds(tiles_at, plan.kt), 0]
+        return [pltpu.make_async_copy(src, v_far.at[g, j], far_sem.at[g, j])]
+
+    start_far(plan, (own, other), far_copies)
+    for g in range(plan.sub):
+        for t in range(plan.kt):
+            out[g * plan.kt + t, stored(g, 0)] = done[g * plan.kt + t, 0]
+
+    def wait(g):
+        for j in range(NB):
+            there = v_far.at[g, j]
+            pltpu.make_async_copy(there, there, far_sem.at[g, j]).wait()
+
+    def one_tile(g, t, v):
+        at = g * plan.kt + t
+        wide = plan.kt * TILE
+        total = weigh(expo[at, :, :TILE], with_ones(late[h][at, 0]))
+        for j in range(NB):
+            total += weigh(expo[at, :, TILE + j * wide:TILE + (j + 1) * wide], v[j])
+        out[at, stored(g, 1)] = finish(plan, total)
+
+    each_view(
+        plan, wait, one_tile,
+        lambda g: [with_ones(far_rows(plan, v_far, g, j)) for j in range(NB)],
+    )
 
 
 def call(kernel, name, out_shape, in_specs, out_specs, scratch, args, flops=0, exps=0, moved=0,
@@ -369,33 +395,31 @@
     planes = [planes[d] for d in order]
     late = [late[d] for d in order]
 
-    result = (ways * tiles, 1, TILE, share)
-
-    def attend(name, branch, given, planes, late, weighs, out_shape):
-        far = pltpu.VMEM((sub, NB, kt, TILE, share), dtype)
-        ins = [given] + planes + late
-        parts = (1 if planes else 0) + (1 if weighs else 0)
-        return call(
-            functools.partial(attend_kernel, plan, branch, weighs, len(planes), len(late)), name,
-            jax.ShapeDtypeStruct(out_shape, dtype),
-            [SMEM] * 2 + [VMEM] * len(ins) + [ANY], ANY if weighs else VMEM,
-            [pltpu.VMEM(result, dtype), far, far, pltpu.SemaphoreType.DMA((3, sub, NB)), sem],
-            (*facts, *ins, brought), flops=plan.pairs * HD * 2 * parts,
-            exps=plan.pairs if planes else 0, moved=2 * size, mib=24,
-        )
-
-    def back(x):
-        return exchange(x.reshape(ways, tiles, 1, TILE, share))
-
-    x0 = back(attend("attend", 0, mixed, planes, [], True, result))
-    expo = attend(
-        "scores", 1, mixed, planes, [], False, (sub * kt, plan.rows, plan.cols)
-    )
-    x1 = back(attend("weigh", 1, expo, [], late, True, result))
+    def result(n):
+        return jax.ShapeDtypeStruct((ways * tiles, n, TILE, share), dtype)
+
+    sems = pltpu.SemaphoreType.DMA
+    far = (sub, NB, kt, TILE, share)
+    expo = jax.ShapeDtypeStruct((sub * kt, plan.rows, plan.cols), dtype)
+    out0, expo = call(
+        functools.partial(core_kernel, plan), "core", (result(1), expo),
+        [SMEM] * 2 + [VMEM] * (1 + plan.planes) + [ANY], (VMEM, VMEM),
+        [pltpu.VMEM((2, *far), dtype), pltpu.VMEM(far, dtype), sems((2, 2, sub, NB)),
+         sems((sub, NB))],
+        (*facts, mixed, *planes, brought), flops=plan.pairs * HD * 6, exps=2 * plan.pairs,
+        moved=2 * size, mib=24,
+    )
+    x = call(
+        functools.partial(weigh_kernel, plan), "weigh", result(2),
+        [SMEM] * 3 + [VMEM] * (2 + plan.planes), VMEM,
+        [pltpu.VMEM(far, dtype), sems((sub, NB))], (*facts, slots, expo, out0, *late),
+        flops=plan.pairs * HD * 2, moved=2 * size, mib=24,
+    )
+    x = exchange(x.reshape(ways, tiles, 2, TILE, share))
     return call(
         functools.partial(last_kernel, plan), "last",
-        jax.ShapeDtypeStruct(queries.shape, dtype), [SMEM, place, place], place, [sem],
-        (slots, x0, x1), moved=2 * size,
+        jax.ShapeDtypeStruct(queries.shape, dtype), [place], place, [sem], (x,),
+        moved=2 * size,
     )
 
 

time: 84.5 us -> 81.7 us (0.967)
  starting transfers between devices: 26.2 us -> 21.3 us
  Pallas kernels: 21.2 us -> 16.5 us
  blocking collectives: 10.9 us -> 14.4 us
  local copies, waits for them, and re-layouts: 1.82 us -> 3.75 us
  waiting for transfers between devices: 23.6 us -> 25.2 us
    all_to_all x3 -> x2, starting transfers between devices: 12.1 us -> 7.32 us  [exchange(): return lax.all_to_all(x, GROUP, split_axis=0, concat_axis=0, tiled=True)]
    pallas_call x8 -> x7, Pallas kernels: 21.2 us -> 16.5 us  [call(): pl.pallas_call(kernel, out_shape=out_shape, in_specs=in_specs, out_specs=...]
    all_to_all x1, blocking collectives: 10.9 us -> 14.4 us  [exchange(): return lax.all_to_all(x, GROUP, split_axis=0, concat_axis=0, tiled=True)]
    ppermute x6, waiting for transfers between devices: 20.3 us -> 21.9 us  [from_plane(): return lax.ppermute(x, 'plane', [((i + by) % size, i) for i in range(size)])]
    unnamed x10 -> x12, local copies, waits for them, and re-layouts: 0.71 us -> 1.85 us
    all_to_all x3 -> x2, waiting for transfers between devices: 2.99 us -> 2.99 us  [exchange(): return lax.all_to_all(x, GROUP, split_axis=0, concat_axis=0, tiled=True)]
  transfers between devices with their start and end apart: 10 -> 9, of which waited for: 6 -> 7; matrix products, arithmetic and copies ran while one was open for 0% -> 0% of each run, Pallas kernels for 24% -> 15%
where the time goes in v3:
time: 81.7 us; the launch traced here: 81.3 us
  waiting for transfers between devices  25.2 us (31%)
  starting transfers between devices  21.3 us (26%)
  Pallas kernels  16.5 us (20%)
  blocking collectives  14.4 us (18%)
  local copies, waits for them, and re-layouts  3.75 us (5%)
    ppermute x6, waiting for transfers between devices, from_plane(): return lax.ppermute(x, 'plane', [((i + by) % size, i) for i in range(size)])  21.9 us
    pallas_call x7, Pallas kernels, call(): pl.pallas_call(kernel, out_shape=out_shape, in_specs=in_specs, out_specs=...  16.5 us
    all_to_all x1, blocking collectives, exchange(): return lax.all_to_all(x, GROUP, split_axis=0, concat_axis=0, tiled=True)  14.4 us
    ppermute x6, starting transfers between devices, from_plane(): return lax.ppermute(x, 'plane', [((i + by) % size, i) for i in range(size)])  12.5 us
    all_to_all x2, starting transfers between devices, exchange(): return lax.all_to_all(x, GROUP, split_axis=0, concat_axis=0, tiled=True)  7.32 us
    all_to_all x2, waiting for transfers between devices, exchange(): return lax.all_to_all(x, GROUP, split_axis=0, concat_axis=0, tiled=True)  2.99 us
    unnamed x12, local copies, waits for them, and re-layouts  1.85 us
  transfers between devices with their start and end apart: 9, of which 7 were waited for; matrix products, arithmetic and copies ran while one was open for 0% of the time, Pallas kernels for 15%

profile of v3, /device:TPU:0, one launch (start us, length us, event | category | flops | bytes accessed | tf_op | source)
XLA Modules:
  0.0 81.3 jit_solution(10798469813926540896)
XLA Ops:
  0.0 1.0 %slice_bitcast_fusion.refs_2_ = bf16[1,2,64,1024]{3,2,1,0:T(8,128)(2,1)S(1)} fusion(bf16[1,2,1,128,1024]{4,3,1,2,0:T(8,128)(2,1)} %bitcast.17), kind=kLoop, calls=%fused_computation | loop fusion | bytes 524288 | tf_op jit(solution)/shard_map/reshape | solution.py:369
  1.0 3.1 %collective-permute-start = (bf16[1,2,64,1024]{3,2,1,0:T(8,128)(2,1)S(1)}, bf16[1,2,64,1024]{3,2,1,0:T(8,128)(2,1)S(1)}, u32[]{:S(2)}, u32[]{:S(2)}) collective-permute-start(bf16[1,2,64,1024]{3,2,1,0:T(8,128)(2,1)S(1)} %slice_bitcast_fusion.refs_2_), channel_id=1, source_target_pairs={{24,0},{0,8},{8,16},{16,24},{25,1},{1,9},{9,17},{17,25},{26,2},{2,... | collective-permute-start | bytes 786440 | tf_op jit(solution)/shard_map/ppermute | solution.py:31
  4.0 0.0 copy-start.4
  4.0 0.0 copy-start.5
  4.1 2.8 %first.1 = bf16[8,1,3,128,128]{4,3,2,1,0:T(8,128)(2,1)} custom-call(s32[2,8]{1,0:T(2,128)} %bitcast.13, s32[2,8]{1,0:T(2,128)} %bitcast.14, bf16[1,2,128,1024]{3,2,1,0:T(8,128)(2,1)} %refs_0_.2, bf16[1,2,128,1024]{3,2,1,0:T(8,128)(2,1)} %refs_1_.1), custom_call_target="tpu_custom_call" | custom-call | bytes 1572864 | tf_op jit(solution)/shard_map/first/pallas_call | solution.py:303
  6.8 3.7 %all-to-all-start = ((bf16[8,1,3,128,128]{4,3,2,1,0:T(8,128)(2,1)}), bf16[8,1,3,128,128]{4,3,2,1,0:T(8,128)(2,1)S(1)}, u32[]{:S(2)}, u32[]{:S(2)}) async-start(bf16[8,1,3,128,128]{4,3,2,1,0:T(8,128)(2,1)} %first.1), calls=%async_computation | async-start | bytes 1572864 | tf_op jit(solution)/shard_map/all_to_all | solution.py:35
  10.6 1.8 %collective-permute-done.refs_0_.refs_1_ = bf16[1,2,64,1024]{3,2,1,0:T(8,128)(2,1)S(1)} collective-permute-done((bf16[1,2,64,1024]{3,2,1,0:T(8,128)(2,1)S(1)}, bf16[1,2,64,1024]{3,2,1,0:T(8,128)(2,1)S(1)}, u32[]{:S(2)}, u32[]{:S(2)}) %collective-permute-start) | collective-permute-done | bytes 262176 | tf_op jit(solution)/shard_map/ppermute | solution.py:31
  12.4 1.7 %collective-permute-start.1 = (bf16[1,2,64,1024]{3,2,1,0:T(8,128)(2,1)S(1)}, bf16[1,2,64,1024]{3,2,1,0:T(8,128)(2,1)S(1)}, u32[]{:S(2)}, u32[]{:S(2)}) collective-permute-start(bf16[1,2,64,1024]{3,2,1,0:T(8,128)(2,1)S(1)} %slice_bitcast_fusion.refs_2_), channel_id=1, source_target_pairs={{8,0},{16,8},{24,16},{0,24},{9,1},{17,9},{25,17},{1,25},{10,2},{18... | collective-permute-start | bytes 786440 | tf_op jit(solution)/shard_map/ppermute | solution.py:31
  14.1 0.0 copy-done.4
  14.1 0.1 reshape.24
  14.2 0.0 copy-done.5
  14.2 0.1 pad_add_fusion.own
  14.3 0.0 copy-start.1
  14.3 1.5 %collective-permute-start.2 = (s32[34]{0:T(128)S(1)}, s32[34]{0:T(128)S(1)}, u32[]{:S(2)}, u32[]{:S(2)}) collective-permute-start(s32[34]{0:T(128)S(1)} %pad_add_fusion.own), channel_id=1, source_target_pairs={{0,4},{4,0},{1,5},{5,1},{2,6},{6,2},{3,7},{7,3},{8,12},{12,8},{9,1... | collective-permute-start | bytes 416 | tf_op jit(solution)/shard_map/ppermute | solution.py:333
  15.8 4.1 %collective-permute-done.1.refs_1_.refs_3_ = bf16[1,2,64,1024]{3,2,1,0:T(8,128)(2,1)S(1)} collective-permute-done((bf16[1,2,64,1024]{3,2,1,0:T(8,128)(2,1)S(1)}, bf16[1,2,64,1024]{3,2,1,0:T(8,128)(2,1)S(1)}, u32[]{:S(2)}, u32[]{:S(2)}) %collective-permute-start.1) | collective-permute-done | bytes 262176 | tf_op jit(solution)/shard_map/ppermute | solution.py:31
  19.9 0.0 copy-start
  19.9 0.3 collective-permute-done.2.other
  20.2 3.0 %all-to-all-done = bf16[8,1,3,128,128]{4,3,2,1,0:T(8,128)(2,1)S(1)} async-done(((bf16[8,1,3,128,128]{4,3,2,1,0:T(8,128)(2,1)}), bf16[8,1,3,128,128]{4,3,2,1,0:T(8,128)(2,1)S(1)}, u32[]{:S(2)}, u32[]{:S(2)}) %all-to-all-start) | async-done | bytes 786464 | tf_op jit(solution)/shard_map/all_to_all | solution.py:35
  23.2 0.8 %slice.10 = bf16[8,2,128,128]{3,2,1,0:T(8,128)(2,1)} slice(bf16[8,3,128,128]{3,2,1,0:T(8,128)(2,1)S(1)} %bitcast.8), slice={[0:8], [0:2], [0:128], [0:128]} | slice | bytes 1048576 | tf_op jit(solution)/shard_map/slice | solution.py:380
  24.0 1.6 %collective-permute-start.3 = (bf16[8,2,128,128]{3,2,1,0:T(8,128)(2,1)}, bf16[8,2,128,128]{3,2,1,0:T(8,128)(2,1)S(1)}, u32[]{:S(2)}, u32[]{:S(2)}) collective-permute-start(bf16[8,2,128,128]{3,2,1,0:T(8,128)(2,1)} %slice.10), channel_id=1, source_target_pairs={{24,0},{0,8},{8,16},{16,24},{25,1},{1,9},{9,17},{17,25},{26,2},{2,... | collective-permute-start | bytes 1572872 | tf_op jit(solution)/shard_map/ppermute | solution.py:31
  25.6 2.2 %collective-permute-start.4 = (bf16[8,2,128,128]{3,2,1,0:T(8,128)(2,1)}, bf16[8,2,128,128]{3,2,1,0:T(8,128)(2,1)S(1)}, u32[]{:S(2)}, u32[]{:S(2)}) collective-permute-start(bf16[8,2,128,128]{3,2,1,0:T(8,128)(2,1)} %slice.10), channel_id=1, source_target_pairs={{8,0},{16,8},{24,16},{0,24},{9,1},{17,9},{25,17},{1,25},{10,2},{18... | collective-permute-start | bytes 1572872 | tf_op jit(solution)/shard_map/ppermute | solution.py:31
  27.8 0.0 copy-done.1
  27.8 0.0 copy-done
  27.8 1.7 %second.1 = bf16[8,1,5,128,128]{4,3,2,1,0:T(8,128)(2,1)} custom-call(s32[2,8]{1,0:T(2,128)S(1)} %bitcast.15, f32[8,128]{1,0:T(8,128)S(1)} %mark.2.mark_ref, bf16[1,2,128,1024]{3,2,1,0:T(8,128)(2,1)S(1)} %copy-done, bf16[1,2,64,1024]{3,2,1,0:T(8,128)(2,1)S(1)} %collective-permute-done.refs_0_.refs_1_, bf16[1,2,64,1024]{3,2,1,0:T(8,128)(2,1)S(1)} %slice_bitcast_fusion.refs_2_, ...), custom_call_target="tpu_custom_call" | custom-call | bytes 2621440 | tf_op jit(solution)/shard_map/second/pallas_call | solution.py:303
  29.5 3.6 %all-to-all-start.1 = ((bf16[8,1,5,128,128]{4,3,2,1,0:T(8,128)(2,1)}), bf16[8,1,5,128,128]{4,3,2,1,0:T(8,128)(2,1)S(1)}, u32[]{:S(2)}, u32[]{:S(2)}) async-start(bf16[8,1,5,128,128]{4,3,2,1,0:T(8,128)(2,1)} %second.1), calls=%async_computation.1 | async-start | bytes 2621440 | tf_op jit(solution)/shard_map/all_to_all | solution.py:35
  33.1 7.8 %collective-permute-done.3.refs_0_ = bf16[8,2,128,128]{3,2,1,0:T(8,128)(2,1)S(1)} collective-permute-done((bf16[8,2,128,128]{3,2,1,0:T(8,128)(2,1)}, bf16[8,2,128,128]{3,2,1,0:T(8,128)(2,1)S(1)}, u32[]{:S(2)}, u32[]{:S(2)}) %collective-permute-start.3) | collective-permute-done | bytes 524320 | tf_op jit(solution)/shard_map/ppermute | solution.py:31
  40.9 6.7 %collective-permute-done.4.refs_1_.refs_2_ = bf16[8,2,128,128]{3,2,1,0:T(8,128)(2,1)S(1)} collective-permute-done((bf16[8,2,128,128]{3,2,1,0:T(8,128)(2,1)}, bf16[8,2,128,128]{3,2,1,0:T(8,128)(2,1)S(1)}, u32[]{:S(2)}, u32[]{:S(2)}) %collective-permute-start.4) | collective-permute-done | bytes 524320 | tf_op jit(solution)/shard_map/ppermute | solution.py:31
  47.6 0.0 copy-start.2
  47.6 0.8 copy-done.2
  48.4 1.1 %collective-permute-start.5 = (bf16[8,1,128,128]{3,2,1,0:T(8,128)(2,1)S(1)}, bf16[8,1,128,128]{3,2,1,0:T(8,128)(2,1)S(1)}, u32[]{:S(2)}, u32[]{:S(2)}) collective-permute-start(bf16[8,1,128,128]{3,2,1,0:T(8,128)(2,1)S(1)} %slice.11.refs_1_), channel_id=1, source_target_pairs={{24,0},{0,8},{8,16},{16,24},{25,1},{1,9},{9,17},{17,25},{26,2},{2,... | collective-permute-start | bytes 786440 | tf_op jit(solution)/shard_map/ppermute | solution.py:31
  49.5 2.8 %collective-permute-start.6 = (bf16[8,1,128,128]{3,2,1,0:T(8,128)(2,1)S(1)}, bf16[8,1,128,128]{3,2,1,0:T(8,128)(2,1)S(1)}, u32[]{:S(2)}, u32[]{:S(2)}) collective-permute-start(bf16[8,1,128,128]{3,2,1,0:T(8,128)(2,1)S(1)} %slice.11.refs_1_), channel_id=1, source_target_pairs={{8,0},{16,8},{24,16},{0,24},{9,1},{17,9},{25,17},{1,25},{10,2},{18... | collective-permute-start | bytes 786440 | tf_op jit(solution)/shard_map/ppermute | solution.py:31
  52.2 0.0 all-to-all-done.1
  52.2 0.0 copy-start.3
  52.2 1.0 %copy-done.3 = bf16[8,2,128,128]{3,2,1,0:T(8,128)(2,1)S(1)} copy-done((bf16[8,2,128,128]{3,2,1,0:T(8,128)(2,1)S(1)}, bf16[8,2,128,128]{3,2,1,0:T(8,128)(2,1)}, u32[]{:S(2)}) %copy-start.3) | copy-done | bytes 524312
  53.3 8.2 %core.1 = (bf16[8,1,128,128]{3,2,1,0:T(8,128)(2,1)S(1)}, bf16[8,256,1152]{2,1,0:T(8,128)(2,1)S(1)}) custom-call(s32[34]{0:T(128)S(1)} %pad_add_fusion.own, s32[34]{0:T(128)S(1)} %collective-permute-done.2.other, bf16[8,5,128,128]{3,2,1,0:T(8,128)(2,1)S(1)} %bitcast.12, bf16[8,2,128,128]{3,2,1,0:T(8,128)(2,1)S(1)} %collective-permute-done.3.refs_0_, ...), custom_call_target="tpu_custom_call" | custom-call | flops 905969664 | bytes 1048576 | tf_op jit(solution)/shard_map/core/pallas_call | solution.py:303
  61.4 0.0 collective-permute-done.5.refs_0_
  61.5 1.6 %collective-permute-done.6.refs_2_ = bf16[8,1,128,128]{3,2,1,0:T(8,128)(2,1)S(1)} collective-permute-done((bf16[8,1,128,128]{3,2,1,0:T(8,128)(2,1)S(1)}, bf16[8,1,128,128]{3,2,1,0:T(8,128)(2,1)S(1)}, u32[]{:S(2)}, u32[]{:S(2)}) %collective-permute-start.6) | collective-permute-done | bytes 262176 | tf_op jit(solution)/shard_map/ppermute | solution.py:31
  63.0 3.1 %weigh.1 = bf16[8,2,128,128]{3,2,1,0:T(8,128)(2,1)S(1)} custom-call(s32[34]{0:T(128)S(1)} %pad_add_fusion.own, s32[34]{0:T(128)S(1)} %collective-permute-done.2.other, s32[2,8]{1,0:T(2,128)S(1)} %bitcast.16, bf16[8,256,1152]{2,1,0:T(8,128)(2,1)S(1)} %get-tuple-element.20.expo, bf16[8,1,128,128]{3,2,1,0:T(8,128)(2,1)S(1)} %get-tuple-element.21.done, ...), custom_call_target="tpu_custom_call" | custom-call | flops 301989888 | bytes 1048576 | tf_op jit(solution)/shard_map/weigh/pallas_call | solution.py:303
  66.1 14.4 %all_to_all.15.x = bf16[8,1,2,128,128]{4,3,2,1,0:T(8,128)(2,1)S(1)} all-to-all(bf16[8,1,2,128,128]{4,3,2,1,0:T(8,128)(2,1)S(1)} %bitcast.11), channel_id=1, replica_groups=mesh['plane'=4,'sub'=2,'tok'=4] {'sub','tok'}, dimensions={0} | all-to-all | bytes 1048576 | tf_op jit(solution)/shard_map/all_to_all | solution.py:35
  80.5 0.8 last.1
  (3 shorter events, 0.0 us)
Async XLA Ops:
  1.0 11.4 %collective-permute-start = (bf16[1,2,64,1024]{3,2,1,0:T(8,128)(2,1)S(1)}, bf16[1,2,64,1024]{3,2,1,0:T(8,128)(2,1)S(1)}, u32[]{:S(2)}, u32[]{:S(2)}) collective-permute-start(bf16[1,2,64,1024]{3,2,1,0:T(8,128)(2,1)S(1)} %slice_bitcast_fusion.refs_2_), channel_id=1, source_target_pairs={{24,0},{0,8},{8,16},{16,24},{25,1},{1,9},{9,17},{17,25},{26,2},{2,... | collective-permute-start | bytes 786440 | tf_op jit(solution)/shard_map/ppermute | solution.py:31
  4.0 10.1 %copy-start.4 = (s32[1,2,4,4]{3,2,1,0:T(4,128)S(1)}, s32[1,2,4,4]{3,2,1,0:T(4,128)}, u32[]{:S(2)}) copy-start(s32[1,2,4,4]{3,2,1,0:T(4,128)} %param.9) | copy-start | bytes 388
  4.0 10.2 %copy-start.5 = (s32[1,2]{1,0:T(1,128)S(1)}, s32[1,2]{1,0:T(1,128)}, u32[]{:S(2)}) copy-start(s32[1,2]{1,0:T(1,128)} %param.10) | copy-start | bytes 28
  6.8 16.3 %all-to-all-start = ((bf16[8,1,3,128,128]{4,3,2,1,0:T(8,128)(2,1)}), bf16[8,1,3,128,128]{4,3,2,1,0:T(8,128)(2,1)S(1)}, u32[]{:S(2)}, u32[]{:S(2)}) async-start(bf16[8,1,3,128,128]{4,3,2,1,0:T(8,128)(2,1)} %first.1), calls=%async_computation | async-start | bytes 1572864 | tf_op jit(solution)/shard_map/all_to_all | solution.py:35
  12.4 7.5 %collective-permute-start.1 = (bf16[1,2,64,1024]{3,2,1,0:T(8,128)(2,1)S(1)}, bf16[1,2,64,1024]{3,2,1,0:T(8,128)(2,1)S(1)}, u32[]{:S(2)}, u32[]{:S(2)}) collective-permute-start(bf16[1,2,64,1024]{3,2,1,0:T(8,128)(2,1)S(1)} %slice_bitcast_fusion.refs_2_), channel_id=1, source_target_pairs={{8,0},{16,8},{24,16},{0,24},{9,1},{17,9},{25,17},{1,25},{10,2},{18... | collective-permute-start | bytes 786440 | tf_op jit(solution)/shard_map/ppermute | solution.py:31
  14.3 13.5 %copy-start.1 = (s32[8,2]{0,1:T(2,128)S(1)}, s32[8,2]{0,1:T(2,128)}, u32[]{:S(2)}) copy-start(s32[8,2]{0,1:T(2,128)} %param.11) | copy-start | bytes 196
  14.3 5.9 %collective-permute-start.2 = (s32[34]{0:T(128)S(1)}, s32[34]{0:T(128)S(1)}, u32[]{:S(2)}, u32[]{:S(2)}) collective-permute-start(s32[34]{0:T(128)S(1)} %pad_add_fusion.own), channel_id=1, source_target_pairs={{0,4},{4,0},{1,5},{5,1},{2,6},{6,2},{3,7},{7,3},{8,12},{12,8},{9,1... | collective-permute-start | bytes 416 | tf_op jit(solution)/shard_map/ppermute | solution.py:333
  19.9 8.0 %copy-start = (bf16[1,2,128,1024]{3,2,1,0:T(8,128)(2,1)S(1)}, bf16[1,2,128,1024]{3,2,1,0:T(8,128)(2,1)}, u32[]{:S(2)}) copy-start(bf16[1,2,128,1024]{3,2,1,0:T(8,128)(2,1)} %refs_0_.3) | copy-start | bytes 1572868
  24.0 16.9 %collective-permute-start.3 = (bf16[8,2,128,128]{3,2,1,0:T(8,128)(2,1)}, bf16[8,2,128,128]{3,2,1,0:T(8,128)(2,1)S(1)}, u32[]{:S(2)}, u32[]{:S(2)}) collective-permute-start(bf16[8,2,128,128]{3,2,1,0:T(8,128)(2,1)} %slice.10), channel_id=1, source_target_pairs={{24,0},{0,8},{8,16},{16,24},{25,1},{1,9},{9,17},{17,25},{26,2},{2,... | collective-permute-start | bytes 1572872 | tf_op jit(solution)/shard_map/ppermute | solution.py:31
  25.6 22.0 %collective-permute-start.4 = (bf16[8,2,128,128]{3,2,1,0:T(8,128)(2,1)}, bf16[8,2,128,128]{3,2,1,0:T(8,128)(2,1)S(1)}, u32[]{:S(2)}, u32[]{:S(2)}) collective-permute-start(bf16[8,2,128,128]{3,2,1,0:T(8,128)(2,1)} %slice.10), channel_id=1, source_target_pairs={{8,0},{16,8},{24,16},{0,24},{9,1},{17,9},{25,17},{1,25},{10,2},{18... | collective-permute-start | bytes 1572872 | tf_op jit(solution)/shard_map/ppermute | solution.py:31
  29.5 22.7 %all-to-all-start.1 = ((bf16[8,1,5,128,128]{4,3,2,1,0:T(8,128)(2,1)}), bf16[8,1,5,128,128]{4,3,2,1,0:T(8,128)(2,1)S(1)}, u32[]{:S(2)}, u32[]{:S(2)}) async-start(bf16[8,1,5,128,128]{4,3,2,1,0:T(8,128)(2,1)} %second.1), calls=%async_computation.1 | async-start | bytes 2621440 | tf_op jit(solution)/shard_map/all_to_all | solution.py:35
  47.6 0.8 copy-start.2
  48.4 13.0 %collective-permute-start.5 = (bf16[8,1,128,128]{3,2,1,0:T(8,128)(2,1)S(1)}, bf16[8,1,128,128]{3,2,1,0:T(8,128)(2,1)S(1)}, u32[]{:S(2)}, u32[]{:S(2)}) collective-permute-start(bf16[8,1,128,128]{3,2,1,0:T(8,128)(2,1)S(1)} %slice.11.refs_1_), channel_id=1, source_target_pairs={{24,0},{0,8},{8,16},{16,24},{25,1},{1,9},{9,17},{17,25},{26,2},{2,... | collective-permute-start | bytes 786440 | tf_op jit(solution)/shard_map/ppermute | solution.py:31
  49.5 13.6 %collective-permute-start.6 = (bf16[8,1,128,128]{3,2,1,0:T(8,128)(2,1)S(1)}, bf16[8,1,128,128]{3,2,1,0:T(8,128)(2,1)S(1)}, u32[]{:S(2)}, u32[]{:S(2)}) collective-permute-start(bf16[8,1,128,128]{3,2,1,0:T(8,128)(2,1)S(1)} %slice.11.refs_1_), channel_id=1, source_target_pairs={{8,0},{16,8},{24,16},{0,24},{9,1},{17,9},{25,17},{1,25},{10,2},{18... | collective-permute-start | bytes 786440 | tf_op jit(solution)/shard_map/ppermute | solution.py:31
  52.2 1.0 %copy-start.3 = (bf16[8,2,128,128]{3,2,1,0:T(8,128)(2,1)S(1)}, bf16[8,2,128,128]{3,2,1,0:T(8,128)(2,1)}, u32[]{:S(2)}) copy-start(bf16[8,2,128,128]{3,2,1,0:T(8,128)(2,1)} %copy-done.2) | copy-start | bytes 1572868

commit v4 on v3

--- a/solution.py
+++ b/solution.py
@@ -378,8 +378,9 @@
     early, arrived, facts = lax.optimization_barrier((early, arrived, facts))
 
     planes = around(early[:, :2])
-    brought = mark([planes[d] for d in shifts], MARK_FLOPS[1])
-    last_values, brought = lax.optimization_barrier((early[:, 2:], brought))
+    last_values, planes = lax.optimization_barrier((early[:, 2:], planes))
+    brought = mark([last_values], MARK_FLOPS[1])
+    last_values, brought = lax.optimization_barrier((last_values, brought))
     late = around(last_values)
     moves = [Move(0, 0, 0), Move(0, 1, 1)]
     for d in order:
@@ -403,17 +404,17 @@
     expo = jax.ShapeDtypeStruct((sub * kt, plan.rows, plan.cols), dtype)
     out0, expo = call(
         functools.partial(core_kernel, plan), "core", (result(1), expo),
-        [SMEM] * 2 + [VMEM] * (1 + plan.planes) + [ANY], (VMEM, VMEM),
+        [SMEM] * 2 + [VMEM] + [ANY if d else VMEM for d in order] + [ANY], (VMEM, VMEM),
         [pltpu.VMEM((2, *far), dtype), pltpu.VMEM(far, dtype), sems((2, 2, sub, NB)),
          sems((sub, NB))],
         (*facts, mixed, *planes, brought), flops=plan.pairs * HD * 6, exps=2 * plan.pairs,
-        moved=2 * size, mib=24,
+        moved=2 * size, mib=12,
     )
     x = call(
         functools.partial(weigh_kernel, plan), "weigh", result(2),
         [SMEM] * 3 + [VMEM] * (2 + plan.planes), VMEM,
         [pltpu.VMEM(far, dtype), sems((sub, NB))], (*facts, slots, expo, out0, *late),
-        flops=plan.pairs * HD * 2, moved=2 * size, mib=24,
+        flops=plan.pairs * HD * 2, moved=2 * size, mib=12,
     )
     x = exchange(x.reshape(ways, tiles, 2, TILE, share))
     return call(

time: 81.7 us -> 81.7 us (level)
  no operation moved by 1% of the time
where the time goes in v4:
time: 81.7 us; the launch traced here: 81.3 us
  waiting for transfers between devices  25.2 us (31%)
  starting transfers between devices  21.3 us (26%)
  Pallas kernels  16.5 us (20%)
  blocking collectives  14.4 us (18%)
  local copies, waits for them, and re-layouts  3.75 us (5%)
    ppermute x6, waiting for transfers between devices, from_plane(): return lax.ppermute(x, 'plane', [((i + by) % size, i) for i in range(size)])  21.9 us
    pallas_call x7, Pallas kernels, call(): pl.pallas_call(kernel, out_shape=out_shape, in_specs=in_specs, out_specs=...  16.5 us
    all_to_all x1, blocking collectives, exchange(): return lax.all_to_all(x, GROUP, split_axis=0, concat_axis=0, tiled=True)  14.4 us
    ppermute x6, starting transfers between devices, from_plane(): return lax.ppermute(x, 'plane', [((i + by) % size, i) for i in range(size)])  12.5 us
    all_to_all x2, starting transfers between devices, exchange(): return lax.all_to_all(x, GROUP, split_axis=0, concat_axis=0, tiled=True)  7.32 us
    all_to_all x2, waiting for transfers between devices, exchange(): return lax.all_to_all(x, GROUP, split_axis=0, concat_axis=0, tiled=True)  2.99 us
    unnamed x12, local copies, waits for them, and re-layouts  1.85 us
  transfers between devices with their start and end apart: 9, of which 7 were waited for; matrix products, arithmetic and copies ran while one was open for 0% of the time, Pallas kernels for 15%

profile of v4, /device:TPU:0, one launch (start us, length us, event | category | flops | bytes accessed | tf_op | source)
XLA Modules:
  0.0 81.3 jit_solution(16143908299311788573)
XLA Ops:
  0.0 1.0 %slice_bitcast_fusion.refs_2_ = bf16[1,2,64,1024]{3,2,1,0:T(8,128)(2,1)S(1)} fusion(bf16[1,2,1,128,1024]{4,3,1,2,0:T(8,128)(2,1)} %bitcast.17), kind=kLoop, calls=%fused_computation | loop fusion | bytes 524288 | tf_op jit(solution)/shard_map/reshape | solution.py:369
  1.0 3.1 %collective-permute-start = (bf16[1,2,64,1024]{3,2,1,0:T(8,128)(2,1)S(1)}, bf16[1,2,64,1024]{3,2,1,0:T(8,128)(2,1)S(1)}, u32[]{:S(2)}, u32[]{:S(2)}) collective-permute-start(bf16[1,2,64,1024]{3,2,1,0:T(8,128)(2,1)S(1)} %slice_bitcast_fusion.refs_2_), channel_id=1, source_target_pairs={{24,0},{0,8},{8,16},{16,24},{25,1},{1,9},{9,17},{17,25},{26,2},{2,... | collective-permute-start | bytes 786440 | tf_op jit(solution)/shard_map/ppermute | solution.py:31
  4.0 0.0 copy-start.4
  4.0 0.0 copy-start.5
  4.1 2.8 %first.1 = bf16[8,1,3,128,128]{4,3,2,1,0:T(8,128)(2,1)} custom-call(s32[2,8]{1,0:T(2,128)} %bitcast.13, s32[2,8]{1,0:T(2,128)} %bitcast.14, bf16[1,2,128,1024]{3,2,1,0:T(8,128)(2,1)} %refs_0_.2, bf16[1,2,128,1024]{3,2,1,0:T(8,128)(2,1)} %refs_1_.1), custom_call_target="tpu_custom_call" | custom-call | bytes 1572864 | tf_op jit(solution)/shard_map/first/pallas_call | solution.py:303
  6.8 3.7 %all-to-all-start = ((bf16[8,1,3,128,128]{4,3,2,1,0:T(8,128)(2,1)}), bf16[8,1,3,128,128]{4,3,2,1,0:T(8,128)(2,1)S(1)}, u32[]{:S(2)}, u32[]{:S(2)}) async-start(bf16[8,1,3,128,128]{4,3,2,1,0:T(8,128)(2,1)} %first.1), calls=%async_computation | async-start | bytes 1572864 | tf_op jit(solution)/shard_map/all_to_all | solution.py:35
  10.6 1.8 %collective-permute-done.refs_0_.refs_1_ = bf16[1,2,64,1024]{3,2,1,0:T(8,128)(2,1)S(1)} collective-permute-done((bf16[1,2,64,1024]{3,2,1,0:T(8,128)(2,1)S(1)}, bf16[1,2,64,1024]{3,2,1,0:T(8,128)(2,1)S(1)}, u32[]{:S(2)}, u32[]{:S(2)}) %collective-permute-start) | collective-permute-done | bytes 262176 | tf_op jit(solution)/shard_map/ppermute | solution.py:31
  12.4 1.7 %collective-permute-start.1 = (bf16[1,2,64,1024]{3,2,1,0:T(8,128)(2,1)S(1)}, bf16[1,2,64,1024]{3,2,1,0:T(8,128)(2,1)S(1)}, u32[]{:S(2)}, u32[]{:S(2)}) collective-permute-start(bf16[1,2,64,1024]{3,2,1,0:T(8,128)(2,1)S(1)} %slice_bitcast_fusion.refs_2_), channel_id=1, source_target_pairs={{8,0},{16,8},{24,16},{0,24},{9,1},{17,9},{25,17},{1,25},{10,2},{18... | collective-permute-start | bytes 786440 | tf_op jit(solution)/shard_map/ppermute | solution.py:31
  14.1 0.0 copy-done.4
  14.1 0.1 reshape.24
  14.2 0.0 copy-done.5
  14.2 0.1 pad_add_fusion.own
  14.3 0.0 copy-start.1
  14.3 1.5 %collective-permute-start.2 = (s32[34]{0:T(128)S(1)}, s32[34]{0:T(128)S(1)}, u32[]{:S(2)}, u32[]{:S(2)}) collective-permute-start(s32[34]{0:T(128)S(1)} %pad_add_fusion.own), channel_id=1, source_target_pairs={{0,4},{4,0},{1,5},{5,1},{2,6},{6,2},{3,7},{7,3},{8,12},{12,8},{9,1... | collective-permute-start | bytes 416 | tf_op jit(solution)/shard_map/ppermute | solution.py:333
  15.8 4.1 %collective-permute-done.1.refs_1_.refs_3_ = bf16[1,2,64,1024]{3,2,1,0:T(8,128)(2,1)S(1)} collective-permute-done((bf16[1,2,64,1024]{3,2,1,0:T(8,128)(2,1)S(1)}, bf16[1,2,64,1024]{3,2,1,0:T(8,128)(2,1)S(1)}, u32[]{:S(2)}, u32[]{:S(2)}) %collective-permute-start.1) | collective-permute-done | bytes 262176 | tf_op jit(solution)/shard_map/ppermute | solution.py:31
  19.9 0.0 copy-start
  19.9 0.3 collective-permute-done.2.other
  20.2 3.0 %all-to-all-done = bf16[8,1,3,128,128]{4,3,2,1,0:T(8,128)(2,1)S(1)} async-done(((bf16[8,1,3,128,128]{4,3,2,1,0:T(8,128)(2,1)}), bf16[8,1,3,128,128]{4,3,2,1,0:T(8,128)(2,1)S(1)}, u32[]{:S(2)}, u32[]{:S(2)}) %all-to-all-start) | async-done | bytes 786464 | tf_op jit(solution)/shard_map/all_to_all | solution.py:35
  23.2 0.8 %slice.11 = bf16[8,2,128,128]{3,2,1,0:T(8,128)(2,1)} slice(bf16[8,3,128,128]{3,2,1,0:T(8,128)(2,1)S(1)} %bitcast.8), slice={[0:8], [0:2], [0:128], [0:128]} | slice | bytes 1048576 | tf_op jit(solution)/shard_map/slice | solution.py:380
  24.0 1.6 %collective-permute-start.3 = (bf16[8,2,128,128]{3,2,1,0:T(8,128)(2,1)}, bf16[8,2,128,128]{3,2,1,0:T(8,128)(2,1)S(1)}, u32[]{:S(2)}, u32[]{:S(2)}) collective-permute-start(bf16[8,2,128,128]{3,2,1,0:T(8,128)(2,1)} %slice.11), channel_id=1, source_target_pairs={{24,0},{0,8},{8,16},{16,24},{25,1},{1,9},{9,17},{17,25},{26,2},{2,... | collective-permute-start | bytes 1572872 | tf_op jit(solution)/shard_map/ppermute | solution.py:31
  25.6 2.2 %collective-permute-start.4 = (bf16[8,2,128,128]{3,2,1,0:T(8,128)(2,1)}, bf16[8,2,128,128]{3,2,1,0:T(8,128)(2,1)S(1)}, u32[]{:S(2)}, u32[]{:S(2)}) collective-permute-start(bf16[8,2,128,128]{3,2,1,0:T(8,128)(2,1)} %slice.11), channel_id=1, source_target_pairs={{8,0},{16,8},{24,16},{0,24},{9,1},{17,9},{25,17},{1,25},{10,2},{18... | collective-permute-start | bytes 1572872 | tf_op jit(solution)/shard_map/ppermute | solution.py:31
  27.8 0.0 copy-done.1
  27.8 0.0 copy-done
  27.8 1.7 %second.1 = bf16[8,1,5,128,128]{4,3,2,1,0:T(8,128)(2,1)} custom-call(s32[2,8]{1,0:T(2,128)S(1)} %bitcast.15, f32[8,128]{1,0:T(8,128)S(1)} %mark.2.mark_ref, bf16[1,2,128,1024]{3,2,1,0:T(8,128)(2,1)S(1)} %copy-done, bf16[1,2,64,1024]{3,2,1,0:T(8,128)(2,1)S(1)} %collective-permute-done.refs_0_.refs_1_, bf16[1,2,64,1024]{3,2,1,0:T(8,128)(2,1)S(1)} %slice_bitcast_fusion.refs_2_, ...), custom_call_target="tpu_custom_call" | custom-call | bytes 2621440 | tf_op jit(solution)/shard_map/second/pallas_call | solution.py:303
  29.5 3.6 %all-to-all-start.1 = ((bf16[8,1,5,128,128]{4,3,2,1,0:T(8,128)(2,1)}), bf16[8,1,5,128,128]{4,3,2,1,0:T(8,128)(2,1)S(1)}, u32[]{:S(2)}, u32[]{:S(2)}) async-start(bf16[8,1,5,128,128]{4,3,2,1,0:T(8,128)(2,1)} %second.1), calls=%async_computation.1 | async-start | bytes 2621440 | tf_op jit(solution)/shard_map/all_to_all | solution.py:35
  33.1 7.8 %collective-permute-done.3.refs_0_ = bf16[8,2,128,128]{3,2,1,0:T(8,128)(2,1)S(1)} collective-permute-done((bf16[8,2,128,128]{3,2,1,0:T(8,128)(2,1)}, bf16[8,2,128,128]{3,2,1,0:T(8,128)(2,1)S(1)}, u32[]{:S(2)}, u32[]{:S(2)}) %collective-permute-start.3) | collective-permute-done | bytes 524320 | tf_op jit(solution)/shard_map/ppermute | solution.py:31
  40.9 6.7 %collective-permute-done.4.refs_2_ = bf16[8,2,128,128]{3,2,1,0:T(8,128)(2,1)S(1)} collective-permute-done((bf16[8,2,128,128]{3,2,1,0:T(8,128)(2,1)}, bf16[8,2,128,128]{3,2,1,0:T(8,128)(2,1)S(1)}, u32[]{:S(2)}, u32[]{:S(2)}) %collective-permute-start.4) | collective-permute-done | bytes 524320 | tf_op jit(solution)/shard_map/ppermute | solution.py:31
  47.6 0.0 copy-start.2
  47.6 0.8 copy-done.2
  48.4 1.1 %collective-permute-start.5 = (bf16[8,1,128,128]{3,2,1,0:T(8,128)(2,1)S(1)}, bf16[8,1,128,128]{3,2,1,0:T(8,128)(2,1)S(1)}, u32[]{:S(2)}, u32[]{:S(2)}) collective-permute-start(bf16[8,1,128,128]{3,2,1,0:T(8,128)(2,1)S(1)} %slice.10.refs_0_.refs_1_), channel_id=1, source_target_pairs={{24,0},{0,8},{8,16},{16,24},{25,1},{1,9},{9,17},{17,25},{26,2},{2,... | collective-permute-start | bytes 786440 | tf_op jit(solution)/shard_map/ppermute | solution.py:31
  49.5 2.8 %collective-permute-start.6 = (bf16[8,1,128,128]{3,2,1,0:T(8,128)(2,1)S(1)}, bf16[8,1,128,128]{3,2,1,0:T(8,128)(2,1)S(1)}, u32[]{:S(2)}, u32[]{:S(2)}) collective-permute-start(bf16[8,1,128,128]{3,2,1,0:T(8,128)(2,1)S(1)} %slice.10.refs_0_.refs_1_), channel_id=1, source_target_pairs={{8,0},{16,8},{24,16},{0,24},{9,1},{17,9},{25,17},{1,25},{10,2},{18... | collective-permute-start | bytes 786440 | tf_op jit(solution)/shard_map/ppermute | solution.py:31
  52.2 0.0 all-to-all-done.1
  52.2 0.0 copy-start.3
  52.2 1.0 %copy-done.3 = bf16[8,2,128,128]{3,2,1,0:T(8,128)(2,1)S(1)} copy-done((bf16[8,2,128,128]{3,2,1,0:T(8,128)(2,1)S(1)}, bf16[8,2,128,128]{3,2,1,0:T(8,128)(2,1)}, u32[]{:S(2)}) %copy-start.3) | copy-done | bytes 524312
  53.3 8.2 %core.1 = (bf16[8,1,128,128]{3,2,1,0:T(8,128)(2,1)S(1)}, bf16[8,256,1152]{2,1,0:T(8,128)(2,1)S(1)}) custom-call(s32[34]{0:T(128)S(1)} %pad_add_fusion.own, s32[34]{0:T(128)S(1)} %collective-permute-done.2.other, bf16[8,5,128,128]{3,2,1,0:T(8,128)(2,1)S(1)} %bitcast.12, bf16[8,2,128,128]{3,2,1,0:T(8,128)(2,1)S(1)} %collective-permute-done.3.refs_0_, ...), custom_call_target="tpu_custom_call" | custom-call | flops 905969664 | bytes 1048576 | tf_op jit(solution)/shard_map/core/pallas_call | solution.py:303
  61.4 0.0 collective-permute-done.5.refs_0_
  61.5 1.6 %collective-permute-done.6.refs_2_ = bf16[8,1,128,128]{3,2,1,0:T(8,128)(2,1)S(1)} collective-permute-done((bf16[8,1,128,128]{3,2,1,0:T(8,128)(2,1)S(1)}, bf16[8,1,128,128]{3,2,1,0:T(8,128)(2,1)S(1)}, u32[]{:S(2)}, u32[]{:S(2)}) %collective-permute-start.6) | collective-permute-done | bytes 262176 | tf_op jit(solution)/shard_map/ppermute | solution.py:31
  63.0 3.1 %weigh.1 = bf16[8,2,128,128]{3,2,1,0:T(8,128)(2,1)S(1)} custom-call(s32[34]{0:T(128)S(1)} %pad_add_fusion.own, s32[34]{0:T(128)S(1)} %collective-permute-done.2.other, s32[2,8]{1,0:T(2,128)S(1)} %bitcast.16, bf16[8,256,1152]{2,1,0:T(8,128)(2,1)S(1)} %get-tuple-element.26.expo, bf16[8,1,128,128]{3,2,1,0:T(8,128)(2,1)S(1)} %get-tuple-element.27.done, ...), custom_call_target="tpu_custom_call" | custom-call | flops 301989888 | bytes 1048576 | tf_op jit(solution)/shard_map/weigh/pallas_call | solution.py:303
  66.1 14.4 %all_to_all.15.x = bf16[8,1,2,128,128]{4,3,2,1,0:T(8,128)(2,1)S(1)} all-to-all(bf16[8,1,2,128,128]{4,3,2,1,0:T(8,128)(2,1)S(1)} %bitcast.11), channel_id=1, replica_groups=mesh['plane'=4,'sub'=2,'tok'=4] {'sub','tok'}, dimensions={0} | all-to-all | bytes 1048576 | tf_op jit(solution)/shard_map/all_to_all | solution.py:35
  80.5 0.8 last.1
  (3 shorter events, 0.0 us)
Async XLA Ops:
  1.0 11.4 %collective-permute-start = (bf16[1,2,64,1024]{3,2,1,0:T(8,128)(2,1)S(1)}, bf16[1,2,64,1024]{3,2,1,0:T(8,128)(2,1)S(1)}, u32[]{:S(2)}, u32[]{:S(2)}) collective-permute-start(bf16[1,2,64,1024]{3,2,1,0:T(8,128)(2,1)S(1)} %slice_bitcast_fusion.refs_2_), channel_id=1, source_target_pairs={{24,0},{0,8},{8,16},{16,24},{25,1},{1,9},{9,17},{17,25},{26,2},{2,... | collective-permute-start | bytes 786440 | tf_op jit(solution)/shard_map/ppermute | solution.py:31
  4.0 10.1 %copy-start.4 = (s32[1,2,4,4]{3,2,1,0:T(4,128)S(1)}, s32[1,2,4,4]{3,2,1,0:T(4,128)}, u32[]{:S(2)}) copy-start(s32[1,2,4,4]{3,2,1,0:T(4,128)} %param.9) | copy-start | bytes 388
  4.0 10.2 %copy-start.5 = (s32[1,2]{1,0:T(1,128)S(1)}, s32[1,2]{1,0:T(1,128)}, u32[]{:S(2)}) copy-start(s32[1,2]{1,0:T(1,128)} %param.10) | copy-start | bytes 28
  6.8 16.3 %all-to-all-start = ((bf16[8,1,3,128,128]{4,3,2,1,0:T(8,128)(2,1)}), bf16[8,1,3,128,128]{4,3,2,1,0:T(8,128)(2,1)S(1)}, u32[]{:S(2)}, u32[]{:S(2)}) async-start(bf16[8,1,3,128,128]{4,3,2,1,0:T(8,128)(2,1)} %first.1), calls=%async_computation | async-start | bytes 1572864 | tf_op jit(solution)/shard_map/all_to_all | solution.py:35
  12.4 7.5 %collective-permute-start.1 = (bf16[1,2,64,1024]{3,2,1,0:T(8,128)(2,1)S(1)}, bf16[1,2,64,1024]{3,2,1,0:T(8,128)(2,1)S(1)}, u32[]{:S(2)}, u32[]{:S(2)}) collective-permute-start(bf16[1,2,64,1024]{3,2,1,0:T(8,128)(2,1)S(1)} %slice_bitcast_fusion.refs_2_), channel_id=1, source_target_pairs={{8,0},{16,8},{24,16},{0,24},{9,1},{17,9},{25,17},{1,25},{10,2},{18... | collective-permute-start | bytes 786440 | tf_op jit(solution)/shard_map/ppermute | solution.py:31
  14.3 13.5 %copy-start.1 = (s32[8,2]{0,1:T(2,128)S(1)}, s32[8,2]{0,1:T(2,128)}, u32[]{:S(2)}) copy-start(s32[8,2]{0,1:T(2,128)} %param.11) | copy-start | bytes 196
  14.3 5.9 %collective-permute-start.2 = (s32[34]{0:T(128)S(1)}, s32[34]{0:T(128)S(1)}, u32[]{:S(2)}, u32[]{:S(2)}) collective-permute-start(s32[34]{0:T(128)S(1)} %pad_add_fusion.own), channel_id=1, source_target_pairs={{0,4},{4,0},{1,5},{5,1},{2,6},{6,2},{3,7},{7,3},{8,12},{12,8},{9,1... | collective-permute-start | bytes 416 | tf_op jit(solution)/shard_map/ppermute | solution.py:333
  19.9 8.0 %copy-start = (bf16[1,2,128,1024]{3,2,1,0:T(8,128)(2,1)S(1)}, bf16[1,2,128,1024]{3,2,1,0:T(8,128)(2,1)}, u32[]{:S(2)}) copy-start(bf16[1,2,128,1024]{3,2,1,0:T(8,128)(2,1)} %refs_0_.3) | copy-start | bytes 1572868
  24.0 16.9 %collective-permute-start.3 = (bf16[8,2,128,128]{3,2,1,0:T(8,128)(2,1)}, bf16[8,2,128,128]{3,2,1,0:T(8,128)(2,1)S(1)}, u32[]{:S(2)}, u32[]{:S(2)}) collective-permute-start(bf16[8,2,128,128]{3,2,1,0:T(8,128)(2,1)} %slice.11), channel_id=1, source_target_pairs={{24,0},{0,8},{8,16},{16,24},{25,1},{1,9},{9,17},{17,25},{26,2},{2,... | collective-permute-start | bytes 1572872 | tf_op jit(solution)/shard_map/ppermute | solution.py:31
  25.6 22.0 %collective-permute-start.4 = (bf16[8,2,128,128]{3,2,1,0:T(8,128)(2,1)}, bf16[8,2,128,128]{3,2,1,0:T(8,128)(2,1)S(1)}, u32[]{:S(2)}, u32[]{:S(2)}) collective-permute-start(bf16[8,2,128,128]{3,2,1,0:T(8,128)(2,1)} %slice.11), channel_id=1, source_target_pairs={{8,0},{16,8},{24,16},{0,24},{9,1},{17,9},{25,17},{1,25},{10,2},{18... | collective-permute-start | bytes 1572872 | tf_op jit(solution)/shard_map/ppermute | solution.py:31
  29.5 22.7 %all-to-all-start.1 = ((bf16[8,1,5,128,128]{4,3,2,1,0:T(8,128)(2,1)}), bf16[8,1,5,128,128]{4,3,2,1,0:T(8,128)(2,1)S(1)}, u32[]{:S(2)}, u32[]{:S(2)}) async-start(bf16[8,1,5,128,128]{4,3,2,1,0:T(8,128)(2,1)} %second.1), calls=%async_computation.1 | async-start | bytes 2621440 | tf_op jit(solution)/shard_map/all_to_all | solution.py:35
  47.6 0.8 copy-start.2
  48.4 13.0 %collective-permute-start.5 = (bf16[8,1,128,128]{3,2,1,0:T(8,128)(2,1)S(1)}, bf16[8,1,128,128]{3,2,1,0:T(8,128)(2,1)S(1)}, u32[]{:S(2)}, u32[]{:S(2)}) collective-permute-start(bf16[8,1,128,128]{3,2,1,0:T(8,128)(2,1)S(1)} %slice.10.refs_0_.refs_1_), channel_id=1, source_target_pairs={{24,0},{0,8},{8,16},{16,24},{25,1},{1,9},{9,17},{17,25},{26,2},{2,... | collective-permute-start | bytes 786440 | tf_op jit(solution)/shard_map/ppermute | solution.py:31
  49.5 13.6 %collective-permute-start.6 = (bf16[8,1,128,128]{3,2,1,0:T(8,128)(2,1)S(1)}, bf16[8,1,128,128]{3,2,1,0:T(8,128)(2,1)S(1)}, u32[]{:S(2)}, u32[]{:S(2)}) collective-permute-start(bf16[8,1,128,128]{3,2,1,0:T(8,128)(2,1)S(1)} %slice.10.refs_0_.refs_1_), channel_id=1, source_target_pairs={{8,0},{16,8},{24,16},{0,24},{9,1},{17,9},{25,17},{1,25},{10,2},{18... | collective-permute-start | bytes 786440 | tf_op jit(solution)/shard_map/ppermute | solution.py:31
  52.2 1.0 %copy-start.3 = (bf16[8,2,128,128]{3,2,1,0:T(8,128)(2,1)S(1)}, bf16[8,2,128,128]{3,2,1,0:T(8,128)(2,1)}, u32[]{:S(2)}) copy-start(bf16[8,2,128,128]{3,2,1,0:T(8,128)(2,1)} %copy-done.2) | copy-start | bytes 1572868

commit v5 on v3

--- a/solution.py
+++ b/solution.py
@@ -200,51 +200,50 @@
     lax.fori_loop(0, plan.sub, one_view, 0)
 
 
-def core_kernel(plan, own, other, mixed, *refs):
+def first_part_kernel(plan, b, own, other, mixed, *refs):
     n, h = plan.planes, plan.hops
     planes = refs[:n]
-    out, expo_ref, k_far, v_far, k_sem, v_sem = refs[-6:]
+    out, k_far, v_far, k_sem, v_sem = refs[-5:]
     facts = (own, other)
     half = TILE // 2
-    low, high = pl.ds(0, half), pl.ds(half, half)
-    mine = [pl.ds(b * half, half) for b in range(2)]
+    low, high, mine = pl.ds(0, half), pl.ds(half, half), pl.ds(b * half, half)
 
     def far_copies(g, j, d, tiles_at):
         tiles = pl.ds(tiles_at, plan.kt)
-        found = []
-        for b in range(2):
-            found.append((mixed.at[tiles, 2 + d, mine[b]], k_far.at[b, g, j, :, low], k_sem.at[0, b, g, j]))
-            found.append((planes[d].at[tiles, 0, mine[b]], k_far.at[b, g, j, :, high], k_sem.at[1, b, g, j]))
-            if b == 0:
-                found.append((planes[d].at[tiles, 1], v_far.at[g, j], v_sem.at[g, j]))
+        found = [
+            (mixed.at[tiles, 2 + d, mine], k_far.at[g, j, :, low], k_sem.at[0, g, j]),
+            (planes[d].at[tiles, 0, mine], k_far.at[g, j, :, high], k_sem.at[1, g, j]),
+        ]
+        if b == 0:
+            found.append((planes[d].at[tiles, 1], v_far.at[g, j], v_sem.at[g, j]))
         return [pltpu.make_async_copy(*copy) for copy in found]
 
     start_far(plan, facts, far_copies)
 
-    def wait(b, g):
+    def wait(g):
         for j in range(NB):
             for part, rows in enumerate((low, high)):
-                there = k_far.at[b, g, j, :, rows]
-                pltpu.make_async_copy(there, there, k_sem.at[part, b, g, j]).wait()
+                there = k_far.at[g, j, :, rows]
+                pltpu.make_async_copy(there, there, k_sem.at[part, g, j]).wait()
             if b == 0:
                 there = v_far.at[g, j]
                 pltpu.make_async_copy(there, there, v_sem.at[g, j]).wait()
 
-    def expo_of(b, g, t, k):
+    def expo_of(g, t, k):
         at = g * plan.kt + t
         q = split_heads(plan, mixed[at, b])
-        k_own = jnp.concatenate([mixed[at, 2 + h, mine[b]], planes[h][at, 0, mine[b]]], axis=0)
+        k_own = jnp.concatenate([mixed[at, 2 + h, mine], planes[h][at, 0, mine]], axis=0)
         return numerators(
             plan, facts, g, t, scores_of(q, k_own), [scores_of(q, k[j]) for j in range(NB)]
         )
 
-    def keys(b, g):
-        return [far_rows(plan, k_far.at[b], g, j) for j in range(NB)]
+    def keys(g):
+        return [far_rows(plan, k_far, g, j) for j in range(NB)]
 
     def attended(g, t, ready):
         k, v = ready
         at = g * plan.kt + t
-        expo = expo_of(0, g, t, k)
+        expo = expo_of(g, t, k)
         total = weigh(expo[0], with_ones(planes[h][at, 1]))
         for j in range(NB):
             p = jnp.concatenate(expo[1 + j * plan.kt:1 + (j + 1) * plan.kt], axis=1)
@@ -252,14 +251,15 @@
         out[at, 0] = finish(plan, total)
 
     def scored(g, t, k):
-        for i, part in enumerate(expo_of(1, g, t, k)):
-            expo_ref[g * plan.kt + t, :, i * TILE:(i + 1) * TILE] = part
-
-    each_view(
-        plan, functools.partial(wait, 0), attended,
-        lambda g: (keys(0, g), [with_ones(far_rows(plan, v_far, g, j)) for j in range(NB)]),
-    )
-    each_view(plan, functools.partial(wait, 1), scored, functools.partial(keys, 1))
+        for i, part in enumerate(expo_of(g, t, k)):
+            out[g * plan.kt + t, :, i * TILE:(i + 1) * TILE] = part
+
+    if b == 0:
+        each_view(plan, wait, attended, lambda g: (
+            keys(g), [with_ones(far_rows(plan, v_far, g, j)) for j in range(NB)]
+        ))
+    else:
+        each_view(plan, wait, scored, keys)
 
 
 def weigh_kernel(plan, own, other, slots, expo, done, *refs):
@@ -347,7 +347,7 @@
             jax.ShapeDtypeStruct((ways, tiles, pieces, TILE, share), dtype),
             [SMEM, ANY] + [ANY if staged else VMEM] * len(arrays), place, scratch,
             (slots, slots if mark is None else mark, *arrays), moved=pieces * size,
-            mib=62 if staged else 16,
+            mib=62 if staged else 8,
         )
 
     def spread(x):
@@ -363,7 +363,7 @@
     def mark(arrays, flops):
         return call(
             mark_kernel, "mark", jax.ShapeDtypeStruct((8, 128), jnp.float32),
-            [ANY] * len(arrays), VMEM, [], arrays, flops=flops,
+            [ANY] * len(arrays), VMEM, [], arrays, flops=flops, mib=1,
         )
 
     raw = keys.reshape(1, 2, tiles, TILE, width)[:, :, :, :half].reshape(1, 2, tiles * half, width)
@@ -400,20 +400,21 @@
 
     sems = pltpu.SemaphoreType.DMA
     far = (sub, NB, kt, TILE, share)
-    expo = jax.ShapeDtypeStruct((sub * kt, plan.rows, plan.cols), dtype)
-    out0, expo = call(
-        functools.partial(core_kernel, plan), "core", (result(1), expo),
-        [SMEM] * 2 + [VMEM] * (1 + plan.planes) + [ANY], (VMEM, VMEM),
-        [pltpu.VMEM((2, *far), dtype), pltpu.VMEM(far, dtype), sems((2, 2, sub, NB)),
-         sems((sub, NB))],
-        (*facts, mixed, *planes, brought), flops=plan.pairs * HD * 6, exps=2 * plan.pairs,
-        moved=2 * size, mib=24,
+    shapes = result(1), jax.ShapeDtypeStruct((sub * kt, plan.rows, plan.cols), dtype)
+    out0, expo = (
+        call(
+            functools.partial(first_part_kernel, plan, b), ("attend", "scores")[b], shapes[b],
+            [SMEM] * 2 + [VMEM] * (1 + plan.planes) + [ANY], VMEM,
+            [pltpu.VMEM(far, dtype), pltpu.VMEM(far, dtype), sems((2, sub, NB)), sems((sub, NB))],
+            (*facts, mixed, *planes, brought), flops=plan.pairs * HD * (4 - 2 * b),
+            exps=plan.pairs, moved=2 * size, mib=12,
+        ) for b in range(2)
     )
     x = call(
         functools.partial(weigh_kernel, plan), "weigh", result(2),
         [SMEM] * 3 + [VMEM] * (2 + plan.planes), VMEM,
         [pltpu.VMEM(far, dtype), sems((sub, NB))], (*facts, slots, expo, out0, *late),
-        flops=plan.pairs * HD * 2, moved=2 * size, mib=24,
+        flops=plan.pairs * HD * 2, moved=2 * size, mib=12,
     )
     x = exchange(x.reshape(ways, tiles, 2, TILE, share))
     return call(

time: 81.7 us -> 81.5 us (level)
  local copies, waits for them, and re-layouts: 3.75 us -> 1.91 us
  Pallas kernels: 16.5 us -> 17.6 us
    unnamed x12 -> x8, local copies, waits for them, and re-layouts: 1.85 us -> 0.01 us
    pallas_call x7 -> x8, Pallas kernels: 16.5 us -> 17.6 us  [call(): pl.pallas_call(kernel, out_shape=out_shape, in_specs=in_specs, out_specs=...]
  transfers between devices with their start and end apart: 9 -> 9, of which waited for: 7 -> 7; matrix products, arithmetic and copies ran while one was open for 0% -> 0% of each run, Pallas kernels for 15% -> 16%
where the time goes in v5:
time: 81.5 us; the launch traced here: 81.1 us
  waiting for transfers between devices  25.7 us (32%)
  starting transfers between devices  21.3 us (26%)
  Pallas kernels  17.6 us (22%)
  blocking collectives  14.4 us (18%)
  local copies, waits for them, and re-layouts  1.91 us (2%)
    ppermute x6, waiting for transfers between devices, from_plane(): return lax.ppermute(x, 'plane', [((i + by) % size, i) for i in range(size)])  22.4 us
    pallas_call x8, Pallas kernels, call(): pl.pallas_call(kernel, out_shape=out_shape, in_specs=in_specs, out_specs=...  17.6 us
    all_to_all x1, blocking collectives, exchange(): return lax.all_to_all(x, GROUP, split_axis=0, concat_axis=0, tiled=True)  14.4 us
    ppermute x6, starting transfers between devices, from_plane(): return lax.ppermute(x, 'plane', [((i + by) % size, i) for i in range(size)])  12.5 us
    all_to_all x2, starting transfers between devices, exchange(): return lax.all_to_all(x, GROUP, split_axis=0, concat_axis=0, tiled=True)  7.32 us
    all_to_all x2, waiting for transfers between devices, exchange(): return lax.all_to_all(x, GROUP, split_axis=0, concat_axis=0, tiled=True)  2.99 us
  transfers between devices with their start and end apart: 9, of which 7 were waited for; matrix products, arithmetic and copies ran while one was open for 0% of the time, Pallas kernels for 16%

profile of v5, /device:TPU:0, one launch (start us, length us, event | category | flops | bytes accessed | tf_op | source)
XLA Modules:
  0.0 81.1 jit_solution(16401400644434770403)
XLA Ops:
  0.0 1.0 %slice_bitcast_fusion.refs_2_ = bf16[1,2,64,1024]{3,2,1,0:T(8,128)(2,1)S(1)} fusion(bf16[1,2,1,128,1024]{4,3,1,2,0:T(8,128)(2,1)} %bitcast.19), kind=kLoop, calls=%fused_computation | loop fusion | bytes 524288 | tf_op jit(solution)/shard_map/reshape | solution.py:369
  1.0 3.1 %collective-permute-start = (bf16[1,2,64,1024]{3,2,1,0:T(8,128)(2,1)S(1)}, bf16[1,2,64,1024]{3,2,1,0:T(8,128)(2,1)S(1)}, u32[]{:S(2)}, u32[]{:S(2)}) collective-permute-start(bf16[1,2,64,1024]{3,2,1,0:T(8,128)(2,1)S(1)} %slice_bitcast_fusion.refs_2_), channel_id=1, source_target_pairs={{24,0},{0,8},{8,16},{16,24},{25,1},{1,9},{9,17},{17,25},{26,2},{2,... | collective-permute-start | bytes 786440 | tf_op jit(solution)/shard_map/ppermute | solution.py:31
  4.0 0.0 copy-start.2
  4.0 0.0 copy-start.3
  4.1 2.8 %first.1 = bf16[8,1,3,128,128]{4,3,2,1,0:T(8,128)(2,1)} custom-call(s32[2,8]{1,0:T(2,128)} %bitcast.15, s32[2,8]{1,0:T(2,128)} %bitcast.16, bf16[1,2,128,1024]{3,2,1,0:T(8,128)(2,1)} %refs_0_.2, bf16[1,2,128,1024]{3,2,1,0:T(8,128)(2,1)} %refs_1_.1), custom_call_target="tpu_custom_call" | custom-call | bytes 1572864 | tf_op jit(solution)/shard_map/first/pallas_call | solution.py:303
  6.8 3.7 %all-to-all-start = ((bf16[8,1,3,128,128]{4,3,2,1,0:T(8,128)(2,1)}), bf16[8,1,3,128,128]{4,3,2,1,0:T(8,128)(2,1)S(1)}, u32[]{:S(2)}, u32[]{:S(2)}) async-start(bf16[8,1,3,128,128]{4,3,2,1,0:T(8,128)(2,1)} %first.1), calls=%async_computation | async-start | bytes 1572864 | tf_op jit(solution)/shard_map/all_to_all | solution.py:35
  10.6 1.8 %collective-permute-done.refs_0_.refs_1_ = bf16[1,2,64,1024]{3,2,1,0:T(8,128)(2,1)S(1)} collective-permute-done((bf16[1,2,64,1024]{3,2,1,0:T(8,128)(2,1)S(1)}, bf16[1,2,64,1024]{3,2,1,0:T(8,128)(2,1)S(1)}, u32[]{:S(2)}, u32[]{:S(2)}) %collective-permute-start) | collective-permute-done | bytes 262176 | tf_op jit(solution)/shard_map/ppermute | solution.py:31
  12.4 1.7 %collective-permute-start.1 = (bf16[1,2,64,1024]{3,2,1,0:T(8,128)(2,1)S(1)}, bf16[1,2,64,1024]{3,2,1,0:T(8,128)(2,1)S(1)}, u32[]{:S(2)}, u32[]{:S(2)}) collective-permute-start(bf16[1,2,64,1024]{3,2,1,0:T(8,128)(2,1)S(1)} %slice_bitcast_fusion.refs_2_), channel_id=1, source_target_pairs={{8,0},{16,8},{24,16},{0,24},{9,1},{17,9},{25,17},{1,25},{10,2},{18... | collective-permute-start | bytes 786440 | tf_op jit(solution)/shard_map/ppermute | solution.py:31
  14.1 0.0 copy-done.2
  14.1 0.1 reshape.24
  14.2 0.0 copy-done.3
  14.2 0.1 pad_add_fusion.own
  14.3 0.0 copy-start.1
  14.3 1.5 %collective-permute-start.2 = (s32[34]{0:T(128)S(1)}, s32[34]{0:T(128)S(1)}, u32[]{:S(2)}, u32[]{:S(2)}) collective-permute-start(s32[34]{0:T(128)S(1)} %pad_add_fusion.own), channel_id=1, source_target_pairs={{0,4},{4,0},{1,5},{5,1},{2,6},{6,2},{3,7},{7,3},{8,12},{12,8},{9,1... | collective-permute-start | bytes 416 | tf_op jit(solution)/shard_map/ppermute | solution.py:333
  15.8 4.1 %collective-permute-done.1.refs_1_.refs_3_ = bf16[1,2,64,1024]{3,2,1,0:T(8,128)(2,1)S(1)} collective-permute-done((bf16[1,2,64,1024]{3,2,1,0:T(8,128)(2,1)S(1)}, bf16[1,2,64,1024]{3,2,1,0:T(8,128)(2,1)S(1)}, u32[]{:S(2)}, u32[]{:S(2)}) %collective-permute-start.1) | collective-permute-done | bytes 262176 | tf_op jit(solution)/shard_map/ppermute | solution.py:31
  19.9 0.0 copy-start
  19.9 0.3 collective-permute-done.2.other
  20.2 3.0 %all-to-all-done = bf16[8,1,3,128,128]{4,3,2,1,0:T(8,128)(2,1)S(1)} async-done(((bf16[8,1,3,128,128]{4,3,2,1,0:T(8,128)(2,1)}), bf16[8,1,3,128,128]{4,3,2,1,0:T(8,128)(2,1)S(1)}, u32[]{:S(2)}, u32[]{:S(2)}) %all-to-all-start) | async-done | bytes 786464 | tf_op jit(solution)/shard_map/all_to_all | solution.py:35
  23.2 0.8 %slice.10 = bf16[8,2,128,128]{3,2,1,0:T(8,128)(2,1)} slice(bf16[8,3,128,128]{3,2,1,0:T(8,128)(2,1)S(1)} %bitcast.8), slice={[0:8], [0:2], [0:128], [0:128]} | slice | bytes 1048576 | tf_op jit(solution)/shard_map/slice | solution.py:380
  24.0 1.6 %collective-permute-start.3 = (bf16[8,2,128,128]{3,2,1,0:T(8,128)(2,1)}, bf16[8,2,128,128]{3,2,1,0:T(8,128)(2,1)S(1)}, u32[]{:S(2)}, u32[]{:S(2)}) collective-permute-start(bf16[8,2,128,128]{3,2,1,0:T(8,128)(2,1)} %slice.10), channel_id=1, source_target_pairs={{24,0},{0,8},{8,16},{16,24},{25,1},{1,9},{9,17},{17,25},{26,2},{2,... | collective-permute-start | bytes 1572872 | tf_op jit(solution)/shard_map/ppermute | solution.py:31
  25.6 2.2 %collective-permute-start.4 = (bf16[8,2,128,128]{3,2,1,0:T(8,128)(2,1)}, bf16[8,2,128,128]{3,2,1,0:T(8,128)(2,1)S(1)}, u32[]{:S(2)}, u32[]{:S(2)}) collective-permute-start(bf16[8,2,128,128]{3,2,1,0:T(8,128)(2,1)} %slice.10), channel_id=1, source_target_pairs={{8,0},{16,8},{24,16},{0,24},{9,1},{17,9},{25,17},{1,25},{10,2},{18... | collective-permute-start | bytes 1572872 | tf_op jit(solution)/shard_map/ppermute | solution.py:31
  27.8 0.0 copy-done.1
  27.8 0.0 copy-done
  27.8 1.7 %second.1 = bf16[8,1,5,128,128]{4,3,2,1,0:T(8,128)(2,1)} custom-call(s32[2,8]{1,0:T(2,128)S(1)} %bitcast.17, f32[8,128]{1,0:T(8,128)S(1)} %mark.2.mark_ref, bf16[1,2,128,1024]{3,2,1,0:T(8,128)(2,1)S(1)} %copy-done, bf16[1,2,64,1024]{3,2,1,0:T(8,128)(2,1)S(1)} %collective-permute-done.refs_0_.refs_1_, bf16[1,2,64,1024]{3,2,1,0:T(8,128)(2,1)S(1)} %slice_bitcast_fusion.refs_2_, ...), custom_call_target="tpu_custom_call" | custom-call | bytes 2621440 | tf_op jit(solution)/shard_map/second/pallas_call | solution.py:303
  29.5 3.6 %all-to-all-start.1 = ((bf16[8,1,5,128,128]{4,3,2,1,0:T(8,128)(2,1)}), bf16[8,1,5,128,128]{4,3,2,1,0:T(8,128)(2,1)S(1)}, u32[]{:S(2)}, u32[]{:S(2)}) async-start(bf16[8,1,5,128,128]{4,3,2,1,0:T(8,128)(2,1)} %second.1), calls=%async_computation.1 | async-start | bytes 2621440 | tf_op jit(solution)/shard_map/all_to_all | solution.py:35
  33.1 7.8 %collective-permute-done.3.refs_0_ = bf16[8,2,128,128]{3,2,1,0:T(8,128)(2,1)S(1)} collective-permute-done((bf16[8,2,128,128]{3,2,1,0:T(8,128)(2,1)}, bf16[8,2,128,128]{3,2,1,0:T(8,128)(2,1)S(1)}, u32[]{:S(2)}, u32[]{:S(2)}) %collective-permute-start.3) | collective-permute-done | bytes 524320 | tf_op jit(solution)/shard_map/ppermute | solution.py:31
  40.9 6.7 %collective-permute-done.4.refs_1_.refs_2_ = bf16[8,2,128,128]{3,2,1,0:T(8,128)(2,1)S(1)} collective-permute-done((bf16[8,2,128,128]{3,2,1,0:T(8,128)(2,1)}, bf16[8,2,128,128]{3,2,1,0:T(8,128)(2,1)S(1)}, u32[]{:S(2)}, u32[]{:S(2)}) %collective-permute-start.4) | collective-permute-done | bytes 524320 | tf_op jit(solution)/shard_map/ppermute | solution.py:31
  47.6 1.1 %collective-permute-start.5 = (bf16[8,1,128,128]{3,2,1,0:T(8,128)(2,1)S(1)}, bf16[8,1,128,128]{3,2,1,0:T(8,128)(2,1)}, u32[]{:S(2)}, u32[]{:S(2)}) collective-permute-start(bf16[8,1,128,128]{3,2,1,0:T(8,128)(2,1)S(1)} %slice.11.refs_1_), channel_id=1, source_target_pairs={{24,0},{0,8},{8,16},{16,24},{25,1},{1,9},{9,17},{17,25},{26,2},{2,... | collective-permute-start | bytes 786440 | tf_op jit(solution)/shard_map/ppermute | solution.py:31
  48.7 2.8 %collective-permute-start.6 = (bf16[8,1,128,128]{3,2,1,0:T(8,128)(2,1)S(1)}, bf16[8,1,128,128]{3,2,1,0:T(8,128)(2,1)}, u32[]{:S(2)}, u32[]{:S(2)}) collective-permute-start(bf16[8,1,128,128]{3,2,1,0:T(8,128)(2,1)S(1)} %slice.11.refs_1_), channel_id=1, source_target_pairs={{8,0},{16,8},{24,16},{0,24},{9,1},{17,9},{25,17},{1,25},{10,2},{18... | collective-permute-start | bytes 786440 | tf_op jit(solution)/shard_map/ppermute | solution.py:31
  51.4 0.0 all-to-all-done.1
  51.4 3.7 %scores.1.expo = bf16[8,256,1152]{2,1,0:T(8,128)(2,1)S(1)} custom-call(s32[34]{0:T(128)S(1)} %pad_add_fusion.own, s32[34]{0:T(128)S(1)} %collective-permute-done.2.other, bf16[8,5,128,128]{3,2,1,0:T(8,128)(2,1)S(1)} %bitcast.12, bf16[8,2,128,128]{3,2,1,0:T(8,128)(2,1)S(1)} %collective-permute-done.3.refs_0_, bf16[8,3,128,128]{3,2,1,0:T(8,128)(2,1)S(1)} %bitcast.10, ...), custom_call_target="tpu_custom_call" | custom-call | flops 301989888 | bytes 1048576 | tf_op jit(solution)/shard_map/scores/pallas_call | solution.py:303
  55.1 5.1 %attend.1.done = bf16[8,1,128,128]{3,2,1,0:T(8,128)(2,1)S(1)} custom-call(s32[34]{0:T(128)S(1)} %pad_add_fusion.own, s32[34]{0:T(128)S(1)} %collective-permute-done.2.other, bf16[8,5,128,128]{3,2,1,0:T(8,128)(2,1)S(1)} %bitcast.13, bf16[8,2,128,128]{3,2,1,0:T(8,128)(2,1)S(1)} %collective-permute-done.3.refs_0_, bf16[8,3,128,128]{3,2,1,0:T(8,128)(2,1)S(1)} %bitcast.11, ...), custom_call_target="tpu_custom_call" | custom-call | flops 603979776 | bytes 1048576 | tf_op jit(solution)/shard_map/attend/pallas_call | solution.py:303
  60.3 0.0 collective-permute-done.5.refs_0_
  60.3 2.1 %collective-permute-done.6.refs_2_ = bf16[8,1,128,128]{3,2,1,0:T(8,128)(2,1)} collective-permute-done((bf16[8,1,128,128]{3,2,1,0:T(8,128)(2,1)S(1)}, bf16[8,1,128,128]{3,2,1,0:T(8,128)(2,1)}, u32[]{:S(2)}, u32[]{:S(2)}) %collective-permute-start.6) | collective-permute-done | bytes 262176 | tf_op jit(solution)/shard_map/ppermute | solution.py:31
  62.3 3.6 %weigh.1 = bf16[8,2,128,128]{3,2,1,0:T(8,128)(2,1)S(1)} custom-call(s32[34]{0:T(128)S(1)} %pad_add_fusion.own, s32[34]{0:T(128)S(1)} %collective-permute-done.2.other, s32[2,8]{1,0:T(2,128)S(1)} %bitcast.18, bf16[8,256,1152]{2,1,0:T(8,128)(2,1)S(1)} %scores.1.expo, bf16[8,1,128,128]{3,2,1,0:T(8,128)(2,1)S(1)} %attend.1.done, ...), custom_call_target="tpu_custom_call" | custom-call | flops 301989888 | bytes 1048576 | tf_op jit(solution)/shard_map/weigh/pallas_call | solution.py:303
  65.9 14.4 %all_to_all.15.x = bf16[8,1,2,128,128]{4,3,2,1,0:T(8,128)(2,1)S(1)} all-to-all(bf16[8,1,2,128,128]{4,3,2,1,0:T(8,128)(2,1)S(1)} %bitcast.14), channel_id=1, replica_groups=mesh['plane'=4,'sub'=2,'tok'=4] {'sub','tok'}, dimensions={0} | all-to-all | bytes 1048576 | tf_op jit(solution)/shard_map/all_to_all | solution.py:35
  80.3 0.8 last.1
  (3 shorter events, 0.0 us)
Async XLA Ops:
  1.0 11.4 %collective-permute-start = (bf16[1,2,64,1024]{3,2,1,0:T(8,128)(2,1)S(1)}, bf16[1,2,64,1024]{3,2,1,0:T(8,128)(2,1)S(1)}, u32[]{:S(2)}, u32[]{:S(2)}) collective-permute-start(bf16[1,2,64,1024]{3,2,1,0:T(8,128)(2,1)S(1)} %slice_bitcast_fusion.refs_2_), channel_id=1, source_target_pairs={{24,0},{0,8},{8,16},{16,24},{25,1},{1,9},{9,17},{17,25},{26,2},{2,... | collective-permute-start | bytes 786440 | tf_op jit(solution)/shard_map/ppermute | solution.py:31
  4.0 10.1 %copy-start.2 = (s32[1,2,4,4]{3,2,1,0:T(4,128)S(1)}, s32[1,2,4,4]{3,2,1,0:T(4,128)}, u32[]{:S(2)}) copy-start(s32[1,2,4,4]{3,2,1,0:T(4,128)} %param.9) | copy-start | bytes 388
  4.0 10.2 %copy-start.3 = (s32[1,2]{1,0:T(1,128)S(1)}, s32[1,2]{1,0:T(1,128)}, u32[]{:S(2)}) copy-start(s32[1,2]{1,0:T(1,128)} %param.10) | copy-start | bytes 28
  6.8 16.3 %all-to-all-start = ((bf16[8,1,3,128,128]{4,3,2,1,0:T(8,128)(2,1)}), bf16[8,1,3,128,128]{4,3,2,1,0:T(8,128)(2,1)S(1)}, u32[]{:S(2)}, u32[]{:S(2)}) async-start(bf16[8,1,3,128,128]{4,3,2,1,0:T(8,128)(2,1)} %first.1), calls=%async_computation | async-start | bytes 1572864 | tf_op jit(solution)/shard_map/all_to_all | solution.py:35
  12.4 7.5 %collective-permute-start.1 = (bf16[1,2,64,1024]{3,2,1,0:T(8,128)(2,1)S(1)}, bf16[1,2,64,1024]{3,2,1,0:T(8,128)(2,1)S(1)}, u32[]{:S(2)}, u32[]{:S(2)}) collective-permute-start(bf16[1,2,64,1024]{3,2,1,0:T(8,128)(2,1)S(1)} %slice_bitcast_fusion.refs_2_), channel_id=1, source_target_pairs={{8,0},{16,8},{24,16},{0,24},{9,1},{17,9},{25,17},{1,25},{10,2},{18... | collective-permute-start | bytes 786440 | tf_op jit(solution)/shard_map/ppermute | solution.py:31
  14.3 13.5 %copy-start.1 = (s32[8,2]{0,1:T(2,128)S(1)}, s32[8,2]{0,1:T(2,128)}, u32[]{:S(2)}) copy-start(s32[8,2]{0,1:T(2,128)} %param.11) | copy-start | bytes 196
  14.3 5.9 %collective-permute-start.2 = (s32[34]{0:T(128)S(1)}, s32[34]{0:T(128)S(1)}, u32[]{:S(2)}, u32[]{:S(2)}) collective-permute-start(s32[34]{0:T(128)S(1)} %pad_add_fusion.own), channel_id=1, source_target_pairs={{0,4},{4,0},{1,5},{5,1},{2,6},{6,2},{3,7},{7,3},{8,12},{12,8},{9,1... | collective-permute-start | bytes 416 | tf_op jit(solution)/shard_map/ppermute | solution.py:333
  19.9 8.0 %copy-start = (bf16[1,2,128,1024]{3,2,1,0:T(8,128)(2,1)S(1)}, bf16[1,2,128,1024]{3,2,1,0:T(8,128)(2,1)}, u32[]{:S(2)}) copy-start(bf16[1,2,128,1024]{3,2,1,0:T(8,128)(2,1)} %refs_0_.3) | copy-start | bytes 1572868
  24.0 16.9 %collective-permute-start.3 = (bf16[8,2,128,128]{3,2,1,0:T(8,128)(2,1)}, bf16[8,2,128,128]{3,2,1,0:T(8,128)(2,1)S(1)}, u32[]{:S(2)}, u32[]{:S(2)}) collective-permute-start(bf16[8,2,128,128]{3,2,1,0:T(8,128)(2,1)} %slice.10), channel_id=1, source_target_pairs={{24,0},{0,8},{8,16},{16,24},{25,1},{1,9},{9,17},{17,25},{26,2},{2,... | collective-permute-start | bytes 1572872 | tf_op jit(solution)/shard_map/ppermute | solution.py:31
  25.6 22.0 %collective-permute-start.4 = (bf16[8,2,128,128]{3,2,1,0:T(8,128)(2,1)}, bf16[8,2,128,128]{3,2,1,0:T(8,128)(2,1)S(1)}, u32[]{:S(2)}, u32[]{:S(2)}) collective-permute-start(bf16[8,2,128,128]{3,2,1,0:T(8,128)(2,1)} %slice.10), channel_id=1, source_target_pairs={{8,0},{16,8},{24,16},{0,24},{9,1},{17,9},{25,17},{1,25},{10,2},{18... | collective-permute-start | bytes 1572872 | tf_op jit(solution)/shard_map/ppermute | solution.py:31
  29.5 21.9 %all-to-all-start.1 = ((bf16[8,1,5,128,128]{4,3,2,1,0:T(8,128)(2,1)}), bf16[8,1,5,128,128]{4,3,2,1,0:T(8,128)(2,1)S(1)}, u32[]{:S(2)}, u32[]{:S(2)}) async-start(bf16[8,1,5,128,128]{4,3,2,1,0:T(8,128)(2,1)} %second.1), calls=%async_computation.1 | async-start | bytes 2621440 | tf_op jit(solution)/shard_map/all_to_all | solution.py:35
  47.6 12.7 %collective-permute-start.5 = (bf16[8,1,128,128]{3,2,1,0:T(8,128)(2,1)S(1)}, bf16[8,1,128,128]{3,2,1,0:T(8,128)(2,1)}, u32[]{:S(2)}, u32[]{:S(2)}) collective-permute-start(bf16[8,1,128,128]{3,2,1,0:T(8,128)(2,1)S(1)} %slice.11.refs_1_), channel_id=1, source_target_pairs={{24,0},{0,8},{8,16},{16,24},{25,1},{1,9},{9,17},{17,25},{26,2},{2,... | collective-permute-start | bytes 786440 | tf_op jit(solution)/shard_map/ppermute | solution.py:31
  48.7 13.7 %collective-permute-start.6 = (bf16[8,1,128,128]{3,2,1,0:T(8,128)(2,1)S(1)}, bf16[8,1,128,128]{3,2,1,0:T(8,128)(2,1)}, u32[]{:S(2)}, u32[]{:S(2)}) collective-permute-start(bf16[8,1,128,128]{3,2,1,0:T(8,128)(2,1)S(1)} %slice.11.refs_1_), channel_id=1, source_target_pairs={{8,0},{16,8},{24,16},{0,24},{9,1},{17,9},{25,17},{1,25},{10,2},{18... | collective-permute-start | bytes 786440 | tf_op jit(solution)/shard_map/ppermute | solution.py:31

commit v6 on v5

--- a/solution.py
+++ b/solution.py
@@ -12,7 +12,7 @@
 TILE = 128
 NB = 2
 REACH = 2
-MARK_FLOPS = (4 * 10 ** 9, 10 ** 10)
+MARK_FLOPS = (4 * 10 ** 9, 2 * 10 ** 9, 10 ** 10)
 GROUP = ("sub", "tok")
 
 NEG_SCORE = -1e30
@@ -378,8 +378,9 @@
     early, arrived, facts = lax.optimization_barrier((early, arrived, facts))
 
     planes = around(early[:, :2])
-    brought = mark([planes[d] for d in shifts], MARK_FLOPS[1])
-    last_values, brought = lax.optimization_barrier((early[:, 2:], brought))
+    leads = mark([planes[shifts[0]]], MARK_FLOPS[1])
+    brought = mark([planes[d] for d in shifts[1:]], MARK_FLOPS[2])
+    last_values, leads = lax.optimization_barrier((early[:, 2:], leads))
     late = around(last_values)
     moves = [Move(0, 0, 0), Move(0, 1, 1)]
     for d in order:
@@ -404,9 +405,9 @@
     out0, expo = (
         call(
             functools.partial(first_part_kernel, plan, b), ("attend", "scores")[b], shapes[b],
-            [SMEM] * 2 + [VMEM] * (1 + plan.planes) + [ANY], VMEM,
+            [SMEM] * 2 + [VMEM] * (1 + plan.planes) + [ANY] * 2, VMEM,
             [pltpu.VMEM(far, dtype), pltpu.VMEM(far, dtype), sems((2, sub, NB)), sems((sub, NB))],
-            (*facts, mixed, *planes, brought), flops=plan.pairs * HD * (4 - 2 * b),
+            (*facts, mixed, *planes, leads, brought), flops=plan.pairs * HD * (4 - 2 * b),
             exps=plan.pairs, moved=2 * size, mib=12,
         ) for b in range(2)
     )

time: 81.5 us -> 78.1 us (0.958)
  waiting for transfers between devices: 25.7 us -> 20.8 us
  starting transfers between devices: 21.3 us -> 23.9 us
  blocking collectives: 14.4 us -> 13.2 us
    ppermute x6, waiting for transfers between devices: 22.4 us -> 17.4 us  [from_plane(): return lax.ppermute(x, 'plane', [((i + by) % size, i) for i in range(size)])]
    ppermute x6, starting transfers between devices: 12.5 us -> 15.1 us  [from_plane(): return lax.ppermute(x, 'plane', [((i + by) % size, i) for i in range(size)])]
    all_to_all x1, blocking collectives: 14.4 us -> 13.2 us  [exchange(): return lax.all_to_all(x, GROUP, split_axis=0, concat_axis=0, tiled=True)]
    pallas_call x8 -> x9, Pallas kernels: 17.6 us -> 17.6 us  [call(): pl.pallas_call(kernel, out_shape=out_shape, in_specs=in_specs, out_specs=...]
  transfers between devices with their start and end apart: 9 -> 9, of which waited for: 7 -> 7; matrix products, arithmetic and copies ran while one was open for 0% -> 0% of each run, Pallas kernels for 16% -> 17%
where the time goes in v6:
time: 78.1 us; the launch traced here: 77.7 us
  starting transfers between devices  23.9 us (31%)
  waiting for transfers between devices  20.8 us (27%)
  Pallas kernels  17.6 us (23%)
  blocking collectives  13.2 us (17%)
  local copies, waits for them, and re-layouts  1.91 us (2%)
    pallas_call x9, Pallas kernels, call(): pl.pallas_call(kernel, out_shape=out_shape, in_specs=in_specs, out_specs=...  17.6 us
    ppermute x6, waiting for transfers between devices, from_plane(): return lax.ppermute(x, 'plane', [((i + by) % size, i) for i in range(size)])  17.4 us
    ppermute x6, starting transfers between devices, from_plane(): return lax.ppermute(x, 'plane', [((i + by) % size, i) for i in range(size)])  15.1 us
    all_to_all x1, blocking collectives, exchange(): return lax.all_to_all(x, GROUP, split_axis=0, concat_axis=0, tiled=True)  13.2 us
    all_to_all x2, starting transfers between devices, exchange(): return lax.all_to_all(x, GROUP, split_axis=0, concat_axis=0, tiled=True)  7.32 us
    all_to_all x2, waiting for transfers between devices, exchange(): return lax.all_to_all(x, GROUP, split_axis=0, concat_axis=0, tiled=True)  3.09 us
  transfers between devices with their start and end apart: 9, of which 7 were waited for; matrix products, arithmetic and copies ran while one was open for 0% of the time, Pallas kernels for 17%

profile of v6, /device:TPU:0, one launch (start us, length us, event | category | flops | bytes accessed | tf_op | source)
XLA Modules:
  0.0 77.7 jit_solution(15583517403097638459)
XLA Ops:
  0.0 1.0 %slice_bitcast_fusion.refs_2_ = bf16[1,2,64,1024]{3,2,1,0:T(8,128)(2,1)S(1)} fusion(bf16[1,2,1,128,1024]{4,3,1,2,0:T(8,128)(2,1)} %bitcast.19), kind=kLoop, calls=%fused_computation | loop fusion | bytes 524288 | tf_op jit(solution)/shard_map/reshape | solution.py:369
  1.0 3.1 %collective-permute-start = (bf16[1,2,64,1024]{3,2,1,0:T(8,128)(2,1)S(1)}, bf16[1,2,64,1024]{3,2,1,0:T(8,128)(2,1)S(1)}, u32[]{:S(2)}, u32[]{:S(2)}) collective-permute-start(bf16[1,2,64,1024]{3,2,1,0:T(8,128)(2,1)S(1)} %slice_bitcast_fusion.refs_2_), channel_id=1, source_target_pairs={{24,0},{0,8},{8,16},{16,24},{25,1},{1,9},{9,17},{17,25},{26,2},{2,... | collective-permute-start | bytes 786440 | tf_op jit(solution)/shard_map/ppermute | solution.py:31
  4.0 0.0 copy-start.2
  4.0 0.0 copy-start.3
  4.1 2.8 %first.1 = bf16[8,1,3,128,128]{4,3,2,1,0:T(8,128)(2,1)} custom-call(s32[2,8]{1,0:T(2,128)} %bitcast.15, s32[2,8]{1,0:T(2,128)} %bitcast.16, bf16[1,2,128,1024]{3,2,1,0:T(8,128)(2,1)} %refs_0_.2, bf16[1,2,128,1024]{3,2,1,0:T(8,128)(2,1)} %refs_1_.1), custom_call_target="tpu_custom_call" | custom-call | bytes 1572864 | tf_op jit(solution)/shard_map/first/pallas_call | solution.py:303
  6.8 3.7 %all-to-all-start = ((bf16[8,1,3,128,128]{4,3,2,1,0:T(8,128)(2,1)}), bf16[8,1,3,128,128]{4,3,2,1,0:T(8,128)(2,1)S(1)}, u32[]{:S(2)}, u32[]{:S(2)}) async-start(bf16[8,1,3,128,128]{4,3,2,1,0:T(8,128)(2,1)} %first.1), calls=%async_computation | async-start | bytes 1572864 | tf_op jit(solution)/shard_map/all_to_all | solution.py:35
  10.6 1.8 %collective-permute-done.refs_0_.refs_1_ = bf16[1,2,64,1024]{3,2,1,0:T(8,128)(2,1)S(1)} collective-permute-done((bf16[1,2,64,1024]{3,2,1,0:T(8,128)(2,1)S(1)}, bf16[1,2,64,1024]{3,2,1,0:T(8,128)(2,1)S(1)}, u32[]{:S(2)}, u32[]{:S(2)}) %collective-permute-start) | collective-permute-done | bytes 262176 | tf_op jit(solution)/shard_map/ppermute | solution.py:31
  12.4 1.7 %collective-permute-start.1 = (bf16[1,2,64,1024]{3,2,1,0:T(8,128)(2,1)S(1)}, bf16[1,2,64,1024]{3,2,1,0:T(8,128)(2,1)S(1)}, u32[]{:S(2)}, u32[]{:S(2)}) collective-permute-start(bf16[1,2,64,1024]{3,2,1,0:T(8,128)(2,1)S(1)} %slice_bitcast_fusion.refs_2_), channel_id=1, source_target_pairs={{8,0},{16,8},{24,16},{0,24},{9,1},{17,9},{25,17},{1,25},{10,2},{18... | collective-permute-start | bytes 786440 | tf_op jit(solution)/shard_map/ppermute | solution.py:31
  14.1 0.0 copy-done.2
  14.1 0.1 reshape.24
  14.2 0.0 copy-done.3
  14.2 0.1 pad_add_fusion.own
  14.3 0.0 copy-start.1
  14.3 1.5 %collective-permute-start.2 = (s32[34]{0:T(128)S(1)}, s32[34]{0:T(128)S(1)}, u32[]{:S(2)}, u32[]{:S(2)}) collective-permute-start(s32[34]{0:T(128)S(1)} %pad_add_fusion.own), channel_id=1, source_target_pairs={{0,4},{4,0},{1,5},{5,1},{2,6},{6,2},{3,7},{7,3},{8,12},{12,8},{9,1... | collective-permute-start | bytes 416 | tf_op jit(solution)/shard_map/ppermute | solution.py:333
  15.8 4.1 %collective-permute-done.1.refs_1_.refs_3_ = bf16[1,2,64,1024]{3,2,1,0:T(8,128)(2,1)S(1)} collective-permute-done((bf16[1,2,64,1024]{3,2,1,0:T(8,128)(2,1)S(1)}, bf16[1,2,64,1024]{3,2,1,0:T(8,128)(2,1)S(1)}, u32[]{:S(2)}, u32[]{:S(2)}) %collective-permute-start.1) | collective-permute-done | bytes 262176 | tf_op jit(solution)/shard_map/ppermute | solution.py:31
  19.9 0.0 copy-start
  19.9 0.3 collective-permute-done.2.other
  20.2 3.0 %all-to-all-done = bf16[8,1,3,128,128]{4,3,2,1,0:T(8,128)(2,1)S(1)} async-done(((bf16[8,1,3,128,128]{4,3,2,1,0:T(8,128)(2,1)}), bf16[8,1,3,128,128]{4,3,2,1,0:T(8,128)(2,1)S(1)}, u32[]{:S(2)}, u32[]{:S(2)}) %all-to-all-start) | async-done | bytes 786464 | tf_op jit(solution)/shard_map/all_to_all | solution.py:35
  23.2 0.8 %slice.10 = bf16[8,2,128,128]{3,2,1,0:T(8,128)(2,1)} slice(bf16[8,3,128,128]{3,2,1,0:T(8,128)(2,1)S(1)} %bitcast.8), slice={[0:8], [0:2], [0:128], [0:128]} | slice | bytes 1048576 | tf_op jit(solution)/shard_map/slice | solution.py:380
  24.0 1.6 %collective-permute-start.3 = (bf16[8,2,128,128]{3,2,1,0:T(8,128)(2,1)}, bf16[8,2,128,128]{3,2,1,0:T(8,128)(2,1)S(1)}, u32[]{:S(2)}, u32[]{:S(2)}) collective-permute-start(bf16[8,2,128,128]{3,2,1,0:T(8,128)(2,1)} %slice.10), channel_id=1, source_target_pairs={{24,0},{0,8},{8,16},{16,24},{25,1},{1,9},{9,17},{17,25},{26,2},{2,... | collective-permute-start | bytes 1572872 | tf_op jit(solution)/shard_map/ppermute | solution.py:31
  25.6 2.2 %collective-permute-start.4 = (bf16[8,2,128,128]{3,2,1,0:T(8,128)(2,1)}, bf16[8,2,128,128]{3,2,1,0:T(8,128)(2,1)S(1)}, u32[]{:S(2)}, u32[]{:S(2)}) collective-permute-start(bf16[8,2,128,128]{3,2,1,0:T(8,128)(2,1)} %slice.10), channel_id=1, source_target_pairs={{8,0},{16,8},{24,16},{0,24},{9,1},{17,9},{25,17},{1,25},{10,2},{18... | collective-permute-start | bytes 1572872 | tf_op jit(solution)/shard_map/ppermute | solution.py:31
  27.8 0.0 copy-done.1
  27.8 0.0 copy-done
  27.8 1.7 %second.1 = bf16[8,1,5,128,128]{4,3,2,1,0:T(8,128)(2,1)} custom-call(s32[2,8]{1,0:T(2,128)S(1)} %bitcast.17, f32[8,128]{1,0:T(8,128)S(1)} %mark.3.mark_ref, bf16[1,2,128,1024]{3,2,1,0:T(8,128)(2,1)S(1)} %copy-done, bf16[1,2,64,1024]{3,2,1,0:T(8,128)(2,1)S(1)} %collective-permute-done.refs_0_.refs_1_, bf16[1,2,64,1024]{3,2,1,0:T(8,128)(2,1)S(1)} %slice_bitcast_fusion.refs_2_, ...), custom_call_target="tpu_custom_call" | custom-call | bytes 2621440 | tf_op jit(solution)/shard_map/second/pallas_call | solution.py:303
  29.5 3.6 %all-to-all-start.1 = ((bf16[8,1,5,128,128]{4,3,2,1,0:T(8,128)(2,1)}), bf16[8,1,5,128,128]{4,3,2,1,0:T(8,128)(2,1)S(1)}, u32[]{:S(2)}, u32[]{:S(2)}) async-start(bf16[8,1,5,128,128]{4,3,2,1,0:T(8,128)(2,1)} %second.1), calls=%async_computation.1 | async-start | bytes 2621440 | tf_op jit(solution)/shard_map/all_to_all | solution.py:35
  33.1 7.8 %collective-permute-done.3.refs_0_ = bf16[8,2,128,128]{3,2,1,0:T(8,128)(2,1)S(1)} collective-permute-done((bf16[8,2,128,128]{3,2,1,0:T(8,128)(2,1)}, bf16[8,2,128,128]{3,2,1,0:T(8,128)(2,1)S(1)}, u32[]{:S(2)}, u32[]{:S(2)}) %collective-permute-start.3) | collective-permute-done | bytes 524320 | tf_op jit(solution)/shard_map/ppermute | solution.py:31
  40.9 6.5 %collective-permute-start.5 = (bf16[8,1,128,128]{3,2,1,0:T(8,128)(2,1)S(1)}, bf16[8,1,128,128]{3,2,1,0:T(8,128)(2,1)}, u32[]{:S(2)}, u32[]{:S(2)}) collective-permute-start(bf16[8,1,128,128]{3,2,1,0:T(8,128)(2,1)S(1)} %slice.11.refs_1_), channel_id=1, source_target_pairs={{24,0},{0,8},{8,16},{16,24},{25,1},{1,9},{9,17},{17,25},{26,2},{2,... | collective-permute-start | bytes 786440 | tf_op jit(solution)/shard_map/ppermute | solution.py:31
  47.3 0.0 collective-permute-start.6
  47.3 3.8 %collective-permute-done.4.refs_0_.refs_2_ = bf16[8,2,128,128]{3,2,1,0:T(8,128)(2,1)S(1)} collective-permute-done((bf16[8,2,128,128]{3,2,1,0:T(8,128)(2,1)}, bf16[8,2,128,128]{3,2,1,0:T(8,128)(2,1)S(1)}, u32[]{:S(2)}, u32[]{:S(2)}) %collective-permute-start.4) | collective-permute-done | bytes 524320 | tf_op jit(solution)/shard_map/ppermute | solution.py:31
  51.1 0.1 all-to-all-done.1
  51.2 3.7 %scores.1.expo = bf16[8,256,1152]{2,1,0:T(8,128)(2,1)S(1)} custom-call(s32[34]{0:T(128)S(1)} %pad_add_fusion.own, s32[34]{0:T(128)S(1)} %collective-permute-done.2.other, bf16[8,5,128,128]{3,2,1,0:T(8,128)(2,1)S(1)} %bitcast.12, bf16[8,2,128,128]{3,2,1,0:T(8,128)(2,1)S(1)} %collective-permute-done.3.refs_0_, bf16[8,3,128,128]{3,2,1,0:T(8,128)(2,1)S(1)} %bitcast.10, ...), custom_call_target="tpu_custom_call" | custom-call | flops 301989888 | bytes 1048576 | tf_op jit(solution)/shard_map/scores/pallas_call | solution.py:303
  55.0 5.1 %attend.1.done = bf16[8,1,128,128]{3,2,1,0:T(8,128)(2,1)S(1)} custom-call(s32[34]{0:T(128)S(1)} %pad_add_fusion.own, s32[34]{0:T(128)S(1)} %collective-permute-done.2.other, bf16[8,5,128,128]{3,2,1,0:T(8,128)(2,1)S(1)} %bitcast.13, bf16[8,2,128,128]{3,2,1,0:T(8,128)(2,1)S(1)} %collective-permute-done.3.refs_0_, bf16[8,3,128,128]{3,2,1,0:T(8,128)(2,1)S(1)} %bitcast.11, ...), custom_call_target="tpu_custom_call" | custom-call | flops 603979776 | bytes 1048576 | tf_op jit(solution)/shard_map/attend/pallas_call | solution.py:303
  60.1 0.0 collective-permute-done.5.refs_0_
  60.1 0.0 collective-permute-done.6.refs_2_
  60.1 3.6 %weigh.1 = bf16[8,2,128,128]{3,2,1,0:T(8,128)(2,1)S(1)} custom-call(s32[34]{0:T(128)S(1)} %pad_add_fusion.own, s32[34]{0:T(128)S(1)} %collective-permute-done.2.other, s32[2,8]{1,0:T(2,128)S(1)} %bitcast.18, bf16[8,256,1152]{2,1,0:T(8,128)(2,1)S(1)} %scores.1.expo, bf16[8,1,128,128]{3,2,1,0:T(8,128)(2,1)S(1)} %attend.1.done, ...), custom_call_target="tpu_custom_call" | custom-call | flops 301989888 | bytes 1048576 | tf_op jit(solution)/shard_map/weigh/pallas_call | solution.py:303
  63.7 13.2 %all_to_all.15.x = bf16[8,1,2,128,128]{4,3,2,1,0:T(8,128)(2,1)S(1)} all-to-all(bf16[8,1,2,128,128]{4,3,2,1,0:T(8,128)(2,1)S(1)} %bitcast.14), channel_id=1, replica_groups=mesh['plane'=4,'sub'=2,'tok'=4] {'sub','tok'}, dimensions={0} | all-to-all | bytes 1048576 | tf_op jit(solution)/shard_map/all_to_all | solution.py:35
  76.9 0.8 %last.1 = bf16[1,2,128,1024]{3,2,1,0:T(8,128)(2,1)} custom-call(bf16[8,1,2,128,128]{4,3,2,1,0:T(8,128)(2,1)S(1)} %all_to_all.15.x), custom_call_target="tpu_custom_call" | custom-call | bytes 1048576 | tf_op jit(solution)/shard_map/last/pallas_call | solution.py:303
  (4 shorter events, 0.0 us)
Async XLA Ops:
  1.0 11.4 %collective-permute-start = (bf16[1,2,64,1024]{3,2,1,0:T(8,128)(2,1)S(1)}, bf16[1,2,64,1024]{3,2,1,0:T(8,128)(2,1)S(1)}, u32[]{:S(2)}, u32[]{:S(2)}) collective-permute-start(bf16[1,2,64,1024]{3,2,1,0:T(8,128)(2,1)S(1)} %slice_bitcast_fusion.refs_2_), channel_id=1, source_target_pairs={{24,0},{0,8},{8,16},{16,24},{25,1},{1,9},{9,17},{17,25},{26,2},{2,... | collective-permute-start | bytes 786440 | tf_op jit(solution)/shard_map/ppermute | solution.py:31
  4.0 10.1 %copy-start.2 = (s32[1,2,4,4]{3,2,1,0:T(4,128)S(1)}, s32[1,2,4,4]{3,2,1,0:T(4,128)}, u32[]{:S(2)}) copy-start(s32[1,2,4,4]{3,2,1,0:T(4,128)} %param.9) | copy-start | bytes 388
  4.0 10.2 %copy-start.3 = (s32[1,2]{1,0:T(1,128)S(1)}, s32[1,2]{1,0:T(1,128)}, u32[]{:S(2)}) copy-start(s32[1,2]{1,0:T(1,128)} %param.10) | copy-start | bytes 28
  6.8 16.3 %all-to-all-start = ((bf16[8,1,3,128,128]{4,3,2,1,0:T(8,128)(2,1)}), bf16[8,1,3,128,128]{4,3,2,1,0:T(8,128)(2,1)S(1)}, u32[]{:S(2)}, u32[]{:S(2)}) async-start(bf16[8,1,3,128,128]{4,3,2,1,0:T(8,128)(2,1)} %first.1), calls=%async_computation | async-start | bytes 1572864 | tf_op jit(solution)/shard_map/all_to_all | solution.py:35
  12.4 7.5 %collective-permute-start.1 = (bf16[1,2,64,1024]{3,2,1,0:T(8,128)(2,1)S(1)}, bf16[1,2,64,1024]{3,2,1,0:T(8,128)(2,1)S(1)}, u32[]{:S(2)}, u32[]{:S(2)}) collective-permute-start(bf16[1,2,64,1024]{3,2,1,0:T(8,128)(2,1)S(1)} %slice_bitcast_fusion.refs_2_), channel_id=1, source_target_pairs={{8,0},{16,8},{24,16},{0,24},{9,1},{17,9},{25,17},{1,25},{10,2},{18... | collective-permute-start | bytes 786440 | tf_op jit(solution)/shard_map/ppermute | solution.py:31
  14.3 13.5 %copy-start.1 = (s32[8,2]{0,1:T(2,128)S(1)}, s32[8,2]{0,1:T(2,128)}, u32[]{:S(2)}) copy-start(s32[8,2]{0,1:T(2,128)} %param.11) | copy-start | bytes 196
  14.3 5.9 %collective-permute-start.2 = (s32[34]{0:T(128)S(1)}, s32[34]{0:T(128)S(1)}, u32[]{:S(2)}, u32[]{:S(2)}) collective-permute-start(s32[34]{0:T(128)S(1)} %pad_add_fusion.own), channel_id=1, source_target_pairs={{0,4},{4,0},{1,5},{5,1},{2,6},{6,2},{3,7},{7,3},{8,12},{12,8},{9,1... | collective-permute-start | bytes 416 | tf_op jit(solution)/shard_map/ppermute | solution.py:333
  19.9 8.0 %copy-start = (bf16[1,2,128,1024]{3,2,1,0:T(8,128)(2,1)S(1)}, bf16[1,2,128,1024]{3,2,1,0:T(8,128)(2,1)}, u32[]{:S(2)}) copy-start(bf16[1,2,128,1024]{3,2,1,0:T(8,128)(2,1)} %refs_0_.3) | copy-start | bytes 1572868
  24.0 16.9 %collective-permute-start.3 = (bf16[8,2,128,128]{3,2,1,0:T(8,128)(2,1)}, bf16[8,2,128,128]{3,2,1,0:T(8,128)(2,1)S(1)}, u32[]{:S(2)}, u32[]{:S(2)}) collective-permute-start(bf16[8,2,128,128]{3,2,1,0:T(8,128)(2,1)} %slice.10), channel_id=1, source_target_pairs={{24,0},{0,8},{8,16},{16,24},{25,1},{1,9},{9,17},{17,25},{26,2},{2,... | collective-permute-start | bytes 1572872 | tf_op jit(solution)/shard_map/ppermute | solution.py:31
  25.6 25.6 %collective-permute-start.4 = (bf16[8,2,128,128]{3,2,1,0:T(8,128)(2,1)}, bf16[8,2,128,128]{3,2,1,0:T(8,128)(2,1)S(1)}, u32[]{:S(2)}, u32[]{:S(2)}) collective-permute-start(bf16[8,2,128,128]{3,2,1,0:T(8,128)(2,1)} %slice.10), channel_id=1, source_target_pairs={{8,0},{16,8},{24,16},{0,24},{9,1},{17,9},{25,17},{1,25},{10,2},{18... | collective-permute-start | bytes 1572872 | tf_op jit(solution)/shard_map/ppermute | solution.py:31
  29.5 21.7 %all-to-all-start.1 = ((bf16[8,1,5,128,128]{4,3,2,1,0:T(8,128)(2,1)}), bf16[8,1,5,128,128]{4,3,2,1,0:T(8,128)(2,1)S(1)}, u32[]{:S(2)}, u32[]{:S(2)}) async-start(bf16[8,1,5,128,128]{4,3,2,1,0:T(8,128)(2,1)} %second.1), calls=%async_computation.1 | async-start | bytes 2621440 | tf_op jit(solution)/shard_map/all_to_all | solution.py:35
  40.9 19.2 %collective-permute-start.5 = (bf16[8,1,128,128]{3,2,1,0:T(8,128)(2,1)S(1)}, bf16[8,1,128,128]{3,2,1,0:T(8,128)(2,1)}, u32[]{:S(2)}, u32[]{:S(2)}) collective-permute-start(bf16[8,1,128,128]{3,2,1,0:T(8,128)(2,1)S(1)} %slice.11.refs_1_), channel_id=1, source_target_pairs={{24,0},{0,8},{8,16},{16,24},{25,1},{1,9},{9,17},{17,25},{26,2},{2,... | collective-permute-start | bytes 786440 | tf_op jit(solution)/shard_map/ppermute | solution.py:31
  47.3 12.8 %collective-permute-start.6 = (bf16[8,1,128,128]{3,2,1,0:T(8,128)(2,1)S(1)}, bf16[8,1,128,128]{3,2,1,0:T(8,128)(2,1)}, u32[]{:S(2)}, u32[]{:S(2)}) collective-permute-start(bf16[8,1,128,128]{3,2,1,0:T(8,128)(2,1)S(1)} %slice.11.refs_1_), channel_id=1, source_target_pairs={{8,0},{16,8},{24,16},{0,24},{9,1},{17,9},{25,17},{1,25},{10,2},{18... | collective-permute-start | bytes 786440 | tf_op jit(solution)/shard_map/ppermute | solution.py:31

commit v7 on v6

--- a/solution.py
+++ b/solution.py
@@ -20,10 +20,6 @@
 SMEM = pl.BlockSpec(memory_space=pltpu.SMEM)
 VMEM = pl.BlockSpec(memory_space=pltpu.VMEM)
 ANY = pl.BlockSpec(memory_space=pl.ANY)
-
-
-def after(x, *others):
-    return lax.optimization_barrier((x, others))[0]
 
 
 def from_plane(x, by):
@@ -78,7 +74,9 @@
             else:
                 out[w, m, move.piece, to] = source[:, lanes]
     if plan.whole_lanes:
-        pltpu.make_async_copy(out, out, sem).wait()
+        first = min(move.piece for move in moves)
+        filled = out.at[:, :, first:max(move.piece for move in moves) + 1]
+        pltpu.make_async_copy(filled, filled, sem).wait()
 
 
 def last_kernel(plan, x, out, sem):
@@ -117,9 +115,9 @@
     for g in range(plan.sub):
         for j in range(NB):
             at = fact(plan, facts, g, NB * plan.kt * plan.kt + j) + (plan.hops * plan.sub + g)
-            tiles_at = lax.rem(at, plan.sub) * plan.kt
+            tiles_at = (at & (plan.sub - 1)) * plan.kt
             for d in range(plan.planes):
-                @pl.when(lax.div(at, plan.sub) == d)
+                @pl.when((at >> (plan.sub - 1)) == d)
                 def _():
                     for copy in copies_of(g, j, d, tiles_at):
                         copy.start()
@@ -299,7 +297,7 @@
 
 
 def call(kernel, name, out_shape, in_specs, out_specs, scratch, args, flops=0, exps=0, moved=0,
-         mib=8):
+         mib=8, aliases={}):
     return pl.pallas_call(
         kernel,
         out_shape=out_shape,
@@ -309,6 +307,7 @@
         compiler_params=pltpu.CompilerParams(vmem_limit_bytes=mib * 2 ** 20),
         cost_estimate=pl.CostEstimate(flops=flops, bytes_accessed=moved, transcendentals=exps),
         name=name,
+        input_output_aliases=aliases,
     )(*args)
 
 
@@ -336,29 +335,28 @@
     place = ANY if plan.whole_lanes else VMEM
     sem = pltpu.SemaphoreType.DMA(())
 
-    def pack(name, arrays, moves, pieces, staged=False, mark=None):
+    def pack(name, arrays, moves, pieces, staged=False, mark=None, begun=None):
         staged = staged and plan.whole_lanes
         scratch = [sem]
         if staged:
             scratch.append(pltpu.VMEM((len(moves), tiles, TILE, width), dtype))
             scratch.append(pltpu.SemaphoreType.DMA((len(moves), tiles)))
+        marks = slots if mark is None else mark
         return call(
             functools.partial(pack_kernel, plan, moves, staged), name,
             jax.ShapeDtypeStruct((ways, tiles, pieces, TILE, share), dtype),
-            [SMEM, ANY] + [ANY if staged else VMEM] * len(arrays), place, scratch,
-            (slots, slots if mark is None else mark, *arrays), moved=pieces * size,
-            mib=62 if staged else 8,
+            [SMEM, ANY] + [ANY if staged else VMEM] * len(arrays) + [ANY] * (begun is not None),
+            place, scratch,
+            (slots, marks, *arrays) + (() if begun is None else (begun,)),
+            moved=pieces * size, mib=62 if staged else 8,
+            aliases={} if begun is None else {2 + len(arrays): 0},
         )
 
     def spread(x):
         return exchange(x).reshape(ways * tiles, x.shape[2], TILE, share)
 
-    def around(x, chain=False):
-        found, last = {0: x}, ()
-        for d in shifts:
-            found[d] = from_plane(after(x, last), d)
-            last = found[d] if chain else ()
-        return found
+    def around(x):
+        return {d: from_plane(x, d) if d else x for d in (0, *shifts)}
 
     def mark(arrays, flops):
         return call(
@@ -367,7 +365,19 @@
         )
 
     raw = keys.reshape(1, 2, tiles, TILE, width)[:, :, :, :half].reshape(1, 2, tiles * half, width)
-    raw = around(raw, chain=True)
+    begun = None
+    if plan.whole_lanes:
+        begun = pack(
+            "queries", [queries], [Move(0, 0, 0), Move(0, 1, 1)], 2 + plan.planes
+        )
+    found = {0: raw}
+    for i, d in enumerate(shifts):
+        if i and begun is not None:
+            raw, begun, _ = lax.optimization_barrier((raw, begun, found[shifts[i - 1]]))
+        elif i:
+            raw, _ = lax.optimization_barrier((raw, found[shifts[i - 1]]))
+        found[d] = from_plane(raw, d)
+    raw = found
     packed = pack(
         "first", [keys, values],
         [Move(0, b, 0, row=half, rows=half, to=b * half) for b in range(2)]
@@ -382,14 +392,15 @@
     brought = mark([planes[d] for d in shifts[1:]], MARK_FLOPS[2])
     last_values, leads = lax.optimization_barrier((early[:, 2:], leads))
     late = around(last_values)
-    moves = [Move(0, 0, 0), Move(0, 1, 1)]
+    moves = [] if plan.whole_lanes else [Move(0, 0, 0), Move(0, 1, 1)]
     for d in order:
         for b in range(2):
             moves.append(Move(
                 1 + d + hops, b, 2 + d + hops, planes=d, rows=half, pitch=half, to=b * half
             ))
     packed = pack(
-        "second", [queries, *[raw[d] for d in order]], moves, 2 + plan.planes, mark=arrived
+        "second", [queries if begun is None else slots, *[raw[d] for d in order]], moves,
+        2 + plan.planes, mark=arrived, begun=begun
     )
     mixed = spread(packed)
     planes[0] = early

time: 78.1 us -> 78.2 us (level)
  waiting for transfers between devices: 20.8 us -> 17.4 us
  starting transfers between devices: 23.9 us -> 25.9 us
  Pallas kernels: 17.6 us -> 18.9 us
  local copies, waits for them, and re-layouts: 1.91 us -> 2.87 us
    ppermute x6, waiting for transfers between devices: 17.4 us -> 15 us  [from_plane(): return lax.ppermute(x, 'plane', [((i + by) % size, i) for i in range(size)])]
    ppermute x6, starting transfers between devices: 15.1 us -> 16.6 us  [from_plane(): return lax.ppermute(x, 'plane', [((i + by) % size, i) for i in range(size)])]
    pallas_call x9 -> x10, Pallas kernels: 17.6 us -> 18.9 us  [call(): pl.pallas_call(kernel, out_shape=out_shape, in_specs=in_specs, out_specs=...]
    unnamed x8 -> x12, local copies, waits for them, and re-layouts: 0.01 us -> 0.97 us
  transfers between devices with their start and end apart: 9 -> 9, of which waited for: 7 -> 5; matrix products, arithmetic and copies ran while one was open for 0% -> 0% of each run, Pallas kernels for 17% -> 19%
where the time goes in v7:
time: 78.2 us; the launch traced here: 77.8 us
  starting transfers between devices  25.9 us (33%)
  Pallas kernels  18.9 us (24%)
  waiting for transfers between devices  17.4 us (22%)
  blocking collectives  12.6 us (16%)
  local copies, waits for them, and re-layouts  2.87 us (4%)
    pallas_call x10, Pallas kernels, call(): pl.pallas_call(kernel, out_shape=out_shape, in_specs=in_specs, out_specs=...  18.9 us
    ppermute x6, starting transfers between devices, from_plane(): return lax.ppermute(x, 'plane', [((i + by) % size, i) for i in range(size)])  16.6 us
    ppermute x6, waiting for transfers between devices, from_plane(): return lax.ppermute(x, 'plane', [((i + by) % size, i) for i in range(size)])  15 us
    all_to_all x1, blocking collectives, exchange(): return lax.all_to_all(x, GROUP, split_axis=0, concat_axis=0, tiled=True)  12.6 us
    all_to_all x2, starting transfers between devices, exchange(): return lax.all_to_all(x, GROUP, split_axis=0, concat_axis=0, tiled=True)  7.32 us
    all_to_all x2, waiting for transfers between devices, exchange(): return lax.all_to_all(x, GROUP, split_axis=0, concat_axis=0, tiled=True)  2.41 us
    ppermute x1, starting transfers between devices, local(): other = lax.ppermute(own, 'sub', [(0, 1), (1, 0)])  2.02 us
  transfers between devices with their start and end apart: 9, of which 5 were waited for; matrix products, arithmetic and copies ran while one was open for 0% of the time, Pallas kernels for 19%

profile of v7, /device:TPU:0, one launch (start us, length us, event | category | flops | bytes accessed | tf_op | source)
XLA Modules:
  0.0 77.8 jit_solution(13602901262515980363)
XLA Ops:
  0.0 1.0 %slice_bitcast_fusion.refs_2_ = bf16[1,2,64,1024]{3,2,1,0:T(8,128)(2,1)S(1)} fusion(bf16[1,2,1,128,1024]{4,3,1,2,0:T(8,128)(2,1)} %bitcast.22), kind=kLoop, calls=%fused_computation | loop fusion | bytes 524288 | tf_op jit(solution)/shard_map/reshape | solution.py:367
  1.0 3.1 %collective-permute-start = (bf16[1,2,64,1024]{3,2,1,0:T(8,128)(2,1)S(1)}, bf16[1,2,64,1024]{3,2,1,0:T(8,128)(2,1)S(1)}, u32[]{:S(2)}, u32[]{:S(2)}) collective-permute-start(bf16[1,2,64,1024]{3,2,1,0:T(8,128)(2,1)S(1)} %slice_bitcast_fusion.refs_2_), channel_id=1, source_target_pairs={{24,0},{0,8},{8,16},{16,24},{25,1},{1,9},{9,17},{17,25},{26,2},{2,... | collective-permute-start | bytes 786440 | tf_op jit(solution)/shard_map/ppermute | solution.py:27
  4.0 0.0 copy-start
  4.0 0.0 copy-start.3
  4.1 2.8 %first.1 = bf16[8,1,3,128,128]{4,3,2,1,0:T(8,128)(2,1)} custom-call(s32[2,8]{1,0:T(2,128)} %bitcast.15, s32[2,8]{1,0:T(2,128)} %bitcast.16, bf16[1,2,128,1024]{3,2,1,0:T(8,128)(2,1)} %refs_0_.2, bf16[1,2,128,1024]{3,2,1,0:T(8,128)(2,1)} %refs_1_.1), custom_call_target="tpu_custom_call" | custom-call | bytes 1572864 | tf_op jit(solution)/shard_map/first/pallas_call | solution.py:301
  6.8 3.7 %all-to-all-start = ((bf16[8,1,3,128,128]{4,3,2,1,0:T(8,128)(2,1)}), bf16[8,1,3,128,128]{4,3,2,1,0:T(8,128)(2,1)S(1)}, u32[]{:S(2)}, u32[]{:S(2)}) async-start(bf16[8,1,3,128,128]{4,3,2,1,0:T(8,128)(2,1)} %first.1), calls=%async_computation | async-start | bytes 1572864 | tf_op jit(solution)/shard_map/all_to_all | solution.py:31
  10.6 0.0 copy-done
  10.6 0.0 copy-done.3
  10.6 0.0 copy-start.4
  10.6 0.0 copy-start.5
  10.6 1.4 %queries.1.refs_4_ = bf16[8,1,5,128,128]{4,3,2,1,0:T(8,128)(2,1)} custom-call(s32[2,8]{1,0:T(2,128)S(1)} %bitcast.17, s32[2,8]{1,0:T(2,128)S(1)} %bitcast.18, bf16[1,2,128,1024]{3,2,1,0:T(8,128)(2,1)S(1)} %copy-done), custom_call_target="tpu_custom_call" | custom-call | bytes 2621440 | tf_op jit(solution)/shard_map/queries/pallas_call | solution.py:301
  12.0 0.4 collective-permute-done.refs_0_.refs_1_
  12.4 0.0 copy-start.1
  12.4 2.0 %collective-permute-start.1 = (bf16[1,2,64,1024]{3,2,1,0:T(8,128)(2,1)S(1)}, bf16[1,2,64,1024]{3,2,1,0:T(8,128)(2,1)S(1)}, u32[]{:S(2)}, u32[]{:S(2)}) collective-permute-start(bf16[1,2,64,1024]{3,2,1,0:T(8,128)(2,1)S(1)} %slice_bitcast_fusion.refs_2_), channel_id=1, source_target_pairs={{8,0},{16,8},{24,16},{0,24},{9,1},{17,9},{25,17},{1,25},{10,2},{18... | collective-permute-start | bytes 786440 | tf_op jit(solution)/shard_map/ppermute | solution.py:27
  14.3 0.0 copy-done.4
  14.3 0.1 reshape.24
  14.4 0.0 copy-done.5
  14.4 0.1 pad_add_fusion.own
  14.5 2.0 %collective-permute-start.2 = (s32[34]{0:T(128)S(1)}, s32[34]{0:T(128)S(1)}, u32[]{:S(2)}, u32[]{:S(2)}) collective-permute-start(s32[34]{0:T(128)S(1)} %pad_add_fusion.own), channel_id=1, source_target_pairs={{0,4},{4,0},{1,5},{5,1},{2,6},{6,2},{3,7},{7,3},{8,12},{12,8},{9,1... | collective-permute-start | bytes 416 | tf_op jit(solution)/shard_map/ppermute | solution.py:332
  16.5 4.3 %collective-permute-done.1.refs_1_.refs_3_ = bf16[1,2,64,1024]{3,2,1,0:T(8,128)(2,1)S(1)} collective-permute-done((bf16[1,2,64,1024]{3,2,1,0:T(8,128)(2,1)S(1)}, bf16[1,2,64,1024]{3,2,1,0:T(8,128)(2,1)S(1)}, u32[]{:S(2)}, u32[]{:S(2)}) %collective-permute-start.1) | collective-permute-done | bytes 262176 | tf_op jit(solution)/shard_map/ppermute | solution.py:27
  20.8 0.0 copy-done.1
  20.8 0.0 collective-permute-done.2.other
  20.8 2.4 %all-to-all-done = bf16[8,1,3,128,128]{4,3,2,1,0:T(8,128)(2,1)S(1)} async-done(((bf16[8,1,3,128,128]{4,3,2,1,0:T(8,128)(2,1)}), bf16[8,1,3,128,128]{4,3,2,1,0:T(8,128)(2,1)S(1)}, u32[]{:S(2)}, u32[]{:S(2)}) %all-to-all-start) | async-done | bytes 786464 | tf_op jit(solution)/shard_map/all_to_all | solution.py:31
  23.2 0.8 %slice.10 = bf16[8,2,128,128]{3,2,1,0:T(8,128)(2,1)} slice(bf16[8,3,128,128]{3,2,1,0:T(8,128)(2,1)S(1)} %bitcast.8), slice={[0:8], [0:2], [0:128], [0:128]} | slice | bytes 1048576 | tf_op jit(solution)/shard_map/slice | solution.py:390
  24.0 1.6 %collective-permute-start.3 = (bf16[8,2,128,128]{3,2,1,0:T(8,128)(2,1)}, bf16[8,2,128,128]{3,2,1,0:T(8,128)(2,1)S(1)}, u32[]{:S(2)}, u32[]{:S(2)}) collective-permute-start(bf16[8,2,128,128]{3,2,1,0:T(8,128)(2,1)} %slice.10), channel_id=1, source_target_pairs={{24,0},{0,8},{8,16},{16,24},{25,1},{1,9},{9,17},{17,25},{26,2},{2,... | collective-permute-start | bytes 1572872 | tf_op jit(solution)/shard_map/ppermute | solution.py:27
  25.6 2.2 %collective-permute-start.4 = (bf16[8,2,128,128]{3,2,1,0:T(8,128)(2,1)}, bf16[8,2,128,128]{3,2,1,0:T(8,128)(2,1)S(1)}, u32[]{:S(2)}, u32[]{:S(2)}) collective-permute-start(bf16[8,2,128,128]{3,2,1,0:T(8,128)(2,1)} %slice.10), channel_id=1, source_target_pairs={{8,0},{16,8},{24,16},{0,24},{9,1},{17,9},{25,17},{1,25},{10,2},{18... | collective-permute-start | bytes 1572872 | tf_op jit(solution)/shard_map/ppermute | solution.py:27
  27.8 0.0 copy-start.2
  27.8 0.9 %copy-done.2 = bf16[1,2,64,1024]{3,2,1,0:T(8,128)(2,1)S(1)} copy-done((bf16[1,2,64,1024]{3,2,1,0:T(8,128)(2,1)S(1)}, bf16[1,2,64,1024]{3,2,1,0:T(8,128)(2,1)}, u32[]{:S(2)}) %copy-start.2) | copy-done | bytes 262168
  28.8 1.5 %second.1 = bf16[8,1,5,128,128]{4,3,2,1,0:T(8,128)(2,1)} custom-call(s32[2,8]{1,0:T(2,128)S(1)} %bitcast.19, f32[8,128]{1,0:T(8,128)S(1)} %mark.3.mark_ref, s32[2,8]{1,0:T(2,128)S(1)} %bitcast.20, bf16[1,2,64,1024]{3,2,1,0:T(8,128)(2,1)S(1)} %copy-done.2, bf16[1,2,64,1024]{3,2,1,0:T(8,128)(2,1)S(1)} %slice_bitcast_fusion.refs_2_, ...), custom_call_target="tpu_custom_call", output_to_operand_aliasing={{}: (6, {})} | custom-call | bytes 2621440 | tf_op jit(solution)/shard_map/second/pallas_call | solution.py:301
  30.3 3.6 %all-to-all-start.1 = ((bf16[8,1,5,128,128]{4,3,2,1,0:T(8,128)(2,1)}), bf16[8,1,5,128,128]{4,3,2,1,0:T(8,128)(2,1)S(1)}, u32[]{:S(2)}, u32[]{:S(2)}) async-start(bf16[8,1,5,128,128]{4,3,2,1,0:T(8,128)(2,1)} %second.1), calls=%async_computation.1 | async-start | bytes 2621440 | tf_op jit(solution)/shard_map/all_to_all | solution.py:31
  33.9 7.0 %collective-permute-done.3.refs_0_ = bf16[8,2,128,128]{3,2,1,0:T(8,128)(2,1)S(1)} collective-permute-done((bf16[8,2,128,128]{3,2,1,0:T(8,128)(2,1)}, bf16[8,2,128,128]{3,2,1,0:T(8,128)(2,1)S(1)}, u32[]{:S(2)}, u32[]{:S(2)}) %collective-permute-start.3) | collective-permute-done | bytes 524320 | tf_op jit(solution)/shard_map/ppermute | solution.py:27
  40.9 3.6 %collective-permute-start.5 = (bf16[8,1,128,128]{3,2,1,0:T(8,128)(2,1)S(1)}, bf16[8,1,128,128]{3,2,1,0:T(8,128)(2,1)}, u32[]{:S(2)}, u32[]{:S(2)}) collective-permute-start(bf16[8,1,128,128]{3,2,1,0:T(8,128)(2,1)S(1)} %slice.11.refs_1_), channel_id=1, source_target_pairs={{24,0},{0,8},{8,16},{16,24},{25,1},{1,9},{9,17},{17,25},{26,2},{2,... | collective-permute-start | bytes 786440 | tf_op jit(solution)/shard_map/ppermute | solution.py:27
  44.5 4.1 %collective-permute-start.6 = (bf16[8,1,128,128]{3,2,1,0:T(8,128)(2,1)S(1)}, bf16[8,1,128,128]{3,2,1,0:T(8,128)(2,1)}, u32[]{:S(2)}, u32[]{:S(2)}) collective-permute-start(bf16[8,1,128,128]{3,2,1,0:T(8,128)(2,1)S(1)} %slice.11.refs_1_), channel_id=1, source_target_pairs={{8,0},{16,8},{24,16},{0,24},{9,1},{17,9},{25,17},{1,25},{10,2},{18... | collective-permute-start | bytes 786440 | tf_op jit(solution)/shard_map/ppermute | solution.py:27
  48.6 3.4 %collective-permute-done.4.refs_0_.refs_2_ = bf16[8,2,128,128]{3,2,1,0:T(8,128)(2,1)S(1)} collective-permute-done((bf16[8,2,128,128]{3,2,1,0:T(8,128)(2,1)}, bf16[8,2,128,128]{3,2,1,0:T(8,128)(2,1)S(1)}, u32[]{:S(2)}, u32[]{:S(2)}) %collective-permute-start.4) | collective-permute-done | bytes 524320 | tf_op jit(solution)/shard_map/ppermute | solution.py:27
  52.0 0.0 all-to-all-done.1
  52.0 3.7 %scores.1.expo = bf16[8,256,1152]{2,1,0:T(8,128)(2,1)S(1)} custom-call(s32[34]{0:T(128)S(1)} %pad_add_fusion.own, s32[34]{0:T(128)S(1)} %collective-permute-done.2.other, bf16[8,5,128,128]{3,2,1,0:T(8,128)(2,1)S(1)} %bitcast.12, bf16[8,2,128,128]{3,2,1,0:T(8,128)(2,1)S(1)} %collective-permute-done.3.refs_0_, bf16[8,3,128,128]{3,2,1,0:T(8,128)(2,1)S(1)} %bitcast.10, ...), custom_call_target="tpu_custom_call" | custom-call | flops 301989888 | bytes 1048576 | tf_op jit(solution)/shard_map/scores/pallas_call | solution.py:301
  55.7 5.1 %attend.1.done = bf16[8,1,128,128]{3,2,1,0:T(8,128)(2,1)S(1)} custom-call(s32[34]{0:T(128)S(1)} %pad_add_fusion.own, s32[34]{0:T(128)S(1)} %collective-permute-done.2.other, bf16[8,5,128,128]{3,2,1,0:T(8,128)(2,1)S(1)} %bitcast.13, bf16[8,2,128,128]{3,2,1,0:T(8,128)(2,1)S(1)} %collective-permute-done.3.refs_0_, bf16[8,3,128,128]{3,2,1,0:T(8,128)(2,1)S(1)} %bitcast.11, ...), custom_call_target="tpu_custom_call" | custom-call | flops 603979776 | bytes 1048576 | tf_op jit(solution)/shard_map/attend/pallas_call | solution.py:301
  60.9 0.0 collective-permute-done.5.refs_0_
  60.9 0.0 collective-permute-done.6.refs_2_
  60.9 3.6 %weigh.1 = bf16[8,2,128,128]{3,2,1,0:T(8,128)(2,1)S(1)} custom-call(s32[34]{0:T(128)S(1)} %pad_add_fusion.own, s32[34]{0:T(128)S(1)} %collective-permute-done.2.other, s32[2,8]{1,0:T(2,128)S(1)} %bitcast.21, bf16[8,256,1152]{2,1,0:T(8,128)(2,1)S(1)} %scores.1.expo, bf16[8,1,128,128]{3,2,1,0:T(8,128)(2,1)S(1)} %attend.1.done, ...), custom_call_target="tpu_custom_call" | custom-call | flops 301989888 | bytes 1048576 | tf_op jit(solution)/shard_map/weigh/pallas_call | solution.py:301
  64.5 12.6 %all_to_all.15.x = bf16[8,1,2,128,128]{4,3,2,1,0:T(8,128)(2,1)S(1)} all-to-all(bf16[8,1,2,128,128]{4,3,2,1,0:T(8,128)(2,1)S(1)} %bitcast.14), channel_id=1, replica_groups=mesh['plane'=4,'sub'=2,'tok'=4] {'sub','tok'}, dimensions={0} | all-to-all | bytes 1048576 | tf_op jit(solution)/shard_map/all_to_all | solution.py:31
  77.0 0.8 %last.1 = bf16[1,2,128,1024]{3,2,1,0:T(8,128)(2,1)} custom-call(bf16[8,1,2,128,128]{4,3,2,1,0:T(8,128)(2,1)S(1)} %all_to_all.15.x), custom_call_target="tpu_custom_call" | custom-call | bytes 1048576 | tf_op jit(solution)/shard_map/last/pallas_call | solution.py:301
  (4 shorter events, 0.0 us)
Async XLA Ops:
  1.0 11.4 %collective-permute-start = (bf16[1,2,64,1024]{3,2,1,0:T(8,128)(2,1)S(1)}, bf16[1,2,64,1024]{3,2,1,0:T(8,128)(2,1)S(1)}, u32[]{:S(2)}, u32[]{:S(2)}) collective-permute-start(bf16[1,2,64,1024]{3,2,1,0:T(8,128)(2,1)S(1)} %slice_bitcast_fusion.refs_2_), channel_id=1, source_target_pairs={{24,0},{0,8},{8,16},{16,24},{25,1},{1,9},{9,17},{17,25},{26,2},{2,... | collective-permute-start | bytes 786440 | tf_op jit(solution)/shard_map/ppermute | solution.py:27
  4.0 6.5 %copy-start = (bf16[1,2,128,1024]{3,2,1,0:T(8,128)(2,1)S(1)}, bf16[1,2,128,1024]{3,2,1,0:T(8,128)(2,1)}, u32[]{:S(2)}) copy-start(bf16[1,2,128,1024]{3,2,1,0:T(8,128)(2,1)} %refs_0_.3) | copy-start | bytes 1572868
  4.0 6.5 %copy-start.3 = (s32[8,2]{0,1:T(2,128)S(1)}, s32[8,2]{0,1:T(2,128)}, u32[]{:S(2)}) copy-start(s32[8,2]{0,1:T(2,128)} %param.11) | copy-start | bytes 196
  6.8 16.3 %all-to-all-start = ((bf16[8,1,3,128,128]{4,3,2,1,0:T(8,128)(2,1)}), bf16[8,1,3,128,128]{4,3,2,1,0:T(8,128)(2,1)S(1)}, u32[]{:S(2)}, u32[]{:S(2)}) async-start(bf16[8,1,3,128,128]{4,3,2,1,0:T(8,128)(2,1)} %first.1), calls=%async_computation | async-start | bytes 1572864 | tf_op jit(solution)/shard_map/all_to_all | solution.py:31
  10.6 3.7 %copy-start.4 = (s32[1,2,4,4]{3,2,1,0:T(4,128)S(1)}, s32[1,2,4,4]{3,2,1,0:T(4,128)}, u32[]{:S(2)}) copy-start(s32[1,2,4,4]{3,2,1,0:T(4,128)} %param.9) | copy-start | bytes 388
  10.6 3.8 %copy-start.5 = (s32[1,2]{1,0:T(1,128)S(1)}, s32[1,2]{1,0:T(1,128)}, u32[]{:S(2)}) copy-start(s32[1,2]{1,0:T(1,128)} %param.10) | copy-start | bytes 28
  12.4 8.4 %copy-start.1 = (bf16[1,2,64,1024]{3,2,1,0:T(8,128)(2,1)}, bf16[1,2,64,1024]{3,2,1,0:T(8,128)(2,1)S(1)}, u32[]{:S(2)}) copy-start(bf16[1,2,64,1024]{3,2,1,0:T(8,128)(2,1)S(1)} %collective-permute-done.refs_0_.refs_1_) | copy-start | bytes 786436
  12.4 8.4 %collective-permute-start.1 = (bf16[1,2,64,1024]{3,2,1,0:T(8,128)(2,1)S(1)}, bf16[1,2,64,1024]{3,2,1,0:T(8,128)(2,1)S(1)}, u32[]{:S(2)}, u32[]{:S(2)}) collective-permute-start(bf16[1,2,64,1024]{3,2,1,0:T(8,128)(2,1)S(1)} %slice_bitcast_fusion.refs_2_), channel_id=1, source_target_pairs={{8,0},{16,8},{24,16},{0,24},{9,1},{17,9},{25,17},{1,25},{10,2},{18... | collective-permute-start | bytes 786440 | tf_op jit(solution)/shard_map/ppermute | solution.py:27
  14.5 6.3 %collective-permute-start.2 = (s32[34]{0:T(128)S(1)}, s32[34]{0:T(128)S(1)}, u32[]{:S(2)}, u32[]{:S(2)}) collective-permute-start(s32[34]{0:T(128)S(1)} %pad_add_fusion.own), channel_id=1, source_target_pairs={{0,4},{4,0},{1,5},{5,1},{2,6},{6,2},{3,7},{7,3},{8,12},{12,8},{9,1... | collective-permute-start | bytes 416 | tf_op jit(solution)/shard_map/ppermute | solution.py:332
  24.0 16.9 %collective-permute-start.3 = (bf16[8,2,128,128]{3,2,1,0:T(8,128)(2,1)}, bf16[8,2,128,128]{3,2,1,0:T(8,128)(2,1)S(1)}, u32[]{:S(2)}, u32[]{:S(2)}) collective-permute-start(bf16[8,2,128,128]{3,2,1,0:T(8,128)(2,1)} %slice.10), channel_id=1, source_target_pairs={{24,0},{0,8},{8,16},{16,24},{25,1},{1,9},{9,17},{17,25},{26,2},{2,... | collective-permute-start | bytes 1572872 | tf_op jit(solution)/shard_map/ppermute | solution.py:27
  25.6 26.4 %collective-permute-start.4 = (bf16[8,2,128,128]{3,2,1,0:T(8,128)(2,1)}, bf16[8,2,128,128]{3,2,1,0:T(8,128)(2,1)S(1)}, u32[]{:S(2)}, u32[]{:S(2)}) collective-permute-start(bf16[8,2,128,128]{3,2,1,0:T(8,128)(2,1)} %slice.10), channel_id=1, source_target_pairs={{8,0},{16,8},{24,16},{0,24},{9,1},{17,9},{25,17},{1,25},{10,2},{18... | collective-permute-start | bytes 1572872 | tf_op jit(solution)/shard_map/ppermute | solution.py:27
  27.8 0.9 %copy-start.2 = (bf16[1,2,64,1024]{3,2,1,0:T(8,128)(2,1)S(1)}, bf16[1,2,64,1024]{3,2,1,0:T(8,128)(2,1)}, u32[]{:S(2)}) copy-start(bf16[1,2,64,1024]{3,2,1,0:T(8,128)(2,1)} %copy-done.1) | copy-start | bytes 786436
  30.3 21.7 %all-to-all-start.1 = ((bf16[8,1,5,128,128]{4,3,2,1,0:T(8,128)(2,1)}), bf16[8,1,5,128,128]{4,3,2,1,0:T(8,128)(2,1)S(1)}, u32[]{:S(2)}, u32[]{:S(2)}) async-start(bf16[8,1,5,128,128]{4,3,2,1,0:T(8,128)(2,1)} %second.1), calls=%async_computation.1 | async-start | bytes 2621440 | tf_op jit(solution)/shard_map/all_to_all | solution.py:31
  40.9 20.0 %collective-permute-start.5 = (bf16[8,1,128,128]{3,2,1,0:T(8,128)(2,1)S(1)}, bf16[8,1,128,128]{3,2,1,0:T(8,128)(2,1)}, u32[]{:S(2)}, u32[]{:S(2)}) collective-permute-start(bf16[8,1,128,128]{3,2,1,0:T(8,128)(2,1)S(1)} %slice.11.refs_1_), channel_id=1, source_target_pairs={{24,0},{0,8},{8,16},{16,24},{25,1},{1,9},{9,17},{17,25},{26,2},{2,... | collective-permute-start | bytes 786440 | tf_op jit(solution)/shard_map/ppermute | solution.py:27
  44.5 16.3 %collective-permute-start.6 = (bf16[8,1,128,128]{3,2,1,0:T(8,128)(2,1)S(1)}, bf16[8,1,128,128]{3,2,1,0:T(8,128)(2,1)}, u32[]{:S(2)}, u32[]{:S(2)}) collective-permute-start(bf16[8,1,128,128]{3,2,1,0:T(8,128)(2,1)S(1)} %slice.11.refs_1_), channel_id=1, source_target_pairs={{8,0},{16,8},{24,16},{0,24},{9,1},{17,9},{25,17},{1,25},{10,2},{18... | collective-permute-start | bytes 786440 | tf_op jit(solution)/shard_map/ppermute | solution.py:27

commit v8 on v4

--- a/solution.py
+++ b/solution.py
@@ -12,7 +12,7 @@
 TILE = 128
 NB = 2
 REACH = 2
-MARK_FLOPS = (4 * 10 ** 9, 10 ** 10)
+MARK_FLOPS = (4 * 10 ** 9, 2 * 10 ** 9, 10 ** 10)
 GROUP = ("sub", "tok")
 
 NEG_SCORE = -1e30
@@ -117,9 +117,9 @@
     for g in range(plan.sub):
         for j in range(NB):
             at = fact(plan, facts, g, NB * plan.kt * plan.kt + j) + (plan.hops * plan.sub + g)
-            tiles_at = lax.rem(at, plan.sub) * plan.kt
+            tiles_at = (at & (plan.sub - 1)) * plan.kt
             for d in range(plan.planes):
-                @pl.when(lax.div(at, plan.sub) == d)
+                @pl.when((at >> (plan.sub - 1)) == d)
                 def _():
                     for copy in copies_of(g, j, d, tiles_at):
                         copy.start()
@@ -347,7 +347,7 @@
             jax.ShapeDtypeStruct((ways, tiles, pieces, TILE, share), dtype),
             [SMEM, ANY] + [ANY if staged else VMEM] * len(arrays), place, scratch,
             (slots, slots if mark is None else mark, *arrays), moved=pieces * size,
-            mib=62 if staged else 16,
+            mib=62 if staged else 8,
         )
 
     def spread(x):
@@ -363,7 +363,7 @@
     def mark(arrays, flops):
         return call(
             mark_kernel, "mark", jax.ShapeDtypeStruct((8, 128), jnp.float32),
-            [ANY] * len(arrays), VMEM, [], arrays, flops=flops,
+            [ANY] * len(arrays), VMEM, [], arrays, flops=flops, mib=1,
         )
 
     raw = keys.reshape(1, 2, tiles, TILE, width)[:, :, :, :half].reshape(1, 2, tiles * half, width)
@@ -378,9 +378,9 @@
     early, arrived, facts = lax.optimization_barrier((early, arrived, facts))
 
     planes = around(early[:, :2])
-    last_values, planes = lax.optimization_barrier((early[:, 2:], planes))
-    brought = mark([last_values], MARK_FLOPS[1])
-    last_values, brought = lax.optimization_barrier((last_values, brought))
+    leads = mark([planes[shifts[0]]], MARK_FLOPS[1])
+    brought = mark([planes[d] for d in shifts[1:]], MARK_FLOPS[2])
+    last_values, leads = lax.optimization_barrier((early[:, 2:], leads))
     late = around(last_values)
     moves = [Move(0, 0, 0), Move(0, 1, 1)]
     for d in order:
@@ -404,15 +404,15 @@
     expo = jax.ShapeDtypeStruct((sub * kt, plan.rows, plan.cols), dtype)
     out0, expo = call(
         functools.partial(core_kernel, plan), "core", (result(1), expo),
-        [SMEM] * 2 + [VMEM] + [ANY if d else VMEM for d in order] + [ANY], (VMEM, VMEM),
+        [SMEM] * 2 + [VMEM] * (1 + plan.planes) + [ANY] * 2, (VMEM, VMEM),
         [pltpu.VMEM((2, *far), dtype), pltpu.VMEM(far, dtype), sems((2, 2, sub, NB)),
          sems((sub, NB))],
-        (*facts, mixed, *planes, brought), flops=plan.pairs * HD * 6, exps=2 * plan.pairs,
-        moved=2 * size, mib=12,
+        (*facts, mixed, *planes, leads, brought), flops=plan.pairs * HD * 6,
+        exps=2 * plan.pairs, moved=2 * size, mib=12,
     )
     x = call(
         functools.partial(weigh_kernel, plan), "weigh", result(2),
-        [SMEM] * 3 + [VMEM] * (2 + plan.planes), VMEM,
+        [SMEM] * 3 + [VMEM] * 2 + [ANY if d else VMEM for d in order], VMEM,
         [pltpu.VMEM(far, dtype), sems((sub, NB))], (*facts, slots, expo, out0, *late),
         flops=plan.pairs * HD * 2, moved=2 * size, mib=12,
     )

time: 81.7 us -> 77.5 us (0.949)
  waiting for transfers between devices: 25.2 us -> 20.8 us
  starting transfers between devices: 21.3 us -> 24 us
  local copies, waits for them, and re-layouts: 3.75 us -> 1.91 us
  blocking collectives: 14.4 us -> 13.2 us
    ppermute x6, waiting for transfers between devices: 21.9 us -> 17.6 us  [from_plane(): return lax.ppermute(x, 'plane', [((i + by) % size, i) for i in range(size)])]
    ppermute x6, starting transfers between devices: 12.5 us -> 15.1 us  [from_plane(): return lax.ppermute(x, 'plane', [((i + by) % size, i) for i in range(size)])]
    unnamed x12 -> x8, local copies, waits for them, and re-layouts: 1.85 us -> 0.01 us
    all_to_all x1, blocking collectives: 14.4 us -> 13.2 us  [exchange(): return lax.all_to_all(x, GROUP, split_axis=0, concat_axis=0, tiled=True)]
    pallas_call x7 -> x8, Pallas kernels: 16.5 us -> 17 us  [call(): pl.pallas_call(kernel, out_shape=out_shape, in_specs=in_specs, out_specs=...]
  transfers between devices with their start and end apart: 9 -> 9, of which waited for: 7 -> 6; matrix products, arithmetic and copies ran while one was open for 0% -> 0% of each run, Pallas kernels for 15% -> 17%
where the time goes in v8:
time: 77.5 us; the launch traced here: 77.1 us
  starting transfers between devices  24 us (31%)
  waiting for transfers between devices  20.8 us (27%)
  Pallas kernels  17 us (22%)
  blocking collectives  13.2 us (17%)
  local copies, waits for them, and re-layouts  1.91 us (2%)
    ppermute x6, waiting for transfers between devices, from_plane(): return lax.ppermute(x, 'plane', [((i + by) % size, i) for i in range(size)])  17.6 us
    pallas_call x8, Pallas kernels, call(): pl.pallas_call(kernel, out_shape=out_shape, in_specs=in_specs, out_specs=...  17 us
    ppermute x6, starting transfers between devices, from_plane(): return lax.ppermute(x, 'plane', [((i + by) % size, i) for i in range(size)])  15.1 us
    all_to_all x1, blocking collectives, exchange(): return lax.all_to_all(x, GROUP, split_axis=0, concat_axis=0, tiled=True)  13.2 us
    all_to_all x2, starting transfers between devices, exchange(): return lax.all_to_all(x, GROUP, split_axis=0, concat_axis=0, tiled=True)  7.32 us
    all_to_all x2, waiting for transfers between devices, exchange(): return lax.all_to_all(x, GROUP, split_axis=0, concat_axis=0, tiled=True)  2.99 us
  transfers between devices with their start and end apart: 9, of which 6 were waited for; matrix products, arithmetic and copies ran while one was open for 0% of the time, Pallas kernels for 17%

profile of v8, /device:TPU:0, one launch (start us, length us, event | category | flops | bytes accessed | tf_op | source)
XLA Modules:
  0.0 77.1 jit_solution(2927193576752448927)
XLA Ops:
  0.0 1.0 %slice_bitcast_fusion.refs_2_ = bf16[1,2,64,1024]{3,2,1,0:T(8,128)(2,1)S(1)} fusion(bf16[1,2,1,128,1024]{4,3,1,2,0:T(8,128)(2,1)} %bitcast.17), kind=kLoop, calls=%fused_computation | loop fusion | bytes 524288 | tf_op jit(solution)/shard_map/reshape | solution.py:369
  1.0 3.1 %collective-permute-start = (bf16[1,2,64,1024]{3,2,1,0:T(8,128)(2,1)S(1)}, bf16[1,2,64,1024]{3,2,1,0:T(8,128)(2,1)S(1)}, u32[]{:S(2)}, u32[]{:S(2)}) collective-permute-start(bf16[1,2,64,1024]{3,2,1,0:T(8,128)(2,1)S(1)} %slice_bitcast_fusion.refs_2_), channel_id=1, source_target_pairs={{24,0},{0,8},{8,16},{16,24},{25,1},{1,9},{9,17},{17,25},{26,2},{2,... | collective-permute-start | bytes 786440 | tf_op jit(solution)/shard_map/ppermute | solution.py:31
  4.0 0.0 copy-start.2
  4.0 0.0 copy-start.3
  4.1 2.7 %first.1 = bf16[8,1,3,128,128]{4,3,2,1,0:T(8,128)(2,1)} custom-call(s32[2,8]{1,0:T(2,128)} %bitcast.13, s32[2,8]{1,0:T(2,128)} %bitcast.14, bf16[1,2,128,1024]{3,2,1,0:T(8,128)(2,1)} %refs_0_.2, bf16[1,2,128,1024]{3,2,1,0:T(8,128)(2,1)} %refs_1_.1), custom_call_target="tpu_custom_call" | custom-call | bytes 1572864 | tf_op jit(solution)/shard_map/first/pallas_call | solution.py:303
  6.8 3.7 %all-to-all-start = ((bf16[8,1,3,128,128]{4,3,2,1,0:T(8,128)(2,1)}), bf16[8,1,3,128,128]{4,3,2,1,0:T(8,128)(2,1)S(1)}, u32[]{:S(2)}, u32[]{:S(2)}) async-start(bf16[8,1,3,128,128]{4,3,2,1,0:T(8,128)(2,1)} %first.1), calls=%async_computation | async-start | bytes 1572864 | tf_op jit(solution)/shard_map/all_to_all | solution.py:35
  10.5 1.8 %collective-permute-done.refs_0_.refs_1_ = bf16[1,2,64,1024]{3,2,1,0:T(8,128)(2,1)S(1)} collective-permute-done((bf16[1,2,64,1024]{3,2,1,0:T(8,128)(2,1)S(1)}, bf16[1,2,64,1024]{3,2,1,0:T(8,128)(2,1)S(1)}, u32[]{:S(2)}, u32[]{:S(2)}) %collective-permute-start) | collective-permute-done | bytes 262176 | tf_op jit(solution)/shard_map/ppermute | solution.py:31
  12.4 1.7 %collective-permute-start.1 = (bf16[1,2,64,1024]{3,2,1,0:T(8,128)(2,1)S(1)}, bf16[1,2,64,1024]{3,2,1,0:T(8,128)(2,1)S(1)}, u32[]{:S(2)}, u32[]{:S(2)}) collective-permute-start(bf16[1,2,64,1024]{3,2,1,0:T(8,128)(2,1)S(1)} %slice_bitcast_fusion.refs_2_), channel_id=1, source_target_pairs={{8,0},{16,8},{24,16},{0,24},{9,1},{17,9},{25,17},{1,25},{10,2},{18... | collective-permute-start | bytes 786440 | tf_op jit(solution)/shard_map/ppermute | solution.py:31
  14.1 0.0 copy-done.2
  14.1 0.1 reshape.24
  14.2 0.0 copy-done.3
  14.2 0.1 pad_add_fusion.own
  14.3 0.0 copy-start.1
  14.3 1.5 %collective-permute-start.2 = (s32[34]{0:T(128)S(1)}, s32[34]{0:T(128)S(1)}, u32[]{:S(2)}, u32[]{:S(2)}) collective-permute-start(s32[34]{0:T(128)S(1)} %pad_add_fusion.own), channel_id=1, source_target_pairs={{0,4},{4,0},{1,5},{5,1},{2,6},{6,2},{3,7},{7,3},{8,12},{12,8},{9,1... | collective-permute-start | bytes 416 | tf_op jit(solution)/shard_map/ppermute | solution.py:333
  15.8 4.1 %collective-permute-done.1.refs_1_.refs_3_ = bf16[1,2,64,1024]{3,2,1,0:T(8,128)(2,1)S(1)} collective-permute-done((bf16[1,2,64,1024]{3,2,1,0:T(8,128)(2,1)S(1)}, bf16[1,2,64,1024]{3,2,1,0:T(8,128)(2,1)S(1)}, u32[]{:S(2)}, u32[]{:S(2)}) %collective-permute-start.1) | collective-permute-done | bytes 262176 | tf_op jit(solution)/shard_map/ppermute | solution.py:31
  19.9 0.0 copy-start
  19.9 0.3 collective-permute-done.2.other
  20.2 3.0 %all-to-all-done = bf16[8,1,3,128,128]{4,3,2,1,0:T(8,128)(2,1)S(1)} async-done(((bf16[8,1,3,128,128]{4,3,2,1,0:T(8,128)(2,1)}), bf16[8,1,3,128,128]{4,3,2,1,0:T(8,128)(2,1)S(1)}, u32[]{:S(2)}, u32[]{:S(2)}) %all-to-all-start) | async-done | bytes 786464 | tf_op jit(solution)/shard_map/all_to_all | solution.py:35
  23.1 0.8 %slice.10 = bf16[8,2,128,128]{3,2,1,0:T(8,128)(2,1)} slice(bf16[8,3,128,128]{3,2,1,0:T(8,128)(2,1)S(1)} %bitcast.8), slice={[0:8], [0:2], [0:128], [0:128]} | slice | bytes 1048576 | tf_op jit(solution)/shard_map/slice | solution.py:380
  24.0 1.6 %collective-permute-start.3 = (bf16[8,2,128,128]{3,2,1,0:T(8,128)(2,1)}, bf16[8,2,128,128]{3,2,1,0:T(8,128)(2,1)S(1)}, u32[]{:S(2)}, u32[]{:S(2)}) collective-permute-start(bf16[8,2,128,128]{3,2,1,0:T(8,128)(2,1)} %slice.10), channel_id=1, source_target_pairs={{24,0},{0,8},{8,16},{16,24},{25,1},{1,9},{9,17},{17,25},{26,2},{2,... | collective-permute-start | bytes 1572872 | tf_op jit(solution)/shard_map/ppermute | solution.py:31
  25.6 2.2 %collective-permute-start.4 = (bf16[8,2,128,128]{3,2,1,0:T(8,128)(2,1)}, bf16[8,2,128,128]{3,2,1,0:T(8,128)(2,1)}, u32[]{:S(2)}, u32[]{:S(2)}) collective-permute-start(bf16[8,2,128,128]{3,2,1,0:T(8,128)(2,1)} %slice.10), channel_id=1, source_target_pairs={{8,0},{16,8},{24,16},{0,24},{9,1},{17,9},{25,17},{1,25},{10,2},{18... | collective-permute-start | bytes 1572872 | tf_op jit(solution)/shard_map/ppermute | solution.py:31
  27.8 0.0 copy-done.1
  27.8 0.0 copy-done
  27.8 1.6 %second.1 = bf16[8,1,5,128,128]{4,3,2,1,0:T(8,128)(2,1)} custom-call(s32[2,8]{1,0:T(2,128)S(1)} %bitcast.15, f32[8,128]{1,0:T(8,128)S(1)} %mark.3.mark_ref, bf16[1,2,128,1024]{3,2,1,0:T(8,128)(2,1)S(1)} %copy-done, bf16[1,2,64,1024]{3,2,1,0:T(8,128)(2,1)S(1)} %collective-permute-done.refs_0_.refs_1_, bf16[1,2,64,1024]{3,2,1,0:T(8,128)(2,1)S(1)} %slice_bitcast_fusion.refs_2_, ...), custom_call_target="tpu_custom_call" | custom-call | bytes 2621440 | tf_op jit(solution)/shard_map/second/pallas_call | solution.py:303
  29.4 3.6 %all-to-all-start.1 = ((bf16[8,1,5,128,128]{4,3,2,1,0:T(8,128)(2,1)}), bf16[8,1,5,128,128]{4,3,2,1,0:T(8,128)(2,1)S(1)}, u32[]{:S(2)}, u32[]{:S(2)}) async-start(bf16[8,1,5,128,128]{4,3,2,1,0:T(8,128)(2,1)} %second.1), calls=%async_computation.1 | async-start | bytes 2621440 | tf_op jit(solution)/shard_map/all_to_all | solution.py:35
  33.1 7.8 %collective-permute-done.3.refs_0_ = bf16[8,2,128,128]{3,2,1,0:T(8,128)(2,1)S(1)} collective-permute-done((bf16[8,2,128,128]{3,2,1,0:T(8,128)(2,1)}, bf16[8,2,128,128]{3,2,1,0:T(8,128)(2,1)S(1)}, u32[]{:S(2)}, u32[]{:S(2)}) %collective-permute-start.3) | collective-permute-done | bytes 524320 | tf_op jit(solution)/shard_map/ppermute | solution.py:31
  40.9 6.5 %collective-permute-start.5 = (bf16[8,1,128,128]{3,2,1,0:T(8,128)(2,1)S(1)}, bf16[8,1,128,128]{3,2,1,0:T(8,128)(2,1)S(1)}, u32[]{:S(2)}, u32[]{:S(2)}) collective-permute-start(bf16[8,1,128,128]{3,2,1,0:T(8,128)(2,1)S(1)} %slice.11.refs_1_), channel_id=1, source_target_pairs={{24,0},{0,8},{8,16},{16,24},{25,1},{1,9},{9,17},{17,25},{26,2},{2,... | collective-permute-start | bytes 786440 | tf_op jit(solution)/shard_map/ppermute | solution.py:31
  47.3 0.0 collective-permute-start.6
  47.3 3.9 %collective-permute-done.4.refs_0_.refs_2_ = bf16[8,2,128,128]{3,2,1,0:T(8,128)(2,1)} collective-permute-done((bf16[8,2,128,128]{3,2,1,0:T(8,128)(2,1)}, bf16[8,2,128,128]{3,2,1,0:T(8,128)(2,1)}, u32[]{:S(2)}, u32[]{:S(2)}) %collective-permute-start.4) | collective-permute-done | bytes 524320 | tf_op jit(solution)/shard_map/ppermute | solution.py:31
  51.2 0.0 all-to-all-done.1
  51.2 8.7 %core.1 = (bf16[8,1,128,128]{3,2,1,0:T(8,128)(2,1)S(1)}, bf16[8,256,1152]{2,1,0:T(8,128)(2,1)S(1)}) custom-call(s32[34]{0:T(128)S(1)} %pad_add_fusion.own, s32[34]{0:T(128)S(1)} %collective-permute-done.2.other, bf16[8,5,128,128]{3,2,1,0:T(8,128)(2,1)S(1)} %bitcast.12, bf16[8,2,128,128]{3,2,1,0:T(8,128)(2,1)S(1)} %collective-permute-done.3.refs_0_, ...), custom_call_target="tpu_custom_call" | custom-call | flops 905969664 | bytes 1048576 | tf_op jit(solution)/shard_map/core/pallas_call | solution.py:303
  59.9 0.0 collective-permute-done.5.refs_0_
  60.0 0.0 collective-permute-done.6.refs_2_
  60.0 3.1 %weigh.1 = bf16[8,2,128,128]{3,2,1,0:T(8,128)(2,1)S(1)} custom-call(s32[34]{0:T(128)S(1)} %pad_add_fusion.own, s32[34]{0:T(128)S(1)} %collective-permute-done.2.other, s32[2,8]{1,0:T(2,128)S(1)} %bitcast.16, bf16[8,256,1152]{2,1,0:T(8,128)(2,1)S(1)} %get-tuple-element.20.expo, bf16[8,1,128,128]{3,2,1,0:T(8,128)(2,1)S(1)} %get-tuple-element.21.done, ...), custom_call_target="tpu_custom_call" | custom-call | flops 301989888 | bytes 1048576 | tf_op jit(solution)/shard_map/weigh/pallas_call | solution.py:303
  63.1 13.2 %all_to_all.15.x = bf16[8,1,2,128,128]{4,3,2,1,0:T(8,128)(2,1)S(1)} all-to-all(bf16[8,1,2,128,128]{4,3,2,1,0:T(8,128)(2,1)S(1)} %bitcast.11), channel_id=1, replica_groups=mesh['plane'=4,'sub'=2,'tok'=4] {'sub','tok'}, dimensions={0} | all-to-all | bytes 1048576 | tf_op jit(solution)/shard_map/all_to_all | solution.py:35
  76.3 0.8 %last.1 = bf16[1,2,128,1024]{3,2,1,0:T(8,128)(2,1)} custom-call(bf16[8,1,2,128,128]{4,3,2,1,0:T(8,128)(2,1)S(1)} %all_to_all.15.x), custom_call_target="tpu_custom_call" | custom-call | bytes 1048576 | tf_op jit(solution)/shard_map/last/pallas_call | solution.py:303
  (4 shorter events, 0.0 us)
Async XLA Ops:
  1.0 11.4 %collective-permute-start = (bf16[1,2,64,1024]{3,2,1,0:T(8,128)(2,1)S(1)}, bf16[1,2,64,1024]{3,2,1,0:T(8,128)(2,1)S(1)}, u32[]{:S(2)}, u32[]{:S(2)}) collective-permute-start(bf16[1,2,64,1024]{3,2,1,0:T(8,128)(2,1)S(1)} %slice_bitcast_fusion.refs_2_), channel_id=1, source_target_pairs={{24,0},{0,8},{8,16},{16,24},{25,1},{1,9},{9,17},{17,25},{26,2},{2,... | collective-permute-start | bytes 786440 | tf_op jit(solution)/shard_map/ppermute | solution.py:31
  4.0 10.1 %copy-start.2 = (s32[1,2,4,4]{3,2,1,0:T(4,128)S(1)}, s32[1,2,4,4]{3,2,1,0:T(4,128)}, u32[]{:S(2)}) copy-start(s32[1,2,4,4]{3,2,1,0:T(4,128)} %param.9) | copy-start | bytes 388
  4.0 10.2 %copy-start.3 = (s32[1,2]{1,0:T(1,128)S(1)}, s32[1,2]{1,0:T(1,128)}, u32[]{:S(2)}) copy-start(s32[1,2]{1,0:T(1,128)} %param.10) | copy-start | bytes 28
  6.8 16.3 %all-to-all-start = ((bf16[8,1,3,128,128]{4,3,2,1,0:T(8,128)(2,1)}), bf16[8,1,3,128,128]{4,3,2,1,0:T(8,128)(2,1)S(1)}, u32[]{:S(2)}, u32[]{:S(2)}) async-start(bf16[8,1,3,128,128]{4,3,2,1,0:T(8,128)(2,1)} %first.1), calls=%async_computation | async-start | bytes 1572864 | tf_op jit(solution)/shard_map/all_to_all | solution.py:35
  12.4 7.5 %collective-permute-start.1 = (bf16[1,2,64,1024]{3,2,1,0:T(8,128)(2,1)S(1)}, bf16[1,2,64,1024]{3,2,1,0:T(8,128)(2,1)S(1)}, u32[]{:S(2)}, u32[]{:S(2)}) collective-permute-start(bf16[1,2,64,1024]{3,2,1,0:T(8,128)(2,1)S(1)} %slice_bitcast_fusion.refs_2_), channel_id=1, source_target_pairs={{8,0},{16,8},{24,16},{0,24},{9,1},{17,9},{25,17},{1,25},{10,2},{18... | collective-permute-start | bytes 786440 | tf_op jit(solution)/shard_map/ppermute | solution.py:31
  14.3 13.5 %copy-start.1 = (s32[8,2]{0,1:T(2,128)S(1)}, s32[8,2]{0,1:T(2,128)}, u32[]{:S(2)}) copy-start(s32[8,2]{0,1:T(2,128)} %param.11) | copy-start | bytes 196
  14.3 5.9 %collective-permute-start.2 = (s32[34]{0:T(128)S(1)}, s32[34]{0:T(128)S(1)}, u32[]{:S(2)}, u32[]{:S(2)}) collective-permute-start(s32[34]{0:T(128)S(1)} %pad_add_fusion.own), channel_id=1, source_target_pairs={{0,4},{4,0},{1,5},{5,1},{2,6},{6,2},{3,7},{7,3},{8,12},{12,8},{9,1... | collective-permute-start | bytes 416 | tf_op jit(solution)/shard_map/ppermute | solution.py:333
  19.9 7.9 %copy-start = (bf16[1,2,128,1024]{3,2,1,0:T(8,128)(2,1)S(1)}, bf16[1,2,128,1024]{3,2,1,0:T(8,128)(2,1)}, u32[]{:S(2)}) copy-start(bf16[1,2,128,1024]{3,2,1,0:T(8,128)(2,1)} %refs_0_.3) | copy-start | bytes 1572868
  24.0 16.9 %collective-permute-start.3 = (bf16[8,2,128,128]{3,2,1,0:T(8,128)(2,1)}, bf16[8,2,128,128]{3,2,1,0:T(8,128)(2,1)S(1)}, u32[]{:S(2)}, u32[]{:S(2)}) collective-permute-start(bf16[8,2,128,128]{3,2,1,0:T(8,128)(2,1)} %slice.10), channel_id=1, source_target_pairs={{24,0},{0,8},{8,16},{16,24},{25,1},{1,9},{9,17},{17,25},{26,2},{2,... | collective-permute-start | bytes 1572872 | tf_op jit(solution)/shard_map/ppermute | solution.py:31
  25.6 25.7 %collective-permute-start.4 = (bf16[8,2,128,128]{3,2,1,0:T(8,128)(2,1)}, bf16[8,2,128,128]{3,2,1,0:T(8,128)(2,1)}, u32[]{:S(2)}, u32[]{:S(2)}) collective-permute-start(bf16[8,2,128,128]{3,2,1,0:T(8,128)(2,1)} %slice.10), channel_id=1, source_target_pairs={{8,0},{16,8},{24,16},{0,24},{9,1},{17,9},{25,17},{1,25},{10,2},{18... | collective-permute-start | bytes 1572872 | tf_op jit(solution)/shard_map/ppermute | solution.py:31
  29.4 21.8 %all-to-all-start.1 = ((bf16[8,1,5,128,128]{4,3,2,1,0:T(8,128)(2,1)}), bf16[8,1,5,128,128]{4,3,2,1,0:T(8,128)(2,1)S(1)}, u32[]{:S(2)}, u32[]{:S(2)}) async-start(bf16[8,1,5,128,128]{4,3,2,1,0:T(8,128)(2,1)} %second.1), calls=%async_computation.1 | async-start | bytes 2621440 | tf_op jit(solution)/shard_map/all_to_all | solution.py:35
  40.9 19.1 %collective-permute-start.5 = (bf16[8,1,128,128]{3,2,1,0:T(8,128)(2,1)S(1)}, bf16[8,1,128,128]{3,2,1,0:T(8,128)(2,1)S(1)}, u32[]{:S(2)}, u32[]{:S(2)}) collective-permute-start(bf16[8,1,128,128]{3,2,1,0:T(8,128)(2,1)S(1)} %slice.11.refs_1_), channel_id=1, source_target_pairs={{24,0},{0,8},{8,16},{16,24},{25,1},{1,9},{9,17},{17,25},{26,2},{2,... | collective-permute-start | bytes 786440 | tf_op jit(solution)/shard_map/ppermute | solution.py:31
  47.3 12.6 %collective-permute-start.6 = (bf16[8,1,128,128]{3,2,1,0:T(8,128)(2,1)S(1)}, bf16[8,1,128,128]{3,2,1,0:T(8,128)(2,1)S(1)}, u32[]{:S(2)}, u32[]{:S(2)}) collective-permute-start(bf16[8,1,128,128]{3,2,1,0:T(8,128)(2,1)S(1)} %slice.11.refs_1_), channel_id=1, source_target_pairs={{8,0},{16,8},{24,16},{0,24},{9,1},{17,9},{25,17},{1,25},{10,2},{18... | collective-permute-start | bytes 786440 | tf_op jit(solution)/shard_map/ppermute | solution.py:31

commit v9 on v8

--- a/solution.py
+++ b/solution.py
@@ -81,6 +81,42 @@
         pltpu.make_async_copy(out, out, sem).wait()
 
 
+def first_kernel(plan, slots_ref, keys, values, out, stage, slots, stage_sem, slots_sem, sem):
+    ways, tiles, _, _, share = out.shape
+    half = TILE // 2
+    ask = pltpu.make_async_copy(slots_ref, slots, slots_sem)
+    ask.start()
+    fetched = []
+    for i, (src, row, rows) in enumerate(((keys, half, half), (values, 0, TILE))):
+        for s in range(2):
+            for m in range(tiles):
+                there = stage.at[2 * i + s, m, pl.ds(0, rows)]
+                copy = pltpu.make_async_copy(
+                    src.at[0, s, pl.ds(m * TILE + row, rows)], there, stage_sem.at[2 * i + s, m]
+                )
+                copy.start()
+                fetched.append((i, s, m, there, copy))
+    ask.wait()
+    view = lax.axis_index("plane") * plan.sub + lax.axis_index("sub")
+    lead = slots[0, view]
+    for i, s, m, there, copy in fetched:
+        branch = jnp.where(lead == s, 0, 1)
+        copy.wait()
+        for w in range(ways):
+            if i == 0:
+                to = out.at[w, m, 0, pl.ds(pl.multiple_of(branch * half, half), half)]
+            else:
+                to = out.at[w, m, 1 + branch]
+            pltpu.make_async_copy(there.at[:, pl.ds(w * share, share)], to, sem).start()
+    pltpu.make_async_copy(out, out, sem).wait()
+
+
+def split_kernel(x, head, tail):
+    pieces = head.shape[1]
+    head[...] = x[:, :pieces]
+    tail[...] = x[:, pieces:]
+
+
 def last_kernel(plan, x, out, sem):
     ways, tiles, slots, _, share = x.shape
     for s in range(slots):
@@ -255,11 +291,19 @@
         for i, part in enumerate(expo_of(1, g, t, k)):
             expo_ref[g * plan.kt + t, :, i * TILE:(i + 1) * TILE] = part
 
-    each_view(
-        plan, functools.partial(wait, 0), attended,
-        lambda g: (keys(0, g), [with_ones(far_rows(plan, v_far, g, j)) for j in range(NB)]),
-    )
-    each_view(plan, functools.partial(wait, 1), scored, functools.partial(keys, 1))
+    def wait_both(g):
+        wait(0, g)
+        wait(1, g)
+
+    def prepare(g):
+        v = [with_ones(far_rows(plan, v_far, g, j)) for j in range(NB)]
+        return (keys(0, g), v), keys(1, g)
+
+    def both(g, t, ready):
+        attended(g, t, ready[0])
+        scored(g, t, ready[1])
+
+    each_view(plan, wait_both, both, prepare)
 
 
 def weigh_kernel(plan, own, other, slots, expo, done, *refs):
@@ -368,19 +412,33 @@
 
     raw = keys.reshape(1, 2, tiles, TILE, width)[:, :, :, :half].reshape(1, 2, tiles * half, width)
     raw = around(raw, chain=True)
-    packed = pack(
-        "first", [keys, values],
-        [Move(0, b, 0, row=half, rows=half, to=b * half) for b in range(2)]
-        + [Move(1, b, 1 + b) for b in range(2)], 3, staged=True,
-    )
+    if plan.whole_lanes:
+        packed = call(
+            functools.partial(first_kernel, plan), "first",
+            jax.ShapeDtypeStruct((ways, tiles, 3, TILE, share), dtype), [ANY] * 3, ANY,
+            [pltpu.VMEM((4, tiles, TILE, width), dtype), pltpu.SMEM(slots.shape, jnp.int32),
+             pltpu.SemaphoreType.DMA((4, tiles)), sem, sem],
+            (slots, keys, values), moved=3 * size, mib=62,
+        )
+    else:
+        packed = pack(
+            "first", [keys, values],
+            [Move(0, b, 0, row=half, rows=half, to=b * half) for b in range(2)]
+            + [Move(1, b, 1 + b) for b in range(2)], 3,
+        )
     early = spread(packed)
     arrived = mark([raw[d] for d in shifts], MARK_FLOPS[0])
     early, arrived, facts = lax.optimization_barrier((early, arrived, facts))
 
-    planes = around(early[:, :2])
+    heads, last_values = call(
+        split_kernel, "split",
+        tuple(jax.ShapeDtypeStruct((ways * tiles, n, TILE, share), dtype) for n in (2, 1)),
+        [VMEM], (VMEM, VMEM), [], (early,), moved=size,
+    )
+    planes = around(heads)
     leads = mark([planes[shifts[0]]], MARK_FLOPS[1])
     brought = mark([planes[d] for d in shifts[1:]], MARK_FLOPS[2])
-    last_values, leads = lax.optimization_barrier((early[:, 2:], leads))
+    last_values, leads = lax.optimization_barrier((last_values, leads))
     late = around(last_values)
     moves = [Move(0, 0, 0), Move(0, 1, 1)]
     for d in order:
@@ -408,7 +466,7 @@
         [pltpu.VMEM((2, *far), dtype), pltpu.VMEM(far, dtype), sems((2, 2, sub, NB)),
          sems((sub, NB))],
         (*facts, mixed, *planes, leads, brought), flops=plan.pairs * HD * 6,
-        exps=2 * plan.pairs, moved=2 * size, mib=12,
+        exps=2 * plan.pairs, moved=2 * size, mib=12 if kt <= 4 else 32,
     )
     x = call(
         functools.partial(weigh_kernel, plan), "weigh", result(2),

time: 77.5 us -> 76.7 us (0.990)
  local copies, waits for them, and re-layouts: 1.91 us -> 1.07 us
    slice x2 -> x0, local copies, waits for them, and re-layouts: 0.85 us -> none  [the longest x1 0.83 us: local(): planes = around(early[:, :2])]
    pallas_call x8 -> x9, Pallas kernels: 17 us -> 17.2 us  [call(): pl.pallas_call(kernel, out_shape=out_shape, in_specs=in_specs, out_specs=...]
  transfers between devices with their start and end apart: 9 -> 9, of which waited for: 6 -> 5; matrix products, arithmetic and copies ran while one was open for 0% -> 0% of each run, Pallas kernels for 17% -> 16%
where the time goes in v9:
time: 76.7 us; the launch traced here: 76.3 us
  starting transfers between devices  24 us (31%)
  waiting for transfers between devices  20.8 us (27%)
  Pallas kernels  17.2 us (22%)
  blocking collectives  13.1 us (17%)
  local copies, waits for them, and re-layouts  1.07 us (1%)
    ppermute x6, waiting for transfers between devices, from_plane(): return lax.ppermute(x, 'plane', [((i + by) % size, i) for i in range(size)])  18.3 us
    pallas_call x9, Pallas kernels, call(): pl.pallas_call(kernel, out_shape=out_shape, in_specs=in_specs, out_specs=...  17.2 us
    ppermute x6, starting transfers between devices, from_plane(): return lax.ppermute(x, 'plane', [((i + by) % size, i) for i in range(size)])  15.2 us
    all_to_all x1, blocking collectives, exchange(): return lax.all_to_all(x, GROUP, split_axis=0, concat_axis=0, tiled=True)  13.1 us
    all_to_all x2, starting transfers between devices, exchange(): return lax.all_to_all(x, GROUP, split_axis=0, concat_axis=0, tiled=True)  7.32 us
    all_to_all x2, waiting for transfers between devices, exchange(): return lax.all_to_all(x, GROUP, split_axis=0, concat_axis=0, tiled=True)  2.49 us
    ppermute x1, starting transfers between devices, local(): other = lax.ppermute(own, 'sub', [(0, 1), (1, 0)])  1.54 us
  transfers between devices with their start and end apart: 9, of which 5 were waited for; matrix products, arithmetic and copies ran while one was open for 0% of the time, Pallas kernels for 16%

profile of v9, /device:TPU:0, one launch (start us, length us, event | category | flops | bytes accessed | tf_op | source)
XLA Modules:
  0.0 76.3 jit_solution(9009158123560336872)
XLA Ops:
  0.0 1.0 %slice_bitcast_fusion.refs_2_ = bf16[1,2,64,1024]{3,2,1,0:T(8,128)(2,1)S(1)} fusion(bf16[1,2,1,128,1024]{4,3,1,2,0:T(8,128)(2,1)} %bitcast.15), kind=kLoop, calls=%fused_computation | loop fusion | bytes 524288 | tf_op jit(solution)/shard_map/reshape | solution.py:413
  1.0 3.1 %collective-permute-start = (bf16[1,2,64,1024]{3,2,1,0:T(8,128)(2,1)S(1)}, bf16[1,2,64,1024]{3,2,1,0:T(8,128)(2,1)S(1)}, u32[]{:S(2)}, u32[]{:S(2)}) collective-permute-start(bf16[1,2,64,1024]{3,2,1,0:T(8,128)(2,1)S(1)} %slice_bitcast_fusion.refs_2_), channel_id=1, source_target_pairs={{24,0},{0,8},{8,16},{16,24},{25,1},{1,9},{9,17},{17,25},{26,2},{2,... | collective-permute-start | bytes 786440 | tf_op jit(solution)/shard_map/ppermute | solution.py:31
  4.0 0.0 copy-start.2
  4.0 0.0 copy-start.3
  4.1 2.0 %first.1 = bf16[8,1,3,128,128]{4,3,2,1,0:T(8,128)(2,1)} custom-call(s32[2,8]{1,0:T(2,128)} %bitcast.12, bf16[1,2,128,1024]{3,2,1,0:T(8,128)(2,1)} %keys.1, bf16[1,2,128,1024]{3,2,1,0:T(8,128)(2,1)} %values.1), custom_call_target="tpu_custom_call" | custom-call | bytes 1572864 | tf_op jit(solution)/shard_map/first/pallas_call | solution.py:347
  6.0 3.7 %all-to-all-start = ((bf16[8,1,3,128,128]{4,3,2,1,0:T(8,128)(2,1)}), bf16[8,1,3,128,128]{4,3,2,1,0:T(8,128)(2,1)S(1)}, u32[]{:S(2)}, u32[]{:S(2)}) async-start(bf16[8,1,3,128,128]{4,3,2,1,0:T(8,128)(2,1)} %first.1), calls=%async_computation | async-start | bytes 1572864 | tf_op jit(solution)/shard_map/all_to_all | solution.py:35
  9.8 2.6 %collective-permute-done.refs_0_.refs_1_ = bf16[1,2,64,1024]{3,2,1,0:T(8,128)(2,1)S(1)} collective-permute-done((bf16[1,2,64,1024]{3,2,1,0:T(8,128)(2,1)S(1)}, bf16[1,2,64,1024]{3,2,1,0:T(8,128)(2,1)S(1)}, u32[]{:S(2)}, u32[]{:S(2)}) %collective-permute-start) | collective-permute-done | bytes 262176 | tf_op jit(solution)/shard_map/ppermute | solution.py:31
  12.4 1.7 %collective-permute-start.1 = (bf16[1,2,64,1024]{3,2,1,0:T(8,128)(2,1)S(1)}, bf16[1,2,64,1024]{3,2,1,0:T(8,128)(2,1)S(1)}, u32[]{:S(2)}, u32[]{:S(2)}) collective-permute-start(bf16[1,2,64,1024]{3,2,1,0:T(8,128)(2,1)S(1)} %slice_bitcast_fusion.refs_2_), channel_id=1, source_target_pairs={{8,0},{16,8},{24,16},{0,24},{9,1},{17,9},{25,17},{1,25},{10,2},{18... | collective-permute-start | bytes 786440 | tf_op jit(solution)/shard_map/ppermute | solution.py:31
  14.1 0.0 copy-done.2
  14.1 0.1 reshape.24
  14.2 0.0 copy-done.3
  14.2 0.1 pad_add_fusion.own
  14.3 0.0 copy-start
  14.3 0.0 copy-start.1
  14.3 1.5 %collective-permute-start.2 = (s32[34]{0:T(128)S(1)}, s32[34]{0:T(128)S(1)}, u32[]{:S(2)}, u32[]{:S(2)}) collective-permute-start(s32[34]{0:T(128)S(1)} %pad_add_fusion.own), channel_id=1, source_target_pairs={{0,4},{4,0},{1,5},{5,1},{2,6},{6,2},{3,7},{7,3},{8,12},{12,8},{9,1... | collective-permute-start | bytes 416 | tf_op jit(solution)/shard_map/ppermute | solution.py:377
  15.8 4.0 %collective-permute-done.1.refs_1_.refs_3_ = bf16[1,2,64,1024]{3,2,1,0:T(8,128)(2,1)S(1)} collective-permute-done((bf16[1,2,64,1024]{3,2,1,0:T(8,128)(2,1)S(1)}, bf16[1,2,64,1024]{3,2,1,0:T(8,128)(2,1)S(1)}, u32[]{:S(2)}, u32[]{:S(2)}) %collective-permute-start.1) | collective-permute-done | bytes 262176 | tf_op jit(solution)/shard_map/ppermute | solution.py:31
  19.9 0.0 collective-permute-done.2.other
  19.9 2.5 %all-to-all-done = bf16[8,1,3,128,128]{4,3,2,1,0:T(8,128)(2,1)S(1)} async-done(((bf16[8,1,3,128,128]{4,3,2,1,0:T(8,128)(2,1)}), bf16[8,1,3,128,128]{4,3,2,1,0:T(8,128)(2,1)S(1)}, u32[]{:S(2)}, u32[]{:S(2)}) %all-to-all-start) | async-done | bytes 786464 | tf_op jit(solution)/shard_map/all_to_all | solution.py:35
  22.4 0.8 %split.1 = (bf16[8,2,128,128]{3,2,1,0:T(8,128)(2,1)}, bf16[8,1,128,128]{3,2,1,0:T(8,128)(2,1)S(1)}) custom-call(bf16[8,3,128,128]{3,2,1,0:T(8,128)(2,1)S(1)} %bitcast.8), custom_call_target="tpu_custom_call" | custom-call | bytes 524288 | tf_op jit(solution)/shard_map/split/pallas_call | solution.py:347
  23.2 1.6 %collective-permute-start.3 = (bf16[8,2,128,128]{3,2,1,0:T(8,128)(2,1)}, bf16[8,2,128,128]{3,2,1,0:T(8,128)(2,1)S(1)}, u32[]{:S(2)}, u32[]{:S(2)}) collective-permute-start(bf16[8,2,128,128]{3,2,1,0:T(8,128)(2,1)} %get-tuple-element.21), channel_id=1, source_target_pairs={{24,0},{0,8},{8,16},{16,24},{25,1},{1,9},{9,17},{17,25},{26,2},{2,... | collective-permute-start | bytes 1572872 | tf_op jit(solution)/shard_map/ppermute | solution.py:31
  24.8 2.2 %collective-permute-start.4 = (bf16[8,2,128,128]{3,2,1,0:T(8,128)(2,1)}, bf16[8,2,128,128]{3,2,1,0:T(8,128)(2,1)}, u32[]{:S(2)}, u32[]{:S(2)}) collective-permute-start(bf16[8,2,128,128]{3,2,1,0:T(8,128)(2,1)} %get-tuple-element.21), channel_id=1, source_target_pairs={{8,0},{16,8},{24,16},{0,24},{9,1},{17,9},{25,17},{1,25},{10,2},{18... | collective-permute-start | bytes 1572872 | tf_op jit(solution)/shard_map/ppermute | solution.py:31
  27.0 0.0 copy-done
  27.0 0.0 copy-done.1
  27.0 1.7 %second.1 = bf16[8,1,5,128,128]{4,3,2,1,0:T(8,128)(2,1)} custom-call(s32[2,8]{1,0:T(2,128)S(1)} %bitcast.13, f32[8,128]{1,0:T(8,128)S(1)} %mark.3.mark_ref, bf16[1,2,128,1024]{3,2,1,0:T(8,128)(2,1)S(1)} %copy-done, bf16[1,2,64,1024]{3,2,1,0:T(8,128)(2,1)S(1)} %collective-permute-done.refs_0_.refs_1_, bf16[1,2,64,1024]{3,2,1,0:T(8,128)(2,1)S(1)} %slice_bitcast_fusion.refs_2_, ...), custom_call_target="tpu_custom_call" | custom-call | bytes 2621440 | tf_op jit(solution)/shard_map/second/pallas_call | solution.py:347
  28.7 3.6 %all-to-all-start.1 = ((bf16[8,1,5,128,128]{4,3,2,1,0:T(8,128)(2,1)}), bf16[8,1,5,128,128]{4,3,2,1,0:T(8,128)(2,1)S(1)}, u32[]{:S(2)}, u32[]{:S(2)}) async-start(bf16[8,1,5,128,128]{4,3,2,1,0:T(8,128)(2,1)} %second.1), calls=%async_computation.1 | async-start | bytes 2621440 | tf_op jit(solution)/shard_map/all_to_all | solution.py:35
  32.3 7.8 %collective-permute-done.3.refs_0_ = bf16[8,2,128,128]{3,2,1,0:T(8,128)(2,1)S(1)} collective-permute-done((bf16[8,2,128,128]{3,2,1,0:T(8,128)(2,1)}, bf16[8,2,128,128]{3,2,1,0:T(8,128)(2,1)S(1)}, u32[]{:S(2)}, u32[]{:S(2)}) %collective-permute-start.3) | collective-permute-done | bytes 524320 | tf_op jit(solution)/shard_map/ppermute | solution.py:31
  40.1 6.5 %collective-permute-start.5 = (bf16[8,1,128,128]{3,2,1,0:T(8,128)(2,1)S(1)}, bf16[8,1,128,128]{3,2,1,0:T(8,128)(2,1)S(1)}, u32[]{:S(2)}, u32[]{:S(2)}) collective-permute-start(bf16[8,1,128,128]{3,2,1,0:T(8,128)(2,1)S(1)} %get-tuple-element.26.refs_1_), channel_id=1, source_target_pairs={{24,0},{0,8},{8,16},{16,24},{25,1},{1,9},{9,17},{17,25},{26,2},{2,... | collective-permute-start | bytes 786440 | tf_op jit(solution)/shard_map/ppermute | solution.py:31
  46.6 0.0 collective-permute-start.6
  46.6 3.8 %collective-permute-done.4.refs_0_.refs_2_ = bf16[8,2,128,128]{3,2,1,0:T(8,128)(2,1)} collective-permute-done((bf16[8,2,128,128]{3,2,1,0:T(8,128)(2,1)}, bf16[8,2,128,128]{3,2,1,0:T(8,128)(2,1)}, u32[]{:S(2)}, u32[]{:S(2)}) %collective-permute-start.4) | collective-permute-done | bytes 524320 | tf_op jit(solution)/shard_map/ppermute | solution.py:31
  50.4 0.0 all-to-all-done.1
  50.4 8.8 %core.1 = (bf16[8,1,128,128]{3,2,1,0:T(8,128)(2,1)S(1)}, bf16[8,256,1152]{2,1,0:T(8,128)(2,1)S(1)}) custom-call(s32[34]{0:T(128)S(1)} %pad_add_fusion.own, s32[34]{0:T(128)S(1)} %collective-permute-done.2.other, bf16[8,5,128,128]{3,2,1,0:T(8,128)(2,1)S(1)} %bitcast.11, bf16[8,2,128,128]{3,2,1,0:T(8,128)(2,1)S(1)} %collective-permute-done.3.refs_0_, ...), custom_call_target="tpu_custom_call" | custom-call | flops 905969664 | bytes 1048576 | tf_op jit(solution)/shard_map/core/pallas_call | solution.py:347
  59.3 0.0 collective-permute-done.5.refs_0_
  59.3 0.0 collective-permute-done.6.refs_2_
  59.3 3.1 %weigh.1 = bf16[8,2,128,128]{3,2,1,0:T(8,128)(2,1)S(1)} custom-call(s32[34]{0:T(128)S(1)} %pad_add_fusion.own, s32[34]{0:T(128)S(1)} %collective-permute-done.2.other, s32[2,8]{1,0:T(2,128)S(1)} %bitcast.14, bf16[8,256,1152]{2,1,0:T(8,128)(2,1)S(1)} %get-tuple-element.24.expo, bf16[8,1,128,128]{3,2,1,0:T(8,128)(2,1)S(1)} %get-tuple-element.25.done, ...), custom_call_target="tpu_custom_call" | custom-call | flops 301989888 | bytes 1048576 | tf_op jit(solution)/shard_map/weigh/pallas_call | solution.py:347
  62.4 13.1 %all_to_all.15.x = bf16[8,1,2,128,128]{4,3,2,1,0:T(8,128)(2,1)S(1)} all-to-all(bf16[8,1,2,128,128]{4,3,2,1,0:T(8,128)(2,1)S(1)} %bitcast.10), channel_id=1, replica_groups=mesh['plane'=4,'sub'=2,'tok'=4] {'sub','tok'}, dimensions={0} | all-to-all | bytes 1048576 | tf_op jit(solution)/shard_map/all_to_all | solution.py:35
  75.5 0.8 %last.1 = bf16[1,2,128,1024]{3,2,1,0:T(8,128)(2,1)} custom-call(bf16[8,1,2,128,128]{4,3,2,1,0:T(8,128)(2,1)S(1)} %all_to_all.15.x), custom_call_target="tpu_custom_call" | custom-call | bytes 1048576 | tf_op jit(solution)/shard_map/last/pallas_call | solution.py:347
  (3 shorter events, 0.0 us)
Async XLA Ops:
  1.0 11.4 %collective-permute-start = (bf16[1,2,64,1024]{3,2,1,0:T(8,128)(2,1)S(1)}, bf16[1,2,64,1024]{3,2,1,0:T(8,128)(2,1)S(1)}, u32[]{:S(2)}, u32[]{:S(2)}) collective-permute-start(bf16[1,2,64,1024]{3,2,1,0:T(8,128)(2,1)S(1)} %slice_bitcast_fusion.refs_2_), channel_id=1, source_target_pairs={{24,0},{0,8},{8,16},{16,24},{25,1},{1,9},{9,17},{17,25},{26,2},{2,... | collective-permute-start | bytes 786440 | tf_op jit(solution)/shard_map/ppermute | solution.py:31
  4.0 10.1 %copy-start.2 = (s32[1,2,4,4]{3,2,1,0:T(4,128)S(1)}, s32[1,2,4,4]{3,2,1,0:T(4,128)}, u32[]{:S(2)}) copy-start(s32[1,2,4,4]{3,2,1,0:T(4,128)} %param.9) | copy-start | bytes 388
  4.0 10.2 %copy-start.3 = (s32[1,2]{1,0:T(1,128)S(1)}, s32[1,2]{1,0:T(1,128)}, u32[]{:S(2)}) copy-start(s32[1,2]{1,0:T(1,128)} %param.10) | copy-start | bytes 28
  6.0 16.3 %all-to-all-start = ((bf16[8,1,3,128,128]{4,3,2,1,0:T(8,128)(2,1)}), bf16[8,1,3,128,128]{4,3,2,1,0:T(8,128)(2,1)S(1)}, u32[]{:S(2)}, u32[]{:S(2)}) async-start(bf16[8,1,3,128,128]{4,3,2,1,0:T(8,128)(2,1)} %first.1), calls=%async_computation | async-start | bytes 1572864 | tf_op jit(solution)/shard_map/all_to_all | solution.py:35
  12.4 7.5 %collective-permute-start.1 = (bf16[1,2,64,1024]{3,2,1,0:T(8,128)(2,1)S(1)}, bf16[1,2,64,1024]{3,2,1,0:T(8,128)(2,1)S(1)}, u32[]{:S(2)}, u32[]{:S(2)}) collective-permute-start(bf16[1,2,64,1024]{3,2,1,0:T(8,128)(2,1)S(1)} %slice_bitcast_fusion.refs_2_), channel_id=1, source_target_pairs={{8,0},{16,8},{24,16},{0,24},{9,1},{17,9},{25,17},{1,25},{10,2},{18... | collective-permute-start | bytes 786440 | tf_op jit(solution)/shard_map/ppermute | solution.py:31
  14.3 12.7 %copy-start = (bf16[1,2,128,1024]{3,2,1,0:T(8,128)(2,1)S(1)}, bf16[1,2,128,1024]{3,2,1,0:T(8,128)(2,1)}, u32[]{:S(2)}) copy-start(bf16[1,2,128,1024]{3,2,1,0:T(8,128)(2,1)} %refs_0_.1) | copy-start | bytes 1572868
  14.3 12.7 %copy-start.1 = (s32[8,2]{0,1:T(2,128)S(1)}, s32[8,2]{0,1:T(2,128)}, u32[]{:S(2)}) copy-start(s32[8,2]{0,1:T(2,128)} %param.11) | copy-start | bytes 196
  14.3 5.6 %collective-permute-start.2 = (s32[34]{0:T(128)S(1)}, s32[34]{0:T(128)S(1)}, u32[]{:S(2)}, u32[]{:S(2)}) collective-permute-start(s32[34]{0:T(128)S(1)} %pad_add_fusion.own), channel_id=1, source_target_pairs={{0,4},{4,0},{1,5},{5,1},{2,6},{6,2},{3,7},{7,3},{8,12},{12,8},{9,1... | collective-permute-start | bytes 416 | tf_op jit(solution)/shard_map/ppermute | solution.py:377
  23.2 16.9 %collective-permute-start.3 = (bf16[8,2,128,128]{3,2,1,0:T(8,128)(2,1)}, bf16[8,2,128,128]{3,2,1,0:T(8,128)(2,1)S(1)}, u32[]{:S(2)}, u32[]{:S(2)}) collective-permute-start(bf16[8,2,128,128]{3,2,1,0:T(8,128)(2,1)} %get-tuple-element.21), channel_id=1, source_target_pairs={{24,0},{0,8},{8,16},{16,24},{25,1},{1,9},{9,17},{17,25},{26,2},{2,... | collective-permute-start | bytes 1572872 | tf_op jit(solution)/shard_map/ppermute | solution.py:31
  24.8 25.7 %collective-permute-start.4 = (bf16[8,2,128,128]{3,2,1,0:T(8,128)(2,1)}, bf16[8,2,128,128]{3,2,1,0:T(8,128)(2,1)}, u32[]{:S(2)}, u32[]{:S(2)}) collective-permute-start(bf16[8,2,128,128]{3,2,1,0:T(8,128)(2,1)} %get-tuple-element.21), channel_id=1, source_target_pairs={{8,0},{16,8},{24,16},{0,24},{9,1},{17,9},{25,17},{1,25},{10,2},{18... | collective-permute-start | bytes 1572872 | tf_op jit(solution)/shard_map/ppermute | solution.py:31
  28.7 21.7 %all-to-all-start.1 = ((bf16[8,1,5,128,128]{4,3,2,1,0:T(8,128)(2,1)}), bf16[8,1,5,128,128]{4,3,2,1,0:T(8,128)(2,1)S(1)}, u32[]{:S(2)}, u32[]{:S(2)}) async-start(bf16[8,1,5,128,128]{4,3,2,1,0:T(8,128)(2,1)} %second.1), calls=%async_computation.1 | async-start | bytes 2621440 | tf_op jit(solution)/shard_map/all_to_all | solution.py:35
  40.1 19.2 %collective-permute-start.5 = (bf16[8,1,128,128]{3,2,1,0:T(8,128)(2,1)S(1)}, bf16[8,1,128,128]{3,2,1,0:T(8,128)(2,1)S(1)}, u32[]{:S(2)}, u32[]{:S(2)}) collective-permute-start(bf16[8,1,128,128]{3,2,1,0:T(8,128)(2,1)S(1)} %get-tuple-element.26.refs_1_), channel_id=1, source_target_pairs={{24,0},{0,8},{8,16},{16,24},{25,1},{1,9},{9,17},{17,25},{26,2},{2,... | collective-permute-start | bytes 786440 | tf_op jit(solution)/shard_map/ppermute | solution.py:31
  46.6 12.7 %collective-permute-start.6 = (bf16[8,1,128,128]{3,2,1,0:T(8,128)(2,1)S(1)}, bf16[8,1,128,128]{3,2,1,0:T(8,128)(2,1)S(1)}, u32[]{:S(2)}, u32[]{:S(2)}) collective-permute-start(bf16[8,1,128,128]{3,2,1,0:T(8,128)(2,1)S(1)} %get-tuple-element.26.refs_1_), channel_id=1, source_target_pairs={{8,0},{16,8},{24,16},{0,24},{9,1},{17,9},{25,17},{1,25},{10,2},{18... | collective-permute-start | bytes 786440 | tf_op jit(solution)/shard_map/ppermute | solution.py:31

commit v10 on v9

--- a/solution.py
+++ b/solution.py
@@ -291,19 +291,11 @@
         for i, part in enumerate(expo_of(1, g, t, k)):
             expo_ref[g * plan.kt + t, :, i * TILE:(i + 1) * TILE] = part
 
-    def wait_both(g):
-        wait(0, g)
-        wait(1, g)
-
-    def prepare(g):
-        v = [with_ones(far_rows(plan, v_far, g, j)) for j in range(NB)]
-        return (keys(0, g), v), keys(1, g)
-
-    def both(g, t, ready):
-        attended(g, t, ready[0])
-        scored(g, t, ready[1])
-
-    each_view(plan, wait_both, both, prepare)
+    each_view(
+        plan, functools.partial(wait, 0), attended,
+        lambda g: (keys(0, g), [with_ones(far_rows(plan, v_far, g, j)) for j in range(NB)]),
+    )
+    each_view(plan, functools.partial(wait, 1), scored, functools.partial(keys, 1))
 
 
 def weigh_kernel(plan, own, other, slots, expo, done, *refs):
@@ -450,7 +442,6 @@
         "second", [queries, *[raw[d] for d in order]], moves, 2 + plan.planes, mark=arrived
     )
     mixed = spread(packed)
-    planes[0] = early
     planes = [planes[d] for d in order]
     late = [late[d] for d in order]
 
@@ -462,7 +453,7 @@
     expo = jax.ShapeDtypeStruct((sub * kt, plan.rows, plan.cols), dtype)
     out0, expo = call(
         functools.partial(core_kernel, plan), "core", (result(1), expo),
-        [SMEM] * 2 + [VMEM] * (1 + plan.planes) + [ANY] * 2, (VMEM, VMEM),
+        [SMEM] * 2 + [VMEM] + [ANY if d else VMEM for d in order] + [ANY] * 2, (VMEM, VMEM),
         [pltpu.VMEM((2, *far), dtype), pltpu.VMEM(far, dtype), sems((2, 2, sub, NB)),
          sems((sub, NB))],
         (*facts, mixed, *planes, leads, brought), flops=plan.pairs * HD * 6,

time: 76.7 us -> 75.7 us (0.987)
  Pallas kernels: 17.2 us -> 16.3 us
    pallas_call x9, Pallas kernels: 17.2 us -> 16.3 us  [call(): pl.pallas_call(kernel, out_shape=out_shape, in_specs=in_specs, out_specs=...]
  transfers between devices with their start and end apart: 9 -> 9, of which waited for: 5 -> 6; matrix products, arithmetic and copies ran while one was open for 0% -> 0% of each run, Pallas kernels for 16% -> 16%
where the time goes in v10:
time: 75.7 us; the launch traced here: 75.3 us
  starting transfers between devices  23.6 us (31%)
  waiting for transfers between devices  21.2 us (28%)
  Pallas kernels  16.3 us (22%)
  blocking collectives  13 us (17%)
  local copies, waits for them, and re-layouts  1.07 us (1%)
    ppermute x6, waiting for transfers between devices, from_plane(): return lax.ppermute(x, 'plane', [((i + by) % size, i) for i in range(size)])  18.5 us
    pallas_call x9, Pallas kernels, call(): pl.pallas_call(kernel, out_shape=out_shape, in_specs=in_specs, out_specs=...  16.3 us
    ppermute x6, starting transfers between devices, from_plane(): return lax.ppermute(x, 'plane', [((i + by) % size, i) for i in range(size)])  14.8 us
    all_to_all x1, blocking collectives, exchange(): return lax.all_to_all(x, GROUP, split_axis=0, concat_axis=0, tiled=True)  13 us
    all_to_all x2, starting transfers between devices, exchange(): return lax.all_to_all(x, GROUP, split_axis=0, concat_axis=0, tiled=True)  7.31 us
    all_to_all x2, waiting for transfers between devices, exchange(): return lax.all_to_all(x, GROUP, split_axis=0, concat_axis=0, tiled=True)  2.7 us
    ppermute x1, starting transfers between devices, local(): other = lax.ppermute(own, 'sub', [(0, 1), (1, 0)])  1.54 us
  transfers between devices with their start and end apart: 9, of which 6 were waited for; matrix products, arithmetic and copies ran while one was open for 0% of the time, Pallas kernels for 16%

profile of v10, /device:TPU:0, one launch (start us, length us, event | category | flops | bytes accessed | tf_op | source)
XLA Modules:
  0.0 75.3 jit_solution(15169335447458618812)
XLA Ops:
  0.0 1.0 %slice_bitcast_fusion.refs_2_ = bf16[1,2,64,1024]{3,2,1,0:T(8,128)(2,1)S(1)} fusion(bf16[1,2,1,128,1024]{4,3,1,2,0:T(8,128)(2,1)} %bitcast.14), kind=kLoop, calls=%fused_computation | loop fusion | bytes 524288 | tf_op jit(solution)/shard_map/reshape | solution.py:405
  1.0 3.1 %collective-permute-start = (bf16[1,2,64,1024]{3,2,1,0:T(8,128)(2,1)S(1)}, bf16[1,2,64,1024]{3,2,1,0:T(8,128)(2,1)S(1)}, u32[]{:S(2)}, u32[]{:S(2)}) collective-permute-start(bf16[1,2,64,1024]{3,2,1,0:T(8,128)(2,1)S(1)} %slice_bitcast_fusion.refs_2_), channel_id=1, source_target_pairs={{24,0},{0,8},{8,16},{16,24},{25,1},{1,9},{9,17},{17,25},{26,2},{2,... | collective-permute-start | bytes 786440 | tf_op jit(solution)/shard_map/ppermute | solution.py:31
  4.0 0.0 copy-start.2
  4.0 0.0 copy-start.3
  4.1 2.0 %first.1 = bf16[8,1,3,128,128]{4,3,2,1,0:T(8,128)(2,1)} custom-call(s32[2,8]{1,0:T(2,128)} %bitcast.11, bf16[1,2,128,1024]{3,2,1,0:T(8,128)(2,1)} %keys.1, bf16[1,2,128,1024]{3,2,1,0:T(8,128)(2,1)} %values.1), custom_call_target="tpu_custom_call" | custom-call | bytes 1572864 | tf_op jit(solution)/shard_map/first/pallas_call | solution.py:339
  6.0 3.7 %all-to-all-start = ((bf16[8,1,3,128,128]{4,3,2,1,0:T(8,128)(2,1)}), bf16[8,1,3,128,128]{4,3,2,1,0:T(8,128)(2,1)S(1)}, u32[]{:S(2)}, u32[]{:S(2)}) async-start(bf16[8,1,3,128,128]{4,3,2,1,0:T(8,128)(2,1)} %first.1), calls=%async_computation | async-start | bytes 1572864 | tf_op jit(solution)/shard_map/all_to_all | solution.py:35
  9.8 2.6 %collective-permute-done.refs_0_.refs_1_ = bf16[1,2,64,1024]{3,2,1,0:T(8,128)(2,1)S(1)} collective-permute-done((bf16[1,2,64,1024]{3,2,1,0:T(8,128)(2,1)S(1)}, bf16[1,2,64,1024]{3,2,1,0:T(8,128)(2,1)S(1)}, u32[]{:S(2)}, u32[]{:S(2)}) %collective-permute-start) | collective-permute-done | bytes 262176 | tf_op jit(solution)/shard_map/ppermute | solution.py:31
  12.4 1.7 %collective-permute-start.1 = (bf16[1,2,64,1024]{3,2,1,0:T(8,128)(2,1)S(1)}, bf16[1,2,64,1024]{3,2,1,0:T(8,128)(2,1)S(1)}, u32[]{:S(2)}, u32[]{:S(2)}) collective-permute-start(bf16[1,2,64,1024]{3,2,1,0:T(8,128)(2,1)S(1)} %slice_bitcast_fusion.refs_2_), channel_id=1, source_target_pairs={{8,0},{16,8},{24,16},{0,24},{9,1},{17,9},{25,17},{1,25},{10,2},{18... | collective-permute-start | bytes 786440 | tf_op jit(solution)/shard_map/ppermute | solution.py:31
  14.1 0.0 copy-done.2
  14.1 0.1 reshape.24
  14.2 0.0 copy-done.3
  14.2 0.1 pad_add_fusion.own
  14.3 0.0 copy-start
  14.3 0.0 copy-start.1
  14.3 1.5 %collective-permute-start.2 = (s32[34]{0:T(128)S(1)}, s32[34]{0:T(128)S(1)}, u32[]{:S(2)}, u32[]{:S(2)}) collective-permute-start(s32[34]{0:T(128)S(1)} %pad_add_fusion.own), channel_id=1, source_target_pairs={{0,4},{4,0},{1,5},{5,1},{2,6},{6,2},{3,7},{7,3},{8,12},{12,8},{9,1... | collective-permute-start | bytes 416 | tf_op jit(solution)/shard_map/ppermute | solution.py:369
  15.8 4.0 %collective-permute-done.1.refs_1_.refs_3_ = bf16[1,2,64,1024]{3,2,1,0:T(8,128)(2,1)S(1)} collective-permute-done((bf16[1,2,64,1024]{3,2,1,0:T(8,128)(2,1)S(1)}, bf16[1,2,64,1024]{3,2,1,0:T(8,128)(2,1)S(1)}, u32[]{:S(2)}, u32[]{:S(2)}) %collective-permute-start.1) | collective-permute-done | bytes 262176 | tf_op jit(solution)/shard_map/ppermute | solution.py:31
  19.9 0.0 collective-permute-done.2.other
  19.9 2.5 %all-to-all-done = bf16[8,1,3,128,128]{4,3,2,1,0:T(8,128)(2,1)S(1)} async-done(((bf16[8,1,3,128,128]{4,3,2,1,0:T(8,128)(2,1)}), bf16[8,1,3,128,128]{4,3,2,1,0:T(8,128)(2,1)S(1)}, u32[]{:S(2)}, u32[]{:S(2)}) %all-to-all-start) | async-done | bytes 786464 | tf_op jit(solution)/shard_map/all_to_all | solution.py:35
  22.4 0.1 split.1
  22.4 1.6 %collective-permute-start.3 = (bf16[8,2,128,128]{3,2,1,0:T(8,128)(2,1)S(1)}, bf16[8,2,128,128]{3,2,1,0:T(8,128)(2,1)}, u32[]{:S(2)}, u32[]{:S(2)}) collective-permute-start(bf16[8,2,128,128]{3,2,1,0:T(8,128)(2,1)S(1)} %get-tuple-element.21.refs_1_), channel_id=1, source_target_pairs={{24,0},{0,8},{8,16},{16,24},{25,1},{1,9},{9,17},{17,25},{26,2},{2,... | collective-permute-start | bytes 1572872 | tf_op jit(solution)/shard_map/ppermute | solution.py:31
  24.0 2.2 %collective-permute-start.4 = (bf16[8,2,128,128]{3,2,1,0:T(8,128)(2,1)S(1)}, bf16[8,2,128,128]{3,2,1,0:T(8,128)(2,1)}, u32[]{:S(2)}, u32[]{:S(2)}) collective-permute-start(bf16[8,2,128,128]{3,2,1,0:T(8,128)(2,1)S(1)} %get-tuple-element.21.refs_1_), channel_id=1, source_target_pairs={{8,0},{16,8},{24,16},{0,24},{9,1},{17,9},{25,17},{1,25},{10,2},{18... | collective-permute-start | bytes 1572872 | tf_op jit(solution)/shard_map/ppermute | solution.py:31
  26.3 0.0 copy-done
  26.3 0.0 copy-done.1
  26.3 1.7 %second.1 = bf16[8,1,5,128,128]{4,3,2,1,0:T(8,128)(2,1)} custom-call(s32[2,8]{1,0:T(2,128)S(1)} %bitcast.12, f32[8,128]{1,0:T(8,128)S(1)} %mark.3.mark_ref, bf16[1,2,128,1024]{3,2,1,0:T(8,128)(2,1)S(1)} %copy-done, bf16[1,2,64,1024]{3,2,1,0:T(8,128)(2,1)S(1)} %collective-permute-done.refs_0_.refs_1_, bf16[1,2,64,1024]{3,2,1,0:T(8,128)(2,1)S(1)} %slice_bitcast_fusion.refs_2_, ...), custom_call_target="tpu_custom_call" | custom-call | bytes 2621440 | tf_op jit(solution)/shard_map/second/pallas_call | solution.py:339
  28.0 3.6 %all-to-all-start.1 = ((bf16[8,1,5,128,128]{4,3,2,1,0:T(8,128)(2,1)}), bf16[8,1,5,128,128]{4,3,2,1,0:T(8,128)(2,1)S(1)}, u32[]{:S(2)}, u32[]{:S(2)}) async-start(bf16[8,1,5,128,128]{4,3,2,1,0:T(8,128)(2,1)} %second.1), calls=%async_computation.1 | async-start | bytes 2621440 | tf_op jit(solution)/shard_map/all_to_all | solution.py:35
  31.6 7.7 %collective-permute-done.3.refs_0_ = bf16[8,2,128,128]{3,2,1,0:T(8,128)(2,1)} collective-permute-done((bf16[8,2,128,128]{3,2,1,0:T(8,128)(2,1)S(1)}, bf16[8,2,128,128]{3,2,1,0:T(8,128)(2,1)}, u32[]{:S(2)}, u32[]{:S(2)}) %collective-permute-start.3) | collective-permute-done | bytes 524320 | tf_op jit(solution)/shard_map/ppermute | solution.py:31
  39.2 6.1 %collective-permute-start.5 = (bf16[8,1,128,128]{3,2,1,0:T(8,128)(2,1)S(1)}, bf16[8,1,128,128]{3,2,1,0:T(8,128)(2,1)S(1)}, u32[]{:S(2)}, u32[]{:S(2)}) collective-permute-start(bf16[8,1,128,128]{3,2,1,0:T(8,128)(2,1)S(1)} %get-tuple-element.26.refs_1_), channel_id=1, source_target_pairs={{24,0},{0,8},{8,16},{16,24},{25,1},{1,9},{9,17},{17,25},{26,2},{2,... | collective-permute-start | bytes 786440 | tf_op jit(solution)/shard_map/ppermute | solution.py:31
  45.3 0.0 collective-permute-start.6
  45.3 4.2 %collective-permute-done.4.refs_0_.refs_2_ = bf16[8,2,128,128]{3,2,1,0:T(8,128)(2,1)} collective-permute-done((bf16[8,2,128,128]{3,2,1,0:T(8,128)(2,1)S(1)}, bf16[8,2,128,128]{3,2,1,0:T(8,128)(2,1)}, u32[]{:S(2)}, u32[]{:S(2)}) %collective-permute-start.4) | collective-permute-done | bytes 524320 | tf_op jit(solution)/shard_map/ppermute | solution.py:31
  49.5 0.2 all-to-all-done.1
  49.7 8.7 %core.1 = (bf16[8,1,128,128]{3,2,1,0:T(8,128)(2,1)S(1)}, bf16[8,256,1152]{2,1,0:T(8,128)(2,1)S(1)}) custom-call(s32[34]{0:T(128)S(1)} %pad_add_fusion.own, s32[34]{0:T(128)S(1)} %collective-permute-done.2.other, bf16[8,5,128,128]{3,2,1,0:T(8,128)(2,1)S(1)} %bitcast.10, bf16[8,2,128,128]{3,2,1,0:T(8,128)(2,1)} %collective-permute-done.3.refs_0_, ...), custom_call_target="tpu_custom_call" | custom-call | flops 905969664 | bytes 1048576 | tf_op jit(solution)/shard_map/core/pallas_call | solution.py:339
  58.4 0.0 collective-permute-done.5.refs_0_
  58.4 0.0 collective-permute-done.6.refs_2_
  58.5 3.1 %weigh.1 = bf16[8,2,128,128]{3,2,1,0:T(8,128)(2,1)S(1)} custom-call(s32[34]{0:T(128)S(1)} %pad_add_fusion.own, s32[34]{0:T(128)S(1)} %collective-permute-done.2.other, s32[2,8]{1,0:T(2,128)S(1)} %bitcast.13, bf16[8,256,1152]{2,1,0:T(8,128)(2,1)S(1)} %get-tuple-element.24.expo, bf16[8,1,128,128]{3,2,1,0:T(8,128)(2,1)S(1)} %get-tuple-element.25.done, ...), custom_call_target="tpu_custom_call" | custom-call | flops 301989888 | bytes 1048576 | tf_op jit(solution)/shard_map/weigh/pallas_call | solution.py:339
  61.6 13.0 %all_to_all.15.x = bf16[8,1,2,128,128]{4,3,2,1,0:T(8,128)(2,1)S(1)} all-to-all(bf16[8,1,2,128,128]{4,3,2,1,0:T(8,128)(2,1)S(1)} %bitcast.9), channel_id=1, replica_groups=mesh['plane'=4,'sub'=2,'tok'=4] {'sub','tok'}, dimensions={0} | all-to-all | bytes 1048576 | tf_op jit(solution)/shard_map/all_to_all | solution.py:35
  74.6 0.8 %last.1 = bf16[1,2,128,1024]{3,2,1,0:T(8,128)(2,1)} custom-call(bf16[8,1,2,128,128]{4,3,2,1,0:T(8,128)(2,1)S(1)} %all_to_all.15.x), custom_call_target="tpu_custom_call" | custom-call | bytes 1048576 | tf_op jit(solution)/shard_map/last/pallas_call | solution.py:339
  (3 shorter events, 0.0 us)
Async XLA Ops:
  1.0 11.4 %collective-permute-start = (bf16[1,2,64,1024]{3,2,1,0:T(8,128)(2,1)S(1)}, bf16[1,2,64,1024]{3,2,1,0:T(8,128)(2,1)S(1)}, u32[]{:S(2)}, u32[]{:S(2)}) collective-permute-start(bf16[1,2,64,1024]{3,2,1,0:T(8,128)(2,1)S(1)} %slice_bitcast_fusion.refs_2_), channel_id=1, source_target_pairs={{24,0},{0,8},{8,16},{16,24},{25,1},{1,9},{9,17},{17,25},{26,2},{2,... | collective-permute-start | bytes 786440 | tf_op jit(solution)/shard_map/ppermute | solution.py:31
  4.0 10.1 %copy-start.2 = (s32[1,2,4,4]{3,2,1,0:T(4,128)S(1)}, s32[1,2,4,4]{3,2,1,0:T(4,128)}, u32[]{:S(2)}) copy-start(s32[1,2,4,4]{3,2,1,0:T(4,128)} %param.9) | copy-start | bytes 388
  4.0 10.2 %copy-start.3 = (s32[1,2]{1,0:T(1,128)S(1)}, s32[1,2]{1,0:T(1,128)}, u32[]{:S(2)}) copy-start(s32[1,2]{1,0:T(1,128)} %param.10) | copy-start | bytes 28
  6.0 16.3 %all-to-all-start = ((bf16[8,1,3,128,128]{4,3,2,1,0:T(8,128)(2,1)}), bf16[8,1,3,128,128]{4,3,2,1,0:T(8,128)(2,1)S(1)}, u32[]{:S(2)}, u32[]{:S(2)}) async-start(bf16[8,1,3,128,128]{4,3,2,1,0:T(8,128)(2,1)} %first.1), calls=%async_computation | async-start | bytes 1572864 | tf_op jit(solution)/shard_map/all_to_all | solution.py:35
  12.4 7.5 %collective-permute-start.1 = (bf16[1,2,64,1024]{3,2,1,0:T(8,128)(2,1)S(1)}, bf16[1,2,64,1024]{3,2,1,0:T(8,128)(2,1)S(1)}, u32[]{:S(2)}, u32[]{:S(2)}) collective-permute-start(bf16[1,2,64,1024]{3,2,1,0:T(8,128)(2,1)S(1)} %slice_bitcast_fusion.refs_2_), channel_id=1, source_target_pairs={{8,0},{16,8},{24,16},{0,24},{9,1},{17,9},{25,17},{1,25},{10,2},{18... | collective-permute-start | bytes 786440 | tf_op jit(solution)/shard_map/ppermute | solution.py:31
  14.3 12.0 %copy-start = (bf16[1,2,128,1024]{3,2,1,0:T(8,128)(2,1)S(1)}, bf16[1,2,128,1024]{3,2,1,0:T(8,128)(2,1)}, u32[]{:S(2)}) copy-start(bf16[1,2,128,1024]{3,2,1,0:T(8,128)(2,1)} %refs_0_.1) | copy-start | bytes 1572868
  14.3 12.0 %copy-start.1 = (s32[8,2]{0,1:T(2,128)S(1)}, s32[8,2]{0,1:T(2,128)}, u32[]{:S(2)}) copy-start(s32[8,2]{0,1:T(2,128)} %param.11) | copy-start | bytes 196
  14.3 5.6 %collective-permute-start.2 = (s32[34]{0:T(128)S(1)}, s32[34]{0:T(128)S(1)}, u32[]{:S(2)}, u32[]{:S(2)}) collective-permute-start(s32[34]{0:T(128)S(1)} %pad_add_fusion.own), channel_id=1, source_target_pairs={{0,4},{4,0},{1,5},{5,1},{2,6},{6,2},{3,7},{7,3},{8,12},{12,8},{9,1... | collective-permute-start | bytes 416 | tf_op jit(solution)/shard_map/ppermute | solution.py:369
  22.4 16.8 %collective-permute-start.3 = (bf16[8,2,128,128]{3,2,1,0:T(8,128)(2,1)S(1)}, bf16[8,2,128,128]{3,2,1,0:T(8,128)(2,1)}, u32[]{:S(2)}, u32[]{:S(2)}) collective-permute-start(bf16[8,2,128,128]{3,2,1,0:T(8,128)(2,1)S(1)} %get-tuple-element.21.refs_1_), channel_id=1, source_target_pairs={{24,0},{0,8},{8,16},{16,24},{25,1},{1,9},{9,17},{17,25},{26,2},{2,... | collective-permute-start | bytes 1572872 | tf_op jit(solution)/shard_map/ppermute | solution.py:31
  24.0 25.4 %collective-permute-start.4 = (bf16[8,2,128,128]{3,2,1,0:T(8,128)(2,1)S(1)}, bf16[8,2,128,128]{3,2,1,0:T(8,128)(2,1)}, u32[]{:S(2)}, u32[]{:S(2)}) collective-permute-start(bf16[8,2,128,128]{3,2,1,0:T(8,128)(2,1)S(1)} %get-tuple-element.21.refs_1_), channel_id=1, source_target_pairs={{8,0},{16,8},{24,16},{0,24},{9,1},{17,9},{25,17},{1,25},{10,2},{18... | collective-permute-start | bytes 1572872 | tf_op jit(solution)/shard_map/ppermute | solution.py:31
  28.0 21.7 %all-to-all-start.1 = ((bf16[8,1,5,128,128]{4,3,2,1,0:T(8,128)(2,1)}), bf16[8,1,5,128,128]{4,3,2,1,0:T(8,128)(2,1)S(1)}, u32[]{:S(2)}, u32[]{:S(2)}) async-start(bf16[8,1,5,128,128]{4,3,2,1,0:T(8,128)(2,1)} %second.1), calls=%async_computation.1 | async-start | bytes 2621440 | tf_op jit(solution)/shard_map/all_to_all | solution.py:35
  39.2 19.2 %collective-permute-start.5 = (bf16[8,1,128,128]{3,2,1,0:T(8,128)(2,1)S(1)}, bf16[8,1,128,128]{3,2,1,0:T(8,128)(2,1)S(1)}, u32[]{:S(2)}, u32[]{:S(2)}) collective-permute-start(bf16[8,1,128,128]{3,2,1,0:T(8,128)(2,1)S(1)} %get-tuple-element.26.refs_1_), channel_id=1, source_target_pairs={{24,0},{0,8},{8,16},{16,24},{25,1},{1,9},{9,17},{17,25},{26,2},{2,... | collective-permute-start | bytes 786440 | tf_op jit(solution)/shard_map/ppermute | solution.py:31
  45.3 13.2 %collective-permute-start.6 = (bf16[8,1,128,128]{3,2,1,0:T(8,128)(2,1)S(1)}, bf16[8,1,128,128]{3,2,1,0:T(8,128)(2,1)S(1)}, u32[]{:S(2)}, u32[]{:S(2)}) collective-permute-start(bf16[8,1,128,128]{3,2,1,0:T(8,128)(2,1)S(1)} %get-tuple-element.26.refs_1_), channel_id=1, source_target_pairs={{8,0},{16,8},{24,16},{0,24},{9,1},{17,9},{25,17},{1,25},{10,2},{18... | collective-permute-start | bytes 786440 | tf_op jit(solution)/shard_map/ppermute | solution.py:31

commit v11 on v10

--- a/solution.py
+++ b/solution.py
@@ -111,6 +111,19 @@
     pltpu.make_async_copy(out, out, sem).wait()
 
 
+def raw_kernel(keys, out, sem):
+    half = TILE // 2
+    for s in range(2):
+        for m in range(keys.shape[2] // TILE):
+            for i in range(2):
+                rows = half // 2
+                pltpu.make_async_copy(
+                    keys.at[0, s, pl.ds(m * TILE + i * rows, rows)],
+                    out.at[0, s, pl.ds(m * half + i * rows, rows)], sem,
+                ).start()
+    pltpu.make_async_copy(out, out, sem).wait()
+
+
 def split_kernel(x, head, tail):
     pieces = head.shape[1]
     head[...] = x[:, :pieces]
@@ -245,17 +258,19 @@
     low, high = pl.ds(0, half), pl.ds(half, half)
     mine = [pl.ds(b * half, half) for b in range(2)]
 
-    def far_copies(g, j, d, tiles_at):
+    def far_copies(b, g, j, d, tiles_at):
         tiles = pl.ds(tiles_at, plan.kt)
-        found = []
-        for b in range(2):
-            found.append((mixed.at[tiles, 2 + d, mine[b]], k_far.at[b, g, j, :, low], k_sem.at[0, b, g, j]))
-            found.append((planes[d].at[tiles, 0, mine[b]], k_far.at[b, g, j, :, high], k_sem.at[1, b, g, j]))
-            if b == 0:
-                found.append((planes[d].at[tiles, 1], v_far.at[g, j], v_sem.at[g, j]))
+        to, sem = k_far.at[b, g, j], k_sem.at[:, b, g, j]
+        found = [
+            (mixed.at[tiles, 2 + d, mine[b]], to.at[:, low], sem.at[0]),
+            (planes[d].at[tiles, 0, mine[b]], to.at[:, high], sem.at[1]),
+        ]
+        if b == 0:
+            found.append((planes[d].at[tiles, 1], v_far.at[g, j], v_sem.at[g, j]))
         return [pltpu.make_async_copy(*copy) for copy in found]
 
-    start_far(plan, facts, far_copies)
+    for b in range(2):
+        start_far(plan, facts, functools.partial(far_copies, b))
 
     def wait(b, g):
         for j in range(NB):
@@ -402,7 +417,10 @@
             [ANY] * len(arrays), VMEM, [], arrays, flops=flops, mib=1,
         )
 
-    raw = keys.reshape(1, 2, tiles, TILE, width)[:, :, :, :half].reshape(1, 2, tiles * half, width)
+    raw = call(
+        raw_kernel, "raw", jax.ShapeDtypeStruct((1, 2, tiles * half, width), dtype), [ANY], ANY,
+        [sem], (keys,), moved=size, mib=1,
+    )
     raw = around(raw, chain=True)
     if plan.whole_lanes:
         packed = call(

time: 75.7 us -> 76.1 us (level)
    unnamed x8 -> x10, local copies, waits for them, and re-layouts: 0.01 us -> 1.06 us
    reshape x1 -> x0, local copies, waits for them, and re-layouts: 0.97 us -> none  [local(): keys.reshape(1, 2, tiles, TILE, width)[:, :, :, :half]]
    pallas_call x9 -> x10, Pallas kernels: 16.3 us -> 16.5 us  [call(): pl.pallas_call(kernel, out_shape=out_shape, in_specs=in_specs, out_specs=...]
where the time goes in v11:
time: 76.1 us; the launch traced here: 75.7 us
  starting transfers between devices  23.6 us (31%)
  waiting for transfers between devices  21.3 us (28%)
  Pallas kernels  16.5 us (22%)
  blocking collectives  13.1 us (17%)
  local copies, waits for them, and re-layouts  1.14 us (1%)
    ppermute x6, waiting for transfers between devices, from_plane(): return lax.ppermute(x, 'plane', [((i + by) % size, i) for i in range(size)])  18.6 us
    pallas_call x10, Pallas kernels, call(): pl.pallas_call(kernel, out_shape=out_shape, in_specs=in_specs, out_specs=...  16.5 us
    ppermute x6, starting transfers between devices, from_plane(): return lax.ppermute(x, 'plane', [((i + by) % size, i) for i in range(size)])  14.7 us
    all_to_all x1, blocking collectives, exchange(): return lax.all_to_all(x, GROUP, split_axis=0, concat_axis=0, tiled=True)  13.1 us
    all_to_all x2, starting transfers between devices, exchange(): return lax.all_to_all(x, GROUP, split_axis=0, concat_axis=0, tiled=True)  7.33 us
    all_to_all x2, waiting for transfers between devices, exchange(): return lax.all_to_all(x, GROUP, split_axis=0, concat_axis=0, tiled=True)  2.68 us
    ppermute x1, starting transfers between devices, local(): other = lax.ppermute(own, 'sub', [(0, 1), (1, 0)])  1.54 us
  transfers between devices with their start and end apart: 9, of which 6 were waited for; matrix products, arithmetic and copies ran while one was open for 0% of the time, Pallas kernels for 16%

profile of v11, /device:TPU:0, one launch (start us, length us, event | category | flops | bytes accessed | tf_op | source)
XLA Modules:
  0.0 75.7 jit_solution(1977952118225645319)
XLA Ops:
  0.0 0.0 copy-start
  0.0 1.0 %copy-done = bf16[1,2,128,1024]{3,2,1,0:T(8,128)(2,1)S(1)} copy-done((bf16[1,2,128,1024]{3,2,1,0:T(8,128)(2,1)S(1)}, bf16[1,2,128,1024]{3,2,1,0:T(8,128)(2,1)}, u32[]{:S(2)}) %copy-start) | copy-done | bytes 524312
  1.0 0.3 raw.1.refs_2_
  1.4 3.1 %collective-permute-start = (bf16[1,2,64,1024]{3,2,1,0:T(8,128)(2,1)S(1)}, bf16[1,2,64,1024]{3,2,1,0:T(8,128)(2,1)S(1)}, u32[]{:S(2)}, u32[]{:S(2)}) collective-permute-start(bf16[1,2,64,1024]{3,2,1,0:T(8,128)(2,1)S(1)} %raw.1.refs_2_), channel_id=1, source_target_pairs={{24,0},{0,8},{8,16},{16,24},{25,1},{1,9},{9,17},{17,25},{26,2},{2,... | collective-permute-start | bytes 786440 | tf_op jit(solution)/shard_map/ppermute | solution.py:31
  4.4 0.0 copy-start.3
  4.4 0.0 copy-start.4
  4.4 1.9 %first.1 = bf16[8,1,3,128,128]{4,3,2,1,0:T(8,128)(2,1)} custom-call(s32[2,8]{1,0:T(2,128)} %bitcast.8, bf16[1,2,128,1024]{3,2,1,0:T(8,128)(2,1)} %keys.3, bf16[1,2,128,1024]{3,2,1,0:T(8,128)(2,1)} %values.1), custom_call_target="tpu_custom_call" | custom-call | bytes 1572864 | tf_op jit(solution)/shard_map/first/pallas_call | solution.py:354
  6.4 3.7 %all-to-all-start = ((bf16[8,1,3,128,128]{4,3,2,1,0:T(8,128)(2,1)}), bf16[8,1,3,128,128]{4,3,2,1,0:T(8,128)(2,1)S(1)}, u32[]{:S(2)}, u32[]{:S(2)}) async-start(bf16[8,1,3,128,128]{4,3,2,1,0:T(8,128)(2,1)} %first.1), calls=%async_computation | async-start | bytes 1572864 | tf_op jit(solution)/shard_map/all_to_all | solution.py:35
  10.2 2.6 %collective-permute-done.refs_0_.refs_1_ = bf16[1,2,64,1024]{3,2,1,0:T(8,128)(2,1)S(1)} collective-permute-done((bf16[1,2,64,1024]{3,2,1,0:T(8,128)(2,1)S(1)}, bf16[1,2,64,1024]{3,2,1,0:T(8,128)(2,1)S(1)}, u32[]{:S(2)}, u32[]{:S(2)}) %collective-permute-start) | collective-permute-done | bytes 262176 | tf_op jit(solution)/shard_map/ppermute | solution.py:31
  12.8 1.7 %collective-permute-start.1 = (bf16[1,2,64,1024]{3,2,1,0:T(8,128)(2,1)S(1)}, bf16[1,2,64,1024]{3,2,1,0:T(8,128)(2,1)S(1)}, u32[]{:S(2)}, u32[]{:S(2)}) collective-permute-start(bf16[1,2,64,1024]{3,2,1,0:T(8,128)(2,1)S(1)} %raw.1.refs_2_), channel_id=1, source_target_pairs={{8,0},{16,8},{24,16},{0,24},{9,1},{17,9},{25,17},{1,25},{10,2},{18... | collective-permute-start | bytes 786440 | tf_op jit(solution)/shard_map/ppermute | solution.py:31
  14.5 0.0 copy-done.3
  14.5 0.1 reshape.16
  14.6 0.0 copy-done.4
  14.6 0.1 pad_add_fusion.own
  14.7 0.0 copy-start.1
  14.7 0.0 copy-start.2
  14.7 1.5 %collective-permute-start.2 = (s32[34]{0:T(128)S(1)}, s32[34]{0:T(128)S(1)}, u32[]{:S(2)}, u32[]{:S(2)}) collective-permute-start(s32[34]{0:T(128)S(1)} %pad_add_fusion.own), channel_id=1, source_target_pairs={{0,4},{4,0},{1,5},{5,1},{2,6},{6,2},{3,7},{7,3},{8,12},{12,8},{9,1... | collective-permute-start | bytes 416 | tf_op jit(solution)/shard_map/ppermute | solution.py:384
  16.2 4.0 %collective-permute-done.1.refs_1_.refs_3_ = bf16[1,2,64,1024]{3,2,1,0:T(8,128)(2,1)S(1)} collective-permute-done((bf16[1,2,64,1024]{3,2,1,0:T(8,128)(2,1)S(1)}, bf16[1,2,64,1024]{3,2,1,0:T(8,128)(2,1)S(1)}, u32[]{:S(2)}, u32[]{:S(2)}) %collective-permute-start.1) | collective-permute-done | bytes 262176 | tf_op jit(solution)/shard_map/ppermute | solution.py:31
  20.3 0.0 collective-permute-done.2.other
  20.3 2.5 %all-to-all-done = bf16[8,1,3,128,128]{4,3,2,1,0:T(8,128)(2,1)S(1)} async-done(((bf16[8,1,3,128,128]{4,3,2,1,0:T(8,128)(2,1)}), bf16[8,1,3,128,128]{4,3,2,1,0:T(8,128)(2,1)S(1)}, u32[]{:S(2)}, u32[]{:S(2)}) %all-to-all-start) | async-done | bytes 786464 | tf_op jit(solution)/shard_map/all_to_all | solution.py:35
  22.8 0.1 split.1
  22.8 1.6 %collective-permute-start.3 = (bf16[8,2,128,128]{3,2,1,0:T(8,128)(2,1)S(1)}, bf16[8,2,128,128]{3,2,1,0:T(8,128)(2,1)}, u32[]{:S(2)}, u32[]{:S(2)}) collective-permute-start(bf16[8,2,128,128]{3,2,1,0:T(8,128)(2,1)S(1)} %get-tuple-element.21.refs_1_), channel_id=1, source_target_pairs={{24,0},{0,8},{8,16},{16,24},{25,1},{1,9},{9,17},{17,25},{26,2},{2,... | collective-permute-start | bytes 1572872 | tf_op jit(solution)/shard_map/ppermute | solution.py:31
  24.4 2.2 %collective-permute-start.4 = (bf16[8,2,128,128]{3,2,1,0:T(8,128)(2,1)S(1)}, bf16[8,2,128,128]{3,2,1,0:T(8,128)(2,1)}, u32[]{:S(2)}, u32[]{:S(2)}) collective-permute-start(bf16[8,2,128,128]{3,2,1,0:T(8,128)(2,1)S(1)} %get-tuple-element.21.refs_1_), channel_id=1, source_target_pairs={{8,0},{16,8},{24,16},{0,24},{9,1},{17,9},{25,17},{1,25},{10,2},{18... | collective-permute-start | bytes 1572872 | tf_op jit(solution)/shard_map/ppermute | solution.py:31
  26.7 0.0 copy-done.1
  26.7 0.0 copy-done.2
  26.7 1.7 %second.1 = bf16[8,1,5,128,128]{4,3,2,1,0:T(8,128)(2,1)} custom-call(s32[2,8]{1,0:T(2,128)S(1)} %bitcast.9, f32[8,128]{1,0:T(8,128)S(1)} %mark.3.mark_ref, bf16[1,2,128,1024]{3,2,1,0:T(8,128)(2,1)S(1)} %copy-done.1, bf16[1,2,64,1024]{3,2,1,0:T(8,128)(2,1)S(1)} %collective-permute-done.refs_0_.refs_1_, bf16[1,2,64,1024]{3,2,1,0:T(8,128)(2,1)S(1)} %raw.1.refs_2_, ...), custom_call_target="tpu_custom_call" | custom-call | bytes 2621440 | tf_op jit(solution)/shard_map/second/pallas_call | solution.py:354
  28.4 3.6 %all-to-all-start.1 = ((bf16[8,1,5,128,128]{4,3,2,1,0:T(8,128)(2,1)}), bf16[8,1,5,128,128]{4,3,2,1,0:T(8,128)(2,1)S(1)}, u32[]{:S(2)}, u32[]{:S(2)}) async-start(bf16[8,1,5,128,128]{4,3,2,1,0:T(8,128)(2,1)} %second.1), calls=%async_computation.1 | async-start | bytes 2621440 | tf_op jit(solution)/shard_map/all_to_all | solution.py:35
  31.9 7.7 %collective-permute-done.3.refs_0_ = bf16[8,2,128,128]{3,2,1,0:T(8,128)(2,1)} collective-permute-done((bf16[8,2,128,128]{3,2,1,0:T(8,128)(2,1)S(1)}, bf16[8,2,128,128]{3,2,1,0:T(8,128)(2,1)}, u32[]{:S(2)}, u32[]{:S(2)}) %collective-permute-start.3) | collective-permute-done | bytes 524320 | tf_op jit(solution)/shard_map/ppermute | solution.py:31
  39.6 6.0 %collective-permute-start.5 = (bf16[8,1,128,128]{3,2,1,0:T(8,128)(2,1)S(1)}, bf16[8,1,128,128]{3,2,1,0:T(8,128)(2,1)S(1)}, u32[]{:S(2)}, u32[]{:S(2)}) collective-permute-start(bf16[8,1,128,128]{3,2,1,0:T(8,128)(2,1)S(1)} %get-tuple-element.26.refs_1_), channel_id=1, source_target_pairs={{24,0},{0,8},{8,16},{16,24},{25,1},{1,9},{9,17},{17,25},{26,2},{2,... | collective-permute-start | bytes 786440 | tf_op jit(solution)/shard_map/ppermute | solution.py:31
  45.7 0.0 collective-permute-start.6
  45.7 4.2 %collective-permute-done.4.refs_0_.refs_2_ = bf16[8,2,128,128]{3,2,1,0:T(8,128)(2,1)} collective-permute-done((bf16[8,2,128,128]{3,2,1,0:T(8,128)(2,1)S(1)}, bf16[8,2,128,128]{3,2,1,0:T(8,128)(2,1)}, u32[]{:S(2)}, u32[]{:S(2)}) %collective-permute-start.4) | collective-permute-done | bytes 524320 | tf_op jit(solution)/shard_map/ppermute | solution.py:31
  49.9 0.2 all-to-all-done.1
  50.1 8.7 %core.1 = (bf16[8,1,128,128]{3,2,1,0:T(8,128)(2,1)S(1)}, bf16[8,256,1152]{2,1,0:T(8,128)(2,1)S(1)}) custom-call(s32[34]{0:T(128)S(1)} %pad_add_fusion.own, s32[34]{0:T(128)S(1)} %collective-permute-done.2.other, bf16[8,5,128,128]{3,2,1,0:T(8,128)(2,1)S(1)} %bitcast.7, bf16[8,2,128,128]{3,2,1,0:T(8,128)(2,1)} %collective-permute-done.3.refs_0_, ...), custom_call_target="tpu_custom_call" | custom-call | flops 905969664 | bytes 1048576 | tf_op jit(solution)/shard_map/core/pallas_call | solution.py:354
  58.8 0.0 collective-permute-done.5.refs_0_
  58.8 0.0 collective-permute-done.6.refs_2_
  58.8 3.1 %weigh.1 = bf16[8,2,128,128]{3,2,1,0:T(8,128)(2,1)S(1)} custom-call(s32[34]{0:T(128)S(1)} %pad_add_fusion.own, s32[34]{0:T(128)S(1)} %collective-permute-done.2.other, s32[2,8]{1,0:T(2,128)S(1)} %bitcast.10, bf16[8,256,1152]{2,1,0:T(8,128)(2,1)S(1)} %get-tuple-element.24.expo, bf16[8,1,128,128]{3,2,1,0:T(8,128)(2,1)S(1)} %get-tuple-element.25.done, ...), custom_call_target="tpu_custom_call" | custom-call | flops 301989888 | bytes 1048576 | tf_op jit(solution)/shard_map/weigh/pallas_call | solution.py:354
  61.9 13.1 %all_to_all.15.x = bf16[8,1,2,128,128]{4,3,2,1,0:T(8,128)(2,1)S(1)} all-to-all(bf16[8,1,2,128,128]{4,3,2,1,0:T(8,128)(2,1)S(1)} %bitcast.6), channel_id=1, replica_groups=mesh['plane'=4,'sub'=2,'tok'=4] {'sub','tok'}, dimensions={0} | all-to-all | bytes 1048576 | tf_op jit(solution)/shard_map/all_to_all | solution.py:35
  74.9 0.8 %last.1 = bf16[1,2,128,1024]{3,2,1,0:T(8,128)(2,1)} custom-call(bf16[8,1,2,128,128]{4,3,2,1,0:T(8,128)(2,1)S(1)} %all_to_all.15.x), custom_call_target="tpu_custom_call" | custom-call | bytes 1048576 | tf_op jit(solution)/shard_map/last/pallas_call | solution.py:354
  (3 shorter events, 0.0 us)
Async XLA Ops:
  0.0 1.0 %copy-start = (bf16[1,2,128,1024]{3,2,1,0:T(8,128)(2,1)S(1)}, bf16[1,2,128,1024]{3,2,1,0:T(8,128)(2,1)}, u32[]{:S(2)}) copy-start(bf16[1,2,128,1024]{3,2,1,0:T(8,128)(2,1)} %keys.3) | copy-start | bytes 1572868
  1.4 11.4 %collective-permute-start = (bf16[1,2,64,1024]{3,2,1,0:T(8,128)(2,1)S(1)}, bf16[1,2,64,1024]{3,2,1,0:T(8,128)(2,1)S(1)}, u32[]{:S(2)}, u32[]{:S(2)}) collective-permute-start(bf16[1,2,64,1024]{3,2,1,0:T(8,128)(2,1)S(1)} %raw.1.refs_2_), channel_id=1, source_target_pairs={{24,0},{0,8},{8,16},{16,24},{25,1},{1,9},{9,17},{17,25},{26,2},{2,... | collective-permute-start | bytes 786440 | tf_op jit(solution)/shard_map/ppermute | solution.py:31
  4.4 10.1 %copy-start.3 = (s32[1,2,4,4]{3,2,1,0:T(4,128)S(1)}, s32[1,2,4,4]{3,2,1,0:T(4,128)}, u32[]{:S(2)}) copy-start(s32[1,2,4,4]{3,2,1,0:T(4,128)} %param.9) | copy-start | bytes 388
  4.4 10.2 %copy-start.4 = (s32[1,2]{1,0:T(1,128)S(1)}, s32[1,2]{1,0:T(1,128)}, u32[]{:S(2)}) copy-start(s32[1,2]{1,0:T(1,128)} %param.10) | copy-start | bytes 28
  6.4 16.3 %all-to-all-start = ((bf16[8,1,3,128,128]{4,3,2,1,0:T(8,128)(2,1)}), bf16[8,1,3,128,128]{4,3,2,1,0:T(8,128)(2,1)S(1)}, u32[]{:S(2)}, u32[]{:S(2)}) async-start(bf16[8,1,3,128,128]{4,3,2,1,0:T(8,128)(2,1)} %first.1), calls=%async_computation | async-start | bytes 1572864 | tf_op jit(solution)/shard_map/all_to_all | solution.py:35
  12.8 7.5 %collective-permute-start.1 = (bf16[1,2,64,1024]{3,2,1,0:T(8,128)(2,1)S(1)}, bf16[1,2,64,1024]{3,2,1,0:T(8,128)(2,1)S(1)}, u32[]{:S(2)}, u32[]{:S(2)}) collective-permute-start(bf16[1,2,64,1024]{3,2,1,0:T(8,128)(2,1)S(1)} %raw.1.refs_2_), channel_id=1, source_target_pairs={{8,0},{16,8},{24,16},{0,24},{9,1},{17,9},{25,17},{1,25},{10,2},{18... | collective-permute-start | bytes 786440 | tf_op jit(solution)/shard_map/ppermute | solution.py:31
  14.7 12.0 %copy-start.1 = (bf16[1,2,128,1024]{3,2,1,0:T(8,128)(2,1)S(1)}, bf16[1,2,128,1024]{3,2,1,0:T(8,128)(2,1)}, u32[]{:S(2)}) copy-start(bf16[1,2,128,1024]{3,2,1,0:T(8,128)(2,1)} %refs_0_.1) | copy-start | bytes 1572868
  14.7 12.0 %copy-start.2 = (s32[8,2]{0,1:T(2,128)S(1)}, s32[8,2]{0,1:T(2,128)}, u32[]{:S(2)}) copy-start(s32[8,2]{0,1:T(2,128)} %param.11) | copy-start | bytes 196
  14.7 5.6 %collective-permute-start.2 = (s32[34]{0:T(128)S(1)}, s32[34]{0:T(128)S(1)}, u32[]{:S(2)}, u32[]{:S(2)}) collective-permute-start(s32[34]{0:T(128)S(1)} %pad_add_fusion.own), channel_id=1, source_target_pairs={{0,4},{4,0},{1,5},{5,1},{2,6},{6,2},{3,7},{7,3},{8,12},{12,8},{9,1... | collective-permute-start | bytes 416 | tf_op jit(solution)/shard_map/ppermute | solution.py:384
  22.8 16.8 %collective-permute-start.3 = (bf16[8,2,128,128]{3,2,1,0:T(8,128)(2,1)S(1)}, bf16[8,2,128,128]{3,2,1,0:T(8,128)(2,1)}, u32[]{:S(2)}, u32[]{:S(2)}) collective-permute-start(bf16[8,2,128,128]{3,2,1,0:T(8,128)(2,1)S(1)} %get-tuple-element.21.refs_1_), channel_id=1, source_target_pairs={{24,0},{0,8},{8,16},{16,24},{25,1},{1,9},{9,17},{17,25},{26,2},{2,... | collective-permute-start | bytes 1572872 | tf_op jit(solution)/shard_map/ppermute | solution.py:31
  24.4 25.4 %collective-permute-start.4 = (bf16[8,2,128,128]{3,2,1,0:T(8,128)(2,1)S(1)}, bf16[8,2,128,128]{3,2,1,0:T(8,128)(2,1)}, u32[]{:S(2)}, u32[]{:S(2)}) collective-permute-start(bf16[8,2,128,128]{3,2,1,0:T(8,128)(2,1)S(1)} %get-tuple-element.21.refs_1_), channel_id=1, source_target_pairs={{8,0},{16,8},{24,16},{0,24},{9,1},{17,9},{25,17},{1,25},{10,2},{18... | collective-permute-start | bytes 1572872 | tf_op jit(solution)/shard_map/ppermute | solution.py:31
  28.4 21.7 %all-to-all-start.1 = ((bf16[8,1,5,128,128]{4,3,2,1,0:T(8,128)(2,1)}), bf16[8,1,5,128,128]{4,3,2,1,0:T(8,128)(2,1)S(1)}, u32[]{:S(2)}, u32[]{:S(2)}) async-start(bf16[8,1,5,128,128]{4,3,2,1,0:T(8,128)(2,1)} %second.1), calls=%async_computation.1 | async-start | bytes 2621440 | tf_op jit(solution)/shard_map/all_to_all | solution.py:35
  39.6 19.1 %collective-permute-start.5 = (bf16[8,1,128,128]{3,2,1,0:T(8,128)(2,1)S(1)}, bf16[8,1,128,128]{3,2,1,0:T(8,128)(2,1)S(1)}, u32[]{:S(2)}, u32[]{:S(2)}) collective-permute-start(bf16[8,1,128,128]{3,2,1,0:T(8,128)(2,1)S(1)} %get-tuple-element.26.refs_1_), channel_id=1, source_target_pairs={{24,0},{0,8},{8,16},{16,24},{25,1},{1,9},{9,17},{17,25},{26,2},{2,... | collective-permute-start | bytes 786440 | tf_op jit(solution)/shard_map/ppermute | solution.py:31
  45.7 13.1 %collective-permute-start.6 = (bf16[8,1,128,128]{3,2,1,0:T(8,128)(2,1)S(1)}, bf16[8,1,128,128]{3,2,1,0:T(8,128)(2,1)S(1)}, u32[]{:S(2)}, u32[]{:S(2)}) collective-permute-start(bf16[8,1,128,128]{3,2,1,0:T(8,128)(2,1)S(1)} %get-tuple-element.26.refs_1_), channel_id=1, source_target_pairs={{8,0},{16,8},{24,16},{0,24},{9,1},{17,9},{25,17},{1,25},{10,2},{18... | collective-permute-start | bytes 786440 | tf_op jit(solution)/shard_map/ppermute | solution.py:31

commit v12 on v11

--- a/solution.py
+++ b/solution.py
@@ -111,19 +111,6 @@
     pltpu.make_async_copy(out, out, sem).wait()
 
 
-def raw_kernel(keys, out, sem):
-    half = TILE // 2
-    for s in range(2):
-        for m in range(keys.shape[2] // TILE):
-            for i in range(2):
-                rows = half // 2
-                pltpu.make_async_copy(
-                    keys.at[0, s, pl.ds(m * TILE + i * rows, rows)],
-                    out.at[0, s, pl.ds(m * half + i * rows, rows)], sem,
-                ).start()
-    pltpu.make_async_copy(out, out, sem).wait()
-
-
 def split_kernel(x, head, tail):
     pieces = head.shape[1]
     head[...] = x[:, :pieces]
@@ -202,8 +189,8 @@
             bias = jnp.where(keep, 0.0, NEG_SCORE)
             parts.append(far[j][:, k * TILE:(k + 1) * TILE] + bias)
     top = functools.reduce(jnp.maximum, parts)
-    top = jnp.max(top, axis=1, keepdims=True)
-    return [jnp.exp2((part - top) * factor).astype(jnp.bfloat16) for part in parts]
+    top = jnp.max(top, axis=1, keepdims=True) * factor
+    return [jnp.exp2(part * factor - top).astype(jnp.bfloat16) for part in parts]
 
 
 def with_ones(v):
@@ -417,10 +404,7 @@
             [ANY] * len(arrays), VMEM, [], arrays, flops=flops, mib=1,
         )
 
-    raw = call(
-        raw_kernel, "raw", jax.ShapeDtypeStruct((1, 2, tiles * half, width), dtype), [ANY], ANY,
-        [sem], (keys,), moved=size, mib=1,
-    )
+    raw = keys.reshape(1, 2, tiles, TILE, width)[:, :, :, :half].reshape(1, 2, tiles * half, width)
     raw = around(raw, chain=True)
     if plan.whole_lanes:
         packed = call(

time: 76.1 us -> 75.7 us (level)
    unnamed x10 -> x8, local copies, waits for them, and re-layouts: 1.06 us -> 0.01 us
    reshape x0 -> x1, local copies, waits for them, and re-layouts: none -> 0.97 us  [local(): keys.reshape(1, 2, tiles, TILE, width)[:, :, :, :half]]
    pallas_call x10 -> x9, Pallas kernels: 16.5 us -> 16.1 us  [call(): pl.pallas_call(kernel, out_shape=out_shape, in_specs=in_specs, out_specs=...]
where the time goes in v12:
time: 75.7 us; the launch traced here: 75.3 us
  starting transfers between devices  23.6 us (31%)
  waiting for transfers between devices  21.2 us (28%)
  Pallas kernels  16.1 us (21%)
  blocking collectives  13.2 us (17%)
  local copies, waits for them, and re-layouts  1.07 us (1%)
    ppermute x6, waiting for transfers between devices, from_plane(): return lax.ppermute(x, 'plane', [((i + by) % size, i) for i in range(size)])  18.5 us
    pallas_call x9, Pallas kernels, call(): pl.pallas_call(kernel, out_shape=out_shape, in_specs=in_specs, out_specs=...  16.1 us
    ppermute x6, starting transfers between devices, from_plane(): return lax.ppermute(x, 'plane', [((i + by) % size, i) for i in range(size)])  14.8 us
    all_to_all x1, blocking collectives, exchange(): return lax.all_to_all(x, GROUP, split_axis=0, concat_axis=0, tiled=True)  13.2 us
    all_to_all x2, starting transfers between devices, exchange(): return lax.all_to_all(x, GROUP, split_axis=0, concat_axis=0, tiled=True)  7.32 us
    all_to_all x2, waiting for transfers between devices, exchange(): return lax.all_to_all(x, GROUP, split_axis=0, concat_axis=0, tiled=True)  2.71 us
    ppermute x1, starting transfers between devices, local(): other = lax.ppermute(own, 'sub', [(0, 1), (1, 0)])  1.54 us
  transfers between devices with their start and end apart: 9, of which 6 were waited for; matrix products, arithmetic and copies ran while one was open for 0% of the time, Pallas kernels for 16%

profile of v12, /device:TPU:0, one launch (start us, length us, event | category | flops | bytes accessed | tf_op | source)
XLA Modules:
  0.0 75.3 jit_solution(14633887132791196537)
XLA Ops:
  0.0 1.0 %slice_bitcast_fusion.refs_2_ = bf16[1,2,64,1024]{3,2,1,0:T(8,128)(2,1)S(1)} fusion(bf16[1,2,1,128,1024]{4,3,1,2,0:T(8,128)(2,1)} %bitcast.14), kind=kLoop, calls=%fused_computation | loop fusion | bytes 524288 | tf_op jit(solution)/shard_map/reshape | solution.py:407
  1.0 3.1 %collective-permute-start = (bf16[1,2,64,1024]{3,2,1,0:T(8,128)(2,1)S(1)}, bf16[1,2,64,1024]{3,2,1,0:T(8,128)(2,1)S(1)}, u32[]{:S(2)}, u32[]{:S(2)}) collective-permute-start(bf16[1,2,64,1024]{3,2,1,0:T(8,128)(2,1)S(1)} %slice_bitcast_fusion.refs_2_), channel_id=1, source_target_pairs={{24,0},{0,8},{8,16},{16,24},{25,1},{1,9},{9,17},{17,25},{26,2},{2,... | collective-permute-start | bytes 786440 | tf_op jit(solution)/shard_map/ppermute | solution.py:31
  4.0 0.0 copy-start.2
  4.0 0.0 copy-start.3
  4.1 2.0 %first.1 = bf16[8,1,3,128,128]{4,3,2,1,0:T(8,128)(2,1)} custom-call(s32[2,8]{1,0:T(2,128)} %bitcast.11, bf16[1,2,128,1024]{3,2,1,0:T(8,128)(2,1)} %keys.1, bf16[1,2,128,1024]{3,2,1,0:T(8,128)(2,1)} %values.1), custom_call_target="tpu_custom_call" | custom-call | bytes 1572864 | tf_op jit(solution)/shard_map/first/pallas_call | solution.py:341
  6.0 3.7 %all-to-all-start = ((bf16[8,1,3,128,128]{4,3,2,1,0:T(8,128)(2,1)}), bf16[8,1,3,128,128]{4,3,2,1,0:T(8,128)(2,1)S(1)}, u32[]{:S(2)}, u32[]{:S(2)}) async-start(bf16[8,1,3,128,128]{4,3,2,1,0:T(8,128)(2,1)} %first.1), calls=%async_computation | async-start | bytes 1572864 | tf_op jit(solution)/shard_map/all_to_all | solution.py:35
  9.8 2.6 %collective-permute-done.refs_0_.refs_1_ = bf16[1,2,64,1024]{3,2,1,0:T(8,128)(2,1)S(1)} collective-permute-done((bf16[1,2,64,1024]{3,2,1,0:T(8,128)(2,1)S(1)}, bf16[1,2,64,1024]{3,2,1,0:T(8,128)(2,1)S(1)}, u32[]{:S(2)}, u32[]{:S(2)}) %collective-permute-start) | collective-permute-done | bytes 262176 | tf_op jit(solution)/shard_map/ppermute | solution.py:31
  12.4 1.7 %collective-permute-start.1 = (bf16[1,2,64,1024]{3,2,1,0:T(8,128)(2,1)S(1)}, bf16[1,2,64,1024]{3,2,1,0:T(8,128)(2,1)S(1)}, u32[]{:S(2)}, u32[]{:S(2)}) collective-permute-start(bf16[1,2,64,1024]{3,2,1,0:T(8,128)(2,1)S(1)} %slice_bitcast_fusion.refs_2_), channel_id=1, source_target_pairs={{8,0},{16,8},{24,16},{0,24},{9,1},{17,9},{25,17},{1,25},{10,2},{18... | collective-permute-start | bytes 786440 | tf_op jit(solution)/shard_map/ppermute | solution.py:31
  14.1 0.0 copy-done.2
  14.1 0.1 reshape.24
  14.2 0.0 copy-done.3
  14.2 0.1 pad_add_fusion.own
  14.3 0.0 copy-start
  14.3 0.0 copy-start.1
  14.3 1.5 %collective-permute-start.2 = (s32[34]{0:T(128)S(1)}, s32[34]{0:T(128)S(1)}, u32[]{:S(2)}, u32[]{:S(2)}) collective-permute-start(s32[34]{0:T(128)S(1)} %pad_add_fusion.own), channel_id=1, source_target_pairs={{0,4},{4,0},{1,5},{5,1},{2,6},{6,2},{3,7},{7,3},{8,12},{12,8},{9,1... | collective-permute-start | bytes 416 | tf_op jit(solution)/shard_map/ppermute | solution.py:371
  15.8 4.0 %collective-permute-done.1.refs_1_.refs_3_ = bf16[1,2,64,1024]{3,2,1,0:T(8,128)(2,1)S(1)} collective-permute-done((bf16[1,2,64,1024]{3,2,1,0:T(8,128)(2,1)S(1)}, bf16[1,2,64,1024]{3,2,1,0:T(8,128)(2,1)S(1)}, u32[]{:S(2)}, u32[]{:S(2)}) %collective-permute-start.1) | collective-permute-done | bytes 262176 | tf_op jit(solution)/shard_map/ppermute | solution.py:31
  19.9 0.0 collective-permute-done.2.other
  19.9 2.5 %all-to-all-done = bf16[8,1,3,128,128]{4,3,2,1,0:T(8,128)(2,1)S(1)} async-done(((bf16[8,1,3,128,128]{4,3,2,1,0:T(8,128)(2,1)}), bf16[8,1,3,128,128]{4,3,2,1,0:T(8,128)(2,1)S(1)}, u32[]{:S(2)}, u32[]{:S(2)}) %all-to-all-start) | async-done | bytes 786464 | tf_op jit(solution)/shard_map/all_to_all | solution.py:35
  22.4 0.1 split.1
  22.4 1.6 %collective-permute-start.3 = (bf16[8,2,128,128]{3,2,1,0:T(8,128)(2,1)S(1)}, bf16[8,2,128,128]{3,2,1,0:T(8,128)(2,1)}, u32[]{:S(2)}, u32[]{:S(2)}) collective-permute-start(bf16[8,2,128,128]{3,2,1,0:T(8,128)(2,1)S(1)} %get-tuple-element.21.refs_1_), channel_id=1, source_target_pairs={{24,0},{0,8},{8,16},{16,24},{25,1},{1,9},{9,17},{17,25},{26,2},{2,... | collective-permute-start | bytes 1572872 | tf_op jit(solution)/shard_map/ppermute | solution.py:31
  24.0 2.3 %collective-permute-start.4 = (bf16[8,2,128,128]{3,2,1,0:T(8,128)(2,1)S(1)}, bf16[8,2,128,128]{3,2,1,0:T(8,128)(2,1)}, u32[]{:S(2)}, u32[]{:S(2)}) collective-permute-start(bf16[8,2,128,128]{3,2,1,0:T(8,128)(2,1)S(1)} %get-tuple-element.21.refs_1_), channel_id=1, source_target_pairs={{8,0},{16,8},{24,16},{0,24},{9,1},{17,9},{25,17},{1,25},{10,2},{18... | collective-permute-start | bytes 1572872 | tf_op jit(solution)/shard_map/ppermute | solution.py:31
  26.3 0.0 copy-done
  26.3 0.0 copy-done.1
  26.3 1.7 %second.1 = bf16[8,1,5,128,128]{4,3,2,1,0:T(8,128)(2,1)} custom-call(s32[2,8]{1,0:T(2,128)S(1)} %bitcast.12, f32[8,128]{1,0:T(8,128)S(1)} %mark.3.mark_ref, bf16[1,2,128,1024]{3,2,1,0:T(8,128)(2,1)S(1)} %copy-done, bf16[1,2,64,1024]{3,2,1,0:T(8,128)(2,1)S(1)} %collective-permute-done.refs_0_.refs_1_, bf16[1,2,64,1024]{3,2,1,0:T(8,128)(2,1)S(1)} %slice_bitcast_fusion.refs_2_, ...), custom_call_target="tpu_custom_call" | custom-call | bytes 2621440 | tf_op jit(solution)/shard_map/second/pallas_call | solution.py:341
  28.0 3.6 %all-to-all-start.1 = ((bf16[8,1,5,128,128]{4,3,2,1,0:T(8,128)(2,1)}), bf16[8,1,5,128,128]{4,3,2,1,0:T(8,128)(2,1)S(1)}, u32[]{:S(2)}, u32[]{:S(2)}) async-start(bf16[8,1,5,128,128]{4,3,2,1,0:T(8,128)(2,1)} %second.1), calls=%async_computation.1 | async-start | bytes 2621440 | tf_op jit(solution)/shard_map/all_to_all | solution.py:35
  31.6 7.7 %collective-permute-done.3.refs_0_ = bf16[8,2,128,128]{3,2,1,0:T(8,128)(2,1)} collective-permute-done((bf16[8,2,128,128]{3,2,1,0:T(8,128)(2,1)S(1)}, bf16[8,2,128,128]{3,2,1,0:T(8,128)(2,1)}, u32[]{:S(2)}, u32[]{:S(2)}) %collective-permute-start.3) | collective-permute-done | bytes 524320 | tf_op jit(solution)/shard_map/ppermute | solution.py:31
  39.3 6.1 %collective-permute-start.5 = (bf16[8,1,128,128]{3,2,1,0:T(8,128)(2,1)S(1)}, bf16[8,1,128,128]{3,2,1,0:T(8,128)(2,1)S(1)}, u32[]{:S(2)}, u32[]{:S(2)}) collective-permute-start(bf16[8,1,128,128]{3,2,1,0:T(8,128)(2,1)S(1)} %get-tuple-element.26.refs_1_), channel_id=1, source_target_pairs={{24,0},{0,8},{8,16},{16,24},{25,1},{1,9},{9,17},{17,25},{26,2},{2,... | collective-permute-start | bytes 786440 | tf_op jit(solution)/shard_map/ppermute | solution.py:31
  45.3 0.0 collective-permute-start.6
  45.3 4.2 %collective-permute-done.4.refs_0_.refs_2_ = bf16[8,2,128,128]{3,2,1,0:T(8,128)(2,1)} collective-permute-done((bf16[8,2,128,128]{3,2,1,0:T(8,128)(2,1)S(1)}, bf16[8,2,128,128]{3,2,1,0:T(8,128)(2,1)}, u32[]{:S(2)}, u32[]{:S(2)}) %collective-permute-start.4) | collective-permute-done | bytes 524320 | tf_op jit(solution)/shard_map/ppermute | solution.py:31
  49.5 0.2 all-to-all-done.1
  49.7 8.5 %core.1 = (bf16[8,1,128,128]{3,2,1,0:T(8,128)(2,1)S(1)}, bf16[8,256,1152]{2,1,0:T(8,128)(2,1)S(1)}) custom-call(s32[34]{0:T(128)S(1)} %pad_add_fusion.own, s32[34]{0:T(128)S(1)} %collective-permute-done.2.other, bf16[8,5,128,128]{3,2,1,0:T(8,128)(2,1)S(1)} %bitcast.10, bf16[8,2,128,128]{3,2,1,0:T(8,128)(2,1)} %collective-permute-done.3.refs_0_, ...), custom_call_target="tpu_custom_call" | custom-call | flops 905969664 | bytes 1048576 | tf_op jit(solution)/shard_map/core/pallas_call | solution.py:341
  58.2 0.0 collective-permute-done.5.refs_0_
  58.2 0.0 collective-permute-done.6.refs_2_
  58.2 3.1 %weigh.1 = bf16[8,2,128,128]{3,2,1,0:T(8,128)(2,1)S(1)} custom-call(s32[34]{0:T(128)S(1)} %pad_add_fusion.own, s32[34]{0:T(128)S(1)} %collective-permute-done.2.other, s32[2,8]{1,0:T(2,128)S(1)} %bitcast.13, bf16[8,256,1152]{2,1,0:T(8,128)(2,1)S(1)} %get-tuple-element.24.expo, bf16[8,1,128,128]{3,2,1,0:T(8,128)(2,1)S(1)} %get-tuple-element.25.done, ...), custom_call_target="tpu_custom_call" | custom-call | flops 301989888 | bytes 1048576 | tf_op jit(solution)/shard_map/weigh/pallas_call | solution.py:341
  61.3 13.2 %all_to_all.15.x = bf16[8,1,2,128,128]{4,3,2,1,0:T(8,128)(2,1)S(1)} all-to-all(bf16[8,1,2,128,128]{4,3,2,1,0:T(8,128)(2,1)S(1)} %bitcast.9), channel_id=1, replica_groups=mesh['plane'=4,'sub'=2,'tok'=4] {'sub','tok'}, dimensions={0} | all-to-all | bytes 1048576 | tf_op jit(solution)/shard_map/all_to_all | solution.py:35
  74.6 0.8 %last.1 = bf16[1,2,128,1024]{3,2,1,0:T(8,128)(2,1)} custom-call(bf16[8,1,2,128,128]{4,3,2,1,0:T(8,128)(2,1)S(1)} %all_to_all.15.x), custom_call_target="tpu_custom_call" | custom-call | bytes 1048576 | tf_op jit(solution)/shard_map/last/pallas_call | solution.py:341
  (3 shorter events, 0.0 us)
Async XLA Ops:
  1.0 11.4 %collective-permute-start = (bf16[1,2,64,1024]{3,2,1,0:T(8,128)(2,1)S(1)}, bf16[1,2,64,1024]{3,2,1,0:T(8,128)(2,1)S(1)}, u32[]{:S(2)}, u32[]{:S(2)}) collective-permute-start(bf16[1,2,64,1024]{3,2,1,0:T(8,128)(2,1)S(1)} %slice_bitcast_fusion.refs_2_), channel_id=1, source_target_pairs={{24,0},{0,8},{8,16},{16,24},{25,1},{1,9},{9,17},{17,25},{26,2},{2,... | collective-permute-start | bytes 786440 | tf_op jit(solution)/shard_map/ppermute | solution.py:31
  4.0 10.1 %copy-start.2 = (s32[1,2,4,4]{3,2,1,0:T(4,128)S(1)}, s32[1,2,4,4]{3,2,1,0:T(4,128)}, u32[]{:S(2)}) copy-start(s32[1,2,4,4]{3,2,1,0:T(4,128)} %param.9) | copy-start | bytes 388
  4.0 10.2 %copy-start.3 = (s32[1,2]{1,0:T(1,128)S(1)}, s32[1,2]{1,0:T(1,128)}, u32[]{:S(2)}) copy-start(s32[1,2]{1,0:T(1,128)} %param.10) | copy-start | bytes 28
  6.0 16.3 %all-to-all-start = ((bf16[8,1,3,128,128]{4,3,2,1,0:T(8,128)(2,1)}), bf16[8,1,3,128,128]{4,3,2,1,0:T(8,128)(2,1)S(1)}, u32[]{:S(2)}, u32[]{:S(2)}) async-start(bf16[8,1,3,128,128]{4,3,2,1,0:T(8,128)(2,1)} %first.1), calls=%async_computation | async-start | bytes 1572864 | tf_op jit(solution)/shard_map/all_to_all | solution.py:35
  12.4 7.5 %collective-permute-start.1 = (bf16[1,2,64,1024]{3,2,1,0:T(8,128)(2,1)S(1)}, bf16[1,2,64,1024]{3,2,1,0:T(8,128)(2,1)S(1)}, u32[]{:S(2)}, u32[]{:S(2)}) collective-permute-start(bf16[1,2,64,1024]{3,2,1,0:T(8,128)(2,1)S(1)} %slice_bitcast_fusion.refs_2_), channel_id=1, source_target_pairs={{8,0},{16,8},{24,16},{0,24},{9,1},{17,9},{25,17},{1,25},{10,2},{18... | collective-permute-start | bytes 786440 | tf_op jit(solution)/shard_map/ppermute | solution.py:31
  14.3 12.0 %copy-start = (bf16[1,2,128,1024]{3,2,1,0:T(8,128)(2,1)S(1)}, bf16[1,2,128,1024]{3,2,1,0:T(8,128)(2,1)}, u32[]{:S(2)}) copy-start(bf16[1,2,128,1024]{3,2,1,0:T(8,128)(2,1)} %refs_0_.1) | copy-start | bytes 1572868
  14.3 12.0 %copy-start.1 = (s32[8,2]{0,1:T(2,128)S(1)}, s32[8,2]{0,1:T(2,128)}, u32[]{:S(2)}) copy-start(s32[8,2]{0,1:T(2,128)} %param.11) | copy-start | bytes 196
  14.3 5.6 %collective-permute-start.2 = (s32[34]{0:T(128)S(1)}, s32[34]{0:T(128)S(1)}, u32[]{:S(2)}, u32[]{:S(2)}) collective-permute-start(s32[34]{0:T(128)S(1)} %pad_add_fusion.own), channel_id=1, source_target_pairs={{0,4},{4,0},{1,5},{5,1},{2,6},{6,2},{3,7},{7,3},{8,12},{12,8},{9,1... | collective-permute-start | bytes 416 | tf_op jit(solution)/shard_map/ppermute | solution.py:371
  22.4 16.8 %collective-permute-start.3 = (bf16[8,2,128,128]{3,2,1,0:T(8,128)(2,1)S(1)}, bf16[8,2,128,128]{3,2,1,0:T(8,128)(2,1)}, u32[]{:S(2)}, u32[]{:S(2)}) collective-permute-start(bf16[8,2,128,128]{3,2,1,0:T(8,128)(2,1)S(1)} %get-tuple-element.21.refs_1_), channel_id=1, source_target_pairs={{24,0},{0,8},{8,16},{16,24},{25,1},{1,9},{9,17},{17,25},{26,2},{2,... | collective-permute-start | bytes 1572872 | tf_op jit(solution)/shard_map/ppermute | solution.py:31
  24.0 25.5 %collective-permute-start.4 = (bf16[8,2,128,128]{3,2,1,0:T(8,128)(2,1)S(1)}, bf16[8,2,128,128]{3,2,1,0:T(8,128)(2,1)}, u32[]{:S(2)}, u32[]{:S(2)}) collective-permute-start(bf16[8,2,128,128]{3,2,1,0:T(8,128)(2,1)S(1)} %get-tuple-element.21.refs_1_), channel_id=1, source_target_pairs={{8,0},{16,8},{24,16},{0,24},{9,1},{17,9},{25,17},{1,25},{10,2},{18... | collective-permute-start | bytes 1572872 | tf_op jit(solution)/shard_map/ppermute | solution.py:31
  28.0 21.7 %all-to-all-start.1 = ((bf16[8,1,5,128,128]{4,3,2,1,0:T(8,128)(2,1)}), bf16[8,1,5,128,128]{4,3,2,1,0:T(8,128)(2,1)S(1)}, u32[]{:S(2)}, u32[]{:S(2)}) async-start(bf16[8,1,5,128,128]{4,3,2,1,0:T(8,128)(2,1)} %second.1), calls=%async_computation.1 | async-start | bytes 2621440 | tf_op jit(solution)/shard_map/all_to_all | solution.py:35
  39.3 19.0 %collective-permute-start.5 = (bf16[8,1,128,128]{3,2,1,0:T(8,128)(2,1)S(1)}, bf16[8,1,128,128]{3,2,1,0:T(8,128)(2,1)S(1)}, u32[]{:S(2)}, u32[]{:S(2)}) collective-permute-start(bf16[8,1,128,128]{3,2,1,0:T(8,128)(2,1)S(1)} %get-tuple-element.26.refs_1_), channel_id=1, source_target_pairs={{24,0},{0,8},{8,16},{16,24},{25,1},{1,9},{9,17},{17,25},{26,2},{2,... | collective-permute-start | bytes 786440 | tf_op jit(solution)/shard_map/ppermute | solution.py:31
  45.3 12.9 %collective-permute-start.6 = (bf16[8,1,128,128]{3,2,1,0:T(8,128)(2,1)S(1)}, bf16[8,1,128,128]{3,2,1,0:T(8,128)(2,1)S(1)}, u32[]{:S(2)}, u32[]{:S(2)}) collective-permute-start(bf16[8,1,128,128]{3,2,1,0:T(8,128)(2,1)S(1)} %get-tuple-element.26.refs_1_), channel_id=1, source_target_pairs={{8,0},{16,8},{24,16},{0,24},{9,1},{17,9},{25,17},{1,25},{10,2},{18... | collective-permute-start | bytes 786440 | tf_op jit(solution)/shard_map/ppermute | solution.py:31

commit v13 on v12

--- a/solution.py
+++ b/solution.py
@@ -233,7 +233,8 @@
             lax.fori_loop(0, plan.kt // count, some, 0)
         return carry
 
-    lax.fori_loop(0, plan.sub, one_view, 0)
+    for g in range(plan.sub):
+        one_view(g, 0)
 
 
 def core_kernel(plan, own, other, mixed, *refs):

time: 75.7 us -> 75.7 us (level)
  transfers between devices with their start and end apart: 9 -> 9, of which waited for: 6 -> 6; matrix products, arithmetic and copies ran while one was open for 0% -> 0% of each run, Pallas kernels for 16% -> 17%
where the time goes in v13:
time: 75.7 us; the launch traced here: 75.4 us
  starting transfers between devices  23.6 us (31%)
  waiting for transfers between devices  21.2 us (28%)
  Pallas kernels  16.4 us (22%)
  blocking collectives  12.9 us (17%)
  local copies, waits for them, and re-layouts  1.07 us (1%)
    ppermute x6, waiting for transfers between devices, from_plane(): return lax.ppermute(x, 'plane', [((i + by) % size, i) for i in range(size)])  18.5 us
    pallas_call x9, Pallas kernels, call(): pl.pallas_call(kernel, out_shape=out_shape, in_specs=in_specs, out_specs=...  16.4 us
    ppermute x6, starting transfers between devices, from_plane(): return lax.ppermute(x, 'plane', [((i + by) % size, i) for i in range(size)])  14.8 us
    all_to_all x1, blocking collectives, exchange(): return lax.all_to_all(x, GROUP, split_axis=0, concat_axis=0, tiled=True)  12.9 us
    all_to_all x2, starting transfers between devices, exchange(): return lax.all_to_all(x, GROUP, split_axis=0, concat_axis=0, tiled=True)  7.31 us
    all_to_all x2, waiting for transfers between devices, exchange(): return lax.all_to_all(x, GROUP, split_axis=0, concat_axis=0, tiled=True)  2.7 us
    ppermute x1, starting transfers between devices, local(): other = lax.ppermute(own, 'sub', [(0, 1), (1, 0)])  1.54 us
  transfers between devices with their start and end apart: 9, of which 6 were waited for; matrix products, arithmetic and copies ran while one was open for 0% of the time, Pallas kernels for 17%

profile of v13, /device:TPU:0, one launch (start us, length us, event | category | flops | bytes accessed | tf_op | source)
XLA Modules:
  0.0 75.4 jit_solution(12546847292138112112)
XLA Ops:
  0.0 1.0 %slice_bitcast_fusion.refs_2_ = bf16[1,2,64,1024]{3,2,1,0:T(8,128)(2,1)S(1)} fusion(bf16[1,2,1,128,1024]{4,3,1,2,0:T(8,128)(2,1)} %bitcast.14), kind=kLoop, calls=%fused_computation | loop fusion | bytes 524288 | tf_op jit(solution)/shard_map/reshape | solution.py:408
  1.0 3.1 %collective-permute-start = (bf16[1,2,64,1024]{3,2,1,0:T(8,128)(2,1)S(1)}, bf16[1,2,64,1024]{3,2,1,0:T(8,128)(2,1)S(1)}, u32[]{:S(2)}, u32[]{:S(2)}) collective-permute-start(bf16[1,2,64,1024]{3,2,1,0:T(8,128)(2,1)S(1)} %slice_bitcast_fusion.refs_2_), channel_id=1, source_target_pairs={{24,0},{0,8},{8,16},{16,24},{25,1},{1,9},{9,17},{17,25},{26,2},{2,... | collective-permute-start | bytes 786440 | tf_op jit(solution)/shard_map/ppermute | solution.py:31
  4.0 0.0 copy-start.2
  4.0 0.0 copy-start.3
  4.1 2.0 %first.1 = bf16[8,1,3,128,128]{4,3,2,1,0:T(8,128)(2,1)} custom-call(s32[2,8]{1,0:T(2,128)} %bitcast.11, bf16[1,2,128,1024]{3,2,1,0:T(8,128)(2,1)} %keys.1, bf16[1,2,128,1024]{3,2,1,0:T(8,128)(2,1)} %values.1), custom_call_target="tpu_custom_call" | custom-call | bytes 1572864 | tf_op jit(solution)/shard_map/first/pallas_call | solution.py:342
  6.0 3.7 %all-to-all-start = ((bf16[8,1,3,128,128]{4,3,2,1,0:T(8,128)(2,1)}), bf16[8,1,3,128,128]{4,3,2,1,0:T(8,128)(2,1)S(1)}, u32[]{:S(2)}, u32[]{:S(2)}) async-start(bf16[8,1,3,128,128]{4,3,2,1,0:T(8,128)(2,1)} %first.1), calls=%async_computation | async-start | bytes 1572864 | tf_op jit(solution)/shard_map/all_to_all | solution.py:35
  9.8 2.6 %collective-permute-done.refs_0_.refs_1_ = bf16[1,2,64,1024]{3,2,1,0:T(8,128)(2,1)S(1)} collective-permute-done((bf16[1,2,64,1024]{3,2,1,0:T(8,128)(2,1)S(1)}, bf16[1,2,64,1024]{3,2,1,0:T(8,128)(2,1)S(1)}, u32[]{:S(2)}, u32[]{:S(2)}) %collective-permute-start) | collective-permute-done | bytes 262176 | tf_op jit(solution)/shard_map/ppermute | solution.py:31
  12.4 1.7 %collective-permute-start.1 = (bf16[1,2,64,1024]{3,2,1,0:T(8,128)(2,1)S(1)}, bf16[1,2,64,1024]{3,2,1,0:T(8,128)(2,1)S(1)}, u32[]{:S(2)}, u32[]{:S(2)}) collective-permute-start(bf16[1,2,64,1024]{3,2,1,0:T(8,128)(2,1)S(1)} %slice_bitcast_fusion.refs_2_), channel_id=1, source_target_pairs={{8,0},{16,8},{24,16},{0,24},{9,1},{17,9},{25,17},{1,25},{10,2},{18... | collective-permute-start | bytes 786440 | tf_op jit(solution)/shard_map/ppermute | solution.py:31
  14.1 0.0 copy-done.2
  14.1 0.1 reshape.24
  14.2 0.0 copy-done.3
  14.2 0.1 pad_add_fusion.own
  14.3 0.0 copy-start
  14.3 0.0 copy-start.1
  14.3 1.5 %collective-permute-start.2 = (s32[34]{0:T(128)S(1)}, s32[34]{0:T(128)S(1)}, u32[]{:S(2)}, u32[]{:S(2)}) collective-permute-start(s32[34]{0:T(128)S(1)} %pad_add_fusion.own), channel_id=1, source_target_pairs={{0,4},{4,0},{1,5},{5,1},{2,6},{6,2},{3,7},{7,3},{8,12},{12,8},{9,1... | collective-permute-start | bytes 416 | tf_op jit(solution)/shard_map/ppermute | solution.py:372
  15.8 4.0 %collective-permute-done.1.refs_1_.refs_3_ = bf16[1,2,64,1024]{3,2,1,0:T(8,128)(2,1)S(1)} collective-permute-done((bf16[1,2,64,1024]{3,2,1,0:T(8,128)(2,1)S(1)}, bf16[1,2,64,1024]{3,2,1,0:T(8,128)(2,1)S(1)}, u32[]{:S(2)}, u32[]{:S(2)}) %collective-permute-start.1) | collective-permute-done | bytes 262176 | tf_op jit(solution)/shard_map/ppermute | solution.py:31
  19.9 0.0 collective-permute-done.2.other
  19.9 2.5 %all-to-all-done = bf16[8,1,3,128,128]{4,3,2,1,0:T(8,128)(2,1)S(1)} async-done(((bf16[8,1,3,128,128]{4,3,2,1,0:T(8,128)(2,1)}), bf16[8,1,3,128,128]{4,3,2,1,0:T(8,128)(2,1)S(1)}, u32[]{:S(2)}, u32[]{:S(2)}) %all-to-all-start) | async-done | bytes 786464 | tf_op jit(solution)/shard_map/all_to_all | solution.py:35
  22.4 0.1 split.1
  22.4 1.6 %collective-permute-start.3 = (bf16[8,2,128,128]{3,2,1,0:T(8,128)(2,1)S(1)}, bf16[8,2,128,128]{3,2,1,0:T(8,128)(2,1)}, u32[]{:S(2)}, u32[]{:S(2)}) collective-permute-start(bf16[8,2,128,128]{3,2,1,0:T(8,128)(2,1)S(1)} %get-tuple-element.21.refs_1_), channel_id=1, source_target_pairs={{24,0},{0,8},{8,16},{16,24},{25,1},{1,9},{9,17},{17,25},{26,2},{2,... | collective-permute-start | bytes 1572872 | tf_op jit(solution)/shard_map/ppermute | solution.py:31
  24.0 2.2 %collective-permute-start.4 = (bf16[8,2,128,128]{3,2,1,0:T(8,128)(2,1)S(1)}, bf16[8,2,128,128]{3,2,1,0:T(8,128)(2,1)}, u32[]{:S(2)}, u32[]{:S(2)}) collective-permute-start(bf16[8,2,128,128]{3,2,1,0:T(8,128)(2,1)S(1)} %get-tuple-element.21.refs_1_), channel_id=1, source_target_pairs={{8,0},{16,8},{24,16},{0,24},{9,1},{17,9},{25,17},{1,25},{10,2},{18... | collective-permute-start | bytes 1572872 | tf_op jit(solution)/shard_map/ppermute | solution.py:31
  26.3 0.0 copy-done
  26.3 0.0 copy-done.1
  26.3 1.7 %second.1 = bf16[8,1,5,128,128]{4,3,2,1,0:T(8,128)(2,1)} custom-call(s32[2,8]{1,0:T(2,128)S(1)} %bitcast.12, f32[8,128]{1,0:T(8,128)S(1)} %mark.3.mark_ref, bf16[1,2,128,1024]{3,2,1,0:T(8,128)(2,1)S(1)} %copy-done, bf16[1,2,64,1024]{3,2,1,0:T(8,128)(2,1)S(1)} %collective-permute-done.refs_0_.refs_1_, bf16[1,2,64,1024]{3,2,1,0:T(8,128)(2,1)S(1)} %slice_bitcast_fusion.refs_2_, ...), custom_call_target="tpu_custom_call" | custom-call | bytes 2621440 | tf_op jit(solution)/shard_map/second/pallas_call | solution.py:342
  28.0 3.6 %all-to-all-start.1 = ((bf16[8,1,5,128,128]{4,3,2,1,0:T(8,128)(2,1)}), bf16[8,1,5,128,128]{4,3,2,1,0:T(8,128)(2,1)S(1)}, u32[]{:S(2)}, u32[]{:S(2)}) async-start(bf16[8,1,5,128,128]{4,3,2,1,0:T(8,128)(2,1)} %second.1), calls=%async_computation.1 | async-start | bytes 2621440 | tf_op jit(solution)/shard_map/all_to_all | solution.py:35
  31.6 7.7 %collective-permute-done.3.refs_0_ = bf16[8,2,128,128]{3,2,1,0:T(8,128)(2,1)} collective-permute-done((bf16[8,2,128,128]{3,2,1,0:T(8,128)(2,1)S(1)}, bf16[8,2,128,128]{3,2,1,0:T(8,128)(2,1)}, u32[]{:S(2)}, u32[]{:S(2)}) %collective-permute-start.3) | collective-permute-done | bytes 524320 | tf_op jit(solution)/shard_map/ppermute | solution.py:31
  39.2 6.1 %collective-permute-start.5 = (bf16[8,1,128,128]{3,2,1,0:T(8,128)(2,1)S(1)}, bf16[8,1,128,128]{3,2,1,0:T(8,128)(2,1)S(1)}, u32[]{:S(2)}, u32[]{:S(2)}) collective-permute-start(bf16[8,1,128,128]{3,2,1,0:T(8,128)(2,1)S(1)} %get-tuple-element.26.refs_1_), channel_id=1, source_target_pairs={{24,0},{0,8},{8,16},{16,24},{25,1},{1,9},{9,17},{17,25},{26,2},{2,... | collective-permute-start | bytes 786440 | tf_op jit(solution)/shard_map/ppermute | solution.py:31
  45.3 0.0 collective-permute-start.6
  45.3 4.2 %collective-permute-done.4.refs_0_.refs_2_ = bf16[8,2,128,128]{3,2,1,0:T(8,128)(2,1)} collective-permute-done((bf16[8,2,128,128]{3,2,1,0:T(8,128)(2,1)S(1)}, bf16[8,2,128,128]{3,2,1,0:T(8,128)(2,1)}, u32[]{:S(2)}, u32[]{:S(2)}) %collective-permute-start.4) | collective-permute-done | bytes 524320 | tf_op jit(solution)/shard_map/ppermute | solution.py:31
  49.5 0.2 all-to-all-done.1
  49.7 8.8 %core.1 = (bf16[8,1,128,128]{3,2,1,0:T(8,128)(2,1)S(1)}, bf16[8,256,1152]{2,1,0:T(8,128)(2,1)S(1)}) custom-call(s32[34]{0:T(128)S(1)} %pad_add_fusion.own, s32[34]{0:T(128)S(1)} %collective-permute-done.2.other, bf16[8,5,128,128]{3,2,1,0:T(8,128)(2,1)S(1)} %bitcast.10, bf16[8,2,128,128]{3,2,1,0:T(8,128)(2,1)} %collective-permute-done.3.refs_0_, ...), custom_call_target="tpu_custom_call" | custom-call | flops 905969664 | bytes 1048576 | tf_op jit(solution)/shard_map/core/pallas_call | solution.py:342
  58.5 0.0 collective-permute-done.5.refs_0_
  58.5 0.0 collective-permute-done.6.refs_2_
  58.5 3.1 %weigh.1 = bf16[8,2,128,128]{3,2,1,0:T(8,128)(2,1)S(1)} custom-call(s32[34]{0:T(128)S(1)} %pad_add_fusion.own, s32[34]{0:T(128)S(1)} %collective-permute-done.2.other, s32[2,8]{1,0:T(2,128)S(1)} %bitcast.13, bf16[8,256,1152]{2,1,0:T(8,128)(2,1)S(1)} %get-tuple-element.24.expo, bf16[8,1,128,128]{3,2,1,0:T(8,128)(2,1)S(1)} %get-tuple-element.25.done, ...), custom_call_target="tpu_custom_call" | custom-call | flops 301989888 | bytes 1048576 | tf_op jit(solution)/shard_map/weigh/pallas_call | solution.py:342
  61.7 12.9 %all_to_all.15.x = bf16[8,1,2,128,128]{4,3,2,1,0:T(8,128)(2,1)S(1)} all-to-all(bf16[8,1,2,128,128]{4,3,2,1,0:T(8,128)(2,1)S(1)} %bitcast.9), channel_id=1, replica_groups=mesh['plane'=4,'sub'=2,'tok'=4] {'sub','tok'}, dimensions={0} | all-to-all | bytes 1048576 | tf_op jit(solution)/shard_map/all_to_all | solution.py:35
  74.6 0.8 %last.1 = bf16[1,2,128,1024]{3,2,1,0:T(8,128)(2,1)} custom-call(bf16[8,1,2,128,128]{4,3,2,1,0:T(8,128)(2,1)S(1)} %all_to_all.15.x), custom_call_target="tpu_custom_call" | custom-call | bytes 1048576 | tf_op jit(solution)/shard_map/last/pallas_call | solution.py:342
  (3 shorter events, 0.0 us)
Async XLA Ops:
  1.0 11.4 %collective-permute-start = (bf16[1,2,64,1024]{3,2,1,0:T(8,128)(2,1)S(1)}, bf16[1,2,64,1024]{3,2,1,0:T(8,128)(2,1)S(1)}, u32[]{:S(2)}, u32[]{:S(2)}) collective-permute-start(bf16[1,2,64,1024]{3,2,1,0:T(8,128)(2,1)S(1)} %slice_bitcast_fusion.refs_2_), channel_id=1, source_target_pairs={{24,0},{0,8},{8,16},{16,24},{25,1},{1,9},{9,17},{17,25},{26,2},{2,... | collective-permute-start | bytes 786440 | tf_op jit(solution)/shard_map/ppermute | solution.py:31
  4.0 10.1 %copy-start.2 = (s32[1,2,4,4]{3,2,1,0:T(4,128)S(1)}, s32[1,2,4,4]{3,2,1,0:T(4,128)}, u32[]{:S(2)}) copy-start(s32[1,2,4,4]{3,2,1,0:T(4,128)} %param.9) | copy-start | bytes 388
  4.0 10.2 %copy-start.3 = (s32[1,2]{1,0:T(1,128)S(1)}, s32[1,2]{1,0:T(1,128)}, u32[]{:S(2)}) copy-start(s32[1,2]{1,0:T(1,128)} %param.10) | copy-start | bytes 28
  6.0 16.3 %all-to-all-start = ((bf16[8,1,3,128,128]{4,3,2,1,0:T(8,128)(2,1)}), bf16[8,1,3,128,128]{4,3,2,1,0:T(8,128)(2,1)S(1)}, u32[]{:S(2)}, u32[]{:S(2)}) async-start(bf16[8,1,3,128,128]{4,3,2,1,0:T(8,128)(2,1)} %first.1), calls=%async_computation | async-start | bytes 1572864 | tf_op jit(solution)/shard_map/all_to_all | solution.py:35
  12.4 7.5 %collective-permute-start.1 = (bf16[1,2,64,1024]{3,2,1,0:T(8,128)(2,1)S(1)}, bf16[1,2,64,1024]{3,2,1,0:T(8,128)(2,1)S(1)}, u32[]{:S(2)}, u32[]{:S(2)}) collective-permute-start(bf16[1,2,64,1024]{3,2,1,0:T(8,128)(2,1)S(1)} %slice_bitcast_fusion.refs_2_), channel_id=1, source_target_pairs={{8,0},{16,8},{24,16},{0,24},{9,1},{17,9},{25,17},{1,25},{10,2},{18... | collective-permute-start | bytes 786440 | tf_op jit(solution)/shard_map/ppermute | solution.py:31
  14.3 12.0 %copy-start = (bf16[1,2,128,1024]{3,2,1,0:T(8,128)(2,1)S(1)}, bf16[1,2,128,1024]{3,2,1,0:T(8,128)(2,1)}, u32[]{:S(2)}) copy-start(bf16[1,2,128,1024]{3,2,1,0:T(8,128)(2,1)} %refs_0_.1) | copy-start | bytes 1572868
  14.3 12.0 %copy-start.1 = (s32[8,2]{0,1:T(2,128)S(1)}, s32[8,2]{0,1:T(2,128)}, u32[]{:S(2)}) copy-start(s32[8,2]{0,1:T(2,128)} %param.11) | copy-start | bytes 196
  14.3 5.6 %collective-permute-start.2 = (s32[34]{0:T(128)S(1)}, s32[34]{0:T(128)S(1)}, u32[]{:S(2)}, u32[]{:S(2)}) collective-permute-start(s32[34]{0:T(128)S(1)} %pad_add_fusion.own), channel_id=1, source_target_pairs={{0,4},{4,0},{1,5},{5,1},{2,6},{6,2},{3,7},{7,3},{8,12},{12,8},{9,1... | collective-permute-start | bytes 416 | tf_op jit(solution)/shard_map/ppermute | solution.py:372
  22.4 16.8 %collective-permute-start.3 = (bf16[8,2,128,128]{3,2,1,0:T(8,128)(2,1)S(1)}, bf16[8,2,128,128]{3,2,1,0:T(8,128)(2,1)}, u32[]{:S(2)}, u32[]{:S(2)}) collective-permute-start(bf16[8,2,128,128]{3,2,1,0:T(8,128)(2,1)S(1)} %get-tuple-element.21.refs_1_), channel_id=1, source_target_pairs={{24,0},{0,8},{8,16},{16,24},{25,1},{1,9},{9,17},{17,25},{26,2},{2,... | collective-permute-start | bytes 1572872 | tf_op jit(solution)/shard_map/ppermute | solution.py:31
  24.0 25.4 %collective-permute-start.4 = (bf16[8,2,128,128]{3,2,1,0:T(8,128)(2,1)S(1)}, bf16[8,2,128,128]{3,2,1,0:T(8,128)(2,1)}, u32[]{:S(2)}, u32[]{:S(2)}) collective-permute-start(bf16[8,2,128,128]{3,2,1,0:T(8,128)(2,1)S(1)} %get-tuple-element.21.refs_1_), channel_id=1, source_target_pairs={{8,0},{16,8},{24,16},{0,24},{9,1},{17,9},{25,17},{1,25},{10,2},{18... | collective-permute-start | bytes 1572872 | tf_op jit(solution)/shard_map/ppermute | solution.py:31
  28.0 21.7 %all-to-all-start.1 = ((bf16[8,1,5,128,128]{4,3,2,1,0:T(8,128)(2,1)}), bf16[8,1,5,128,128]{4,3,2,1,0:T(8,128)(2,1)S(1)}, u32[]{:S(2)}, u32[]{:S(2)}) async-start(bf16[8,1,5,128,128]{4,3,2,1,0:T(8,128)(2,1)} %second.1), calls=%async_computation.1 | async-start | bytes 2621440 | tf_op jit(solution)/shard_map/all_to_all | solution.py:35
  39.2 19.3 %collective-permute-start.5 = (bf16[8,1,128,128]{3,2,1,0:T(8,128)(2,1)S(1)}, bf16[8,1,128,128]{3,2,1,0:T(8,128)(2,1)S(1)}, u32[]{:S(2)}, u32[]{:S(2)}) collective-permute-start(bf16[8,1,128,128]{3,2,1,0:T(8,128)(2,1)S(1)} %get-tuple-element.26.refs_1_), channel_id=1, source_target_pairs={{24,0},{0,8},{8,16},{16,24},{25,1},{1,9},{9,17},{17,25},{26,2},{2,... | collective-permute-start | bytes 786440 | tf_op jit(solution)/shard_map/ppermute | solution.py:31
  45.3 13.2 %collective-permute-start.6 = (bf16[8,1,128,128]{3,2,1,0:T(8,128)(2,1)S(1)}, bf16[8,1,128,128]{3,2,1,0:T(8,128)(2,1)S(1)}, u32[]{:S(2)}, u32[]{:S(2)}) collective-permute-start(bf16[8,1,128,128]{3,2,1,0:T(8,128)(2,1)S(1)} %get-tuple-element.26.refs_1_), channel_id=1, source_target_pairs={{8,0},{16,8},{24,16},{0,24},{9,1},{17,9},{25,17},{1,25},{10,2},{18... | collective-permute-start | bytes 786440 | tf_op jit(solution)/shard_map/ppermute | solution.py:31

commit v14 on v12

--- a/solution.py
+++ b/solution.py
@@ -91,17 +91,22 @@
         for s in range(2):
             for m in range(tiles):
                 there = stage.at[2 * i + s, m, pl.ds(0, rows)]
-                copy = pltpu.make_async_copy(
-                    src.at[0, s, pl.ds(m * TILE + row, rows)], there, stage_sem.at[2 * i + s, m]
-                )
-                copy.start()
-                fetched.append((i, s, m, there, copy))
+                copies = [
+                    pltpu.make_async_copy(
+                        src.at[0, s, pl.ds(m * TILE + row + at, rows // 2)],
+                        there.at[pl.ds(at, rows // 2)], stage_sem.at[2 * i + s, m, k],
+                    ) for k, at in enumerate((0, rows // 2))
+                ]
+                for copy in copies:
+                    copy.start()
+                fetched.append((i, s, m, there, copies))
     ask.wait()
     view = lax.axis_index("plane") * plan.sub + lax.axis_index("sub")
     lead = slots[0, view]
-    for i, s, m, there, copy in fetched:
+    for i, s, m, there, copies in fetched:
         branch = jnp.where(lead == s, 0, 1)
-        copy.wait()
+        for copy in copies:
+            copy.wait()
         for w in range(ways):
             if i == 0:
                 to = out.at[w, m, 0, pl.ds(pl.multiple_of(branch * half, half), half)]
@@ -411,7 +416,7 @@
             functools.partial(first_kernel, plan), "first",
             jax.ShapeDtypeStruct((ways, tiles, 3, TILE, share), dtype), [ANY] * 3, ANY,
             [pltpu.VMEM((4, tiles, TILE, width), dtype), pltpu.SMEM(slots.shape, jnp.int32),
-             pltpu.SemaphoreType.DMA((4, tiles)), sem, sem],
+             pltpu.SemaphoreType.DMA((4, tiles, 2)), sem, sem],
             (slots, keys, values), moved=3 * size, mib=62,
         )
     else:

time: 75.7 us -> 75.8 us (level)
  no operation moved by 1% of the time
where the time goes in v14:
time: 75.8 us; the launch traced here: 75.4 us
  starting transfers between devices  23.6 us (31%)
  waiting for transfers between devices  21.2 us (28%)
  Pallas kernels  16.1 us (21%)
  blocking collectives  13.3 us (18%)
  local copies, waits for them, and re-layouts  1.07 us (1%)
    ppermute x6, waiting for transfers between devices, from_plane(): return lax.ppermute(x, 'plane', [((i + by) % size, i) for i in range(size)])  18.5 us
    pallas_call x9, Pallas kernels, call(): pl.pallas_call(kernel, out_shape=out_shape, in_specs=in_specs, out_specs=...  16.1 us
    ppermute x6, starting transfers between devices, from_plane(): return lax.ppermute(x, 'plane', [((i + by) % size, i) for i in range(size)])  14.8 us
    all_to_all x1, blocking collectives, exchange(): return lax.all_to_all(x, GROUP, split_axis=0, concat_axis=0, tiled=True)  13.3 us
    all_to_all x2, starting transfers between devices, exchange(): return lax.all_to_all(x, GROUP, split_axis=0, concat_axis=0, tiled=True)  7.32 us
    all_to_all x2, waiting for transfers between devices, exchange(): return lax.all_to_all(x, GROUP, split_axis=0, concat_axis=0, tiled=True)  2.75 us
    ppermute x1, starting transfers between devices, local(): other = lax.ppermute(own, 'sub', [(0, 1), (1, 0)])  1.54 us
  transfers between devices with their start and end apart: 9, of which 6 were waited for; matrix products, arithmetic and copies ran while one was open for 0% of the time, Pallas kernels for 16%

profile of v14, /device:TPU:0, one launch (start us, length us, event | category | flops | bytes accessed | tf_op | source)
XLA Modules:
  0.0 75.4 jit_solution(14437218239436670346)
XLA Ops:
  0.0 1.0 %slice_bitcast_fusion.refs_2_ = bf16[1,2,64,1024]{3,2,1,0:T(8,128)(2,1)S(1)} fusion(bf16[1,2,1,128,1024]{4,3,1,2,0:T(8,128)(2,1)} %bitcast.14), kind=kLoop, calls=%fused_computation | loop fusion | bytes 524288 | tf_op jit(solution)/shard_map/reshape | solution.py:412
  1.0 3.1 %collective-permute-start = (bf16[1,2,64,1024]{3,2,1,0:T(8,128)(2,1)S(1)}, bf16[1,2,64,1024]{3,2,1,0:T(8,128)(2,1)S(1)}, u32[]{:S(2)}, u32[]{:S(2)}) collective-permute-start(bf16[1,2,64,1024]{3,2,1,0:T(8,128)(2,1)S(1)} %slice_bitcast_fusion.refs_2_), channel_id=1, source_target_pairs={{24,0},{0,8},{8,16},{16,24},{25,1},{1,9},{9,17},{17,25},{26,2},{2,... | collective-permute-start | bytes 786440 | tf_op jit(solution)/shard_map/ppermute | solution.py:31
  4.0 0.0 copy-start.2
  4.0 0.0 copy-start.3
  4.1 2.0 %first.1 = bf16[8,1,3,128,128]{4,3,2,1,0:T(8,128)(2,1)} custom-call(s32[2,8]{1,0:T(2,128)} %bitcast.11, bf16[1,2,128,1024]{3,2,1,0:T(8,128)(2,1)} %keys.1, bf16[1,2,128,1024]{3,2,1,0:T(8,128)(2,1)} %values.1), custom_call_target="tpu_custom_call" | custom-call | bytes 1572864 | tf_op jit(solution)/shard_map/first/pallas_call | solution.py:346
  6.1 3.7 %all-to-all-start = ((bf16[8,1,3,128,128]{4,3,2,1,0:T(8,128)(2,1)}), bf16[8,1,3,128,128]{4,3,2,1,0:T(8,128)(2,1)S(1)}, u32[]{:S(2)}, u32[]{:S(2)}) async-start(bf16[8,1,3,128,128]{4,3,2,1,0:T(8,128)(2,1)} %first.1), calls=%async_computation | async-start | bytes 1572864 | tf_op jit(solution)/shard_map/all_to_all | solution.py:35
  9.8 2.6 %collective-permute-done.refs_0_.refs_1_ = bf16[1,2,64,1024]{3,2,1,0:T(8,128)(2,1)S(1)} collective-permute-done((bf16[1,2,64,1024]{3,2,1,0:T(8,128)(2,1)S(1)}, bf16[1,2,64,1024]{3,2,1,0:T(8,128)(2,1)S(1)}, u32[]{:S(2)}, u32[]{:S(2)}) %collective-permute-start) | collective-permute-done | bytes 262176 | tf_op jit(solution)/shard_map/ppermute | solution.py:31
  12.4 1.7 %collective-permute-start.1 = (bf16[1,2,64,1024]{3,2,1,0:T(8,128)(2,1)S(1)}, bf16[1,2,64,1024]{3,2,1,0:T(8,128)(2,1)S(1)}, u32[]{:S(2)}, u32[]{:S(2)}) collective-permute-start(bf16[1,2,64,1024]{3,2,1,0:T(8,128)(2,1)S(1)} %slice_bitcast_fusion.refs_2_), channel_id=1, source_target_pairs={{8,0},{16,8},{24,16},{0,24},{9,1},{17,9},{25,17},{1,25},{10,2},{18... | collective-permute-start | bytes 786440 | tf_op jit(solution)/shard_map/ppermute | solution.py:31
  14.1 0.0 copy-done.2
  14.1 0.1 reshape.24
  14.2 0.0 copy-done.3
  14.2 0.1 pad_add_fusion.own
  14.3 0.0 copy-start
  14.3 0.0 copy-start.1
  14.3 1.5 %collective-permute-start.2 = (s32[34]{0:T(128)S(1)}, s32[34]{0:T(128)S(1)}, u32[]{:S(2)}, u32[]{:S(2)}) collective-permute-start(s32[34]{0:T(128)S(1)} %pad_add_fusion.own), channel_id=1, source_target_pairs={{0,4},{4,0},{1,5},{5,1},{2,6},{6,2},{3,7},{7,3},{8,12},{12,8},{9,1... | collective-permute-start | bytes 416 | tf_op jit(solution)/shard_map/ppermute | solution.py:376
  15.8 4.0 %collective-permute-done.1.refs_1_.refs_3_ = bf16[1,2,64,1024]{3,2,1,0:T(8,128)(2,1)S(1)} collective-permute-done((bf16[1,2,64,1024]{3,2,1,0:T(8,128)(2,1)S(1)}, bf16[1,2,64,1024]{3,2,1,0:T(8,128)(2,1)S(1)}, u32[]{:S(2)}, u32[]{:S(2)}) %collective-permute-start.1) | collective-permute-done | bytes 262176 | tf_op jit(solution)/shard_map/ppermute | solution.py:31
  19.9 0.0 collective-permute-done.2.other
  19.9 2.5 %all-to-all-done = bf16[8,1,3,128,128]{4,3,2,1,0:T(8,128)(2,1)S(1)} async-done(((bf16[8,1,3,128,128]{4,3,2,1,0:T(8,128)(2,1)}), bf16[8,1,3,128,128]{4,3,2,1,0:T(8,128)(2,1)S(1)}, u32[]{:S(2)}, u32[]{:S(2)}) %all-to-all-start) | async-done | bytes 786464 | tf_op jit(solution)/shard_map/all_to_all | solution.py:35
  22.4 0.1 split.1
  22.5 1.7 %collective-permute-start.3 = (bf16[8,2,128,128]{3,2,1,0:T(8,128)(2,1)S(1)}, bf16[8,2,128,128]{3,2,1,0:T(8,128)(2,1)}, u32[]{:S(2)}, u32[]{:S(2)}) collective-permute-start(bf16[8,2,128,128]{3,2,1,0:T(8,128)(2,1)S(1)} %get-tuple-element.21.refs_1_), channel_id=1, source_target_pairs={{24,0},{0,8},{8,16},{16,24},{25,1},{1,9},{9,17},{17,25},{26,2},{2,... | collective-permute-start | bytes 1572872 | tf_op jit(solution)/shard_map/ppermute | solution.py:31
  24.1 2.2 %collective-permute-start.4 = (bf16[8,2,128,128]{3,2,1,0:T(8,128)(2,1)S(1)}, bf16[8,2,128,128]{3,2,1,0:T(8,128)(2,1)}, u32[]{:S(2)}, u32[]{:S(2)}) collective-permute-start(bf16[8,2,128,128]{3,2,1,0:T(8,128)(2,1)S(1)} %get-tuple-element.21.refs_1_), channel_id=1, source_target_pairs={{8,0},{16,8},{24,16},{0,24},{9,1},{17,9},{25,17},{1,25},{10,2},{18... | collective-permute-start | bytes 1572872 | tf_op jit(solution)/shard_map/ppermute | solution.py:31
  26.3 0.0 copy-done
  26.3 0.0 copy-done.1
  26.3 1.7 %second.1 = bf16[8,1,5,128,128]{4,3,2,1,0:T(8,128)(2,1)} custom-call(s32[2,8]{1,0:T(2,128)S(1)} %bitcast.12, f32[8,128]{1,0:T(8,128)S(1)} %mark.3.mark_ref, bf16[1,2,128,1024]{3,2,1,0:T(8,128)(2,1)S(1)} %copy-done, bf16[1,2,64,1024]{3,2,1,0:T(8,128)(2,1)S(1)} %collective-permute-done.refs_0_.refs_1_, bf16[1,2,64,1024]{3,2,1,0:T(8,128)(2,1)S(1)} %slice_bitcast_fusion.refs_2_, ...), custom_call_target="tpu_custom_call" | custom-call | bytes 2621440 | tf_op jit(solution)/shard_map/second/pallas_call | solution.py:346
  28.0 3.6 %all-to-all-start.1 = ((bf16[8,1,5,128,128]{4,3,2,1,0:T(8,128)(2,1)}), bf16[8,1,5,128,128]{4,3,2,1,0:T(8,128)(2,1)S(1)}, u32[]{:S(2)}, u32[]{:S(2)}) async-start(bf16[8,1,5,128,128]{4,3,2,1,0:T(8,128)(2,1)} %second.1), calls=%async_computation.1 | async-start | bytes 2621440 | tf_op jit(solution)/shard_map/all_to_all | solution.py:35
  31.6 7.7 %collective-permute-done.3.refs_0_ = bf16[8,2,128,128]{3,2,1,0:T(8,128)(2,1)} collective-permute-done((bf16[8,2,128,128]{3,2,1,0:T(8,128)(2,1)S(1)}, bf16[8,2,128,128]{3,2,1,0:T(8,128)(2,1)}, u32[]{:S(2)}, u32[]{:S(2)}) %collective-permute-start.3) | collective-permute-done | bytes 524320 | tf_op jit(solution)/shard_map/ppermute | solution.py:31
  39.3 6.1 %collective-permute-start.5 = (bf16[8,1,128,128]{3,2,1,0:T(8,128)(2,1)S(1)}, bf16[8,1,128,128]{3,2,1,0:T(8,128)(2,1)S(1)}, u32[]{:S(2)}, u32[]{:S(2)}) collective-permute-start(bf16[8,1,128,128]{3,2,1,0:T(8,128)(2,1)S(1)} %get-tuple-element.26.refs_1_), channel_id=1, source_target_pairs={{24,0},{0,8},{8,16},{16,24},{25,1},{1,9},{9,17},{17,25},{26,2},{2,... | collective-permute-start | bytes 786440 | tf_op jit(solution)/shard_map/ppermute | solution.py:31
  45.4 0.0 collective-permute-start.6
  45.4 4.2 %collective-permute-done.4.refs_0_.refs_2_ = bf16[8,2,128,128]{3,2,1,0:T(8,128)(2,1)} collective-permute-done((bf16[8,2,128,128]{3,2,1,0:T(8,128)(2,1)S(1)}, bf16[8,2,128,128]{3,2,1,0:T(8,128)(2,1)}, u32[]{:S(2)}, u32[]{:S(2)}) %collective-permute-start.4) | collective-permute-done | bytes 524320 | tf_op jit(solution)/shard_map/ppermute | solution.py:31
  49.5 0.2 all-to-all-done.1
  49.8 8.5 %core.1 = (bf16[8,1,128,128]{3,2,1,0:T(8,128)(2,1)S(1)}, bf16[8,256,1152]{2,1,0:T(8,128)(2,1)S(1)}) custom-call(s32[34]{0:T(128)S(1)} %pad_add_fusion.own, s32[34]{0:T(128)S(1)} %collective-permute-done.2.other, bf16[8,5,128,128]{3,2,1,0:T(8,128)(2,1)S(1)} %bitcast.10, bf16[8,2,128,128]{3,2,1,0:T(8,128)(2,1)} %collective-permute-done.3.refs_0_, ...), custom_call_target="tpu_custom_call" | custom-call | flops 905969664 | bytes 1048576 | tf_op jit(solution)/shard_map/core/pallas_call | solution.py:346
  58.3 0.0 collective-permute-done.5.refs_0_
  58.3 0.0 collective-permute-done.6.refs_2_
  58.3 3.1 %weigh.1 = bf16[8,2,128,128]{3,2,1,0:T(8,128)(2,1)S(1)} custom-call(s32[34]{0:T(128)S(1)} %pad_add_fusion.own, s32[34]{0:T(128)S(1)} %collective-permute-done.2.other, s32[2,8]{1,0:T(2,128)S(1)} %bitcast.13, bf16[8,256,1152]{2,1,0:T(8,128)(2,1)S(1)} %get-tuple-element.24.expo, bf16[8,1,128,128]{3,2,1,0:T(8,128)(2,1)S(1)} %get-tuple-element.25.done, ...), custom_call_target="tpu_custom_call" | custom-call | flops 301989888 | bytes 1048576 | tf_op jit(solution)/shard_map/weigh/pallas_call | solution.py:346
  61.4 13.3 %all_to_all.15.x = bf16[8,1,2,128,128]{4,3,2,1,0:T(8,128)(2,1)S(1)} all-to-all(bf16[8,1,2,128,128]{4,3,2,1,0:T(8,128)(2,1)S(1)} %bitcast.9), channel_id=1, replica_groups=mesh['plane'=4,'sub'=2,'tok'=4] {'sub','tok'}, dimensions={0} | all-to-all | bytes 1048576 | tf_op jit(solution)/shard_map/all_to_all | solution.py:35
  74.6 0.8 %last.1 = bf16[1,2,128,1024]{3,2,1,0:T(8,128)(2,1)} custom-call(bf16[8,1,2,128,128]{4,3,2,1,0:T(8,128)(2,1)S(1)} %all_to_all.15.x), custom_call_target="tpu_custom_call" | custom-call | bytes 1048576 | tf_op jit(solution)/shard_map/last/pallas_call | solution.py:346
  (3 shorter events, 0.0 us)
Async XLA Ops:
  1.0 11.4 %collective-permute-start = (bf16[1,2,64,1024]{3,2,1,0:T(8,128)(2,1)S(1)}, bf16[1,2,64,1024]{3,2,1,0:T(8,128)(2,1)S(1)}, u32[]{:S(2)}, u32[]{:S(2)}) collective-permute-start(bf16[1,2,64,1024]{3,2,1,0:T(8,128)(2,1)S(1)} %slice_bitcast_fusion.refs_2_), channel_id=1, source_target_pairs={{24,0},{0,8},{8,16},{16,24},{25,1},{1,9},{9,17},{17,25},{26,2},{2,... | collective-permute-start | bytes 786440 | tf_op jit(solution)/shard_map/ppermute | solution.py:31
  4.0 10.1 %copy-start.2 = (s32[1,2,4,4]{3,2,1,0:T(4,128)S(1)}, s32[1,2,4,4]{3,2,1,0:T(4,128)}, u32[]{:S(2)}) copy-start(s32[1,2,4,4]{3,2,1,0:T(4,128)} %param.9) | copy-start | bytes 388
  4.0 10.2 %copy-start.3 = (s32[1,2]{1,0:T(1,128)S(1)}, s32[1,2]{1,0:T(1,128)}, u32[]{:S(2)}) copy-start(s32[1,2]{1,0:T(1,128)} %param.10) | copy-start | bytes 28
  6.1 16.3 %all-to-all-start = ((bf16[8,1,3,128,128]{4,3,2,1,0:T(8,128)(2,1)}), bf16[8,1,3,128,128]{4,3,2,1,0:T(8,128)(2,1)S(1)}, u32[]{:S(2)}, u32[]{:S(2)}) async-start(bf16[8,1,3,128,128]{4,3,2,1,0:T(8,128)(2,1)} %first.1), calls=%async_computation | async-start | bytes 1572864 | tf_op jit(solution)/shard_map/all_to_all | solution.py:35
  12.4 7.5 %collective-permute-start.1 = (bf16[1,2,64,1024]{3,2,1,0:T(8,128)(2,1)S(1)}, bf16[1,2,64,1024]{3,2,1,0:T(8,128)(2,1)S(1)}, u32[]{:S(2)}, u32[]{:S(2)}) collective-permute-start(bf16[1,2,64,1024]{3,2,1,0:T(8,128)(2,1)S(1)} %slice_bitcast_fusion.refs_2_), channel_id=1, source_target_pairs={{8,0},{16,8},{24,16},{0,24},{9,1},{17,9},{25,17},{1,25},{10,2},{18... | collective-permute-start | bytes 786440 | tf_op jit(solution)/shard_map/ppermute | solution.py:31
  14.3 12.1 %copy-start = (bf16[1,2,128,1024]{3,2,1,0:T(8,128)(2,1)S(1)}, bf16[1,2,128,1024]{3,2,1,0:T(8,128)(2,1)}, u32[]{:S(2)}) copy-start(bf16[1,2,128,1024]{3,2,1,0:T(8,128)(2,1)} %refs_0_.1) | copy-start | bytes 1572868
  14.3 12.1 %copy-start.1 = (s32[8,2]{0,1:T(2,128)S(1)}, s32[8,2]{0,1:T(2,128)}, u32[]{:S(2)}) copy-start(s32[8,2]{0,1:T(2,128)} %param.11) | copy-start | bytes 196
  14.3 5.6 %collective-permute-start.2 = (s32[34]{0:T(128)S(1)}, s32[34]{0:T(128)S(1)}, u32[]{:S(2)}, u32[]{:S(2)}) collective-permute-start(s32[34]{0:T(128)S(1)} %pad_add_fusion.own), channel_id=1, source_target_pairs={{0,4},{4,0},{1,5},{5,1},{2,6},{6,2},{3,7},{7,3},{8,12},{12,8},{9,1... | collective-permute-start | bytes 416 | tf_op jit(solution)/shard_map/ppermute | solution.py:376
  22.5 16.8 %collective-permute-start.3 = (bf16[8,2,128,128]{3,2,1,0:T(8,128)(2,1)S(1)}, bf16[8,2,128,128]{3,2,1,0:T(8,128)(2,1)}, u32[]{:S(2)}, u32[]{:S(2)}) collective-permute-start(bf16[8,2,128,128]{3,2,1,0:T(8,128)(2,1)S(1)} %get-tuple-element.21.refs_1_), channel_id=1, source_target_pairs={{24,0},{0,8},{8,16},{16,24},{25,1},{1,9},{9,17},{17,25},{26,2},{2,... | collective-permute-start | bytes 1572872 | tf_op jit(solution)/shard_map/ppermute | solution.py:31
  24.1 25.4 %collective-permute-start.4 = (bf16[8,2,128,128]{3,2,1,0:T(8,128)(2,1)S(1)}, bf16[8,2,128,128]{3,2,1,0:T(8,128)(2,1)}, u32[]{:S(2)}, u32[]{:S(2)}) collective-permute-start(bf16[8,2,128,128]{3,2,1,0:T(8,128)(2,1)S(1)} %get-tuple-element.21.refs_1_), channel_id=1, source_target_pairs={{8,0},{16,8},{24,16},{0,24},{9,1},{17,9},{25,17},{1,25},{10,2},{18... | collective-permute-start | bytes 1572872 | tf_op jit(solution)/shard_map/ppermute | solution.py:31
  28.0 21.7 %all-to-all-start.1 = ((bf16[8,1,5,128,128]{4,3,2,1,0:T(8,128)(2,1)}), bf16[8,1,5,128,128]{4,3,2,1,0:T(8,128)(2,1)S(1)}, u32[]{:S(2)}, u32[]{:S(2)}) async-start(bf16[8,1,5,128,128]{4,3,2,1,0:T(8,128)(2,1)} %second.1), calls=%async_computation.1 | async-start | bytes 2621440 | tf_op jit(solution)/shard_map/all_to_all | solution.py:35
  39.3 19.0 %collective-permute-start.5 = (bf16[8,1,128,128]{3,2,1,0:T(8,128)(2,1)S(1)}, bf16[8,1,128,128]{3,2,1,0:T(8,128)(2,1)S(1)}, u32[]{:S(2)}, u32[]{:S(2)}) collective-permute-start(bf16[8,1,128,128]{3,2,1,0:T(8,128)(2,1)S(1)} %get-tuple-element.26.refs_1_), channel_id=1, source_target_pairs={{24,0},{0,8},{8,16},{16,24},{25,1},{1,9},{9,17},{17,25},{26,2},{2,... | collective-permute-start | bytes 786440 | tf_op jit(solution)/shard_map/ppermute | solution.py:31
  45.4 12.9 %collective-permute-start.6 = (bf16[8,1,128,128]{3,2,1,0:T(8,128)(2,1)S(1)}, bf16[8,1,128,128]{3,2,1,0:T(8,128)(2,1)S(1)}, u32[]{:S(2)}, u32[]{:S(2)}) collective-permute-start(bf16[8,1,128,128]{3,2,1,0:T(8,128)(2,1)S(1)} %get-tuple-element.26.refs_1_), channel_id=1, source_target_pairs={{8,0},{16,8},{24,16},{0,24},{9,1},{17,9},{25,17},{1,25},{10,2},{18... | collective-permute-start | bytes 786440 | tf_op jit(solution)/shard_map/ppermute | solution.py:31
